TPU v7x, 32 devices: a whole 2x2x4 slice. The times are simulated.
32 devices in a mesh: row: 8 (over y, x, core), col: 4 (over z).
Axes of the slice: x: 2, y: 2, z: 4, core: 2. Of those that a mesh axis runs over, the one named last changes fastest.
Arguments:
- frames: float32 [64, 16384], P(None, ('row', 'col')), may hold values from -8 to 8
- start: float32 [32, 16384], P(None, ('row', 'col')), may hold values from -6 to 6
Outputs:
- basis: float32 [32, 16384], P(None, ('row', 'col'))
All inputs are finite; a program needn't handle non-finite values.
Results may differ from a plain program's by a relative error of at most 0.0003.
Values sent between devices are 32-bit elements; how exact they have to be, the bound alone decides.
No kernel may reach another device: no remote copies, remote signals or barrier semaphores. Data moves between devices by JAX's collectives and lax.ppermute only.
A program may use at most 320 MiB of HBM per device.

v0:
```python
import functools
import math
import jax
import jax.numpy as jnp
from jax import lax
from jax.experimental import pallas as pl
from jax.experimental.pallas import tpu as pltpu
from jax.sharding import PartitionSpec as P

VMEM = pl.BlockSpec(memory_space=pltpu.VMEM)
ROWS_BY_COLUMNS = (((1,), (0,)), ((), ()))
ROWS_BY_ROWS = (((1,), (1,)), ((), ()))
RESIDENT_BYTES = 36 << 20
DEGREE_ROWS = 16


def call(body, out_shape, operands, scratch=(), limit=20 << 20, name=None):
    return pl.pallas_call(
        body,
        out_shape=out_shape,
        in_specs=[VMEM] * len(operands),
        out_specs=jax.tree.map(lambda _: VMEM, out_shape),
        scratch_shapes=list(scratch),
        compiler_params=pltpu.CompilerParams(vmem_limit_bytes=limit),
        name=name,
    )(*operands)


def f32(*shape):
    return jax.ShapeDtypeStruct(shape, jnp.float32)


def bf16(*shape):
    return jax.ShapeDtypeStruct(shape, jnp.bfloat16)


def halves(values):
    high = values.astype(jnp.bfloat16)
    return high, (values - high.astype(jnp.float32)).astype(jnp.bfloat16)


def thirds(values):
    high = values.astype(jnp.bfloat16).astype(jnp.float32)
    middle = (values - high).astype(jnp.bfloat16).astype(jnp.float32)
    return high, middle, values - high - middle


def build_kernel(*refs, row_parts, column_parts, tile_rows, tile_columns):
    row_refs = refs[:row_parts]
    column_refs = refs[row_parts : row_parts + column_parts]
    outs = refs[row_parts + column_parts :]
    high_refs, low_refs = outs[:row_parts], outs[row_parts : 2 * row_parts]
    sums_ref, left, right, totals = outs[2 * row_parts :]
    features, width = row_refs[0].shape
    columns = column_parts * width
    scale = math.sqrt(math.log2(math.e) / (0.25 * features))

    for part, ref in enumerate(row_refs):
        span = slice(part * width, (part + 1) * width)
        points = ref[...].T * scale
        high, low = halves(points)
        left[span, 0:features] = high
        left[span, features : 2 * features] = high
        left[span, 2 * features : 3 * features] = low
        first, second, third = thirds(0.5 * jnp.sum(points * points, axis=1, keepdims=True))
        lane = lax.broadcasted_iota(jnp.int32, (width, features), 1)
        tail = jnp.where(lane == 0, first, jnp.where(lane == 1, second, jnp.where(lane == 2, third, 0.0)))
        tail = jnp.where((lane > 2) & (lane < 6), -1.0, tail)
        left[span, 3 * features : 4 * features] = tail.astype(jnp.bfloat16)
    for part, ref in enumerate(column_refs):
        span = slice(part * width, (part + 1) * width)
        points = ref[...] * scale
        high, low = halves(points)
        right[0:features, span] = high
        right[features : 2 * features, span] = low
        right[2 * features : 3 * features, span] = high
        first, second, third = thirds(0.5 * jnp.sum(points * points, axis=0, keepdims=True))
        line = lax.broadcasted_iota(jnp.int32, (features, width), 0)
        tail = jnp.where(line == 3, first, jnp.where(line == 4, second, jnp.where(line == 5, third, 0.0)))
        tail = jnp.where(line < 3, -1.0, tail)
        right[3 * features : 4 * features, span] = tail.astype(jnp.bfloat16)

    for part in range(row_parts):
        high_ref, low_ref = high_refs[part], low_refs[part]

        def step(index, _):
            start = pl.multiple_of(index * tile_rows, tile_rows)
            points = left[pl.ds(part * width + start, tile_rows), :]
            total = jnp.zeros((tile_rows, 128), jnp.float32)
            for first in range(0, columns, tile_columns):
                exponent = lax.dot_general(
                    points,
                    right[:, first : first + tile_columns],
                    ROWS_BY_COLUMNS,
                    preferred_element_type=jnp.float32,
                )
                values = jnp.exp2(exponent)
                high = values.astype(jnp.bfloat16)
                high_ref[pl.ds(start, tile_rows), first : first + tile_columns] = high
                low_ref[pl.ds(start, tile_rows), first : first + tile_columns] = (
                    values - high.astype(jnp.float32)
                ).astype(jnp.bfloat16)
                for lane in range(0, tile_columns, 128):
                    total = total + values[:, lane : lane + 128]
            totals[pl.ds(start, tile_rows), :] = total
            return 0

        lax.fori_loop(0, width // tile_rows, step, 0)
        sums_ref[part : part + 1, :] = jnp.sum(totals[...].T, axis=0, keepdims=True)
    for part in range(row_parts, sums_ref.shape[0]):
        sums_ref[part : part + 1, :] = jnp.zeros((1, width), jnp.float32)


def build(row_pieces, column_pieces):
    features, width = row_pieces[0].shape
    row_parts, column_parts = len(row_pieces), len(column_pieces)
    columns = column_parts * width
    out_shape = (bf16(width, columns),) * (2 * row_parts) + (f32(-(-row_parts // 8) * 8, width),)
    outs = call(
        functools.partial(
            build_kernel, row_parts=row_parts, column_parts=column_parts, tile_rows=256, tile_columns=512
        ),
        out_shape,
        (*row_pieces, *column_pieces),
        scratch=(
            pltpu.VMEM((row_parts * width, 4 * features), jnp.bfloat16),
            pltpu.VMEM((4 * features, columns), jnp.bfloat16),
            pltpu.VMEM((width, 128), jnp.float32),
        ),
        name="build",
    )
    return outs[:row_parts], outs[row_parts : 2 * row_parts], outs[-1]


def sweep(weights, high_refs, low_refs, out_ref, tile):
    rows = weights.shape[0] // 2
    width = high_refs[0].shape[0]
    kept = out_ref.shape[0]
    for first in range(0, out_ref.shape[1], tile):
        span = slice(first, first + tile)
        total = None
        for part, (high_ref, low_ref) in enumerate(zip(high_refs, low_refs)):
            lines = slice(part * width, (part + 1) * width)
            both = lax.dot_general(
                weights[:, lines], high_ref[:, span], ROWS_BY_COLUMNS, preferred_element_type=jnp.float32
            )
            last = lax.dot_general(
                weights[0:rows, lines], low_ref[:, span], ROWS_BY_COLUMNS, preferred_element_type=jnp.float32
            )
            term = both[:kept] + both[rows : rows + kept] + last[:kept]
            total = term if total is None else total + term
        out_ref[:, span] = total


def first_kernel(*refs, parts, peers):
    sums_refs, start_refs = refs[:peers], refs[peers : peers + parts]
    high_refs = refs[peers + parts : peers + 2 * parts]
    low_refs = refs[peers + 2 * parts : peers + 3 * parts]
    out_ref, inverse_ref, weights = refs[peers + 3 * parts :]
    vectors, width = start_refs[0].shape
    rows = weights.shape[0] // 2
    for part in range(parts):
        span = slice(part * width, (part + 1) * width)
        density = sums_refs[0][part : part + 1, :]
        for peer in range(1, peers):
            density = density + sums_refs[peer][part ^ peer : (part ^ peer) + 1, :]
        inverse = 1.0 / density
        if part == 0:
            inverse_ref[...] = inverse
        line = lax.broadcasted_iota(jnp.int32, (rows - vectors, width), 0)
        for first, piece in (
            (0, start_refs[part][...] * inverse),
            (vectors, jnp.where(line == 0, inverse, 0.0)),
        ):
            high, low = halves(piece)
            last = first + piece.shape[0]
            weights[first:last, span] = high
            weights[rows + first : rows + last, span] = low
    sweep(weights, high_refs, low_refs, out_ref, 256)


def second_kernel(*refs, parts):
    piece_refs, high_refs, low_refs = refs[:parts], refs[parts : 2 * parts], refs[2 * parts : 3 * parts]
    out_ref, weights = refs[3 * parts :]
    vectors, width = piece_refs[0].shape
    for part in range(parts):
        span = slice(part * width, (part + 1) * width)
        high, low = halves(piece_refs[part][...])
        weights[0:vectors, span] = high
        weights[vectors:, span] = low
    sweep(weights, high_refs, low_refs, out_ref, 256)


def exact(left, right, dims):
    return lax.dot_general(
        left, right, dims, precision=lax.Precision.HIGHEST, preferred_element_type=jnp.float32
    )


def grown_kernel(*refs):
    inverse_ref, piece_refs, (grown_ref, gram_ref, degree_ref) = refs[0], refs[1:-3], refs[-3:]
    vectors = grown_ref.shape[0]
    total = piece_refs[0][...]
    for ref in piece_refs[1:]:
        total = total + ref[...]
    degree = total[vectors : vectors + 1, :]
    grown = total[0:vectors, :] / degree
    degree_ref[...] = degree
    grown_ref[...] = grown * inverse_ref[...]
    gram_ref[...] = exact(grown, grown, ROWS_BY_ROWS)


def inverse_factor(gram):
    size = gram.shape[0]
    line = lax.broadcasted_iota(jnp.int32, (size, size), 0)
    lane = lax.broadcasted_iota(jnp.int32, (size, size), 1)
    table = jnp.concatenate([gram, jnp.where(line == lane, 1.0, 0.0)], axis=1)
    wide_line = lax.broadcasted_iota(jnp.int32, (size, 2 * size), 0)
    pivots = jnp.zeros((size, 1), jnp.float32)
    tall_line = lax.broadcasted_iota(jnp.int32, (size, 1), 0)
    for step in range(size):
        row = table[step : step + 1, :]
        column = table[:, step : step + 1]
        pivot = row[:, step : step + 1]
        factor = jnp.where(tall_line > step, column * (1.0 / pivot), 0.0)
        pivots = jnp.where(tall_line == step, pivot, pivots)
        table = table - factor * row
    return table[:, size:] * lax.rsqrt(pivots)


def factor_kernel(*refs, count):
    gram = refs[0][...]
    for ref in refs[1:-1]:
        gram = gram + ref[...]
    refs[-1][...] = inverse_factor(gram * (1.0 / count))


def grown_two_kernel(*refs):
    factor_ref, degree_ref, piece_refs, (grown_ref, gram_ref) = refs[0], refs[1], refs[2:-2], refs[-2:]
    total = piece_refs[0][...]
    for ref in piece_refs[1:]:
        total = total + ref[...]
    grown = exact(factor_ref[...], total / degree_ref[...], ROWS_BY_COLUMNS)
    grown_ref[...] = grown
    gram_ref[...] = exact(grown, grown, ROWS_BY_ROWS)


def finish_kernel(*refs, count):
    grown_ref, gram_refs, out_ref = refs[0], refs[1:-1], refs[-1]
    gram = gram_refs[0][...]
    for ref in gram_refs[1:]:
        gram = gram + ref[...]
    out_ref[...] = exact(inverse_factor(gram * (1.0 / count)), grown_ref[...], ROWS_BY_COLUMNS)


def swap(values, axis, mask):
    size = lax.axis_size(axis)
    return lax.ppermute(values, axis, [(index, index ^ mask) for index in range(size)])


def resident_shards(frames, start):
    row_size, column_size = lax.axis_size("row"), lax.axis_size("col")
    count = frames.shape[1] * row_size * column_size
    vectors, width = start.shape
    far = range(2, row_size, 2)

    row_pieces = [frames] + [swap(frames, "col", q) for q in range(1, column_size)]
    column_pieces = {0: frames}
    for p in far:
        column_pieces[p] = swap(frames, "row", p)
    for p in range(0, row_size, 2):
        column_pieces[p ^ 1] = swap(column_pieces[p], "row", 1)
    starts = [start] + [swap(start, "col", q) for q in range(1, column_size)]

    highs, lows, sums = build(row_pieces, [column_pieces[p] for p in range(row_size)])
    all_sums = [sums] + [swap(sums, "col", q) for q in range(1, column_size)]

    def spread(product):
        pieces = [product[:, p * width : (p + 1) * width] for p in range(row_size)]
        others = swap(jnp.concatenate(pieces[1::2], axis=1), "row", 1)
        own = jnp.concatenate(pieces[0::2], axis=1) + others
        pieces = [own[:, p * width : (p + 1) * width] for p in range(row_size // 2)]
        return [pieces[0]] + [swap(pieces[p // 2], "row", p) for p in far]

    def total_gram(gram):
        gram = gram + swap(gram, "row", 1)
        gram = functools.reduce(jnp.add, [swap(gram, "row", p) for p in far], gram)
        return [gram] + [swap(gram, "col", q) for q in range(1, column_size)]

    rows = vectors + DEGREE_ROWS
    columns = row_size * width
    product, inverse = call(
        functools.partial(first_kernel, parts=column_size, peers=column_size),
        (f32(vectors + 8, columns), f32(1, width)),
        (*all_sums, *starts, *highs, *lows),
        scratch=(pltpu.VMEM((2 * rows, column_size * width), jnp.bfloat16),),
        name="first_product",
    )
    weighted, gram, degree = call(
        grown_kernel,
        (f32(vectors, width), f32(vectors, vectors), f32(1, width)),
        (inverse, *spread(product)),
        name="grown",
    )
    pieces = [weighted] + [swap(weighted, "col", q) for q in range(1, column_size)]
    grams = total_gram(gram)
    product = call(
        functools.partial(second_kernel, parts=column_size),
        f32(vectors, columns),
        (*pieces, *highs, *lows),
        scratch=(pltpu.VMEM((2 * vectors, column_size * width), jnp.bfloat16),),
        name="second_product",
    )
    factor = call(
        functools.partial(factor_kernel, count=count), f32(vectors, vectors), grams, name="first_factor"
    )
    grown_two, gram_two = call(
        grown_two_kernel,
        (f32(vectors, width), f32(vectors, vectors)),
        (factor, degree, *spread(product)),
        name="grown_two",
    )
    return call(
        functools.partial(finish_kernel, count=count),
        f32(vectors, width),
        (grown_two, *total_gram(gram_two)),
        name="finish",
    )


def build_block(block_points, block_squares, column_points, column_squares):
    products = lax.dot_general(
        block_points, column_points, (((0,), (0,)), ((), ())), precision=lax.Precision.HIGHEST
    )
    distance = block_squares[:, None] + column_squares[None, :] - 2.0 * products
    return jnp.exp(-distance / (0.5 * block_points.shape[0]))


def stored_shards(frames, start):
    block_points = lax.all_gather(frames, "col", axis=1, tiled=True)
    column_points = lax.all_gather(frames, "row", axis=1, tiled=True)
    block_squares = jnp.sum(block_points * block_points, axis=0)
    column_squares = jnp.sum(column_points * column_points, axis=0)
    frame_count = frames.shape[1] * lax.axis_size("row") * lax.axis_size("col")
    block_rows = block_points.shape[1]
    height = min(512, block_rows)
    stored = [
        build_block(
            block_points[:, first : first + height],
            block_squares[first : first + height],
            column_points,
            column_squares,
        )
        for first in range(0, block_rows, height)
    ]

    def settle(partial_value):
        return lax.psum_scatter(partial_value, "col", scatter_dimension=1, tiled=True)

    def kernel_product(weights):
        spread_weights = lax.all_gather(weights, "row", axis=1, tiled=True)
        return settle(
            jnp.concatenate([exact(spread_weights, part, ROWS_BY_ROWS) for part in stored], axis=1)
        )

    def orthonormal(vectors):
        gram = lax.psum(exact(vectors, vectors, ROWS_BY_ROWS), ("row", "col")) / frame_count
        return jax.scipy.linalg.solve_triangular(jnp.linalg.cholesky(gram), vectors, lower=True)

    sums = jnp.concatenate([jnp.sum(part, axis=1)[None, :] for part in stored], axis=1)
    inverse = 1.0 / settle(sums)
    degree = kernel_product(inverse)
    basis_one = orthonormal(kernel_product(start * inverse) / degree)
    return orthonormal(kernel_product(basis_one * inverse) / degree)


def shards(frames, start):
    row_size, column_size = lax.axis_size("row"), lax.axis_size("col")
    entries = row_size * column_size * frames.shape[1] ** 2
    powers = row_size & (row_size - 1) == 0 and column_size & (column_size - 1) == 0
    if powers and row_size > 1 and 4 * entries <= RESIDENT_BYTES:
        return resident_shards(frames, start)
    return stored_shards(frames, start)


def solution(mesh):
    return jax.shard_map(
        shards,
        mesh=mesh,
        in_specs=(P(None, ("row", "col")), P(None, ("row", "col"))),
        out_specs=P(None, ("row", "col")),
        check_vma=False,
    )
```

profile of v0, /device:TPU:0, one launch (start us, length us, event | category | flops | bytes accessed | tf_op | source)
XLA Modules:
  0.0 118.0 jit_solution(789093832964230742)
XLA Ops:
  0.0 2.9 %collective-permute-start.4 = (f32[64,512]{1,0:T(8,128)}, f32[64,512]{1,0:T(8,128)S(1)}, u32[]{:S(2)}, u32[]{:S(2)}) collective-permute-start(f32[64,512]{1,0:T(8,128)} %refs_4_.2), channel_id=1, source_target_pairs={{0,8},{4,12},{8,0},{12,4},{16,24},{20,28},{24,16},{28,20},{1,9},{5... | collective-permute-start | bytes 393224 | tf_op jit(solution)/shard_map/ppermute | solution.py:258
  2.9 1.5 %collective-permute-start.6 = (f32[64,512]{1,0:T(8,128)}, f32[64,512]{1,0:T(8,128)S(1)}, u32[]{:S(2)}, u32[]{:S(2)}) collective-permute-start(f32[64,512]{1,0:T(8,128)} %refs_4_.2), channel_id=1, source_target_pairs={{0,16},{4,20},{8,24},{12,28},{16,0},{20,4},{24,8},{28,12},{1,17},{... | collective-permute-start | bytes 393224 | tf_op jit(solution)/shard_map/ppermute | solution.py:258
  4.5 2.1 %collective-permute-start = (f32[64,512]{1,0:T(8,128)}, f32[64,512]{1,0:T(8,128)S(1)}, u32[]{:S(2)}, u32[]{:S(2)}) collective-permute-start(f32[64,512]{1,0:T(8,128)} %refs_4_.2), channel_id=1, source_target_pairs={{0,1},{1,0},{2,3},{3,2},{4,5},{5,4},{6,7},{7,6},{8,9},{9,8},{10,11... | collective-permute-start | bytes 393224 | tf_op jit(solution)/shard_map/ppermute | solution.py:258
  6.5 2.6 %collective-permute-start.1 = (f32[64,512]{1,0:T(8,128)}, f32[64,512]{1,0:T(8,128)S(1)}, u32[]{:S(2)}, u32[]{:S(2)}) collective-permute-start(f32[64,512]{1,0:T(8,128)} %refs_4_.2), channel_id=1, source_target_pairs={{0,2},{1,3},{2,0},{3,1},{4,6},{5,7},{6,4},{7,5},{8,10},{9,11},{10,... | collective-permute-start | bytes 393224 | tf_op jit(solution)/shard_map/ppermute | solution.py:258
  9.1 1.8 %collective-permute-start.2 = (f32[64,512]{1,0:T(8,128)}, f32[64,512]{1,0:T(8,128)S(1)}, u32[]{:S(2)}, u32[]{:S(2)}) collective-permute-start(f32[64,512]{1,0:T(8,128)} %refs_4_.2), channel_id=1, source_target_pairs={{0,3},{1,2},{2,1},{3,0},{4,7},{5,6},{6,5},{7,4},{8,11},{9,10},{10,... | collective-permute-start | bytes 393224 | tf_op jit(solution)/shard_map/ppermute | solution.py:258
  11.5 7.3 %collective-permute-done.1.refs_2_ = f32[64,512]{1,0:T(8,128)S(1)} collective-permute-done((f32[64,512]{1,0:T(8,128)}, f32[64,512]{1,0:T(8,128)S(1)}, u32[]{:S(2)}, u32[]{:S(2)}) %collective-permute-start.1) | collective-permute-done | bytes 131104 | tf_op jit(solution)/shard_map/ppermute | solution.py:258
  18.8 2.0 %collective-permute-start.13 = (f32[32,512]{1,0:T(8,128)}, f32[32,512]{1,0:T(8,128)S(1)}, u32[]{:S(2)}, u32[]{:S(2)}) collective-permute-start(f32[32,512]{1,0:T(8,128)} %refs_4_.3), channel_id=1, source_target_pairs={{0,1},{1,0},{2,3},{3,2},{4,5},{5,4},{6,7},{7,6},{8,9},{9,8},{10,11... | collective-permute-start | bytes 196616 | tf_op jit(solution)/shard_map/ppermute | solution.py:258
  20.8 1.1 collective-permute-start.14
  21.9 1.5 %collective-permute-start.15 = (f32[32,512]{1,0:T(8,128)}, f32[32,512]{1,0:T(8,128)S(1)}, u32[]{:S(2)}, u32[]{:S(2)}) collective-permute-start(f32[32,512]{1,0:T(8,128)} %refs_4_.3), channel_id=1, source_target_pairs={{0,3},{1,2},{2,1},{3,0},{4,7},{5,6},{6,5},{7,4},{8,11},{9,10},{10,... | collective-permute-start | bytes 196616 | tf_op jit(solution)/shard_map/ppermute | solution.py:258
  23.3 0.9 copy-done
  24.2 13.0 %build.1 = (bf16[512,4096]{1,0:T(8,128)(2,1)S(1)}, bf16[512,4096]{1,0:T(8,128)(2,1)S(1)}, bf16[512,4096]{1,0:T(8,128)(2,1)S(1)}, bf16[512,4096]{1,0:T(8,128)(2,1...) custom-call(f32[64,512]{1,0:T(8,128)S(1)} %copy-done, ...), custom_call_target="tpu_custom_call" | custom-call | tf_op jit(solution)/shard_map/build/pallas_call | solution.py:18
  37.2 1.0 collective-permute-start.10
  38.3 2.0 %collective-permute-start.11 = (f32[8,512]{1,0:T(8,128)S(1)}, f32[8,512]{1,0:T(8,128)S(1)}, u32[]{:S(2)}, u32[]{:S(2)}) collective-permute-start(f32[8,512]{1,0:T(8,128)S(1)} %get-tuple-element.21.refs_0_), channel_id=1, source_target_pairs={{0,2},{1,3},{2,0},{3,1},{4,6},{5,7},{6,4},{7,5},{8,10},{9,11},{10,... | collective-permute-start | bytes 49160 | tf_op jit(solution)/shard_map/ppermute | solution.py:258
  40.2 1.5 %collective-permute-start.12 = (f32[8,512]{1,0:T(8,128)S(1)}, f32[8,512]{1,0:T(8,128)S(1)}, u32[]{:S(2)}, u32[]{:S(2)}) collective-permute-start(f32[8,512]{1,0:T(8,128)S(1)} %get-tuple-element.21.refs_0_), channel_id=1, source_target_pairs={{0,3},{1,2},{2,1},{3,0},{4,7},{5,6},{6,5},{7,4},{8,11},{9,10},{10,... | collective-permute-start | bytes 49160 | tf_op jit(solution)/shard_map/ppermute | solution.py:258
  41.7 1.2 %collective-permute-done.11.refs_2_ = f32[8,512]{1,0:T(8,128)S(1)} collective-permute-done((f32[8,512]{1,0:T(8,128)S(1)}, f32[8,512]{1,0:T(8,128)S(1)}, u32[]{:S(2)}, u32[]{:S(2)}) %collective-permute-start.11) | collective-permute-done | bytes 16416 | tf_op jit(solution)/shard_map/ppermute | solution.py:258
  42.9 2.9 %collective-permute-done.12.refs_3_ = f32[8,512]{1,0:T(8,128)S(1)} collective-permute-done((f32[8,512]{1,0:T(8,128)S(1)}, f32[8,512]{1,0:T(8,128)S(1)}, u32[]{:S(2)}, u32[]{:S(2)}) %collective-permute-start.12) | collective-permute-done | bytes 16416 | tf_op jit(solution)/shard_map/ppermute | solution.py:258
  45.8 0.8 copy-done.1
  46.6 5.7 %first_product.1 = (f32[40,4096]{1,0:T(8,128)S(1)}, f32[1,512]{1,0:T(1,128)S(1)}) custom-call(f32[8,512]{1,0:T(8,128)S(1)} %get-tuple-element.21.refs_0_, f32[8,512]{1,0:T(8,128)S(1)} %collective-permute-done.10.refs_1_, f32[8,512]{1,0:T(8,128)S(1)} %collective-permute-done.11.refs_2_, f32[8,512]{1,0:T(8,128)S(1)} %collective-permute-done.12.refs_3_, ...), custom_call_target="tpu_custom_call" | custom-call | tf_op jit(solution)/shard_map/first_product/pallas_call | solution.py:18
  52.5 1.6 %collective-permute-done.16 = f32[40,2048]{1,0:T(8,128)S(1)} collective-permute-done((f32[40,2048]{1,0:T(8,128)S(1)}, f32[40,2048]{1,0:T(8,128)S(1)}, u32[]{:S(2)}, u32[]{:S(2)}) %collective-permute-start.16) | collective-permute-done | bytes 327712 | tf_op jit(solution)/shard_map/ppermute | solution.py:258
  54.2 1.6 %collective-permute-start.17 = (f32[40,512]{1,0:T(8,128)S(1)}, f32[40,512]{1,0:T(8,128)S(1)}, u32[]{:S(2)}, u32[]{:S(2)}) collective-permute-start(f32[40,512]{1,0:T(8,128)S(1)} %get-tuple-element.55), channel_id=1, source_target_pairs={{0,8},{4,12},{8,0},{12,4},{16,24},{20,28},{24,16},{28,20},{1,9},{5... | collective-permute-start | bytes 245768 | tf_op jit(solution)/shard_map/ppermute | solution.py:258
  55.8 1.5 %collective-permute-start.18 = (f32[40,512]{1,0:T(8,128)S(1)}, f32[40,512]{1,0:T(8,128)S(1)}, u32[]{:S(2)}, u32[]{:S(2)}) collective-permute-start(f32[40,512]{1,0:T(8,128)S(1)} %get-tuple-element.54), channel_id=1, source_target_pairs={{0,16},{4,20},{8,24},{12,28},{16,0},{20,4},{24,8},{28,12},{1,17},{... | collective-permute-start | bytes 245768 | tf_op jit(solution)/shard_map/ppermute | solution.py:258
  57.8 1.0 collective-permute-done.17.refs_2_
  58.8 2.3 %collective-permute-done.18.refs_3_ = f32[40,512]{1,0:T(8,128)S(1)} collective-permute-done((f32[40,512]{1,0:T(8,128)S(1)}, f32[40,512]{1,0:T(8,128)S(1)}, u32[]{:S(2)}, u32[]{:S(2)}) %collective-permute-start.18) | collective-permute-done | bytes 81952 | tf_op jit(solution)/shard_map/ppermute | solution.py:258
  61.1 1.6 %collective-permute-done.19.refs_4_ = f32[40,512]{1,0:T(8,128)S(1)} collective-permute-done((f32[40,512]{1,0:T(8,128)S(1)}, f32[40,512]{1,0:T(8,128)S(1)}, u32[]{:S(2)}, u32[]{:S(2)}) %collective-permute-start.19) | collective-permute-done | bytes 81952 | tf_op jit(solution)/shard_map/ppermute | solution.py:258
  63.0 2.0 %collective-permute-start.28 = (f32[32,512]{1,0:T(8,128)S(1)}, f32[32,512]{1,0:T(8,128)S(1)}, u32[]{:S(2)}, u32[]{:S(2)}) collective-permute-start(f32[32,512]{1,0:T(8,128)S(1)} %get-tuple-element.34.refs_0_), channel_id=1, source_target_pairs={{0,2},{1,3},{2,0},{3,1},{4,6},{5,7},{6,4},{7,5},{8,10},{9,11},{10,... | collective-permute-start | bytes 196616 | tf_op jit(solution)/shard_map/ppermute | solution.py:258
  65.0 2.4 %collective-permute-start.29 = (f32[32,512]{1,0:T(8,128)S(1)}, f32[32,512]{1,0:T(8,128)S(1)}, u32[]{:S(2)}, u32[]{:S(2)}) collective-permute-start(f32[32,512]{1,0:T(8,128)S(1)} %get-tuple-element.34.refs_0_), channel_id=1, source_target_pairs={{0,3},{1,2},{2,1},{3,0},{4,7},{5,6},{6,5},{7,4},{8,11},{9,10},{10,... | collective-permute-start | bytes 196616 | tf_op jit(solution)/shard_map/ppermute | solution.py:258
  67.3 1.4 %collective-permute-done.28.refs_2_ = f32[32,512]{1,0:T(8,128)S(1)} collective-permute-done((f32[32,512]{1,0:T(8,128)S(1)}, f32[32,512]{1,0:T(8,128)S(1)}, u32[]{:S(2)}, u32[]{:S(2)}) %collective-permute-start.28) | collective-permute-done | bytes 65568 | tf_op jit(solution)/shard_map/ppermute | solution.py:258
  68.8 2.3 %collective-permute-done.29.refs_3_ = f32[32,512]{1,0:T(8,128)S(1)} collective-permute-done((f32[32,512]{1,0:T(8,128)S(1)}, f32[32,512]{1,0:T(8,128)S(1)}, u32[]{:S(2)}, u32[]{:S(2)}) %collective-permute-start.29) | collective-permute-done | bytes 65568 | tf_op jit(solution)/shard_map/ppermute | solution.py:258
  71.0 5.9 %second_product.1 = f32[32,4096]{1,0:T(8,128)S(1)} custom-call(f32[32,512]{1,0:T(8,128)S(1)} %get-tuple-element.34.refs_0_, f32[32,512]{1,0:T(8,128)S(1)} %collective-permute-done.27.refs_1_, f32[32,512]{1,0:T(8,128)S(1)} %collective-permute-done.28.refs_2_, f32[32,512]{1,0:T(8,128)S(1)} %collective-permute-done.29.refs_3_, ...), custom_call_target="tpu_custom_call" | custom-call | tf_op jit(solution)/shard_map/second_product/pallas_call | solution.py:18
  77.6 1.0 collective-permute-done.20
  79.2 0.9 collective-permute-start.22
  80.0 2.1 %collective-permute-start.23 = (f32[32,32]{1,0:T(8,128)S(1)}, f32[32,32]{1,0:T(8,128)S(1)}, u32[]{:S(2)}, u32[]{:S(2)}) collective-permute-start(f32[32,32]{1,0:T(8,128)S(1)} %add.31), channel_id=1, source_target_pairs={{0,24},{4,28},{8,16},{12,20},{16,8},{20,12},{24,0},{28,4},{1,25},{... | collective-permute-start | bytes 12296 | tf_op jit(solution)/shard_map/ppermute | solution.py:258
  82.2 0.6 collective-permute-start.31
  82.8 0.9 collective-permute-start.32
  83.6 2.1 %collective-permute-start.33 = (f32[32,512]{1,0:T(8,128)S(1)}, f32[32,512]{1,0:T(8,128)S(1)}, u32[]{:S(2)}, u32[]{:S(2)}) collective-permute-start(f32[32,512]{1,0:T(8,128)S(1)} %get-tuple-element.57), channel_id=1, source_target_pairs={{0,24},{4,28},{8,16},{12,20},{16,8},{20,12},{24,0},{28,4},{1,25},{... | collective-permute-start | bytes 196616 | tf_op jit(solution)/shard_map/ppermute | solution.py:258
  85.8 2.9 %collective-permute-start.25 = (f32[32,32]{1,0:T(8,128)S(1)}, f32[32,32]{1,0:T(8,128)S(1)}, u32[]{:S(2)}, u32[]{:S(2)}) collective-permute-start(f32[32,32]{1,0:T(8,128)S(1)} %add_add_fusion.1.refs_0_), channel_id=1, source_target_pairs={{0,2},{1,3},{2,0},{3,1},{4,6},{5,7},{6,4},{7,5},{8,10},{9,11},{10,... | collective-permute-start | bytes 12296 | tf_op jit(solution)/shard_map/ppermute | solution.py:258
  88.7 0.8 collective-permute-done.24.refs_1_
  89.6 2.4 %collective-permute-start.26 = (f32[32,32]{1,0:T(8,128)S(1)}, f32[32,32]{1,0:T(8,128)S(1)}, u32[]{:S(2)}, u32[]{:S(2)}) collective-permute-start(f32[32,32]{1,0:T(8,128)S(1)} %add_add_fusion.1.refs_0_), channel_id=1, source_target_pairs={{0,3},{1,2},{2,1},{3,0},{4,7},{5,6},{6,5},{7,4},{8,11},{9,10},{10,... | collective-permute-start | bytes 12296 | tf_op jit(solution)/shard_map/ppermute | solution.py:258
  91.9 3.2 %collective-permute-done.26.refs_3_ = f32[32,32]{1,0:T(8,128)S(1)} collective-permute-done((f32[32,32]{1,0:T(8,128)S(1)}, f32[32,32]{1,0:T(8,128)S(1)}, u32[]{:S(2)}, u32[]{:S(2)}) %collective-permute-start.26) | collective-permute-done | bytes 4128 | tf_op jit(solution)/shard_map/ppermute | solution.py:258
  95.1 2.9 %first_factor.1.refs_0_ = f32[32,32]{1,0:T(8,128)S(1)} custom-call(f32[32,32]{1,0:T(8,128)S(1)} %add_add_fusion.1.refs_0_, f32[32,32]{1,0:T(8,128)S(1)} %collective-permute-done.24.refs_1_, f32[32,32]{1,0:T(8,128)S(1)} %collective-permute-done.25.refs_2_, f32[32,32]{1,0:T(8,128)S(1)} %collective-permute-done.26.refs_3_), custom_call_target="tpu_custom_call" | custom-call | tf_op jit(solution)/shard_map/first_factor/pallas_call | solution.py:18
  98.4 1.2 %collective-permute-done.34 = f32[32,32]{1,0:T(8,128)S(1)} collective-permute-done((f32[32,32]{1,0:T(8,128)S(1)}, f32[32,32]{1,0:T(8,128)S(1)}, u32[]{:S(2)}, u32[]{:S(2)}) %collective-permute-start.34) | collective-permute-done | bytes 4128 | tf_op jit(solution)/shard_map/ppermute | solution.py:258
  100.1 1.1 collective-permute-start.36
  101.2 1.9 %collective-permute-start.37 = (f32[32,32]{1,0:T(8,128)S(1)}, f32[32,32]{1,0:T(8,128)S(1)}, u32[]{:S(2)}, u32[]{:S(2)}) collective-permute-start(f32[32,32]{1,0:T(8,128)S(1)} %add.36), channel_id=1, source_target_pairs={{0,24},{4,28},{8,16},{12,20},{16,8},{20,12},{24,0},{28,4},{1,25},{... | collective-permute-start | bytes 12296 | tf_op jit(solution)/shard_map/ppermute | solution.py:258
  103.9 2.0 %collective-permute-done.37 = f32[32,32]{1,0:T(8,128)S(1)} collective-permute-done((f32[32,32]{1,0:T(8,128)S(1)}, f32[32,32]{1,0:T(8,128)S(1)}, u32[]{:S(2)}, u32[]{:S(2)}) %collective-permute-start.37) | collective-permute-done | bytes 4128 | tf_op jit(solution)/shard_map/ppermute | solution.py:258
  105.9 2.9 %collective-permute-start.39 = (f32[32,32]{1,0:T(8,128)S(1)}, f32[32,32]{1,0:T(8,128)S(1)}, u32[]{:S(2)}, u32[]{:S(2)}) collective-permute-start(f32[32,32]{1,0:T(8,128)S(1)} %add_add_fusion.refs_1_), channel_id=1, source_target_pairs={{0,2},{1,3},{2,0},{3,1},{4,6},{5,7},{6,4},{7,5},{8,10},{9,11},{10,... | collective-permute-start | bytes 12296 | tf_op jit(solution)/shard_map/ppermute | solution.py:258
  108.8 1.5 %collective-permute-start.40 = (f32[32,32]{1,0:T(8,128)S(1)}, f32[32,32]{1,0:T(8,128)S(1)}, u32[]{:S(2)}, u32[]{:S(2)}) collective-permute-start(f32[32,32]{1,0:T(8,128)S(1)} %add_add_fusion.refs_1_), channel_id=1, source_target_pairs={{0,3},{1,2},{2,1},{3,0},{4,7},{5,6},{6,5},{7,4},{8,11},{9,10},{10,... | collective-permute-start | bytes 12296 | tf_op jit(solution)/shard_map/ppermute | solution.py:258
  110.6 3.7 %collective-permute-done.40.refs_4_ = f32[32,32]{1,0:T(8,128)S(1)} collective-permute-done((f32[32,32]{1,0:T(8,128)S(1)}, f32[32,32]{1,0:T(8,128)S(1)}, u32[]{:S(2)}, u32[]{:S(2)}) %collective-permute-start.40) | collective-permute-done | bytes 4128 | tf_op jit(solution)/shard_map/ppermute | solution.py:258
  114.3 3.7 %finish.1 = f32[32,512]{1,0:T(8,128)} custom-call(f32[32,512]{1,0:T(8,128)S(1)} %get-tuple-element.35.refs_0_, f32[32,32]{1,0:T(8,128)S(1)} %add_add_fusion.refs_1_, f32[32,32]{1,0:T(8,128)S(1)} %collective-permute-done.38.refs_2_, f32[32,32]{1,0:T(8,128)S(1)} %collective-permute-done.39.refs_3_, f32[32,32]{1,0:T(8,128)S(1)} %collective-permute-done.40.refs_4_), custom_call_target="tpu_custom_call" | custom-call | tf_op jit(solution)/shard_map/finish/pallas_call | solution.py:18
  (57 shorter events, 5.0 us)
Async XLA Ops:
  0.0 9.1 %collective-permute-start.4 = (f32[64,512]{1,0:T(8,128)}, f32[64,512]{1,0:T(8,128)S(1)}, u32[]{:S(2)}, u32[]{:S(2)}) collective-permute-start(f32[64,512]{1,0:T(8,128)} %refs_4_.2), channel_id=1, source_target_pairs={{0,8},{4,12},{8,0},{12,4},{16,24},{20,28},{24,16},{28,20},{1,9},{5... | collective-permute-start | bytes 393224 | tf_op jit(solution)/shard_map/ppermute | solution.py:258
  2.9 8.0 %collective-permute-start.6 = (f32[64,512]{1,0:T(8,128)}, f32[64,512]{1,0:T(8,128)S(1)}, u32[]{:S(2)}, u32[]{:S(2)}) collective-permute-start(f32[64,512]{1,0:T(8,128)} %refs_4_.2), channel_id=1, source_target_pairs={{0,16},{4,20},{8,24},{12,28},{16,0},{20,4},{24,8},{28,12},{1,17},{... | collective-permute-start | bytes 393224 | tf_op jit(solution)/shard_map/ppermute | solution.py:258
  4.5 6.5 %collective-permute-start.8 = (f32[64,512]{1,0:T(8,128)}, f32[64,512]{1,0:T(8,128)S(1)}, u32[]{:S(2)}, u32[]{:S(2)}) collective-permute-start(f32[64,512]{1,0:T(8,128)} %refs_4_.2), channel_id=1, source_target_pairs={{0,24},{4,28},{8,16},{12,20},{16,8},{20,12},{24,0},{28,4},{1,25},{... | collective-permute-start | bytes 393224 | tf_op jit(solution)/shard_map/ppermute | solution.py:258
  4.5 7.0 %collective-permute-start = (f32[64,512]{1,0:T(8,128)}, f32[64,512]{1,0:T(8,128)S(1)}, u32[]{:S(2)}, u32[]{:S(2)}) collective-permute-start(f32[64,512]{1,0:T(8,128)} %refs_4_.2), channel_id=1, source_target_pairs={{0,1},{1,0},{2,3},{3,2},{4,5},{5,4},{6,7},{7,6},{8,9},{9,8},{10,11... | collective-permute-start | bytes 393224 | tf_op jit(solution)/shard_map/ppermute | solution.py:258
  6.5 12.3 %collective-permute-start.1 = (f32[64,512]{1,0:T(8,128)}, f32[64,512]{1,0:T(8,128)S(1)}, u32[]{:S(2)}, u32[]{:S(2)}) collective-permute-start(f32[64,512]{1,0:T(8,128)} %refs_4_.2), channel_id=1, source_target_pairs={{0,2},{1,3},{2,0},{3,1},{4,6},{5,7},{6,4},{7,5},{8,10},{9,11},{10,... | collective-permute-start | bytes 393224 | tf_op jit(solution)/shard_map/ppermute | solution.py:258
  9.1 9.7 %collective-permute-start.2 = (f32[64,512]{1,0:T(8,128)}, f32[64,512]{1,0:T(8,128)S(1)}, u32[]{:S(2)}, u32[]{:S(2)}) collective-permute-start(f32[64,512]{1,0:T(8,128)} %refs_4_.2), channel_id=1, source_target_pairs={{0,3},{1,2},{2,1},{3,0},{4,7},{5,6},{6,5},{7,4},{8,11},{9,10},{10,... | collective-permute-start | bytes 393224 | tf_op jit(solution)/shard_map/ppermute | solution.py:258
  10.9 9.9 %collective-permute-start.3 = (f32[64,512]{1,0:T(8,128)}, f32[64,512]{1,0:T(8,128)S(1)}, u32[]{:S(2)}, u32[]{:S(2)}) collective-permute-start(f32[64,512]{1,0:T(8,128)} %refs_4_.2), channel_id=1, source_target_pairs={{0,4},{4,0},{8,12},{12,8},{16,20},{20,16},{24,28},{28,24},{1,5},{5... | collective-permute-start | bytes 393224 | tf_op jit(solution)/shard_map/ppermute | solution.py:258
  10.9 10.9 %collective-permute-start.5 = (f32[64,512]{1,0:T(8,128)S(1)}, f32[64,512]{1,0:T(8,128)S(1)}, u32[]{:S(2)}, u32[]{:S(2)}) collective-permute-start(f32[64,512]{1,0:T(8,128)S(1)} %collective-permute-done.4.refs_6_), channel_id=1, source_target_pairs={{0,4},{4,0},{8,12},{12,8},{16,20},{20,16},{24,28},{28,24},{1,5},{5... | collective-permute-start | bytes 393224 | tf_op jit(solution)/shard_map/ppermute | solution.py:258
  11.4 11.9 %collective-permute-start.7 = (f32[64,512]{1,0:T(8,128)S(1)}, f32[64,512]{1,0:T(8,128)S(1)}, u32[]{:S(2)}, u32[]{:S(2)}) collective-permute-start(f32[64,512]{1,0:T(8,128)S(1)} %collective-permute-done.6.refs_8_), channel_id=1, source_target_pairs={{0,4},{4,0},{8,12},{12,8},{16,20},{20,16},{24,28},{28,24},{1,5},{5... | collective-permute-start | bytes 393224 | tf_op jit(solution)/shard_map/ppermute | solution.py:258
  18.8 4.5 %collective-permute-start.9 = (f32[64,512]{1,0:T(8,128)S(1)}, f32[64,512]{1,0:T(8,128)S(1)}, u32[]{:S(2)}, u32[]{:S(2)}) collective-permute-start(f32[64,512]{1,0:T(8,128)S(1)} %collective-permute-done.8.refs_10_), channel_id=1, source_target_pairs={{0,4},{4,0},{8,12},{12,8},{16,20},{20,16},{24,28},{28,24},{1,5},{5... | collective-permute-start | bytes 393224 | tf_op jit(solution)/shard_map/ppermute | solution.py:258
  18.8 21.4 %collective-permute-start.13 = (f32[32,512]{1,0:T(8,128)}, f32[32,512]{1,0:T(8,128)S(1)}, u32[]{:S(2)}, u32[]{:S(2)}) collective-permute-start(f32[32,512]{1,0:T(8,128)} %refs_4_.3), channel_id=1, source_target_pairs={{0,1},{1,0},{2,3},{3,2},{4,5},{5,4},{6,7},{7,6},{8,9},{9,8},{10,11... | collective-permute-start | bytes 196616 | tf_op jit(solution)/shard_map/ppermute | solution.py:258
  20.8 20.9 %collective-permute-start.14 = (f32[32,512]{1,0:T(8,128)}, f32[32,512]{1,0:T(8,128)S(1)}, u32[]{:S(2)}, u32[]{:S(2)}) collective-permute-start(f32[32,512]{1,0:T(8,128)} %refs_4_.3), channel_id=1, source_target_pairs={{0,2},{1,3},{2,0},{3,1},{4,6},{5,7},{6,4},{7,5},{8,10},{9,11},{10,... | collective-permute-start | bytes 196616 | tf_op jit(solution)/shard_map/ppermute | solution.py:258
  21.9 19.8 %collective-permute-start.15 = (f32[32,512]{1,0:T(8,128)}, f32[32,512]{1,0:T(8,128)S(1)}, u32[]{:S(2)}, u32[]{:S(2)}) collective-permute-start(f32[32,512]{1,0:T(8,128)} %refs_4_.3), channel_id=1, source_target_pairs={{0,3},{1,2},{2,1},{3,0},{4,7},{5,6},{6,5},{7,4},{8,11},{9,10},{10,... | collective-permute-start | bytes 196616 | tf_op jit(solution)/shard_map/ppermute | solution.py:258
  23.3 0.9 copy-start
  37.2 4.5 %collective-permute-start.10 = (f32[8,512]{1,0:T(8,128)S(1)}, f32[8,512]{1,0:T(8,128)S(1)}, u32[]{:S(2)}, u32[]{:S(2)}) collective-permute-start(f32[8,512]{1,0:T(8,128)S(1)} %get-tuple-element.21.refs_0_), channel_id=1, source_target_pairs={{0,1},{1,0},{2,3},{3,2},{4,5},{5,4},{6,7},{7,6},{8,9},{9,8},{10,11... | collective-permute-start | bytes 49160 | tf_op jit(solution)/shard_map/ppermute | solution.py:258
  38.3 4.6 %collective-permute-start.11 = (f32[8,512]{1,0:T(8,128)S(1)}, f32[8,512]{1,0:T(8,128)S(1)}, u32[]{:S(2)}, u32[]{:S(2)}) collective-permute-start(f32[8,512]{1,0:T(8,128)S(1)} %get-tuple-element.21.refs_0_), channel_id=1, source_target_pairs={{0,2},{1,3},{2,0},{3,1},{4,6},{5,7},{6,4},{7,5},{8,10},{9,11},{10,... | collective-permute-start | bytes 49160 | tf_op jit(solution)/shard_map/ppermute | solution.py:258
  40.2 5.5 %collective-permute-start.12 = (f32[8,512]{1,0:T(8,128)S(1)}, f32[8,512]{1,0:T(8,128)S(1)}, u32[]{:S(2)}, u32[]{:S(2)}) collective-permute-start(f32[8,512]{1,0:T(8,128)S(1)} %get-tuple-element.21.refs_0_), channel_id=1, source_target_pairs={{0,3},{1,2},{2,1},{3,0},{4,7},{5,6},{6,5},{7,4},{8,11},{9,10},{10,... | collective-permute-start | bytes 49160 | tf_op jit(solution)/shard_map/ppermute | solution.py:258
  45.8 0.8 copy-start.1
  52.5 1.7 %collective-permute-start.16 = (f32[40,2048]{1,0:T(8,128)S(1)}, f32[40,2048]{1,0:T(8,128)S(1)}, u32[]{:S(2)}, u32[]{:S(2)}) collective-permute-start(f32[40,2048]{1,0:T(8,128)S(1)} %pad_maximum_fusion), channel_id=1, source_target_pairs={{0,4},{4,0},{8,12},{12,8},{16,20},{20,16},{24,28},{28,24},{1,5},{5... | collective-permute-start | bytes 983048 | tf_op jit(solution)/shard_map/ppermute | solution.py:258
  54.2 4.6 %collective-permute-start.17 = (f32[40,512]{1,0:T(8,128)S(1)}, f32[40,512]{1,0:T(8,128)S(1)}, u32[]{:S(2)}, u32[]{:S(2)}) collective-permute-start(f32[40,512]{1,0:T(8,128)S(1)} %get-tuple-element.55), channel_id=1, source_target_pairs={{0,8},{4,12},{8,0},{12,4},{16,24},{20,28},{24,16},{28,20},{1,9},{5... | collective-permute-start | bytes 245768 | tf_op jit(solution)/shard_map/ppermute | solution.py:258
  55.8 5.3 %collective-permute-start.18 = (f32[40,512]{1,0:T(8,128)S(1)}, f32[40,512]{1,0:T(8,128)S(1)}, u32[]{:S(2)}, u32[]{:S(2)}) collective-permute-start(f32[40,512]{1,0:T(8,128)S(1)} %get-tuple-element.54), channel_id=1, source_target_pairs={{0,16},{4,20},{8,24},{12,28},{16,0},{20,4},{24,8},{28,12},{1,17},{... | collective-permute-start | bytes 245768 | tf_op jit(solution)/shard_map/ppermute | solution.py:258
  57.3 5.3 %collective-permute-start.19 = (f32[40,512]{1,0:T(8,128)S(1)}, f32[40,512]{1,0:T(8,128)S(1)}, u32[]{:S(2)}, u32[]{:S(2)}) collective-permute-start(f32[40,512]{1,0:T(8,128)S(1)} %get-tuple-element.53), channel_id=1, source_target_pairs={{0,24},{4,28},{8,16},{12,20},{16,8},{20,12},{24,0},{28,4},{1,25},{... | collective-permute-start | bytes 245768 | tf_op jit(solution)/shard_map/ppermute | solution.py:258
  62.9 4.5 %collective-permute-start.27 = (f32[32,512]{1,0:T(8,128)S(1)}, f32[32,512]{1,0:T(8,128)S(1)}, u32[]{:S(2)}, u32[]{:S(2)}) collective-permute-start(f32[32,512]{1,0:T(8,128)S(1)} %get-tuple-element.34.refs_0_), channel_id=1, source_target_pairs={{0,1},{1,0},{2,3},{3,2},{4,5},{5,4},{6,7},{7,6},{8,9},{9,8},{10,11... | collective-permute-start | bytes 196616 | tf_op jit(solution)/shard_map/ppermute | solution.py:258
  63.0 5.8 %collective-permute-start.28 = (f32[32,512]{1,0:T(8,128)S(1)}, f32[32,512]{1,0:T(8,128)S(1)}, u32[]{:S(2)}, u32[]{:S(2)}) collective-permute-start(f32[32,512]{1,0:T(8,128)S(1)} %get-tuple-element.34.refs_0_), channel_id=1, source_target_pairs={{0,2},{1,3},{2,0},{3,1},{4,6},{5,7},{6,4},{7,5},{8,10},{9,11},{10,... | collective-permute-start | bytes 196616 | tf_op jit(solution)/shard_map/ppermute | solution.py:258
  65.0 6.1 %collective-permute-start.29 = (f32[32,512]{1,0:T(8,128)S(1)}, f32[32,512]{1,0:T(8,128)S(1)}, u32[]{:S(2)}, u32[]{:S(2)}) collective-permute-start(f32[32,512]{1,0:T(8,128)S(1)} %get-tuple-element.34.refs_0_), channel_id=1, source_target_pairs={{0,3},{1,2},{2,1},{3,0},{4,7},{5,6},{6,5},{7,4},{8,11},{9,10},{10,... | collective-permute-start | bytes 196616 | tf_op jit(solution)/shard_map/ppermute | solution.py:258
  77.0 5.1 %collective-permute-start.30 = (f32[32,2048]{1,0:T(8,128)S(1)}, f32[32,2048]{1,0:T(8,128)S(1)}, u32[]{:S(2)}, u32[]{:S(2)}) collective-permute-start(f32[32,2048]{1,0:T(8,128)S(1)} %pad_maximum_fusion.1), channel_id=1, source_target_pairs={{0,4},{4,0},{8,12},{12,8},{16,20},{20,16},{24,28},{28,24},{1,5},{5... | collective-permute-start | bytes 786440 | tf_op jit(solution)/shard_map/ppermute | solution.py:258
  77.1 1.5 %collective-permute-start.20 = (f32[32,32]{1,0:T(8,128)S(1)}, f32[32,32]{1,0:T(8,128)S(1)}, u32[]{:S(2)}, u32[]{:S(2)}) collective-permute-start(f32[32,32]{1,0:T(8,128)S(1)} %get-tuple-element.32), channel_id=1, source_target_pairs={{0,4},{4,0},{8,12},{12,8},{16,20},{20,16},{24,28},{28,24},{1,5},{5... | collective-permute-start | bytes 12296 | tf_op jit(solution)/shard_map/ppermute | solution.py:258
  78.6 5.0 %collective-permute-start.21 = (f32[32,32]{1,0:T(8,128)S(1)}, f32[32,32]{1,0:T(8,128)S(1)}, u32[]{:S(2)}, u32[]{:S(2)}) collective-permute-start(f32[32,32]{1,0:T(8,128)S(1)} %add.31), channel_id=1, source_target_pairs={{0,8},{4,12},{8,0},{12,4},{16,24},{20,28},{24,16},{28,20},{1,9},{5... | collective-permute-start | bytes 12296 | tf_op jit(solution)/shard_map/ppermute | solution.py:258
  79.2 6.6 %collective-permute-start.22 = (f32[32,32]{1,0:T(8,128)S(1)}, f32[32,32]{1,0:T(8,128)S(1)}, u32[]{:S(2)}, u32[]{:S(2)}) collective-permute-start(f32[32,32]{1,0:T(8,128)S(1)} %add.31), channel_id=1, source_target_pairs={{0,16},{4,20},{8,24},{12,28},{16,0},{20,4},{24,8},{28,12},{1,17},{... | collective-permute-start | bytes 12296 | tf_op jit(solution)/shard_map/ppermute | solution.py:258
  80.0 5.7 %collective-permute-start.23 = (f32[32,32]{1,0:T(8,128)S(1)}, f32[32,32]{1,0:T(8,128)S(1)}, u32[]{:S(2)}, u32[]{:S(2)}) collective-permute-start(f32[32,32]{1,0:T(8,128)S(1)} %add.31), channel_id=1, source_target_pairs={{0,24},{4,28},{8,16},{12,20},{16,8},{20,12},{24,0},{28,4},{1,25},{... | collective-permute-start | bytes 12296 | tf_op jit(solution)/shard_map/ppermute | solution.py:258
  82.2 15.8 %collective-permute-start.31 = (f32[32,512]{1,0:T(8,128)S(1)}, f32[32,512]{1,0:T(8,128)S(1)}, u32[]{:S(2)}, u32[]{:S(2)}) collective-permute-start(f32[32,512]{1,0:T(8,128)S(1)} %get-tuple-element.59), channel_id=1, source_target_pairs={{0,8},{4,12},{8,0},{12,4},{16,24},{20,28},{24,16},{28,20},{1,9},{5... | collective-permute-start | bytes 196616 | tf_op jit(solution)/shard_map/ppermute | solution.py:258
  82.8 15.2 %collective-permute-start.32 = (f32[32,512]{1,0:T(8,128)S(1)}, f32[32,512]{1,0:T(8,128)S(1)}, u32[]{:S(2)}, u32[]{:S(2)}) collective-permute-start(f32[32,512]{1,0:T(8,128)S(1)} %get-tuple-element.58), channel_id=1, source_target_pairs={{0,16},{4,20},{8,24},{12,28},{16,0},{20,4},{24,8},{28,12},{1,17},{... | collective-permute-start | bytes 196616 | tf_op jit(solution)/shard_map/ppermute | solution.py:258
  83.6 14.4 %collective-permute-start.33 = (f32[32,512]{1,0:T(8,128)S(1)}, f32[32,512]{1,0:T(8,128)S(1)}, u32[]{:S(2)}, u32[]{:S(2)}) collective-permute-start(f32[32,512]{1,0:T(8,128)S(1)} %get-tuple-element.57), channel_id=1, source_target_pairs={{0,24},{4,28},{8,16},{12,20},{16,8},{20,12},{24,0},{28,4},{1,25},{... | collective-permute-start | bytes 196616 | tf_op jit(solution)/shard_map/ppermute | solution.py:258
  85.8 3.8 %collective-permute-start.24 = (f32[32,32]{1,0:T(8,128)S(1)}, f32[32,32]{1,0:T(8,128)S(1)}, u32[]{:S(2)}, u32[]{:S(2)}) collective-permute-start(f32[32,32]{1,0:T(8,128)S(1)} %add_add_fusion.1.refs_0_), channel_id=1, source_target_pairs={{0,1},{1,0},{2,3},{3,2},{4,5},{5,4},{6,7},{7,6},{8,9},{9,8},{10,11... | collective-permute-start | bytes 12296 | tf_op jit(solution)/shard_map/ppermute | solution.py:258
  85.8 6.1 %collective-permute-start.25 = (f32[32,32]{1,0:T(8,128)S(1)}, f32[32,32]{1,0:T(8,128)S(1)}, u32[]{:S(2)}, u32[]{:S(2)}) collective-permute-start(f32[32,32]{1,0:T(8,128)S(1)} %add_add_fusion.1.refs_0_), channel_id=1, source_target_pairs={{0,2},{1,3},{2,0},{3,1},{4,6},{5,7},{6,4},{7,5},{8,10},{9,11},{10,... | collective-permute-start | bytes 12296 | tf_op jit(solution)/shard_map/ppermute | solution.py:258
  89.6 5.5 %collective-permute-start.26 = (f32[32,32]{1,0:T(8,128)S(1)}, f32[32,32]{1,0:T(8,128)S(1)}, u32[]{:S(2)}, u32[]{:S(2)}) collective-permute-start(f32[32,32]{1,0:T(8,128)S(1)} %add_add_fusion.1.refs_0_), channel_id=1, source_target_pairs={{0,3},{1,2},{2,1},{3,0},{4,7},{5,6},{6,5},{7,4},{8,11},{9,10},{10,... | collective-permute-start | bytes 12296 | tf_op jit(solution)/shard_map/ppermute | solution.py:258
  98.4 1.2 %collective-permute-start.34 = (f32[32,32]{1,0:T(8,128)S(1)}, f32[32,32]{1,0:T(8,128)S(1)}, u32[]{:S(2)}, u32[]{:S(2)}) collective-permute-start(f32[32,32]{1,0:T(8,128)S(1)} %get-tuple-element.36), channel_id=1, source_target_pairs={{0,4},{4,0},{8,12},{12,8},{16,20},{20,16},{24,28},{28,24},{1,5},{5... | collective-permute-start | bytes 12296 | tf_op jit(solution)/shard_map/ppermute | solution.py:258
  99.6 3.7 %collective-permute-start.35 = (f32[32,32]{1,0:T(8,128)S(1)}, f32[32,32]{1,0:T(8,128)S(1)}, u32[]{:S(2)}, u32[]{:S(2)}) collective-permute-start(f32[32,32]{1,0:T(8,128)S(1)} %add.36), channel_id=1, source_target_pairs={{0,8},{4,12},{8,0},{12,4},{16,24},{20,28},{24,16},{28,20},{1,9},{5... | collective-permute-start | bytes 12296 | tf_op jit(solution)/shard_map/ppermute | solution.py:258
  100.1 3.7 %collective-permute-start.36 = (f32[32,32]{1,0:T(8,128)S(1)}, f32[32,32]{1,0:T(8,128)S(1)}, u32[]{:S(2)}, u32[]{:S(2)}) collective-permute-start(f32[32,32]{1,0:T(8,128)S(1)} %add.36), channel_id=1, source_target_pairs={{0,16},{4,20},{8,24},{12,28},{16,0},{20,4},{24,8},{28,12},{1,17},{... | collective-permute-start | bytes 12296 | tf_op jit(solution)/shard_map/ppermute | solution.py:258
  101.2 4.6 %collective-permute-start.37 = (f32[32,32]{1,0:T(8,128)S(1)}, f32[32,32]{1,0:T(8,128)S(1)}, u32[]{:S(2)}, u32[]{:S(2)}) collective-permute-start(f32[32,32]{1,0:T(8,128)S(1)} %add.36), channel_id=1, source_target_pairs={{0,24},{4,28},{8,16},{12,20},{16,8},{20,12},{24,0},{28,4},{1,25},{... | collective-permute-start | bytes 12296 | tf_op jit(solution)/shard_map/ppermute | solution.py:258
  105.9 4.4 %collective-permute-start.38 = (f32[32,32]{1,0:T(8,128)S(1)}, f32[32,32]{1,0:T(8,128)S(1)}, u32[]{:S(2)}, u32[]{:S(2)}) collective-permute-start(f32[32,32]{1,0:T(8,128)S(1)} %add_add_fusion.refs_1_), channel_id=1, source_target_pairs={{0,1},{1,0},{2,3},{3,2},{4,5},{5,4},{6,7},{7,6},{8,9},{9,8},{10,11... | collective-permute-start | bytes 12296 | tf_op jit(solution)/shard_map/ppermute | solution.py:258
  105.9 4.7 %collective-permute-start.39 = (f32[32,32]{1,0:T(8,128)S(1)}, f32[32,32]{1,0:T(8,128)S(1)}, u32[]{:S(2)}, u32[]{:S(2)}) collective-permute-start(f32[32,32]{1,0:T(8,128)S(1)} %add_add_fusion.refs_1_), channel_id=1, source_target_pairs={{0,2},{1,3},{2,0},{3,1},{4,6},{5,7},{6,4},{7,5},{8,10},{9,11},{10,... | collective-permute-start | bytes 12296 | tf_op jit(solution)/shard_map/ppermute | solution.py:258
  108.8 5.5 %collective-permute-start.40 = (f32[32,32]{1,0:T(8,128)S(1)}, f32[32,32]{1,0:T(8,128)S(1)}, u32[]{:S(2)}, u32[]{:S(2)}) collective-permute-start(f32[32,32]{1,0:T(8,128)S(1)} %add_add_fusion.refs_1_), channel_id=1, source_target_pairs={{0,3},{1,2},{2,1},{3,0},{4,7},{5,6},{6,5},{7,4},{8,11},{9,10},{10,... | collective-permute-start | bytes 12296 | tf_op jit(solution)/shard_map/ppermute | solution.py:258
where the time goes:
time: 118 us
  starting transfers between devices  49.3 us (42%)
  waiting for transfers between devices  34.7 us (29%)
  Pallas kernels  31.8 us (27%)
  local copies, waits for them, and re-layouts  1.91 us (2%)
    ppermute x41, starting transfers between devices, swap(): lax.ppermute(values, axis, [(index, index ^ mask) for index in range(size)])  49.3 us
    ppermute x41, waiting for transfers between devices, swap(): lax.ppermute(values, axis, [(index, index ^ mask) for index in range(size)])  34.7 us
    pallas_call x7, Pallas kernels, call(): pl.pallas_call(body, out_shape=out_shape, in_specs=[VMEM] * len(operands)...  31.8 us
  transfers between devices with their start and end apart: 41, of which 18 were waited for; matrix products, arithmetic and copies ran while one was open for 0% of the time, Pallas kernels for 13%

commit v1 on v0

v1 whole, which is shorter than its diff:
```python
import functools
import math
import jax
import jax.numpy as jnp
from jax import lax
from jax.experimental import pallas as pl
from jax.experimental.pallas import tpu as pltpu
from jax.sharding import PartitionSpec as P

VMEM = pl.BlockSpec(memory_space=pltpu.VMEM)
ROWS_BY_COLUMNS = (((1,), (0,)), ((), ()))
ROWS_BY_ROWS = (((1,), (1,)), ((), ()))
RESIDENT_BYTES = 36 << 20
DEGREE_ROWS = 16


def call(body, out_shape, operands, scratch=(), limit=20 << 20, flops=0, name=None):
    return pl.pallas_call(
        body,
        out_shape=out_shape,
        in_specs=[VMEM] * len(operands),
        out_specs=jax.tree.map(lambda _: VMEM, out_shape),
        scratch_shapes=list(scratch),
        compiler_params=pltpu.CompilerParams(vmem_limit_bytes=limit),
        cost_estimate=pl.CostEstimate(flops=flops, bytes_accessed=0, transcendentals=0) if flops else None,
        name=name,
    )(*operands)


def f32(*shape):
    return jax.ShapeDtypeStruct(shape, jnp.float32)


def bf16(*shape):
    return jax.ShapeDtypeStruct(shape, jnp.bfloat16)


def halves(values):
    high = values.astype(jnp.bfloat16)
    return high, (values - high.astype(jnp.float32)).astype(jnp.bfloat16)


def thirds(values):
    high = values.astype(jnp.bfloat16).astype(jnp.float32)
    middle = (values - high).astype(jnp.bfloat16).astype(jnp.float32)
    return high, middle, values - high - middle


def row_operand(points, left, span):
    width, features = points.shape
    high, low = halves(points)
    left[span, 0:features] = high
    left[span, features : 2 * features] = high
    left[span, 2 * features : 3 * features] = low
    first, second, third = thirds(0.5 * jnp.sum(points * points, axis=1, keepdims=True))
    lane = lax.broadcasted_iota(jnp.int32, (width, features), 1)
    tail = jnp.where(lane == 0, first, jnp.where(lane == 1, second, jnp.where(lane == 2, third, 0.0)))
    tail = jnp.where((lane > 2) & (lane < 6), -1.0, tail)
    left[span, 3 * features : 4 * features] = tail.astype(jnp.bfloat16)


def column_operand(points, right, span):
    features, width = points.shape
    high, low = halves(points)
    right[0:features, span] = high
    right[features : 2 * features, span] = low
    right[2 * features : 3 * features, span] = high
    first, second, third = thirds(0.5 * jnp.sum(points * points, axis=0, keepdims=True))
    line = lax.broadcasted_iota(jnp.int32, (features, width), 0)
    tail = jnp.where(line == 3, first, jnp.where(line == 4, second, jnp.where(line == 5, third, 0.0)))
    tail = jnp.where(line < 3, -1.0, tail)
    right[3 * features : 4 * features, span] = tail.astype(jnp.bfloat16)


def build_rows(left, right, high_refs, low_refs, totals, sums_ref, tile_rows=256, tile_columns=512):
    width, columns = high_refs[0].shape
    for part, (high_ref, low_ref) in enumerate(zip(high_refs, low_refs)):
        for start in range(0, width, tile_rows):
            lines = slice(start, start + tile_rows)
            points = left[part * width + start : part * width + start + tile_rows, :]
            total = jnp.zeros((tile_rows, 128), jnp.float32)
            for first in range(0, columns, tile_columns):
                span = slice(first, first + tile_columns)
                values = jnp.exp2(
                    lax.dot_general(
                        points, right[:, span], ROWS_BY_COLUMNS, preferred_element_type=jnp.float32
                    )
                )
                high = values.astype(jnp.bfloat16)
                high_ref[lines, span] = high
                low_ref[lines, span] = (values - high.astype(jnp.float32)).astype(jnp.bfloat16)
                for lane in range(0, tile_columns, 128):
                    total = total + values[:, lane : lane + 128]
            totals[lines, :] = total
        sums_ref[part : part + 1, :] = jnp.sum(totals[...].T, axis=0, keepdims=True)
    for part in range(len(high_refs), sums_ref.shape[0]):
        sums_ref[part : part + 1, :] = jnp.zeros((1, width), jnp.float32)


def point_scale(features):
    return math.sqrt(math.log2(math.e) / (0.25 * features))


def build_own_kernel(*refs, column_parts):
    column_refs, (high_ref, low_ref, sums_ref, right, left, totals) = refs[:column_parts], refs[column_parts:]
    features, width = column_refs[0].shape
    scale = point_scale(features)
    row_operand(column_refs[0][...].T * scale, left, slice(0, width))
    for part, ref in enumerate(column_refs):
        column_operand(ref[...] * scale, right, slice(part * width, (part + 1) * width))
    build_rows(left, right, [high_ref], [low_ref], totals, sums_ref)


def build_rest_kernel(*refs, parts):
    right, own_ref, row_refs = refs[0], refs[1], refs[2 : 2 + parts]
    high_refs, low_refs = refs[2 + parts : 2 + 2 * parts], refs[2 + 2 * parts : 2 + 3 * parts]
    sums_ref, left, totals = refs[2 + 3 * parts :]
    features, width = row_refs[0].shape
    scale = point_scale(features)
    for part, ref in enumerate(row_refs):
        row_operand(ref[...].T * scale, left, slice(part * width, (part + 1) * width))
    build_rows(left, right, high_refs, low_refs, totals, sums_ref)
    sums_ref[1 : 1 + parts, :] = sums_ref[0:parts, :]
    sums_ref[0:1, :] = own_ref[0:1, :]


def sweep(weights, high_refs, low_refs, out_ref, which, tile=256):
    rows = weights.shape[0] // 2
    width = high_refs[0].shape[0]
    kept = out_ref.shape[1]
    for place, block in enumerate(which):
        for first in range(0, width, tile):
            span = slice(block * width + first, block * width + first + tile)
            total = None
            for part, (high_ref, low_ref) in enumerate(zip(high_refs, low_refs)):
                lines = slice(part * width, (part + 1) * width)
                both = lax.dot_general(
                    weights[:, lines], high_ref[:, span], ROWS_BY_COLUMNS, preferred_element_type=jnp.float32
                )
                last = lax.dot_general(
                    weights[0:rows, lines], low_ref[:, span], ROWS_BY_COLUMNS, preferred_element_type=jnp.float32
                )
                term = both[:kept] + both[rows : rows + kept] + last[:kept]
                total = term if total is None else total + term
            out_ref[place, :, first : first + tile] = total


def first_kernel(*refs, parts, peers, which):
    sums_refs, start_refs = refs[:peers], refs[peers : peers + parts]
    high_refs = refs[peers + parts : peers + 2 * parts]
    low_refs = refs[peers + 2 * parts : peers + 3 * parts]
    out_ref, inverse_ref, weights = refs[peers + 3 * parts :]
    vectors, width = start_refs[0].shape
    rows = weights.shape[0] // 2
    for part in range(parts):
        span = slice(part * width, (part + 1) * width)
        density = sums_refs[0][part : part + 1, :]
        for peer in range(1, peers):
            density = density + sums_refs[peer][part ^ peer : (part ^ peer) + 1, :]
        inverse = 1.0 / density
        if part == 0:
            inverse_ref[...] = inverse
        line = lax.broadcasted_iota(jnp.int32, (rows - vectors, width), 0)
        for first, piece in (
            (0, start_refs[part][...] * inverse),
            (vectors, jnp.where(line == 0, inverse, 0.0)),
        ):
            high, low = halves(piece)
            last = first + piece.shape[0]
            weights[first:last, span] = high
            weights[rows + first : rows + last, span] = low
    sweep(weights, high_refs, low_refs, out_ref, which)


def again_kernel(*refs, parts, which):
    weights, high_refs, low_refs, out_ref = refs[0], refs[1 : 1 + parts], refs[1 + parts : -1], refs[-1]
    sweep(weights, high_refs, low_refs, out_ref, which)


def second_kernel(*refs, parts, which):
    piece_refs, high_refs, low_refs = refs[:parts], refs[parts : 2 * parts], refs[2 * parts : 3 * parts]
    out_ref, gram_ref, weights = refs[3 * parts :]
    vectors, width = piece_refs[0].shape[0], high_refs[0].shape[0]
    gram = piece_refs[0][:, width:]
    for ref in piece_refs[1:]:
        gram = gram + ref[:, width:]
    gram_ref[...] = gram
    for part in range(parts):
        span = slice(part * width, (part + 1) * width)
        high, low = halves(piece_refs[part][:, 0:width])
        weights[0:vectors, span] = high
        weights[vectors:, span] = low
    sweep(weights, high_refs, low_refs, out_ref, which)
    for place in range(len(which)):
        out_ref[place, :, width:] = gram


def second_again_kernel(*refs, parts, which):
    weights, gram_ref = refs[0], refs[1]
    high_refs, low_refs, out_ref = refs[2 : 2 + parts], refs[2 + parts : -1], refs[-1]
    sweep(weights, high_refs, low_refs, out_ref, which)
    width = high_refs[0].shape[0]
    for place in range(len(which)):
        out_ref[place, :, width:] = gram_ref[...]


def exact(left, right, dims):
    return lax.dot_general(
        left, right, dims, precision=lax.Precision.HIGHEST, preferred_element_type=jnp.float32
    )


def grown_kernel(*refs):
    inverse_ref, piece_refs, (grown_ref, degree_ref) = refs[0], refs[1:-2], refs[-2:]
    vectors = grown_ref.shape[0]
    width = degree_ref.shape[1]
    total = piece_refs[0][...]
    for ref in piece_refs[1:]:
        total = total + ref[...]
    degree = total[vectors : vectors + 1, :]
    grown = total[0:vectors, :] / degree
    degree_ref[...] = degree
    grown_ref[:, 0:width] = grown * inverse_ref[...]
    gram = exact(grown, grown, ROWS_BY_ROWS)
    grown_ref[:, width:] = jnp.concatenate([gram, jnp.zeros((vectors, 128 - vectors), jnp.float32)], axis=1)


def inverse_factor(gram, panel=16):
    size = gram.shape[0]
    shape = (size, 2 * size)
    line = lax.broadcasted_iota(jnp.int32, (size, size), 0)
    lane = lax.broadcasted_iota(jnp.int32, (size, size), 1)
    table = jnp.concatenate([gram, jnp.where(line == lane, 1.0, 0.0)], axis=1)
    tall = lax.broadcasted_iota(jnp.int32, shape, 0)
    pivots = jnp.zeros(shape, jnp.float32)
    for first in range(0, size, panel):
        columns = [jnp.broadcast_to(table[:, step : step + 1], shape) for step in range(first, first + panel)]
        for place, step in enumerate(range(first, first + panel)):
            pivot = columns[place][step : step + 1, :]
            pivots = jnp.where(tall == step, pivot, pivots)
            factor = jnp.where(tall > step, columns[place] * (1.0 / pivot), 0.0)
            for later in range(place + 1, panel):
                columns[later] = columns[later] - factor * columns[later][step : step + 1, :]
            table = table - factor * table[step : step + 1, :]
    return table[:, size:] * lax.rsqrt(pivots[:, size:])


def grown_two_kernel(*refs, count):
    degree_ref, piece_refs, (grown_ref, gram_ref) = refs[0], refs[1:-2], refs[-2:]
    vectors, width = grown_ref.shape
    total = piece_refs[0][...]
    for ref in piece_refs[1:]:
        total = total + ref[...]
    factor = inverse_factor(total[:, width : width + vectors] * (1.0 / count))
    grown = exact(factor, total[:, 0:width] / degree_ref[...], ROWS_BY_COLUMNS)
    grown_ref[...] = grown
    gram_ref[...] = exact(grown, grown, ROWS_BY_ROWS)


def finish_kernel(*refs, count):
    grown_ref, gram_refs, out_ref = refs[0], refs[1:-1], refs[-1]
    gram = gram_refs[0][...]
    for ref in gram_refs[1:]:
        gram = gram + ref[...]
    out_ref[...] = exact(inverse_factor(gram * (1.0 / count)), grown_ref[...], ROWS_BY_COLUMNS)


def swap(values, axis, mask):
    size = lax.axis_size(axis)
    return lax.ppermute(values, axis, [(index, index ^ mask) for index in range(size)])


def resident_shards(frames, start):
    row_size, column_size = lax.axis_size("row"), lax.axis_size("col")
    count = frames.shape[1] * row_size * column_size
    features, width = frames.shape
    vectors = start.shape[0]
    columns = row_size * width
    near, far = range(1, column_size), range(2, row_size, 2)
    even, odd = range(0, row_size, 2), range(1, row_size, 2)

    row_pieces = [swap(frames, "col", q) for q in near]
    even_pieces = [frames] + [swap(frames, "row", p) for p in far]
    odd_pieces = swap(jnp.stack(even_pieces), "row", 1)
    column_pieces = [(odd_pieces[p // 2] if p % 2 else even_pieces[p // 2]) for p in range(row_size)]
    starts = [start] + [swap(start, "col", q) for q in near]

    operands = 4 * features
    work = 2 * width * columns * operands
    totals = pltpu.VMEM((width, 128), jnp.float32)
    high, low, own_sums, right = call(
        functools.partial(build_own_kernel, column_parts=row_size),
        (bf16(width, columns), bf16(width, columns), f32(8, width), bf16(operands, columns)),
        column_pieces,
        scratch=(pltpu.VMEM((width, operands), jnp.bfloat16), totals),
        flops=2 * work,
        name="build_own",
    )
    rest = len(row_pieces)
    *blocks, sums = call(
        functools.partial(build_rest_kernel, parts=rest),
        (bf16(width, columns),) * (2 * rest) + (f32(8, width),),
        (right, own_sums, *row_pieces),
        scratch=(pltpu.VMEM((rest * width, operands), jnp.bfloat16), totals),
        flops=2 * rest * work,
        name="build_rest",
    )
    stored = (high, *blocks[:rest], low, *blocks[rest:])
    all_sums = [sums] + [swap(sums, "col", q) for q in near]

    def spread(evens, odds):
        own = evens + swap(odds, "row", 1)
        return [own[0]] + [swap(own[p // 2], "row", p) for p in far]

    def total_gram(gram):
        gram = gram + swap(gram, "row", 1)
        gram = functools.reduce(jnp.add, [swap(gram, "row", p) for p in far], gram)
        return [gram] + [swap(gram, "col", q) for q in near]

    rows = vectors + DEGREE_ROWS
    work = 2 * 3 * rows * column_size * width * columns
    odds, inverse, weights = call(
        functools.partial(first_kernel, parts=column_size, peers=column_size, which=odd),
        (f32(len(odd), vectors + 8, width), f32(1, width), bf16(2 * rows, column_size * width)),
        (*all_sums, *starts, *stored),
        flops=work,
        name="first_odd",
    )
    evens = call(
        functools.partial(again_kernel, parts=column_size, which=even),
        f32(len(even), vectors + 8, width),
        (weights, *stored),
        flops=work,
        name="first_even",
    )
    weighted, degree = call(
        grown_kernel, (f32(vectors, width + 128), f32(1, width)), (inverse, *spread(evens, odds)), name="grown"
    )
    pieces = [weighted] + [swap(weighted, "col", q) for q in near]
    odds, gram, weights = call(
        functools.partial(second_kernel, parts=column_size, which=odd),
        (f32(len(odd), vectors, width + 128), f32(vectors, 128), bf16(2 * vectors, column_size * width)),
        (*pieces, *stored),
        flops=work,
        name="second_odd",
    )
    evens = call(
        functools.partial(second_again_kernel, parts=column_size, which=even),
        f32(len(even), vectors, width + 128),
        (weights, gram, *stored),
        flops=work,
        name="second_even",
    )
    grown_two, gram_two = call(
        functools.partial(grown_two_kernel, count=count),
        (f32(vectors, width), f32(vectors, vectors)),
        (degree, *spread(evens, odds)),
        name="grown_two",
    )
    return call(
        functools.partial(finish_kernel, count=count),
        f32(vectors, width),
        (grown_two, *total_gram(gram_two)),
        name="finish",
    )


def build_block(block_points, block_squares, column_points, column_squares):
    products = lax.dot_general(
        block_points, column_points, (((0,), (0,)), ((), ())), precision=lax.Precision.HIGHEST
    )
    distance = block_squares[:, None] + column_squares[None, :] - 2.0 * products
    return jnp.exp(-distance / (0.5 * block_points.shape[0]))


def stored_shards(frames, start):
    block_points = lax.all_gather(frames, "col", axis=1, tiled=True)
    column_points = lax.all_gather(frames, "row", axis=1, tiled=True)
    block_squares = jnp.sum(block_points * block_points, axis=0)
    column_squares = jnp.sum(column_points * column_points, axis=0)
    frame_count = frames.shape[1] * lax.axis_size("row") * lax.axis_size("col")
    block_rows = block_points.shape[1]
    height = min(512, block_rows)
    stored = [
        build_block(
            block_points[:, first : first + height],
            block_squares[first : first + height],
            column_points,
            column_squares,
        )
        for first in range(0, block_rows, height)
    ]

    def settle(partial_value):
        return lax.psum_scatter(partial_value, "col", scatter_dimension=1, tiled=True)

    def kernel_product(weights):
        spread_weights = lax.all_gather(weights, "row", axis=1, tiled=True)
        return settle(
            jnp.concatenate([exact(spread_weights, part, ROWS_BY_ROWS) for part in stored], axis=1)
        )

    def orthonormal(vectors):
        gram = lax.psum(exact(vectors, vectors, ROWS_BY_ROWS), ("row", "col")) / frame_count
        return jax.scipy.linalg.solve_triangular(jnp.linalg.cholesky(gram), vectors, lower=True)

    sums = jnp.concatenate([jnp.sum(part, axis=1)[None, :] for part in stored], axis=1)
    inverse = 1.0 / settle(sums)
    degree = kernel_product(inverse)
    basis_one = orthonormal(kernel_product(start * inverse) / degree)
    return orthonormal(kernel_product(basis_one * inverse) / degree)


def shards(frames, start):
    row_size, column_size = lax.axis_size("row"), lax.axis_size("col")
    entries = row_size * column_size * frames.shape[1] ** 2
    powers = row_size & (row_size - 1) == 0 and column_size & (column_size - 1) == 0
    if powers and row_size > 1 and 4 * entries <= RESIDENT_BYTES:
        return resident_shards(frames, start)
    return stored_shards(frames, start)


def solution(mesh):
    return jax.shard_map(
        shards,
        mesh=mesh,
        in_specs=(P(None, ("row", "col")), P(None, ("row", "col"))),
        out_specs=P(None, ("row", "col")),
        check_vma=False,
    )
```

time: 118 us -> 103 us (0.87)
  starting transfers between devices: 49.3 us -> 41.6 us
  Pallas kernels: 31.8 us -> 25.6 us
  waiting for transfers between devices: 34.7 us -> 33 us
    ppermute x41 -> x31, starting transfers between devices: 49.3 us -> 41.6 us  [swap(): lax.ppermute(values, axis, [(index, index ^ mask) for index in range(size)])]
    pallas_call x7 -> x9, Pallas kernels: 31.8 us -> 25.6 us  [call(): pl.pallas_call(body, out_shape=out_shape, in_specs=[VMEM] * len(operands)...]
    ppermute x41 -> x31, waiting for transfers between devices: 34.7 us -> 33 us  [swap(): lax.ppermute(values, axis, [(index, index ^ mask) for index in range(size)])]
  transfers between devices with their start and end apart: 41 -> 31, of which waited for: 18 -> 18; matrix products, arithmetic and copies ran while one was open for 0% -> 0% of each run, Pallas kernels for 13% -> 16%
where the time goes in v1:
time: 103 us; the launch traced here: 102 us
  starting transfers between devices  41.6 us (40%)
  waiting for transfers between devices  33 us (32%)
  Pallas kernels  25.6 us (25%)
  other arithmetic  1.05 us (1%)
    ppermute x31, starting transfers between devices, swap(): lax.ppermute(values, axis, [(index, index ^ mask) for index in range(size)])  41.6 us
    ppermute x31, waiting for transfers between devices, swap(): lax.ppermute(values, axis, [(index, index ^ mask) for index in range(size)])  33 us
    pallas_call x9, Pallas kernels, call(): pl.pallas_call(body, out_shape=out_shape, in_specs=[VMEM] * len(operands)...  25.6 us
  transfers between devices with their start and end apart: 31, of which 18 were waited for; matrix products, arithmetic and copies ran while one was open for 0% of the time, Pallas kernels for 16%

profile of v1, /device:TPU:0, one launch (start us, length us, event | category | flops | bytes accessed | tf_op | source)
XLA Modules:
  0.0 102.4 jit_solution(17361981211923678880)
XLA Ops:
  0.0 2.9 %collective-permute-start = (f32[64,512]{1,0:T(8,128)}, f32[64,512]{1,0:T(8,128)S(1)}, u32[]{:S(2)}, u32[]{:S(2)}) collective-permute-start(f32[64,512]{1,0:T(8,128)} %refs_0_.1), channel_id=1, source_target_pairs={{0,8},{4,12},{8,0},{12,4},{16,24},{20,28},{24,16},{28,20},{1,9},{5... | collective-permute-start | bytes 393224 | tf_op jit(solution)/shard_map/ppermute | solution.py:270
  2.9 1.5 %collective-permute-start.1 = (f32[64,512]{1,0:T(8,128)}, f32[64,512]{1,0:T(8,128)S(1)}, u32[]{:S(2)}, u32[]{:S(2)}) collective-permute-start(f32[64,512]{1,0:T(8,128)} %refs_0_.1), channel_id=1, source_target_pairs={{0,16},{4,20},{8,24},{12,28},{16,0},{20,4},{24,8},{28,12},{1,17},{... | collective-permute-start | bytes 393224 | tf_op jit(solution)/shard_map/ppermute | solution.py:270
  4.5 2.7 %collective-permute-done.refs_2_ = f32[64,512]{1,0:T(8,128)S(1)} collective-permute-done((f32[64,512]{1,0:T(8,128)}, f32[64,512]{1,0:T(8,128)S(1)}, u32[]{:S(2)}, u32[]{:S(2)}) %collective-permute-start) | collective-permute-done | bytes 131104 | tf_op jit(solution)/shard_map/ppermute | solution.py:270
  7.2 3.8 %collective-permute-done.1.refs_4_ = f32[64,512]{1,0:T(8,128)S(1)} collective-permute-done((f32[64,512]{1,0:T(8,128)}, f32[64,512]{1,0:T(8,128)S(1)}, u32[]{:S(2)}, u32[]{:S(2)}) %collective-permute-start.1) | collective-permute-done | bytes 131104 | tf_op jit(solution)/shard_map/ppermute | solution.py:270
  10.9 0.9 pad_maximum_fusion
  12.0 1.6 %collective-permute-start.4 = (f32[64,512]{1,0:T(8,128)}, f32[64,512]{1,0:T(8,128)S(1)}, u32[]{:S(2)}, u32[]{:S(2)}) collective-permute-start(f32[64,512]{1,0:T(8,128)} %refs_0_.1), channel_id=1, source_target_pairs={{0,1},{1,0},{2,3},{3,2},{4,5},{5,4},{6,7},{7,6},{8,9},{9,8},{10,11... | collective-permute-start | bytes 393224 | tf_op jit(solution)/shard_map/ppermute | solution.py:270
  13.6 2.6 %collective-permute-start.5 = (f32[64,512]{1,0:T(8,128)}, f32[64,512]{1,0:T(8,128)S(1)}, u32[]{:S(2)}, u32[]{:S(2)}) collective-permute-start(f32[64,512]{1,0:T(8,128)} %refs_0_.1), channel_id=1, source_target_pairs={{0,2},{1,3},{2,0},{3,1},{4,6},{5,7},{6,4},{7,5},{8,10},{9,11},{10,... | collective-permute-start | bytes 393224 | tf_op jit(solution)/shard_map/ppermute | solution.py:270
  17.1 3.5 %collective-permute-start.11 = (f32[32,512]{1,0:T(8,128)}, f32[32,512]{1,0:T(8,128)S(1)}, u32[]{:S(2)}, u32[]{:S(2)}) collective-permute-start(f32[32,512]{1,0:T(8,128)} %refs_4_.1), channel_id=1, source_target_pairs={{0,2},{1,3},{2,0},{3,1},{4,6},{5,7},{6,4},{7,5},{8,10},{9,11},{10,... | collective-permute-start | bytes 196616 | tf_op jit(solution)/shard_map/ppermute | solution.py:270
  20.6 0.9 copy-done
  21.5 3.0 %build_own.1 = (bf16[512,4096]{1,0:T(8,128)(2,1)S(1)}, bf16[512,4096]{1,0:T(8,128)(2,1)S(1)}, f32[8,512]{1,0:T(8,128)S(1)}, bf16[256,4096]{1,0:T(8,128)(2,1)S(1)}) custom-call(f32[64,512]{1,0:T(8,128)S(1)} %copy-done, f32[64,512]{1,0:T(8,128)S(1)} %get-tuple-element.50.refs_1_, f32[64,512]{1,0:T(8,128)S(1)} %collective-permute-done.refs_2_, ...), custom_call_target="tpu_custom_call" | custom-call | flops 2147483648 | tf_op jit(solution)/shard_map/build_own/pallas_call | solution.py:18
  24.8 1.9 %collective-permute-done.5.refs_3_ = f32[64,512]{1,0:T(8,128)S(1)} collective-permute-done((f32[64,512]{1,0:T(8,128)}, f32[64,512]{1,0:T(8,128)S(1)}, u32[]{:S(2)}, u32[]{:S(2)}) %collective-permute-start.5) | collective-permute-done | bytes 131104 | tf_op jit(solution)/shard_map/ppermute | solution.py:270
  26.7 7.5 %build_rest.1 = (bf16[512,4096]{1,0:T(8,128)(2,1)S(1)}, bf16[512,4096]{1,0:T(8,128)(2,1)S(1)}, bf16[512,4096]{1,0:T(8,128)(2,1)S(1)}, bf16[512,4096]{1,0:T(8,128...) custom-call(bf16[256,4096]{1,0:T(8,128)(2,1)S(1)} %get-tuple-element.26.refs_0_, ...), custom_call_target="tpu_custom_call" | custom-call | flops 6442450944 | tf_op jit(solution)/shard_map/build_rest/pallas_call | solution.py:18
  34.2 6.3 %collective-permute-start.7 = (f32[8,512]{1,0:T(8,128)S(1)}, f32[8,512]{1,0:T(8,128)S(1)}, u32[]{:S(2)}, u32[]{:S(2)}) collective-permute-start(f32[8,512]{1,0:T(8,128)S(1)} %get-tuple-element.28.refs_0_), channel_id=1, source_target_pairs={{0,1},{1,0},{2,3},{3,2},{4,5},{5,4},{6,7},{7,6},{8,9},{9,8},{10,11... | collective-permute-start | bytes 49160 | tf_op jit(solution)/shard_map/ppermute | solution.py:270
  40.5 1.1 %collective-permute-start.8 = (f32[8,512]{1,0:T(8,128)S(1)}, f32[8,512]{1,0:T(8,128)S(1)}, u32[]{:S(2)}, u32[]{:S(2)}) collective-permute-start(f32[8,512]{1,0:T(8,128)S(1)} %get-tuple-element.28.refs_0_), channel_id=1, source_target_pairs={{0,2},{1,3},{2,0},{3,1},{4,6},{5,7},{6,4},{7,5},{8,10},{9,11},{10,... | collective-permute-start | bytes 49160 | tf_op jit(solution)/shard_map/ppermute | solution.py:270
  41.6 1.4 %collective-permute-start.9 = (f32[8,512]{1,0:T(8,128)S(1)}, f32[8,512]{1,0:T(8,128)S(1)}, u32[]{:S(2)}, u32[]{:S(2)}) collective-permute-start(f32[8,512]{1,0:T(8,128)S(1)} %get-tuple-element.28.refs_0_), channel_id=1, source_target_pairs={{0,3},{1,2},{2,1},{3,0},{4,7},{5,6},{6,5},{7,4},{8,11},{9,10},{10,... | collective-permute-start | bytes 49160 | tf_op jit(solution)/shard_map/ppermute | solution.py:270
  43.0 2.1 %collective-permute-done.8.refs_2_ = f32[8,512]{1,0:T(8,128)S(1)} collective-permute-done((f32[8,512]{1,0:T(8,128)S(1)}, f32[8,512]{1,0:T(8,128)S(1)}, u32[]{:S(2)}, u32[]{:S(2)}) %collective-permute-start.8) | collective-permute-done | bytes 16416 | tf_op jit(solution)/shard_map/ppermute | solution.py:270
  45.1 2.0 %collective-permute-done.9.refs_3_ = f32[8,512]{1,0:T(8,128)S(1)} collective-permute-done((f32[8,512]{1,0:T(8,128)S(1)}, f32[8,512]{1,0:T(8,128)S(1)}, u32[]{:S(2)}, u32[]{:S(2)}) %collective-permute-start.9) | collective-permute-done | bytes 16416 | tf_op jit(solution)/shard_map/ppermute | solution.py:270
  47.2 3.1 %first_odd.1 = (f32[4,40,512]{2,1,0:T(8,128)S(1)}, f32[1,512]{1,0:T(1,128)S(1)}, bf16[96,2048]{1,0:T(8,128)(2,1)S(1)}) custom-call(f32[8,512]{1,0:T(8,128)S(1)} %get-tuple-element.28.refs_0_, f32[8,512]{1,0:T(8,128)S(1)} %collective-permute-done.7.refs_1_, f32[8,512]{1,0:T(8,128)S(1)} %collective-permute-done.8.refs_2_, ...), custom_call_target="tpu_custom_call" | custom-call | flops 2415919104 | tf_op jit(solution)/shard_map/first_odd/pallas_call | solution.py:18
  50.3 2.9 %first_even.1 = f32[4,40,512]{2,1,0:T(8,128)S(1)} custom-call(bf16[96,2048]{1,0:T(8,128)(2,1)S(1)} %get-tuple-element.38.refs_0_, bf16[512,4096]{1,0:T(8,128)(2,1)S(1)} %get-tuple-element.29.refs_8_.refs_1_.refs_4_.refs_2_, bf16[512,4096]{1,0:T(8,128)(2,1)S(1)} %get-tuple-element.30.refs_9_.refs_2_.refs_5_.refs_3_, ...), custom_call_target="tpu_custom_call" | custom-call | flops 2415919104 | tf_op jit(solution)/shard_map/first_even/pallas_call | solution.py:18
  53.3 1.3 %collective-permute-start.14 = (f32[40,512]{1,0:T(8,128)S(1)}, f32[40,512]{1,0:T(8,128)S(1)}, u32[]{:S(2)}, u32[]{:S(2)}) collective-permute-start(f32[40,512]{1,0:T(8,128)S(1)} %get-tuple-element.57), channel_id=1, source_target_pairs={{0,8},{4,12},{8,0},{12,4},{16,24},{20,28},{24,16},{28,20},{1,9},{5... | collective-permute-start | bytes 245768 | tf_op jit(solution)/shard_map/ppermute | solution.py:270
  54.6 0.8 collective-permute-start.15
  55.4 1.4 %collective-permute-start.16 = (f32[40,512]{1,0:T(8,128)S(1)}, f32[40,512]{1,0:T(8,128)S(1)}, u32[]{:S(2)}, u32[]{:S(2)}) collective-permute-start(f32[40,512]{1,0:T(8,128)S(1)} %get-tuple-element.55), channel_id=1, source_target_pairs={{0,24},{4,28},{8,16},{12,20},{16,8},{20,12},{24,0},{28,4},{1,25},{... | collective-permute-start | bytes 245768 | tf_op jit(solution)/shard_map/ppermute | solution.py:270
  56.9 1.4 %collective-permute-done.14.refs_2_ = f32[40,512]{1,0:T(8,128)S(1)} collective-permute-done((f32[40,512]{1,0:T(8,128)S(1)}, f32[40,512]{1,0:T(8,128)S(1)}, u32[]{:S(2)}, u32[]{:S(2)}) %collective-permute-start.14) | collective-permute-done | bytes 81952 | tf_op jit(solution)/shard_map/ppermute | solution.py:270
  58.2 1.2 %collective-permute-done.15.refs_3_ = f32[40,512]{1,0:T(8,128)S(1)} collective-permute-done((f32[40,512]{1,0:T(8,128)S(1)}, f32[40,512]{1,0:T(8,128)S(1)}, u32[]{:S(2)}, u32[]{:S(2)}) %collective-permute-start.15) | collective-permute-done | bytes 81952 | tf_op jit(solution)/shard_map/ppermute | solution.py:270
  59.5 1.5 %collective-permute-done.16.refs_4_ = f32[40,512]{1,0:T(8,128)S(1)} collective-permute-done((f32[40,512]{1,0:T(8,128)S(1)}, f32[40,512]{1,0:T(8,128)S(1)}, u32[]{:S(2)}, u32[]{:S(2)}) %collective-permute-start.16) | collective-permute-done | bytes 81952 | tf_op jit(solution)/shard_map/ppermute | solution.py:270
  61.4 1.8 %collective-permute-start.18 = (f32[32,640]{1,0:T(8,128)S(1)}, f32[32,640]{1,0:T(8,128)S(1)}, u32[]{:S(2)}, u32[]{:S(2)}) collective-permute-start(f32[32,640]{1,0:T(8,128)S(1)} %get-tuple-element.41.refs_0_), channel_id=1, source_target_pairs={{0,2},{1,3},{2,0},{3,1},{4,6},{5,7},{6,4},{7,5},{8,10},{9,11},{10,... | collective-permute-start | bytes 245768 | tf_op jit(solution)/shard_map/ppermute | solution.py:270
  63.2 2.4 %collective-permute-start.19 = (f32[32,640]{1,0:T(8,128)S(1)}, f32[32,640]{1,0:T(8,128)S(1)}, u32[]{:S(2)}, u32[]{:S(2)}) collective-permute-start(f32[32,640]{1,0:T(8,128)S(1)} %get-tuple-element.41.refs_0_), channel_id=1, source_target_pairs={{0,3},{1,2},{2,1},{3,0},{4,7},{5,6},{6,5},{7,4},{8,11},{9,10},{10,... | collective-permute-start | bytes 245768 | tf_op jit(solution)/shard_map/ppermute | solution.py:270
  66.0 4.4 %collective-permute-done.18.refs_2_ = f32[32,640]{1,0:T(8,128)S(1)} collective-permute-done((f32[32,640]{1,0:T(8,128)S(1)}, f32[32,640]{1,0:T(8,128)S(1)}, u32[]{:S(2)}, u32[]{:S(2)}) %collective-permute-start.18) | collective-permute-done | bytes 81952 | tf_op jit(solution)/shard_map/ppermute | solution.py:270
  70.4 3.0 %second_odd.1 = (f32[4,32,640]{2,1,0:T(8,128)S(1)}, f32[32,128]{1,0:T(8,128)S(1)}, bf16[64,2048]{1,0:T(8,128)(2,1)S(1)}) custom-call(f32[32,640]{1,0:T(8,128)S(1)} %get-tuple-element.41.refs_0_, f32[32,640]{1,0:T(8,128)S(1)} %collective-permute-done.17.refs_1_, f32[32,640]{1,0:T(8,128)S(1)} %collective-permute-done.18.refs_2_, ...), custom_call_target="tpu_custom_call" | custom-call | flops 2415919104 | tf_op jit(solution)/shard_map/second_odd/pallas_call | solution.py:18
  73.4 3.0 %second_even.1 = f32[4,32,640]{2,1,0:T(8,128)S(1)} custom-call(bf16[64,2048]{1,0:T(8,128)(2,1)S(1)} %get-tuple-element.42.refs_0_, f32[32,128]{1,0:T(8,128)S(1)} %get-tuple-element.43.refs_1_, bf16[512,4096]{1,0:T(8,128)(2,1)S(1)} %get-tuple-element.29.refs_8_.refs_1_.refs_4_.refs_2_, ...), custom_call_target="tpu_custom_call" | custom-call | flops 2415919104 | tf_op jit(solution)/shard_map/second_even/pallas_call | solution.py:18
  76.5 0.8 collective-permute-start.21
  77.3 0.8 collective-permute-start.22
  78.1 2.0 %collective-permute-start.23 = (f32[32,640]{1,0:T(8,128)S(1)}, f32[32,640]{1,0:T(8,128)S(1)}, u32[]{:S(2)}, u32[]{:S(2)}) collective-permute-start(f32[32,640]{1,0:T(8,128)S(1)} %get-tuple-element.51), channel_id=1, source_target_pairs={{0,24},{4,28},{8,16},{12,20},{16,8},{20,12},{24,0},{28,4},{1,25},{... | collective-permute-start | bytes 245768 | tf_op jit(solution)/shard_map/ppermute | solution.py:270
  80.1 1.5 %collective-permute-done.21.refs_2_ = f32[32,640]{1,0:T(8,128)S(1)} collective-permute-done((f32[32,640]{1,0:T(8,128)S(1)}, f32[32,640]{1,0:T(8,128)S(1)}, u32[]{:S(2)}, u32[]{:S(2)}) %collective-permute-start.21) | collective-permute-done | bytes 81952 | tf_op jit(solution)/shard_map/ppermute | solution.py:270
  81.6 2.0 %collective-permute-done.22.refs_3_ = f32[32,640]{1,0:T(8,128)S(1)} collective-permute-done((f32[32,640]{1,0:T(8,128)S(1)}, f32[32,640]{1,0:T(8,128)S(1)}, u32[]{:S(2)}, u32[]{:S(2)}) %collective-permute-start.22) | collective-permute-done | bytes 81952 | tf_op jit(solution)/shard_map/ppermute | solution.py:270
  83.6 1.2 %grown_two.1 = (f32[32,512]{1,0:T(8,128)S(1)}, f32[32,32]{1,0:T(8,128)S(1)}) custom-call(f32[1,512]{1,0:T(1,128)S(1)} %get-tuple-element.40.refs_0_, f32[32,640]{1,0:T(8,128)S(1)} %get-tuple-element.54.refs_1_, f32[32,640]{1,0:T(8,128)S(1)} %collective-permute-done.21.refs_2_, f32[32,640]{1,0:T(8,128)S(1)} %collective-permute-done.22.refs_3_, ...), custom_call_target="tpu_custom_call" | custom-call | tf_op jit(solution)/shard_map/grown_two/pallas_call | solution.py:18
  84.8 1.2 %collective-permute-done.24 = f32[32,32]{1,0:T(8,128)S(1)} collective-permute-done((f32[32,32]{1,0:T(8,128)S(1)}, f32[32,32]{1,0:T(8,128)S(1)}, u32[]{:S(2)}, u32[]{:S(2)}) %collective-permute-start.24) | collective-permute-done | bytes 4128 | tf_op jit(solution)/shard_map/ppermute | solution.py:270
  86.0 1.3 %collective-permute-start.25 = (f32[32,32]{1,0:T(8,128)S(1)}, f32[32,32]{1,0:T(8,128)S(1)}, u32[]{:S(2)}, u32[]{:S(2)}) collective-permute-start(f32[32,32]{1,0:T(8,128)S(1)} %add.20), channel_id=1, source_target_pairs={{0,8},{4,12},{8,0},{12,4},{16,24},{20,28},{24,16},{28,20},{1,9},{5... | collective-permute-start | bytes 12296 | tf_op jit(solution)/shard_map/ppermute | solution.py:270
  87.3 1.0 %collective-permute-start.26 = (f32[32,32]{1,0:T(8,128)S(1)}, f32[32,32]{1,0:T(8,128)S(1)}, u32[]{:S(2)}, u32[]{:S(2)}) collective-permute-start(f32[32,32]{1,0:T(8,128)S(1)} %add.20), channel_id=1, source_target_pairs={{0,16},{4,20},{8,24},{12,28},{16,0},{20,4},{24,8},{28,12},{1,17},{... | collective-permute-start | bytes 12296 | tf_op jit(solution)/shard_map/ppermute | solution.py:270
  88.4 1.1 %collective-permute-start.27 = (f32[32,32]{1,0:T(8,128)S(1)}, f32[32,32]{1,0:T(8,128)S(1)}, u32[]{:S(2)}, u32[]{:S(2)}) collective-permute-start(f32[32,32]{1,0:T(8,128)S(1)} %add.20), channel_id=1, source_target_pairs={{0,24},{4,28},{8,16},{12,20},{16,8},{20,12},{24,0},{28,4},{1,25},{... | collective-permute-start | bytes 12296 | tf_op jit(solution)/shard_map/ppermute | solution.py:270
  89.7 1.3 %collective-permute-done.26 = f32[32,32]{1,0:T(8,128)S(1)} collective-permute-done((f32[32,32]{1,0:T(8,128)S(1)}, f32[32,32]{1,0:T(8,128)S(1)}, u32[]{:S(2)}, u32[]{:S(2)}) %collective-permute-start.26) | collective-permute-done | bytes 4128 | tf_op jit(solution)/shard_map/ppermute | solution.py:270
  91.1 1.9 %collective-permute-done.27 = f32[32,32]{1,0:T(8,128)S(1)} collective-permute-done((f32[32,32]{1,0:T(8,128)S(1)}, f32[32,32]{1,0:T(8,128)S(1)}, u32[]{:S(2)}, u32[]{:S(2)}) %collective-permute-start.27) | collective-permute-done | bytes 4128 | tf_op jit(solution)/shard_map/ppermute | solution.py:270
  93.0 1.4 %collective-permute-start.28 = (f32[32,32]{1,0:T(8,128)S(1)}, f32[32,32]{1,0:T(8,128)S(1)}, u32[]{:S(2)}, u32[]{:S(2)}) collective-permute-start(f32[32,32]{1,0:T(8,128)S(1)} %add_add_fusion.refs_1_), channel_id=1, source_target_pairs={{0,1},{1,0},{2,3},{3,2},{4,5},{5,4},{6,7},{7,6},{8,9},{9,8},{10,11... | collective-permute-start | bytes 12296 | tf_op jit(solution)/shard_map/ppermute | solution.py:270
  94.4 0.8 collective-permute-start.29
  95.2 2.1 %collective-permute-start.30 = (f32[32,32]{1,0:T(8,128)S(1)}, f32[32,32]{1,0:T(8,128)S(1)}, u32[]{:S(2)}, u32[]{:S(2)}) collective-permute-start(f32[32,32]{1,0:T(8,128)S(1)} %add_add_fusion.refs_1_), channel_id=1, source_target_pairs={{0,3},{1,2},{2,1},{3,0},{4,7},{5,6},{6,5},{7,4},{8,11},{9,10},{10,... | collective-permute-start | bytes 12296 | tf_op jit(solution)/shard_map/ppermute | solution.py:270
  97.4 1.9 %collective-permute-done.29.refs_3_ = f32[32,32]{1,0:T(8,128)S(1)} collective-permute-done((f32[32,32]{1,0:T(8,128)S(1)}, f32[32,32]{1,0:T(8,128)S(1)}, u32[]{:S(2)}, u32[]{:S(2)}) %collective-permute-start.29) | collective-permute-done | bytes 4128 | tf_op jit(solution)/shard_map/ppermute | solution.py:270
  99.2 1.5 %collective-permute-done.30.refs_4_ = f32[32,32]{1,0:T(8,128)S(1)} collective-permute-done((f32[32,32]{1,0:T(8,128)S(1)}, f32[32,32]{1,0:T(8,128)S(1)}, u32[]{:S(2)}, u32[]{:S(2)}) %collective-permute-start.30) | collective-permute-done | bytes 4128 | tf_op jit(solution)/shard_map/ppermute | solution.py:270
  100.8 1.6 %finish.1 = f32[32,512]{1,0:T(8,128)} custom-call(f32[32,512]{1,0:T(8,128)S(1)} %get-tuple-element.45.refs_0_, f32[32,32]{1,0:T(8,128)S(1)} %add_add_fusion.refs_1_, f32[32,32]{1,0:T(8,128)S(1)} %collective-permute-done.28.refs_2_, f32[32,32]{1,0:T(8,128)S(1)} %collective-permute-done.29.refs_3_, f32[32,32]{1,0:T(8,128)S(1)} %collective-permute-done.30.refs_4_), custom_call_target="tpu_custom_call" | custom-call | tf_op jit(solution)/shard_map/finish/pallas_call | solution.py:18
  (35 shorter events, 2.6 us)
Async XLA Ops:
  0.0 7.2 %collective-permute-start = (f32[64,512]{1,0:T(8,128)}, f32[64,512]{1,0:T(8,128)S(1)}, u32[]{:S(2)}, u32[]{:S(2)}) collective-permute-start(f32[64,512]{1,0:T(8,128)} %refs_0_.1), channel_id=1, source_target_pairs={{0,8},{4,12},{8,0},{12,4},{16,24},{20,28},{24,16},{28,20},{1,9},{5... | collective-permute-start | bytes 393224 | tf_op jit(solution)/shard_map/ppermute | solution.py:270
  2.9 8.0 %collective-permute-start.1 = (f32[64,512]{1,0:T(8,128)}, f32[64,512]{1,0:T(8,128)S(1)}, u32[]{:S(2)}, u32[]{:S(2)}) collective-permute-start(f32[64,512]{1,0:T(8,128)} %refs_0_.1), channel_id=1, source_target_pairs={{0,16},{4,20},{8,24},{12,28},{16,0},{20,4},{24,8},{28,12},{1,17},{... | collective-permute-start | bytes 393224 | tf_op jit(solution)/shard_map/ppermute | solution.py:270
  4.5 6.5 %collective-permute-start.2 = (f32[64,512]{1,0:T(8,128)}, f32[64,512]{1,0:T(8,128)S(1)}, u32[]{:S(2)}, u32[]{:S(2)}) collective-permute-start(f32[64,512]{1,0:T(8,128)} %refs_0_.1), channel_id=1, source_target_pairs={{0,24},{4,28},{8,16},{12,20},{16,8},{20,12},{24,0},{28,4},{1,25},{... | collective-permute-start | bytes 393224 | tf_op jit(solution)/shard_map/ppermute | solution.py:270
  11.9 5.2 %collective-permute-start.3 = (f32[4,64,512]{2,1,0:T(8,128)S(1)}, f32[4,64,512]{2,1,0:T(8,128)S(1)}, u32[]{:S(2)}, u32[]{:S(2)}) collective-permute-start(f32[4,64,512]{2,1,0:T(8,128)S(1)} %pad_maximum_fusion), channel_id=1, source_target_pairs={{0,4},{4,0},{8,12},{12,8},{16,20},{20,16},{24,28},{28,24},{1,5},{5... | collective-permute-start | bytes 1572872 | tf_op jit(solution)/shard_map/ppermute | solution.py:270
  12.0 12.6 %collective-permute-start.4 = (f32[64,512]{1,0:T(8,128)}, f32[64,512]{1,0:T(8,128)S(1)}, u32[]{:S(2)}, u32[]{:S(2)}) collective-permute-start(f32[64,512]{1,0:T(8,128)} %refs_0_.1), channel_id=1, source_target_pairs={{0,1},{1,0},{2,3},{3,2},{4,5},{5,4},{6,7},{7,6},{8,9},{9,8},{10,11... | collective-permute-start | bytes 393224 | tf_op jit(solution)/shard_map/ppermute | solution.py:270
  13.6 13.1 %collective-permute-start.5 = (f32[64,512]{1,0:T(8,128)}, f32[64,512]{1,0:T(8,128)S(1)}, u32[]{:S(2)}, u32[]{:S(2)}) collective-permute-start(f32[64,512]{1,0:T(8,128)} %refs_0_.1), channel_id=1, source_target_pairs={{0,2},{1,3},{2,0},{3,1},{4,6},{5,7},{6,4},{7,5},{8,10},{9,11},{10,... | collective-permute-start | bytes 393224 | tf_op jit(solution)/shard_map/ppermute | solution.py:270
  16.2 10.5 %collective-permute-start.6 = (f32[64,512]{1,0:T(8,128)}, f32[64,512]{1,0:T(8,128)S(1)}, u32[]{:S(2)}, u32[]{:S(2)}) collective-permute-start(f32[64,512]{1,0:T(8,128)} %refs_0_.1), channel_id=1, source_target_pairs={{0,3},{1,2},{2,1},{3,0},{4,7},{5,6},{6,5},{7,4},{8,11},{9,10},{10,... | collective-permute-start | bytes 393224 | tf_op jit(solution)/shard_map/ppermute | solution.py:270
  16.4 25.2 %collective-permute-start.10 = (f32[32,512]{1,0:T(8,128)}, f32[32,512]{1,0:T(8,128)S(1)}, u32[]{:S(2)}, u32[]{:S(2)}) collective-permute-start(f32[32,512]{1,0:T(8,128)} %refs_4_.1), channel_id=1, source_target_pairs={{0,1},{1,0},{2,3},{3,2},{4,5},{5,4},{6,7},{7,6},{8,9},{9,8},{10,11... | collective-permute-start | bytes 196616 | tf_op jit(solution)/shard_map/ppermute | solution.py:270
  17.1 25.9 %collective-permute-start.11 = (f32[32,512]{1,0:T(8,128)}, f32[32,512]{1,0:T(8,128)S(1)}, u32[]{:S(2)}, u32[]{:S(2)}) collective-permute-start(f32[32,512]{1,0:T(8,128)} %refs_4_.1), channel_id=1, source_target_pairs={{0,2},{1,3},{2,0},{3,1},{4,6},{5,7},{6,4},{7,5},{8,10},{9,11},{10,... | collective-permute-start | bytes 196616 | tf_op jit(solution)/shard_map/ppermute | solution.py:270
  20.6 4.0 %copy-start.1 = (f32[32,512]{1,0:T(8,128)S(1)}, f32[32,512]{1,0:T(8,128)}, u32[]{:S(2)}) copy-start(f32[32,512]{1,0:T(8,128)} %refs_4_.1) | copy-start | bytes 196612
  20.6 0.9 copy-start
  24.6 18.4 %collective-permute-start.12 = (f32[32,512]{1,0:T(8,128)S(1)}, f32[32,512]{1,0:T(8,128)S(1)}, u32[]{:S(2)}, u32[]{:S(2)}) collective-permute-start(f32[32,512]{1,0:T(8,128)S(1)} %copy-done.1), channel_id=1, source_target_pairs={{0,3},{1,2},{2,1},{3,0},{4,7},{5,6},{6,5},{7,4},{8,11},{9,10},{10,... | collective-permute-start | bytes 196616 | tf_op jit(solution)/shard_map/ppermute | solution.py:270
  34.2 8.8 %collective-permute-start.7 = (f32[8,512]{1,0:T(8,128)S(1)}, f32[8,512]{1,0:T(8,128)S(1)}, u32[]{:S(2)}, u32[]{:S(2)}) collective-permute-start(f32[8,512]{1,0:T(8,128)S(1)} %get-tuple-element.28.refs_0_), channel_id=1, source_target_pairs={{0,1},{1,0},{2,3},{3,2},{4,5},{5,4},{6,7},{7,6},{8,9},{9,8},{10,11... | collective-permute-start | bytes 49160 | tf_op jit(solution)/shard_map/ppermute | solution.py:270
  40.5 4.6 %collective-permute-start.8 = (f32[8,512]{1,0:T(8,128)S(1)}, f32[8,512]{1,0:T(8,128)S(1)}, u32[]{:S(2)}, u32[]{:S(2)}) collective-permute-start(f32[8,512]{1,0:T(8,128)S(1)} %get-tuple-element.28.refs_0_), channel_id=1, source_target_pairs={{0,2},{1,3},{2,0},{3,1},{4,6},{5,7},{6,4},{7,5},{8,10},{9,11},{10,... | collective-permute-start | bytes 49160 | tf_op jit(solution)/shard_map/ppermute | solution.py:270
  41.6 5.5 %collective-permute-start.9 = (f32[8,512]{1,0:T(8,128)S(1)}, f32[8,512]{1,0:T(8,128)S(1)}, u32[]{:S(2)}, u32[]{:S(2)}) collective-permute-start(f32[8,512]{1,0:T(8,128)S(1)} %get-tuple-element.28.refs_0_), channel_id=1, source_target_pairs={{0,3},{1,2},{2,1},{3,0},{4,7},{5,6},{6,5},{7,4},{8,11},{9,10},{10,... | collective-permute-start | bytes 49160 | tf_op jit(solution)/shard_map/ppermute | solution.py:270
  50.3 3.0 %collective-permute-start.13 = (f32[4,40,512]{2,1,0:T(8,128)S(1)}, f32[4,40,512]{2,1,0:T(8,128)S(1)}, u32[]{:S(2)}, u32[]{:S(2)}) collective-permute-start(f32[4,40,512]{2,1,0:T(8,128)S(1)} %get-tuple-element.39), channel_id=1, source_target_pairs={{0,4},{4,0},{8,12},{12,8},{16,20},{20,16},{24,28},{28,24},{1,5},{5... | collective-permute-start | bytes 983048 | tf_op jit(solution)/shard_map/ppermute | solution.py:270
  53.3 4.9 %collective-permute-start.14 = (f32[40,512]{1,0:T(8,128)S(1)}, f32[40,512]{1,0:T(8,128)S(1)}, u32[]{:S(2)}, u32[]{:S(2)}) collective-permute-start(f32[40,512]{1,0:T(8,128)S(1)} %get-tuple-element.57), channel_id=1, source_target_pairs={{0,8},{4,12},{8,0},{12,4},{16,24},{20,28},{24,16},{28,20},{1,9},{5... | collective-permute-start | bytes 245768 | tf_op jit(solution)/shard_map/ppermute | solution.py:270
  54.6 4.9 %collective-permute-start.15 = (f32[40,512]{1,0:T(8,128)S(1)}, f32[40,512]{1,0:T(8,128)S(1)}, u32[]{:S(2)}, u32[]{:S(2)}) collective-permute-start(f32[40,512]{1,0:T(8,128)S(1)} %get-tuple-element.56), channel_id=1, source_target_pairs={{0,16},{4,20},{8,24},{12,28},{16,0},{20,4},{24,8},{28,12},{1,17},{... | collective-permute-start | bytes 245768 | tf_op jit(solution)/shard_map/ppermute | solution.py:270
  55.4 5.5 %collective-permute-start.16 = (f32[40,512]{1,0:T(8,128)S(1)}, f32[40,512]{1,0:T(8,128)S(1)}, u32[]{:S(2)}, u32[]{:S(2)}) collective-permute-start(f32[40,512]{1,0:T(8,128)S(1)} %get-tuple-element.55), channel_id=1, source_target_pairs={{0,24},{4,28},{8,16},{12,20},{16,8},{20,12},{24,0},{28,4},{1,25},{... | collective-permute-start | bytes 245768 | tf_op jit(solution)/shard_map/ppermute | solution.py:270
  61.2 4.8 %collective-permute-start.17 = (f32[32,640]{1,0:T(8,128)S(1)}, f32[32,640]{1,0:T(8,128)S(1)}, u32[]{:S(2)}, u32[]{:S(2)}) collective-permute-start(f32[32,640]{1,0:T(8,128)S(1)} %get-tuple-element.41.refs_0_), channel_id=1, source_target_pairs={{0,1},{1,0},{2,3},{3,2},{4,5},{5,4},{6,7},{7,6},{8,9},{9,8},{10,11... | collective-permute-start | bytes 245768 | tf_op jit(solution)/shard_map/ppermute | solution.py:270
  61.4 9.0 %collective-permute-start.18 = (f32[32,640]{1,0:T(8,128)S(1)}, f32[32,640]{1,0:T(8,128)S(1)}, u32[]{:S(2)}, u32[]{:S(2)}) collective-permute-start(f32[32,640]{1,0:T(8,128)S(1)} %get-tuple-element.41.refs_0_), channel_id=1, source_target_pairs={{0,2},{1,3},{2,0},{3,1},{4,6},{5,7},{6,4},{7,5},{8,10},{9,11},{10,... | collective-permute-start | bytes 245768 | tf_op jit(solution)/shard_map/ppermute | solution.py:270
  63.2 7.2 %collective-permute-start.19 = (f32[32,640]{1,0:T(8,128)S(1)}, f32[32,640]{1,0:T(8,128)S(1)}, u32[]{:S(2)}, u32[]{:S(2)}) collective-permute-start(f32[32,640]{1,0:T(8,128)S(1)} %get-tuple-element.41.refs_0_), channel_id=1, source_target_pairs={{0,3},{1,2},{2,1},{3,0},{4,7},{5,6},{6,5},{7,4},{8,11},{9,10},{10,... | collective-permute-start | bytes 245768 | tf_op jit(solution)/shard_map/ppermute | solution.py:270
  73.4 3.0 %collective-permute-start.20 = (f32[4,32,640]{2,1,0:T(8,128)S(1)}, f32[4,32,640]{2,1,0:T(8,128)S(1)}, u32[]{:S(2)}, u32[]{:S(2)}) collective-permute-start(f32[4,32,640]{2,1,0:T(8,128)S(1)} %get-tuple-element.44), channel_id=1, source_target_pairs={{0,4},{4,0},{8,12},{12,8},{16,20},{20,16},{24,28},{28,24},{1,5},{5... | collective-permute-start | bytes 983048 | tf_op jit(solution)/shard_map/ppermute | solution.py:270
  76.5 5.1 %collective-permute-start.21 = (f32[32,640]{1,0:T(8,128)S(1)}, f32[32,640]{1,0:T(8,128)S(1)}, u32[]{:S(2)}, u32[]{:S(2)}) collective-permute-start(f32[32,640]{1,0:T(8,128)S(1)} %get-tuple-element.53), channel_id=1, source_target_pairs={{0,8},{4,12},{8,0},{12,4},{16,24},{20,28},{24,16},{28,20},{1,9},{5... | collective-permute-start | bytes 245768 | tf_op jit(solution)/shard_map/ppermute | solution.py:270
  77.3 6.3 %collective-permute-start.22 = (f32[32,640]{1,0:T(8,128)S(1)}, f32[32,640]{1,0:T(8,128)S(1)}, u32[]{:S(2)}, u32[]{:S(2)}) collective-permute-start(f32[32,640]{1,0:T(8,128)S(1)} %get-tuple-element.52), channel_id=1, source_target_pairs={{0,16},{4,20},{8,24},{12,28},{16,0},{20,4},{24,8},{28,12},{1,17},{... | collective-permute-start | bytes 245768 | tf_op jit(solution)/shard_map/ppermute | solution.py:270
  78.1 5.6 %collective-permute-start.23 = (f32[32,640]{1,0:T(8,128)S(1)}, f32[32,640]{1,0:T(8,128)S(1)}, u32[]{:S(2)}, u32[]{:S(2)}) collective-permute-start(f32[32,640]{1,0:T(8,128)S(1)} %get-tuple-element.51), channel_id=1, source_target_pairs={{0,24},{4,28},{8,16},{12,20},{16,8},{20,12},{24,0},{28,4},{1,25},{... | collective-permute-start | bytes 245768 | tf_op jit(solution)/shard_map/ppermute | solution.py:270
  84.8 1.2 %collective-permute-start.24 = (f32[32,32]{1,0:T(8,128)S(1)}, f32[32,32]{1,0:T(8,128)S(1)}, u32[]{:S(2)}, u32[]{:S(2)}) collective-permute-start(f32[32,32]{1,0:T(8,128)S(1)} %get-tuple-element.46), channel_id=1, source_target_pairs={{0,4},{4,0},{8,12},{12,8},{16,20},{20,16},{24,28},{28,24},{1,5},{5... | collective-permute-start | bytes 12296 | tf_op jit(solution)/shard_map/ppermute | solution.py:270
  86.0 3.7 %collective-permute-start.25 = (f32[32,32]{1,0:T(8,128)S(1)}, f32[32,32]{1,0:T(8,128)S(1)}, u32[]{:S(2)}, u32[]{:S(2)}) collective-permute-start(f32[32,32]{1,0:T(8,128)S(1)} %add.20), channel_id=1, source_target_pairs={{0,8},{4,12},{8,0},{12,4},{16,24},{20,28},{24,16},{28,20},{1,9},{5... | collective-permute-start | bytes 12296 | tf_op jit(solution)/shard_map/ppermute | solution.py:270
  87.3 3.7 %collective-permute-start.26 = (f32[32,32]{1,0:T(8,128)S(1)}, f32[32,32]{1,0:T(8,128)S(1)}, u32[]{:S(2)}, u32[]{:S(2)}) collective-permute-start(f32[32,32]{1,0:T(8,128)S(1)} %add.20), channel_id=1, source_target_pairs={{0,16},{4,20},{8,24},{12,28},{16,0},{20,4},{24,8},{28,12},{1,17},{... | collective-permute-start | bytes 12296 | tf_op jit(solution)/shard_map/ppermute | solution.py:270
  88.4 4.6 %collective-permute-start.27 = (f32[32,32]{1,0:T(8,128)S(1)}, f32[32,32]{1,0:T(8,128)S(1)}, u32[]{:S(2)}, u32[]{:S(2)}) collective-permute-start(f32[32,32]{1,0:T(8,128)S(1)} %add.20), channel_id=1, source_target_pairs={{0,24},{4,28},{8,16},{12,20},{16,8},{20,12},{24,0},{28,4},{1,25},{... | collective-permute-start | bytes 12296 | tf_op jit(solution)/shard_map/ppermute | solution.py:270
  93.0 4.4 %collective-permute-start.28 = (f32[32,32]{1,0:T(8,128)S(1)}, f32[32,32]{1,0:T(8,128)S(1)}, u32[]{:S(2)}, u32[]{:S(2)}) collective-permute-start(f32[32,32]{1,0:T(8,128)S(1)} %add_add_fusion.refs_1_), channel_id=1, source_target_pairs={{0,1},{1,0},{2,3},{3,2},{4,5},{5,4},{6,7},{7,6},{8,9},{9,8},{10,11... | collective-permute-start | bytes 12296 | tf_op jit(solution)/shard_map/ppermute | solution.py:270
  94.4 4.8 %collective-permute-start.29 = (f32[32,32]{1,0:T(8,128)S(1)}, f32[32,32]{1,0:T(8,128)S(1)}, u32[]{:S(2)}, u32[]{:S(2)}) collective-permute-start(f32[32,32]{1,0:T(8,128)S(1)} %add_add_fusion.refs_1_), channel_id=1, source_target_pairs={{0,2},{1,3},{2,0},{3,1},{4,6},{5,7},{6,4},{7,5},{8,10},{9,11},{10,... | collective-permute-start | bytes 12296 | tf_op jit(solution)/shard_map/ppermute | solution.py:270
  95.2 5.5 %collective-permute-start.30 = (f32[32,32]{1,0:T(8,128)S(1)}, f32[32,32]{1,0:T(8,128)S(1)}, u32[]{:S(2)}, u32[]{:S(2)}) collective-permute-start(f32[32,32]{1,0:T(8,128)S(1)} %add_add_fusion.refs_1_), channel_id=1, source_target_pairs={{0,3},{1,2},{2,1},{3,0},{4,7},{5,6},{6,5},{7,4},{8,11},{9,10},{10,... | collective-permute-start | bytes 12296 | tf_op jit(solution)/shard_map/ppermute | solution.py:270

commit v2 on v1

--- a/solution.py
+++ b/solution.py
@@ -101,34 +101,40 @@
     return math.sqrt(math.log2(math.e) / (0.25 * features))
 
 
-def build_own_kernel(*refs, column_parts):
-    column_refs, (high_ref, low_ref, sums_ref, right, left, totals) = refs[:column_parts], refs[column_parts:]
-    features, width = column_refs[0].shape
-    scale = point_scale(features)
-    row_operand(column_refs[0][...].T * scale, left, slice(0, width))
-    for part, ref in enumerate(column_refs):
-        column_operand(ref[...] * scale, right, slice(part * width, (part + 1) * width))
-    build_rows(left, right, [high_ref], [low_ref], totals, sums_ref)
-
-
-def build_rest_kernel(*refs, parts):
-    right, own_ref, row_refs = refs[0], refs[1], refs[2 : 2 + parts]
-    high_refs, low_refs = refs[2 + parts : 2 + 2 * parts], refs[2 + 2 * parts : 2 + 3 * parts]
-    sums_ref, left, totals = refs[2 + 3 * parts :]
+def build_even_kernel(*refs, row_parts, column_parts):
+    row_refs, column_refs = refs[:row_parts], (refs[0], *refs[row_parts : row_parts + column_parts - 1])
+    outs = refs[row_parts + column_parts - 1 :]
+    high_refs, low_refs = outs[:row_parts], outs[row_parts : 2 * row_parts]
+    sums_ref, left, right, totals = outs[2 * row_parts :]
     features, width = row_refs[0].shape
     scale = point_scale(features)
     for part, ref in enumerate(row_refs):
         row_operand(ref[...].T * scale, left, slice(part * width, (part + 1) * width))
+    for part, ref in enumerate(column_refs):
+        column_operand(ref[...] * scale, right, slice(part * width, (part + 1) * width))
     build_rows(left, right, high_refs, low_refs, totals, sums_ref)
-    sums_ref[1 : 1 + parts, :] = sums_ref[0:parts, :]
-    sums_ref[0:1, :] = own_ref[0:1, :]
-
-
-def sweep(weights, high_refs, low_refs, out_ref, which, tile=256):
+
+
+def build_odd_kernel(*refs, row_parts, column_parts):
+    left, even_ref, start_ref, column_refs = refs[0], refs[1], refs[2], refs[3 : 3 + column_parts]
+    outs = refs[3 + column_parts :]
+    high_refs, low_refs = outs[:row_parts], outs[row_parts : 2 * row_parts]
+    packed_ref, right, totals, sums_ref = outs[2 * row_parts :]
+    features, width = column_refs[0].shape
+    vectors = start_ref.shape[0]
+    scale = point_scale(features)
+    for part, ref in enumerate(column_refs):
+        column_operand(ref[...] * scale, right, slice(part * width, (part + 1) * width))
+    build_rows(left, right, high_refs, low_refs, totals, sums_ref)
+    packed_ref[0:vectors, :] = start_ref[...]
+    packed_ref[vectors:, :] = sums_ref[...] + even_ref[...]
+
+
+def sweep(weights, high_refs, low_refs, out_ref, tile=256):
     rows = weights.shape[0] // 2
     width = high_refs[0].shape[0]
     kept = out_ref.shape[1]
-    for place, block in enumerate(which):
+    for block in range(out_ref.shape[0]):
         for first in range(0, width, tile):
             span = slice(block * width + first, block * width + first + tile)
             total = None
@@ -142,42 +148,42 @@
                 )
                 term = both[:kept] + both[rows : rows + kept] + last[:kept]
                 total = term if total is None else total + term
-            out_ref[place, :, first : first + tile] = total
-
-
-def first_kernel(*refs, parts, peers, which):
-    sums_refs, start_refs = refs[:peers], refs[peers : peers + parts]
-    high_refs = refs[peers + parts : peers + 2 * parts]
-    low_refs = refs[peers + 2 * parts : peers + 3 * parts]
-    out_ref, inverse_ref, weights = refs[peers + 3 * parts :]
-    vectors, width = start_refs[0].shape
+            out_ref[block, :, first : first + tile] = total
+
+
+def first_kernel(*refs, parts):
+    packed_refs, high_refs, low_refs = refs[:parts], refs[parts : 2 * parts], refs[2 * parts : 3 * parts]
+    out_ref, inverse_ref, weights = refs[3 * parts :]
     rows = weights.shape[0] // 2
+    vectors = rows - DEGREE_ROWS
+    width = packed_refs[0].shape[1]
     for part in range(parts):
         span = slice(part * width, (part + 1) * width)
-        density = sums_refs[0][part : part + 1, :]
-        for peer in range(1, peers):
-            density = density + sums_refs[peer][part ^ peer : (part ^ peer) + 1, :]
+        density = packed_refs[0][vectors + part : vectors + part + 1, :]
+        for peer in range(1, parts):
+            line = vectors + (part ^ peer)
+            density = density + packed_refs[peer][line : line + 1, :]
         inverse = 1.0 / density
         if part == 0:
             inverse_ref[...] = inverse
-        line = lax.broadcasted_iota(jnp.int32, (rows - vectors, width), 0)
+        line = lax.broadcasted_iota(jnp.int32, (DEGREE_ROWS, width), 0)
         for first, piece in (
-            (0, start_refs[part][...] * inverse),
+            (0, packed_refs[part][0:vectors, :] * inverse),
             (vectors, jnp.where(line == 0, inverse, 0.0)),
         ):
             high, low = halves(piece)
             last = first + piece.shape[0]
             weights[first:last, span] = high
             weights[rows + first : rows + last, span] = low
-    sweep(weights, high_refs, low_refs, out_ref, which)
-
-
-def again_kernel(*refs, parts, which):
+    sweep(weights, high_refs, low_refs, out_ref)
+
+
+def again_kernel(*refs, parts):
     weights, high_refs, low_refs, out_ref = refs[0], refs[1 : 1 + parts], refs[1 + parts : -1], refs[-1]
-    sweep(weights, high_refs, low_refs, out_ref, which)
-
-
-def second_kernel(*refs, parts, which):
+    sweep(weights, high_refs, low_refs, out_ref)
+
+
+def second_kernel(*refs, parts):
     piece_refs, high_refs, low_refs = refs[:parts], refs[parts : 2 * parts], refs[2 * parts : 3 * parts]
     out_ref, gram_ref, weights = refs[3 * parts :]
     vectors, width = piece_refs[0].shape[0], high_refs[0].shape[0]
@@ -190,18 +196,18 @@
         high, low = halves(piece_refs[part][:, 0:width])
         weights[0:vectors, span] = high
         weights[vectors:, span] = low
-    sweep(weights, high_refs, low_refs, out_ref, which)
-    for place in range(len(which)):
-        out_ref[place, :, width:] = gram
-
-
-def second_again_kernel(*refs, parts, which):
+    sweep(weights, high_refs, low_refs, out_ref)
+    for block in range(out_ref.shape[0]):
+        out_ref[block, :, width:] = gram
+
+
+def second_again_kernel(*refs, parts):
     weights, gram_ref = refs[0], refs[1]
     high_refs, low_refs, out_ref = refs[2 : 2 + parts], refs[2 + parts : -1], refs[-1]
-    sweep(weights, high_refs, low_refs, out_ref, which)
+    sweep(weights, high_refs, low_refs, out_ref)
     width = high_refs[0].shape[0]
-    for place in range(len(which)):
-        out_ref[place, :, width:] = gram_ref[...]
+    for block in range(out_ref.shape[0]):
+        out_ref[block, :, width:] = gram_ref[...]
 
 
 def exact(left, right, dims):
@@ -275,38 +281,40 @@
     count = frames.shape[1] * row_size * column_size
     features, width = frames.shape
     vectors = start.shape[0]
-    columns = row_size * width
+    half = row_size // 2
+    columns = half * width
     near, far = range(1, column_size), range(2, row_size, 2)
-    even, odd = range(0, row_size, 2), range(1, row_size, 2)
-
-    row_pieces = [swap(frames, "col", q) for q in near]
-    even_pieces = [frames] + [swap(frames, "row", p) for p in far]
-    odd_pieces = swap(jnp.stack(even_pieces), "row", 1)
-    column_pieces = [(odd_pieces[p // 2] if p % 2 else even_pieces[p // 2]) for p in range(row_size)]
-    starts = [start] + [swap(start, "col", q) for q in near]
+
+    row_pieces = [frames] + [swap(frames, "col", q) for q in near]
+    even_pieces = [swap(frames, "row", p) for p in far]
+    odd_pieces = [swap(piece, "row", 1) for piece in (frames, *even_pieces)]
 
     operands = 4 * features
-    work = 2 * width * columns * operands
+    height = column_size * width
+    work = 2 * 2 * height * columns * operands
+    stored = (bf16(width, columns),) * (2 * column_size)
     totals = pltpu.VMEM((width, 128), jnp.float32)
-    high, low, own_sums, right = call(
-        functools.partial(build_own_kernel, column_parts=row_size),
-        (bf16(width, columns), bf16(width, columns), f32(8, width), bf16(operands, columns)),
-        column_pieces,
-        scratch=(pltpu.VMEM((width, operands), jnp.bfloat16), totals),
-        flops=2 * work,
-        name="build_own",
-    )
-    rest = len(row_pieces)
-    *blocks, sums = call(
-        functools.partial(build_rest_kernel, parts=rest),
-        (bf16(width, columns),) * (2 * rest) + (f32(8, width),),
-        (right, own_sums, *row_pieces),
-        scratch=(pltpu.VMEM((rest * width, operands), jnp.bfloat16), totals),
-        flops=2 * rest * work,
-        name="build_rest",
-    )
-    stored = (high, *blocks[:rest], low, *blocks[rest:])
-    all_sums = [sums] + [swap(sums, "col", q) for q in near]
+    *even, sums, left = call(
+        functools.partial(build_even_kernel, row_parts=column_size, column_parts=half),
+        (*stored, f32(8, width), bf16(height, operands)),
+        (*row_pieces, *even_pieces),
+        scratch=(pltpu.VMEM((operands, columns), jnp.bfloat16), totals),
+        flops=work,
+        name="build_even",
+    )
+    *odd, packed = call(
+        functools.partial(build_odd_kernel, row_parts=column_size, column_parts=half),
+        (*stored, f32(vectors + 8, width)),
+        (left, sums, start, *odd_pieces),
+        scratch=(
+            pltpu.VMEM((operands, columns), jnp.bfloat16),
+            totals,
+            pltpu.VMEM((8, width), jnp.float32),
+        ),
+        flops=work,
+        name="build_odd",
+    )
+    all_packed = [packed] + [swap(packed, "col", q) for q in near]
 
     def spread(evens, odds):
         own = evens + swap(odds, "row", 1)
@@ -318,18 +326,18 @@
         return [gram] + [swap(gram, "col", q) for q in near]
 
     rows = vectors + DEGREE_ROWS
-    work = 2 * 3 * rows * column_size * width * columns
+    work = 2 * 3 * rows * height * columns
     odds, inverse, weights = call(
-        functools.partial(first_kernel, parts=column_size, peers=column_size, which=odd),
-        (f32(len(odd), vectors + 8, width), f32(1, width), bf16(2 * rows, column_size * width)),
-        (*all_sums, *starts, *stored),
+        functools.partial(first_kernel, parts=column_size),
+        (f32(half, vectors + 8, width), f32(1, width), bf16(2 * rows, height)),
+        (*all_packed, *odd),
         flops=work,
         name="first_odd",
     )
     evens = call(
-        functools.partial(again_kernel, parts=column_size, which=even),
-        f32(len(even), vectors + 8, width),
-        (weights, *stored),
+        functools.partial(again_kernel, parts=column_size),
+        f32(half, vectors + 8, width),
+        (weights, *even),
         flops=work,
         name="first_even",
     )
@@ -338,16 +346,16 @@
     )
     pieces = [weighted] + [swap(weighted, "col", q) for q in near]
     odds, gram, weights = call(
-        functools.partial(second_kernel, parts=column_size, which=odd),
-        (f32(len(odd), vectors, width + 128), f32(vectors, 128), bf16(2 * vectors, column_size * width)),
-        (*pieces, *stored),
+        functools.partial(second_kernel, parts=column_size),
+        (f32(half, vectors, width + 128), f32(vectors, 128), bf16(2 * vectors, height)),
+        (*pieces, *odd),
         flops=work,
         name="second_odd",
     )
     evens = call(
-        functools.partial(second_again_kernel, parts=column_size, which=even),
-        f32(len(even), vectors, width + 128),
-        (weights, gram, *stored),
+        functools.partial(second_again_kernel, parts=column_size),
+        f32(half, vectors, width + 128),
+        (weights, gram, *even),
         flops=work,
         name="second_even",
     )

time: 103 us -> 94.6 us (0.918)
  starting transfers between devices: 41.6 us -> 34 us
  waiting for transfers between devices: 33 us -> 35.2 us
  Pallas kernels: 25.6 us -> 24.1 us
    ppermute x31, starting transfers between devices: 41.6 us -> 34 us  [swap(): lax.ppermute(values, axis, [(index, index ^ mask) for index in range(size)])]
    ppermute x31, waiting for transfers between devices: 33 us -> 35.2 us  [swap(): lax.ppermute(values, axis, [(index, index ^ mask) for index in range(size)])]
    pallas_call x9, Pallas kernels: 25.6 us -> 24.1 us  [call(): pl.pallas_call(body, out_shape=out_shape, in_specs=[VMEM] * len(operands)...]
  transfers between devices with their start and end apart: 31 -> 31, of which waited for: 18 -> 19; matrix products, arithmetic and copies ran while one was open for 0% -> 0% of each run, Pallas kernels for 16% -> 12%
where the time goes in v2:
time: 94.6 us; the launch traced here: 94.5 us
  waiting for transfers between devices  35.2 us (37%)
  starting transfers between devices  34 us (36%)
  Pallas kernels  24.1 us (25%)
  local copies, waits for them, and re-layouts  0.96 us (1%)
    ppermute x31, waiting for transfers between devices, swap(): lax.ppermute(values, axis, [(index, index ^ mask) for index in range(size)])  35.2 us
    ppermute x31, starting transfers between devices, swap(): lax.ppermute(values, axis, [(index, index ^ mask) for index in range(size)])  34 us
    pallas_call x9, Pallas kernels, call(): pl.pallas_call(body, out_shape=out_shape, in_specs=[VMEM] * len(operands)...  24.1 us
  transfers between devices with their start and end apart: 31, of which 19 were waited for; matrix products, arithmetic and copies ran while one was open for 0% of the time, Pallas kernels for 12%

profile of v2, /device:TPU:0, one launch (start us, length us, event | category | flops | bytes accessed | tf_op | source)
XLA Modules:
  0.0 94.5 jit_solution(14296773078433553135)
XLA Ops:
  0.0 3.9 %collective-permute-start.5 = (f32[64,512]{1,0:T(8,128)}, f32[64,512]{1,0:T(8,128)S(1)}, u32[]{:S(2)}, u32[]{:S(2)}) collective-permute-start(f32[64,512]{1,0:T(8,128)} %refs_0_.1), channel_id=1, source_target_pairs={{0,24},{4,28},{8,16},{12,20},{16,8},{20,12},{24,0},{28,4},{1,25},{... | collective-permute-start | bytes 393224 | tf_op jit(solution)/shard_map/ppermute | solution.py:276
  3.9 0.5 collective-permute-start.4
  4.5 4.1 %collective-permute-start.2 = (f32[64,512]{1,0:T(8,128)}, f32[64,512]{1,0:T(8,128)S(1)}, u32[]{:S(2)}, u32[]{:S(2)}) collective-permute-start(f32[64,512]{1,0:T(8,128)} %refs_0_.1), channel_id=1, source_target_pairs={{0,3},{1,2},{2,1},{3,0},{4,7},{5,6},{6,5},{7,4},{8,11},{9,10},{10,... | collective-permute-start | bytes 393224 | tf_op jit(solution)/shard_map/ppermute | solution.py:276
  8.5 1.1 %collective-permute-start = (f32[64,512]{1,0:T(8,128)}, f32[64,512]{1,0:T(8,128)S(1)}, u32[]{:S(2)}, u32[]{:S(2)}) collective-permute-start(f32[64,512]{1,0:T(8,128)} %refs_0_.1), channel_id=1, source_target_pairs={{0,1},{1,0},{2,3},{3,2},{4,5},{5,4},{6,7},{7,6},{8,9},{9,8},{10,11... | collective-permute-start | bytes 393224 | tf_op jit(solution)/shard_map/ppermute | solution.py:276
  9.7 0.7 collective-permute-done.4.refs_5_
  10.4 0.2 collective-permute-done.3.refs_4_
  10.7 0.3 collective-permute-start.9
  10.9 2.3 %collective-permute-done.2.refs_3_ = f32[64,512]{1,0:T(8,128)S(1)} collective-permute-done((f32[64,512]{1,0:T(8,128)}, f32[64,512]{1,0:T(8,128)S(1)}, u32[]{:S(2)}, u32[]{:S(2)}) %collective-permute-start.2) | collective-permute-done | bytes 131104 | tf_op jit(solution)/shard_map/ppermute | solution.py:276
  13.2 5.8 %collective-permute-done.1.refs_2_ = f32[64,512]{1,0:T(8,128)S(1)} collective-permute-done((f32[64,512]{1,0:T(8,128)}, f32[64,512]{1,0:T(8,128)S(1)}, u32[]{:S(2)}, u32[]{:S(2)}) %collective-permute-start.1) | collective-permute-done | bytes 131104 | tf_op jit(solution)/shard_map/ppermute | solution.py:276
  19.0 0.9 copy-done
  19.9 5.3 %build_even.1 = (bf16[512,2048]{1,0:T(8,128)(2,1)S(1)}, bf16[512,2048]{1,0:T(8,128)(2,1)S(1)}, bf16[512,2048]{1,0:T(8,128)(2,1)S(1)}, bf16[512,2048]{1,0:T(8,128...) custom-call(f32[64,512]{1,0:T(8,128)S(1)} %copy-done, ...), custom_call_target="tpu_custom_call" | custom-call | flops 4294967296 | tf_op jit(solution)/shard_map/build_even/pallas_call | solution.py:18
  25.2 3.8 %build_odd.1 = (bf16[512,2048]{1,0:T(8,128)(2,1)S(1)}, bf16[512,2048]{1,0:T(8,128)(2,1)S(1)}, bf16[512,2048]{1,0:T(8,128)(2,1)S(1)}, bf16[512,2048]{1,0:T(8,128)...) custom-call(bf16[2048,256]{1,0:T(8,128)(2,1)S(1)} %get-tuple-element, ...), custom_call_target="tpu_custom_call" | custom-call | flops 4294967296 | tf_op jit(solution)/shard_map/build_odd/pallas_call | solution.py:18
  29.1 2.5 %collective-permute-start.12 = (f32[40,512]{1,0:T(8,128)S(1)}, f32[40,512]{1,0:T(8,128)S(1)}, u32[]{:S(2)}, u32[]{:S(2)}) collective-permute-start(f32[40,512]{1,0:T(8,128)S(1)} %get-tuple-element.36.refs_0_), channel_id=1, source_target_pairs={{0,3},{1,2},{2,1},{3,0},{4,7},{5,6},{6,5},{7,4},{8,11},{9,10},{10,... | collective-permute-start | bytes 245768 | tf_op jit(solution)/shard_map/ppermute | solution.py:276
  31.6 1.9 %collective-permute-start.10 = (f32[40,512]{1,0:T(8,128)S(1)}, f32[40,512]{1,0:T(8,128)S(1)}, u32[]{:S(2)}, u32[]{:S(2)}) collective-permute-start(f32[40,512]{1,0:T(8,128)S(1)} %get-tuple-element.36.refs_0_), channel_id=1, source_target_pairs={{0,1},{1,0},{2,3},{3,2},{4,5},{5,4},{6,7},{7,6},{8,9},{9,8},{10,11... | collective-permute-start | bytes 245768 | tf_op jit(solution)/shard_map/ppermute | solution.py:276
  33.5 2.7 %collective-permute-done.12.refs_3_ = f32[40,512]{1,0:T(8,128)S(1)} collective-permute-done((f32[40,512]{1,0:T(8,128)S(1)}, f32[40,512]{1,0:T(8,128)S(1)}, u32[]{:S(2)}, u32[]{:S(2)}) %collective-permute-start.12) | collective-permute-done | bytes 81952 | tf_op jit(solution)/shard_map/ppermute | solution.py:276
  36.3 3.0 %collective-permute-done.11.refs_2_ = f32[40,512]{1,0:T(8,128)S(1)} collective-permute-done((f32[40,512]{1,0:T(8,128)S(1)}, f32[40,512]{1,0:T(8,128)S(1)}, u32[]{:S(2)}, u32[]{:S(2)}) %collective-permute-start.11) | collective-permute-done | bytes 81952 | tf_op jit(solution)/shard_map/ppermute | solution.py:276
  39.3 2.9 %first_odd.1 = (f32[4,40,512]{2,1,0:T(8,128)S(1)}, f32[1,512]{1,0:T(1,128)S(1)}, bf16[96,2048]{1,0:T(8,128)(2,1)S(1)}) custom-call(f32[40,512]{1,0:T(8,128)S(1)} %get-tuple-element.36.refs_0_, f32[40,512]{1,0:T(8,128)S(1)} %collective-permute-done.10.refs_1_, f32[40,512]{1,0:T(8,128)S(1)} %collective-permute-done.11.refs_2_, ...), custom_call_target="tpu_custom_call" | custom-call | flops 1207959552 | tf_op jit(solution)/shard_map/first_odd/pallas_call | solution.py:18
  42.3 3.1 %first_even.1 = f32[4,40,512]{2,1,0:T(8,128)S(1)} custom-call(bf16[96,2048]{1,0:T(8,128)(2,1)S(1)} %get-tuple-element.46.refs_0_, bf16[512,2048]{1,0:T(8,128)(2,1)S(1)} %get-tuple-element.47.refs_1_.refs_2_, bf16[512,2048]{1,0:T(8,128)(2,1)S(1)} %get-tuple-element.48.refs_2_.refs_3_, bf16[512,2048]{1,0:T(8,128)(2,1)S(1)} %get-tuple-element.49.refs_3_.refs_4_, ...), custom_call_target="tpu_custom_call" | custom-call | flops 1207959552 | tf_op jit(solution)/shard_map/first_even/pallas_call | solution.py:18
  45.5 2.5 %collective-permute-start.16 = (f32[40,512]{1,0:T(8,128)S(1)}, f32[40,512]{1,0:T(8,128)S(1)}, u32[]{:S(2)}, u32[]{:S(2)}) collective-permute-start(f32[40,512]{1,0:T(8,128)S(1)} %get-tuple-element.67), channel_id=1, source_target_pairs={{0,24},{4,28},{8,16},{12,20},{16,8},{20,12},{24,0},{28,4},{1,25},{... | collective-permute-start | bytes 245768 | tf_op jit(solution)/shard_map/ppermute | solution.py:276
  48.0 0.5 collective-permute-start.15
  48.5 0.5 collective-permute-start.14
  49.0 2.3 %collective-permute-done.16.refs_4_ = f32[40,512]{1,0:T(8,128)S(1)} collective-permute-done((f32[40,512]{1,0:T(8,128)S(1)}, f32[40,512]{1,0:T(8,128)S(1)}, u32[]{:S(2)}, u32[]{:S(2)}) %collective-permute-start.16) | collective-permute-done | bytes 81952 | tf_op jit(solution)/shard_map/ppermute | solution.py:276
  51.3 1.7 %collective-permute-done.15.refs_3_ = f32[40,512]{1,0:T(8,128)S(1)} collective-permute-done((f32[40,512]{1,0:T(8,128)S(1)}, f32[40,512]{1,0:T(8,128)S(1)}, u32[]{:S(2)}, u32[]{:S(2)}) %collective-permute-start.15) | collective-permute-done | bytes 81952 | tf_op jit(solution)/shard_map/ppermute | solution.py:276
  53.1 0.2 grown.1
  53.3 2.5 %collective-permute-start.19 = (f32[32,640]{1,0:T(8,128)S(1)}, f32[32,640]{1,0:T(8,128)S(1)}, u32[]{:S(2)}, u32[]{:S(2)}) collective-permute-start(f32[32,640]{1,0:T(8,128)S(1)} %get-tuple-element.57.refs_0_), channel_id=1, source_target_pairs={{0,3},{1,2},{2,1},{3,0},{4,7},{5,6},{6,5},{7,4},{8,11},{9,10},{10,... | collective-permute-start | bytes 245768 | tf_op jit(solution)/shard_map/ppermute | solution.py:276
  55.8 1.9 %collective-permute-start.17 = (f32[32,640]{1,0:T(8,128)S(1)}, f32[32,640]{1,0:T(8,128)S(1)}, u32[]{:S(2)}, u32[]{:S(2)}) collective-permute-start(f32[32,640]{1,0:T(8,128)S(1)} %get-tuple-element.57.refs_0_), channel_id=1, source_target_pairs={{0,1},{1,0},{2,3},{3,2},{4,5},{5,4},{6,7},{7,6},{8,9},{9,8},{10,11... | collective-permute-start | bytes 245768 | tf_op jit(solution)/shard_map/ppermute | solution.py:276
  57.7 2.6 %collective-permute-done.19.refs_3_ = f32[32,640]{1,0:T(8,128)S(1)} collective-permute-done((f32[32,640]{1,0:T(8,128)S(1)}, f32[32,640]{1,0:T(8,128)S(1)}, u32[]{:S(2)}, u32[]{:S(2)}) %collective-permute-start.19) | collective-permute-done | bytes 81952 | tf_op jit(solution)/shard_map/ppermute | solution.py:276
  60.4 2.8 %collective-permute-done.18.refs_2_ = f32[32,640]{1,0:T(8,128)S(1)} collective-permute-done((f32[32,640]{1,0:T(8,128)S(1)}, f32[32,640]{1,0:T(8,128)S(1)}, u32[]{:S(2)}, u32[]{:S(2)}) %collective-permute-start.18) | collective-permute-done | bytes 81952 | tf_op jit(solution)/shard_map/ppermute | solution.py:276
  63.2 3.0 %second_odd.1 = (f32[4,32,640]{2,1,0:T(8,128)S(1)}, f32[32,128]{1,0:T(8,128)S(1)}, bf16[64,2048]{1,0:T(8,128)(2,1)S(1)}) custom-call(f32[32,640]{1,0:T(8,128)S(1)} %get-tuple-element.57.refs_0_, f32[32,640]{1,0:T(8,128)S(1)} %collective-permute-done.17.refs_1_, f32[32,640]{1,0:T(8,128)S(1)} %collective-permute-done.18.refs_2_, ...), custom_call_target="tpu_custom_call" | custom-call | flops 1207959552 | tf_op jit(solution)/shard_map/second_odd/pallas_call | solution.py:18
  66.2 3.0 %second_even.1 = f32[4,32,640]{2,1,0:T(8,128)S(1)} custom-call(bf16[64,2048]{1,0:T(8,128)(2,1)S(1)} %get-tuple-element.58.refs_0_, f32[32,128]{1,0:T(8,128)S(1)} %get-tuple-element.59.refs_1_, bf16[512,2048]{1,0:T(8,128)(2,1)S(1)} %get-tuple-element.47.refs_1_.refs_2_, bf16[512,2048]{1,0:T(8,128)(2,1)S(1)} %get-tuple-element.48.refs_2_.refs_3_, ...), custom_call_target="tpu_custom_call" | custom-call | flops 1207959552 | tf_op jit(solution)/shard_map/second_even/pallas_call | solution.py:18
  69.3 1.6 %collective-permute-start.23 = (f32[32,640]{1,0:T(8,128)S(1)}, f32[32,640]{1,0:T(8,128)S(1)}, u32[]{:S(2)}, u32[]{:S(2)}) collective-permute-start(f32[32,640]{1,0:T(8,128)S(1)} %get-tuple-element.63), channel_id=1, source_target_pairs={{0,24},{4,28},{8,16},{12,20},{16,8},{20,12},{24,0},{28,4},{1,25},{... | collective-permute-start | bytes 245768 | tf_op jit(solution)/shard_map/ppermute | solution.py:276
  71.0 1.4 %collective-permute-start.22 = (f32[32,640]{1,0:T(8,128)S(1)}, f32[32,640]{1,0:T(8,128)S(1)}, u32[]{:S(2)}, u32[]{:S(2)}) collective-permute-start(f32[32,640]{1,0:T(8,128)S(1)} %get-tuple-element.64), channel_id=1, source_target_pairs={{0,16},{4,20},{8,24},{12,28},{16,0},{20,4},{24,8},{28,12},{1,17},{... | collective-permute-start | bytes 245768 | tf_op jit(solution)/shard_map/ppermute | solution.py:276
  72.4 0.5 collective-permute-start.21
  72.9 2.4 %collective-permute-done.23.refs_4_ = f32[32,640]{1,0:T(8,128)S(1)} collective-permute-done((f32[32,640]{1,0:T(8,128)S(1)}, f32[32,640]{1,0:T(8,128)S(1)}, u32[]{:S(2)}, u32[]{:S(2)}) %collective-permute-start.23) | collective-permute-done | bytes 81952 | tf_op jit(solution)/shard_map/ppermute | solution.py:276
  75.3 1.6 %collective-permute-done.22.refs_3_ = f32[32,640]{1,0:T(8,128)S(1)} collective-permute-done((f32[32,640]{1,0:T(8,128)S(1)}, f32[32,640]{1,0:T(8,128)S(1)}, u32[]{:S(2)}, u32[]{:S(2)}) %collective-permute-start.22) | collective-permute-done | bytes 81952 | tf_op jit(solution)/shard_map/ppermute | solution.py:276
  77.0 1.2 %grown_two.1 = (f32[32,512]{1,0:T(8,128)S(1)}, f32[32,32]{1,0:T(8,128)S(1)}) custom-call(f32[1,512]{1,0:T(1,128)S(1)} %get-tuple-element.56.refs_0_, f32[32,640]{1,0:T(8,128)S(1)} %get-tuple-element.66.refs_1_, f32[32,640]{1,0:T(8,128)S(1)} %collective-permute-done.21.refs_2_, f32[32,640]{1,0:T(8,128)S(1)} %collective-permute-done.22.refs_3_, ...), custom_call_target="tpu_custom_call" | custom-call | tf_op jit(solution)/shard_map/grown_two/pallas_call | solution.py:18
  78.1 1.2 %collective-permute-done.24 = f32[32,32]{1,0:T(8,128)S(1)} collective-permute-done((f32[32,32]{1,0:T(8,128)S(1)}, f32[32,32]{1,0:T(8,128)S(1)}, u32[]{:S(2)}, u32[]{:S(2)}) %collective-permute-start.24) | collective-permute-done | bytes 4128 | tf_op jit(solution)/shard_map/ppermute | solution.py:276
  79.3 1.5 %collective-permute-start.27 = (f32[32,32]{1,0:T(8,128)S(1)}, f32[32,32]{1,0:T(8,128)S(1)}, u32[]{:S(2)}, u32[]{:S(2)}) collective-permute-start(f32[32,32]{1,0:T(8,128)S(1)} %add.20), channel_id=1, source_target_pairs={{0,24},{4,28},{8,16},{12,20},{16,8},{20,12},{24,0},{28,4},{1,25},{... | collective-permute-start | bytes 12296 | tf_op jit(solution)/shard_map/ppermute | solution.py:276
  80.9 1.4 %collective-permute-start.26 = (f32[32,32]{1,0:T(8,128)S(1)}, f32[32,32]{1,0:T(8,128)S(1)}, u32[]{:S(2)}, u32[]{:S(2)}) collective-permute-start(f32[32,32]{1,0:T(8,128)S(1)} %add.20), channel_id=1, source_target_pairs={{0,16},{4,20},{8,24},{12,28},{16,0},{20,4},{24,8},{28,12},{1,17},{... | collective-permute-start | bytes 12296 | tf_op jit(solution)/shard_map/ppermute | solution.py:276
  82.3 0.5 collective-permute-start.25
  82.8 1.1 %collective-permute-done.27 = f32[32,32]{1,0:T(8,128)S(1)} collective-permute-done((f32[32,32]{1,0:T(8,128)S(1)}, f32[32,32]{1,0:T(8,128)S(1)}, u32[]{:S(2)}, u32[]{:S(2)}) %collective-permute-start.27) | collective-permute-done | bytes 4128 | tf_op jit(solution)/shard_map/ppermute | solution.py:276
  84.0 0.6 collective-permute-done.26
  84.6 1.4 %collective-permute-done.25 = f32[32,32]{1,0:T(8,128)S(1)} collective-permute-done((f32[32,32]{1,0:T(8,128)S(1)}, f32[32,32]{1,0:T(8,128)S(1)}, u32[]{:S(2)}, u32[]{:S(2)}) %collective-permute-start.25) | collective-permute-done | bytes 4128 | tf_op jit(solution)/shard_map/ppermute | solution.py:276
  86.0 2.2 %collective-permute-start.30 = (f32[32,32]{1,0:T(8,128)S(1)}, f32[32,32]{1,0:T(8,128)S(1)}, u32[]{:S(2)}, u32[]{:S(2)}) collective-permute-start(f32[32,32]{1,0:T(8,128)S(1)} %add_add_fusion.refs_1_), channel_id=1, source_target_pairs={{0,3},{1,2},{2,1},{3,0},{4,7},{5,6},{6,5},{7,4},{8,11},{9,10},{10,... | collective-permute-start | bytes 12296 | tf_op jit(solution)/shard_map/ppermute | solution.py:276
  88.2 2.2 %collective-permute-start.28 = (f32[32,32]{1,0:T(8,128)S(1)}, f32[32,32]{1,0:T(8,128)S(1)}, u32[]{:S(2)}, u32[]{:S(2)}) collective-permute-start(f32[32,32]{1,0:T(8,128)S(1)} %add_add_fusion.refs_1_), channel_id=1, source_target_pairs={{0,1},{1,0},{2,3},{3,2},{4,5},{5,4},{6,7},{7,6},{8,9},{9,8},{10,11... | collective-permute-start | bytes 12296 | tf_op jit(solution)/shard_map/ppermute | solution.py:276
  90.4 1.2 %collective-permute-done.30.refs_4_ = f32[32,32]{1,0:T(8,128)S(1)} collective-permute-done((f32[32,32]{1,0:T(8,128)S(1)}, f32[32,32]{1,0:T(8,128)S(1)}, u32[]{:S(2)}, u32[]{:S(2)}) %collective-permute-start.30) | collective-permute-done | bytes 4128 | tf_op jit(solution)/shard_map/ppermute | solution.py:276
  91.6 1.2 %collective-permute-done.29.refs_3_ = f32[32,32]{1,0:T(8,128)S(1)} collective-permute-done((f32[32,32]{1,0:T(8,128)S(1)}, f32[32,32]{1,0:T(8,128)S(1)}, u32[]{:S(2)}, u32[]{:S(2)}) %collective-permute-start.29) | collective-permute-done | bytes 4128 | tf_op jit(solution)/shard_map/ppermute | solution.py:276
  92.9 1.6 %finish.1 = f32[32,512]{1,0:T(8,128)} custom-call(f32[32,512]{1,0:T(8,128)S(1)} %get-tuple-element.61.refs_0_, f32[32,32]{1,0:T(8,128)S(1)} %add_add_fusion.refs_1_, f32[32,32]{1,0:T(8,128)S(1)} %collective-permute-done.28.refs_2_, f32[32,32]{1,0:T(8,128)S(1)} %collective-permute-done.29.refs_3_, f32[32,32]{1,0:T(8,128)S(1)} %collective-permute-done.30.refs_4_), custom_call_target="tpu_custom_call" | custom-call | tf_op jit(solution)/shard_map/finish/pallas_call | solution.py:18
  (33 shorter events, 0.5 us)
Async XLA Ops:
  0.0 8.5 %collective-permute-start.5 = (f32[64,512]{1,0:T(8,128)}, f32[64,512]{1,0:T(8,128)S(1)}, u32[]{:S(2)}, u32[]{:S(2)}) collective-permute-start(f32[64,512]{1,0:T(8,128)} %refs_0_.1), channel_id=1, source_target_pairs={{0,24},{4,28},{8,16},{12,20},{16,8},{20,12},{24,0},{28,4},{1,25},{... | collective-permute-start | bytes 393224 | tf_op jit(solution)/shard_map/ppermute | solution.py:276
  3.9 6.5 %collective-permute-start.4 = (f32[64,512]{1,0:T(8,128)}, f32[64,512]{1,0:T(8,128)S(1)}, u32[]{:S(2)}, u32[]{:S(2)}) collective-permute-start(f32[64,512]{1,0:T(8,128)} %refs_0_.1), channel_id=1, source_target_pairs={{0,16},{4,20},{8,24},{12,28},{16,0},{20,4},{24,8},{28,12},{1,17},{... | collective-permute-start | bytes 393224 | tf_op jit(solution)/shard_map/ppermute | solution.py:276
  4.4 6.3 %collective-permute-start.3 = (f32[64,512]{1,0:T(8,128)}, f32[64,512]{1,0:T(8,128)S(1)}, u32[]{:S(2)}, u32[]{:S(2)}) collective-permute-start(f32[64,512]{1,0:T(8,128)} %refs_0_.1), channel_id=1, source_target_pairs={{0,8},{4,12},{8,0},{12,4},{16,24},{20,28},{24,16},{28,20},{1,9},{5... | collective-permute-start | bytes 393224 | tf_op jit(solution)/shard_map/ppermute | solution.py:276
  4.5 8.7 %collective-permute-start.2 = (f32[64,512]{1,0:T(8,128)}, f32[64,512]{1,0:T(8,128)S(1)}, u32[]{:S(2)}, u32[]{:S(2)}) collective-permute-start(f32[64,512]{1,0:T(8,128)} %refs_0_.1), channel_id=1, source_target_pairs={{0,3},{1,2},{2,1},{3,0},{4,7},{5,6},{6,5},{7,4},{8,11},{9,10},{10,... | collective-permute-start | bytes 393224 | tf_op jit(solution)/shard_map/ppermute | solution.py:276
  8.5 10.4 %collective-permute-start.1 = (f32[64,512]{1,0:T(8,128)}, f32[64,512]{1,0:T(8,128)S(1)}, u32[]{:S(2)}, u32[]{:S(2)}) collective-permute-start(f32[64,512]{1,0:T(8,128)} %refs_0_.1), channel_id=1, source_target_pairs={{0,2},{1,3},{2,0},{3,1},{4,6},{5,7},{6,4},{7,5},{8,10},{9,11},{10,... | collective-permute-start | bytes 393224 | tf_op jit(solution)/shard_map/ppermute | solution.py:276
  8.5 10.4 %collective-permute-start = (f32[64,512]{1,0:T(8,128)}, f32[64,512]{1,0:T(8,128)S(1)}, u32[]{:S(2)}, u32[]{:S(2)}) collective-permute-start(f32[64,512]{1,0:T(8,128)} %refs_0_.1), channel_id=1, source_target_pairs={{0,1},{1,0},{2,3},{3,2},{4,5},{5,4},{6,7},{7,6},{8,9},{9,8},{10,11... | collective-permute-start | bytes 393224 | tf_op jit(solution)/shard_map/ppermute | solution.py:276
  10.4 14.8 %collective-permute-start.6 = (f32[64,512]{1,0:T(8,128)}, f32[64,512]{1,0:T(8,128)S(1)}, u32[]{:S(2)}, u32[]{:S(2)}) collective-permute-start(f32[64,512]{1,0:T(8,128)} %refs_0_.1), channel_id=1, source_target_pairs={{0,4},{4,0},{8,12},{12,8},{16,20},{20,16},{24,28},{28,24},{1,5},{5... | collective-permute-start | bytes 393224 | tf_op jit(solution)/shard_map/ppermute | solution.py:276
  10.7 14.5 %collective-permute-start.9 = (f32[64,512]{1,0:T(8,128)S(1)}, f32[64,512]{1,0:T(8,128)S(1)}, u32[]{:S(2)}, u32[]{:S(2)}) collective-permute-start(f32[64,512]{1,0:T(8,128)S(1)} %collective-permute-done.5.refs_6_), channel_id=1, source_target_pairs={{0,4},{4,0},{8,12},{12,8},{16,20},{20,16},{24,28},{28,24},{1,5},{5... | collective-permute-start | bytes 393224 | tf_op jit(solution)/shard_map/ppermute | solution.py:276
  13.2 12.0 %collective-permute-start.8 = (f32[64,512]{1,0:T(8,128)S(1)}, f32[64,512]{1,0:T(8,128)S(1)}, u32[]{:S(2)}, u32[]{:S(2)}) collective-permute-start(f32[64,512]{1,0:T(8,128)S(1)} %collective-permute-done.4.refs_5_), channel_id=1, source_target_pairs={{0,4},{4,0},{8,12},{12,8},{16,20},{20,16},{24,28},{28,24},{1,5},{5... | collective-permute-start | bytes 393224 | tf_op jit(solution)/shard_map/ppermute | solution.py:276
  19.0 6.2 %collective-permute-start.7 = (f32[64,512]{1,0:T(8,128)S(1)}, f32[64,512]{1,0:T(8,128)S(1)}, u32[]{:S(2)}, u32[]{:S(2)}) collective-permute-start(f32[64,512]{1,0:T(8,128)S(1)} %collective-permute-done.3.refs_4_), channel_id=1, source_target_pairs={{0,4},{4,0},{8,12},{12,8},{16,20},{20,16},{24,28},{28,24},{1,5},{5... | collective-permute-start | bytes 393224 | tf_op jit(solution)/shard_map/ppermute | solution.py:276
  19.0 0.9 copy-start
  19.9 5.3 %copy-start.1 = (f32[32,512]{1,0:T(8,128)S(1)}, f32[32,512]{1,0:T(8,128)}, u32[]{:S(2)}) copy-start(f32[32,512]{1,0:T(8,128)} %refs_2_.1) | copy-start | bytes 196612
  29.1 7.2 %collective-permute-start.12 = (f32[40,512]{1,0:T(8,128)S(1)}, f32[40,512]{1,0:T(8,128)S(1)}, u32[]{:S(2)}, u32[]{:S(2)}) collective-permute-start(f32[40,512]{1,0:T(8,128)S(1)} %get-tuple-element.36.refs_0_), channel_id=1, source_target_pairs={{0,3},{1,2},{2,1},{3,0},{4,7},{5,6},{6,5},{7,4},{8,11},{9,10},{10,... | collective-permute-start | bytes 245768 | tf_op jit(solution)/shard_map/ppermute | solution.py:276
  31.6 7.7 %collective-permute-start.11 = (f32[40,512]{1,0:T(8,128)S(1)}, f32[40,512]{1,0:T(8,128)S(1)}, u32[]{:S(2)}, u32[]{:S(2)}) collective-permute-start(f32[40,512]{1,0:T(8,128)S(1)} %get-tuple-element.36.refs_0_), channel_id=1, source_target_pairs={{0,2},{1,3},{2,0},{3,1},{4,6},{5,7},{6,4},{7,5},{8,10},{9,11},{10,... | collective-permute-start | bytes 245768 | tf_op jit(solution)/shard_map/ppermute | solution.py:276
  31.6 7.7 %collective-permute-start.10 = (f32[40,512]{1,0:T(8,128)S(1)}, f32[40,512]{1,0:T(8,128)S(1)}, u32[]{:S(2)}, u32[]{:S(2)}) collective-permute-start(f32[40,512]{1,0:T(8,128)S(1)} %get-tuple-element.36.refs_0_), channel_id=1, source_target_pairs={{0,1},{1,0},{2,3},{3,2},{4,5},{5,4},{6,7},{7,6},{8,9},{9,8},{10,11... | collective-permute-start | bytes 245768 | tf_op jit(solution)/shard_map/ppermute | solution.py:276
  42.2 3.2 %collective-permute-start.13 = (f32[4,40,512]{2,1,0:T(8,128)S(1)}, f32[4,40,512]{2,1,0:T(8,128)S(1)}, u32[]{:S(2)}, u32[]{:S(2)}) collective-permute-start(f32[4,40,512]{2,1,0:T(8,128)S(1)} %get-tuple-element.55), channel_id=1, source_target_pairs={{0,4},{4,0},{8,12},{12,8},{16,20},{20,16},{24,28},{28,24},{1,5},{5... | collective-permute-start | bytes 983048 | tf_op jit(solution)/shard_map/ppermute | solution.py:276
  45.5 5.8 %collective-permute-start.16 = (f32[40,512]{1,0:T(8,128)S(1)}, f32[40,512]{1,0:T(8,128)S(1)}, u32[]{:S(2)}, u32[]{:S(2)}) collective-permute-start(f32[40,512]{1,0:T(8,128)S(1)} %get-tuple-element.67), channel_id=1, source_target_pairs={{0,24},{4,28},{8,16},{12,20},{16,8},{20,12},{24,0},{28,4},{1,25},{... | collective-permute-start | bytes 245768 | tf_op jit(solution)/shard_map/ppermute | solution.py:276
  48.0 5.0 %collective-permute-start.15 = (f32[40,512]{1,0:T(8,128)S(1)}, f32[40,512]{1,0:T(8,128)S(1)}, u32[]{:S(2)}, u32[]{:S(2)}) collective-permute-start(f32[40,512]{1,0:T(8,128)S(1)} %get-tuple-element.68), channel_id=1, source_target_pairs={{0,16},{4,20},{8,24},{12,28},{16,0},{20,4},{24,8},{28,12},{1,17},{... | collective-permute-start | bytes 245768 | tf_op jit(solution)/shard_map/ppermute | solution.py:276
  48.5 4.6 %collective-permute-start.14 = (f32[40,512]{1,0:T(8,128)S(1)}, f32[40,512]{1,0:T(8,128)S(1)}, u32[]{:S(2)}, u32[]{:S(2)}) collective-permute-start(f32[40,512]{1,0:T(8,128)S(1)} %get-tuple-element.69), channel_id=1, source_target_pairs={{0,8},{4,12},{8,0},{12,4},{16,24},{20,28},{24,16},{28,20},{1,9},{5... | collective-permute-start | bytes 245768 | tf_op jit(solution)/shard_map/ppermute | solution.py:276
  53.3 7.1 %collective-permute-start.19 = (f32[32,640]{1,0:T(8,128)S(1)}, f32[32,640]{1,0:T(8,128)S(1)}, u32[]{:S(2)}, u32[]{:S(2)}) collective-permute-start(f32[32,640]{1,0:T(8,128)S(1)} %get-tuple-element.57.refs_0_), channel_id=1, source_target_pairs={{0,3},{1,2},{2,1},{3,0},{4,7},{5,6},{6,5},{7,4},{8,11},{9,10},{10,... | collective-permute-start | bytes 245768 | tf_op jit(solution)/shard_map/ppermute | solution.py:276
  55.8 7.4 %collective-permute-start.18 = (f32[32,640]{1,0:T(8,128)S(1)}, f32[32,640]{1,0:T(8,128)S(1)}, u32[]{:S(2)}, u32[]{:S(2)}) collective-permute-start(f32[32,640]{1,0:T(8,128)S(1)} %get-tuple-element.57.refs_0_), channel_id=1, source_target_pairs={{0,2},{1,3},{2,0},{3,1},{4,6},{5,7},{6,4},{7,5},{8,10},{9,11},{10,... | collective-permute-start | bytes 245768 | tf_op jit(solution)/shard_map/ppermute | solution.py:276
  55.8 7.4 %collective-permute-start.17 = (f32[32,640]{1,0:T(8,128)S(1)}, f32[32,640]{1,0:T(8,128)S(1)}, u32[]{:S(2)}, u32[]{:S(2)}) collective-permute-start(f32[32,640]{1,0:T(8,128)S(1)} %get-tuple-element.57.refs_0_), channel_id=1, source_target_pairs={{0,1},{1,0},{2,3},{3,2},{4,5},{5,4},{6,7},{7,6},{8,9},{9,8},{10,11... | collective-permute-start | bytes 245768 | tf_op jit(solution)/shard_map/ppermute | solution.py:276
  66.2 3.0 %collective-permute-start.20 = (f32[4,32,640]{2,1,0:T(8,128)S(1)}, f32[4,32,640]{2,1,0:T(8,128)S(1)}, u32[]{:S(2)}, u32[]{:S(2)}) collective-permute-start(f32[4,32,640]{2,1,0:T(8,128)S(1)} %get-tuple-element.60), channel_id=1, source_target_pairs={{0,4},{4,0},{8,12},{12,8},{16,20},{20,16},{24,28},{28,24},{1,5},{5... | collective-permute-start | bytes 983048 | tf_op jit(solution)/shard_map/ppermute | solution.py:276
  69.3 6.0 %collective-permute-start.23 = (f32[32,640]{1,0:T(8,128)S(1)}, f32[32,640]{1,0:T(8,128)S(1)}, u32[]{:S(2)}, u32[]{:S(2)}) collective-permute-start(f32[32,640]{1,0:T(8,128)S(1)} %get-tuple-element.63), channel_id=1, source_target_pairs={{0,24},{4,28},{8,16},{12,20},{16,8},{20,12},{24,0},{28,4},{1,25},{... | collective-permute-start | bytes 245768 | tf_op jit(solution)/shard_map/ppermute | solution.py:276
  71.0 5.9 %collective-permute-start.22 = (f32[32,640]{1,0:T(8,128)S(1)}, f32[32,640]{1,0:T(8,128)S(1)}, u32[]{:S(2)}, u32[]{:S(2)}) collective-permute-start(f32[32,640]{1,0:T(8,128)S(1)} %get-tuple-element.64), channel_id=1, source_target_pairs={{0,16},{4,20},{8,24},{12,28},{16,0},{20,4},{24,8},{28,12},{1,17},{... | collective-permute-start | bytes 245768 | tf_op jit(solution)/shard_map/ppermute | solution.py:276
  72.4 4.5 %collective-permute-start.21 = (f32[32,640]{1,0:T(8,128)S(1)}, f32[32,640]{1,0:T(8,128)S(1)}, u32[]{:S(2)}, u32[]{:S(2)}) collective-permute-start(f32[32,640]{1,0:T(8,128)S(1)} %get-tuple-element.65), channel_id=1, source_target_pairs={{0,8},{4,12},{8,0},{12,4},{16,24},{20,28},{24,16},{28,20},{1,9},{5... | collective-permute-start | bytes 245768 | tf_op jit(solution)/shard_map/ppermute | solution.py:276
  78.1 1.2 %collective-permute-start.24 = (f32[32,32]{1,0:T(8,128)S(1)}, f32[32,32]{1,0:T(8,128)S(1)}, u32[]{:S(2)}, u32[]{:S(2)}) collective-permute-start(f32[32,32]{1,0:T(8,128)S(1)} %get-tuple-element.62), channel_id=1, source_target_pairs={{0,4},{4,0},{8,12},{12,8},{16,20},{20,16},{24,28},{28,24},{1,5},{5... | collective-permute-start | bytes 12296 | tf_op jit(solution)/shard_map/ppermute | solution.py:276
  79.3 4.6 %collective-permute-start.27 = (f32[32,32]{1,0:T(8,128)S(1)}, f32[32,32]{1,0:T(8,128)S(1)}, u32[]{:S(2)}, u32[]{:S(2)}) collective-permute-start(f32[32,32]{1,0:T(8,128)S(1)} %add.20), channel_id=1, source_target_pairs={{0,24},{4,28},{8,16},{12,20},{16,8},{20,12},{24,0},{28,4},{1,25},{... | collective-permute-start | bytes 12296 | tf_op jit(solution)/shard_map/ppermute | solution.py:276
  80.9 3.7 %collective-permute-start.26 = (f32[32,32]{1,0:T(8,128)S(1)}, f32[32,32]{1,0:T(8,128)S(1)}, u32[]{:S(2)}, u32[]{:S(2)}) collective-permute-start(f32[32,32]{1,0:T(8,128)S(1)} %add.20), channel_id=1, source_target_pairs={{0,16},{4,20},{8,24},{12,28},{16,0},{20,4},{24,8},{28,12},{1,17},{... | collective-permute-start | bytes 12296 | tf_op jit(solution)/shard_map/ppermute | solution.py:276
  82.3 3.7 %collective-permute-start.25 = (f32[32,32]{1,0:T(8,128)S(1)}, f32[32,32]{1,0:T(8,128)S(1)}, u32[]{:S(2)}, u32[]{:S(2)}) collective-permute-start(f32[32,32]{1,0:T(8,128)S(1)} %add.20), channel_id=1, source_target_pairs={{0,8},{4,12},{8,0},{12,4},{16,24},{20,28},{24,16},{28,20},{1,9},{5... | collective-permute-start | bytes 12296 | tf_op jit(solution)/shard_map/ppermute | solution.py:276
  86.0 5.6 %collective-permute-start.30 = (f32[32,32]{1,0:T(8,128)S(1)}, f32[32,32]{1,0:T(8,128)S(1)}, u32[]{:S(2)}, u32[]{:S(2)}) collective-permute-start(f32[32,32]{1,0:T(8,128)S(1)} %add_add_fusion.refs_1_), channel_id=1, source_target_pairs={{0,3},{1,2},{2,1},{3,0},{4,7},{5,6},{6,5},{7,4},{8,11},{9,10},{10,... | collective-permute-start | bytes 12296 | tf_op jit(solution)/shard_map/ppermute | solution.py:276
  88.2 4.6 %collective-permute-start.29 = (f32[32,32]{1,0:T(8,128)S(1)}, f32[32,32]{1,0:T(8,128)S(1)}, u32[]{:S(2)}, u32[]{:S(2)}) collective-permute-start(f32[32,32]{1,0:T(8,128)S(1)} %add_add_fusion.refs_1_), channel_id=1, source_target_pairs={{0,2},{1,3},{2,0},{3,1},{4,6},{5,7},{6,4},{7,5},{8,10},{9,11},{10,... | collective-permute-start | bytes 12296 | tf_op jit(solution)/shard_map/ppermute | solution.py:276
  88.2 4.6 %collective-permute-start.28 = (f32[32,32]{1,0:T(8,128)S(1)}, f32[32,32]{1,0:T(8,128)S(1)}, u32[]{:S(2)}, u32[]{:S(2)}) collective-permute-start(f32[32,32]{1,0:T(8,128)S(1)} %add_add_fusion.refs_1_), channel_id=1, source_target_pairs={{0,1},{1,0},{2,3},{3,2},{4,5},{5,4},{6,7},{7,6},{8,9},{9,8},{10,11... | collective-permute-start | bytes 12296 | tf_op jit(solution)/shard_map/ppermute | solution.py:276

commit v3 on v2

v3 whole, which is shorter than its diff:
```python
import functools
import math
import jax
import jax.numpy as jnp
from jax import lax
from jax.experimental import pallas as pl
from jax.experimental.pallas import tpu as pltpu
from jax.sharding import PartitionSpec as P

VMEM = pl.BlockSpec(memory_space=pltpu.VMEM)
ROWS_BY_COLUMNS = (((1,), (0,)), ((), ()))
ROWS_BY_ROWS = (((1,), (1,)), ((), ()))
RESIDENT_BYTES = 36 << 20
DEGREE_ROWS = 16


def call(body, out_shape, operands, scratch=(), limit=14 << 20, flops=0, name=None):
    return pl.pallas_call(
        body,
        out_shape=out_shape,
        in_specs=[VMEM] * len(operands),
        out_specs=jax.tree.map(lambda _: VMEM, out_shape),
        scratch_shapes=list(scratch),
        compiler_params=pltpu.CompilerParams(vmem_limit_bytes=limit),
        cost_estimate=pl.CostEstimate(flops=flops, bytes_accessed=0, transcendentals=0) if flops else None,
        name=name,
    )(*operands)


def f32(*shape):
    return jax.ShapeDtypeStruct(shape, jnp.float32)


def bf16(*shape):
    return jax.ShapeDtypeStruct(shape, jnp.bfloat16)


def halves(values):
    high = values.astype(jnp.bfloat16)
    return high, (values - high.astype(jnp.float32)).astype(jnp.bfloat16)


def thirds(values):
    high = values.astype(jnp.bfloat16).astype(jnp.float32)
    middle = (values - high).astype(jnp.bfloat16).astype(jnp.float32)
    return high, middle, values - high - middle


def row_operand(points, left, span):
    width, features = points.shape
    high, low = halves(points)
    left[span, 0:features] = high
    left[span, features : 2 * features] = high
    left[span, 2 * features : 3 * features] = low
    first, second, third = thirds(0.5 * jnp.sum(points * points, axis=1, keepdims=True))
    lane = lax.broadcasted_iota(jnp.int32, (width, features), 1)
    tail = jnp.where(lane == 0, first, jnp.where(lane == 1, second, jnp.where(lane == 2, third, 0.0)))
    tail = jnp.where((lane > 2) & (lane < 6), -1.0, tail)
    left[span, 3 * features : 4 * features] = tail.astype(jnp.bfloat16)


def column_operand(points, right, span):
    features, width = points.shape
    high, low = halves(points)
    right[0:features, span] = high
    right[features : 2 * features, span] = low
    right[2 * features : 3 * features, span] = high
    first, second, third = thirds(0.5 * jnp.sum(points * points, axis=0, keepdims=True))
    line = lax.broadcasted_iota(jnp.int32, (features, width), 0)
    tail = jnp.where(line == 3, first, jnp.where(line == 4, second, jnp.where(line == 5, third, 0.0)))
    tail = jnp.where(line < 3, -1.0, tail)
    right[3 * features : 4 * features, span] = tail.astype(jnp.bfloat16)


def build_rows(left, right, high_ref, low_ref, totals, tile_rows=256, tile_columns=512):
    width = left.shape[0]
    for start in range(0, width, tile_rows):
        lines = slice(start, start + tile_rows)
        points = left[lines, :]
        total = jnp.zeros((tile_rows, 128), jnp.float32)
        for first in range(0, right.shape[1], tile_columns):
            span = slice(first, first + tile_columns)
            values = jnp.exp2(
                lax.dot_general(points, right[:, span], ROWS_BY_COLUMNS, preferred_element_type=jnp.float32)
            )
            high = values.astype(jnp.bfloat16)
            high_ref[lines, span] = high
            low_ref[lines, span] = (values - high.astype(jnp.float32)).astype(jnp.bfloat16)
            for lane in range(0, tile_columns, 128):
                total = total + values[:, lane : lane + 128]
        totals[lines, :] = total
    return jnp.sum(totals[...].T, axis=0, keepdims=True)


def point_scale(features):
    return math.sqrt(math.log2(math.e) / (0.25 * features))


def build_near_kernel(*refs, row_parts, column_parts):
    row_refs, column_refs = refs[:row_parts], (refs[0], *refs[row_parts : row_parts + column_parts - 1])
    outs = refs[row_parts + column_parts - 1 :]
    sums_ref, left_ref, right, totals = outs[2 * row_parts :]
    features, width = row_refs[0].shape
    scale = point_scale(features)
    for part, ref in enumerate(column_refs):
        column_operand(ref[...] * scale, right, slice(part * width, (part + 1) * width))
    for part, (high_ref, low_ref) in enumerate(pairs(outs[: 2 * row_parts])):
        lines = slice(part * width, (part + 1) * width)
        row_operand(row_refs[part][...].T * scale, left_ref, lines)
        sums_ref[part : part + 1, :] = build_rows(left_ref.at[lines, :], right, high_ref, low_ref, totals)
    sums_ref[row_parts:, :] = jnp.zeros((sums_ref.shape[0] - row_parts, width), jnp.float32)


def build_far_kernel(*refs, row_parts, column_parts):
    left_ref, sums_ref, start_ref, column_refs = refs[0], refs[1], refs[2], refs[3 : 3 + column_parts]
    outs = refs[3 + column_parts :]
    packed_ref, right, totals = outs[2 * row_parts :]
    vectors, width = start_ref.shape
    scale = point_scale(column_refs[0].shape[0])
    packed_ref[0:vectors, :] = start_ref[...]
    packed_ref[vectors:, :] = sums_ref[...]
    for part, ref in enumerate(column_refs):
        column_operand(ref[...] * scale, right, slice(part * width, (part + 1) * width))
    for part, (high_ref, low_ref) in enumerate(pairs(outs[: 2 * row_parts])):
        lines = slice(part * width, (part + 1) * width)
        line = vectors + part
        packed_ref[line : line + 1, :] += build_rows(left_ref.at[lines, :], right, high_ref, low_ref, totals)


def sweep(weights, parts, stores, block, initial=None, tile=256):
    rows = weights.shape[0] // 2
    width = stores[0][0].shape[0]
    pieces = []
    for first in range(0, width, tile):
        span = slice(block * width + first, block * width + first + tile)
        total = None if initial is None else initial[:, first : first + tile]
        for part, (high_ref, low_ref) in zip(parts, stores):
            lines = slice(part * width, (part + 1) * width)
            both = lax.dot_general(
                weights[:, lines], high_ref[:, span], ROWS_BY_COLUMNS, preferred_element_type=jnp.float32
            )
            last = lax.dot_general(
                weights[0:rows, lines], low_ref[:, span], ROWS_BY_COLUMNS, preferred_element_type=jnp.float32
            )
            term = both[0:rows] + both[rows:] + last
            total = term if total is None else total + term
        pieces.append(total)
    return jnp.concatenate(pieces, axis=1)


def pairs(refs):
    return list(zip(refs[0::2], refs[1::2]))


def place_of(block, odd):
    return block // 2, block % 2 + (2 if odd else 0)


def halved(refs, parts):
    return pairs(refs[: 2 * parts]), pairs(refs[2 * parts : 4 * parts])


def first_kernel(*refs, parts):
    packed_refs, stores = refs[:parts], halved(refs[parts : 5 * parts], parts)
    out_ref, inverse_ref, weights = refs[5 * parts :]
    rows = weights.shape[0] // 2
    vectors = rows - DEGREE_ROWS
    width = packed_refs[0].shape[1]
    kept = out_ref.shape[1]
    for part in range(parts):
        span = slice(part * width, (part + 1) * width)
        density = packed_refs[0][vectors + part : vectors + part + 1, :]
        for peer in range(1, parts):
            line = vectors + (part ^ peer)
            density = density + packed_refs[peer][line : line + 1, :]
        inverse = 1.0 / density
        if part == 0:
            inverse_ref[...] = inverse
        line = lax.broadcasted_iota(jnp.int32, (DEGREE_ROWS, width), 0)
        for first, piece in (
            (0, packed_refs[part][0:vectors, :] * inverse),
            (vectors, jnp.where(line == 0, inverse, 0.0)),
        ):
            high, low = halves(piece)
            last = first + piece.shape[0]
            weights[first:last, span] = high
            weights[rows + first : rows + last, span] = low
    for block in range(out_ref.shape[0]):
        half, place = place_of(block, True)
        out_ref[block] = sweep(weights, range(parts), stores[half], place)[0:kept]


def far_kernel(*refs, parts):
    weights, stores, out_ref = refs[0], halved(refs[1 : 1 + 4 * parts], parts), refs[-1]
    for index in range(out_ref.shape[0]):
        half, place = place_of(1 + index, False)
        out_ref[index] = sweep(weights, range(parts), stores[half], place)[0 : out_ref.shape[1]]


def own_kernel(*refs, parts):
    weights, stores, out_ref = refs[0], pairs(refs[2 : 2 + 2 * parts]), refs[-1]
    out_ref[...] = sweep(weights, range(parts), stores, 0)[0 : out_ref.shape[0]]


def second_start_kernel(piece_ref, high_ref, low_ref, far_high_ref, far_low_ref, odd_ref, even_ref, weights):
    vectors, width = piece_ref.shape[0], high_ref.shape[0]
    high, low = halves(piece_ref[:, 0:width])
    weights[0:vectors, :] = high
    weights[vectors:, :] = low
    stores = (high_ref, low_ref), (far_high_ref, far_low_ref)
    for odd, out_ref in ((True, odd_ref), (False, even_ref)):
        for block in range(out_ref.shape[0]):
            half, place = place_of(block, odd)
            out_ref[block] = sweep(weights, (0,), [stores[half]], place)


def second_odd_kernel(*refs, parts):
    piece_refs, partial_ref = refs[: 1 + parts], refs[1 + parts]
    stores = halved(refs[2 + parts : 2 + 5 * parts], parts)
    out_ref, gram_ref, weights = refs[2 + 5 * parts :]
    vectors, width = piece_refs[0].shape[0], stores[0][0][0].shape[0]
    gram = piece_refs[0][:, width:]
    for part, ref in enumerate(piece_refs[1:]):
        gram = gram + ref[:, width:]
        span = slice(part * width, (part + 1) * width)
        high, low = halves(ref[:, 0:width])
        weights[0:vectors, span] = high
        weights[vectors:, span] = low
    gram_ref[...] = gram
    for block in range(out_ref.shape[0]):
        half, place = place_of(block, True)
        out_ref[block, :, 0:width] = sweep(weights, range(parts), stores[half], place, partial_ref[block])
        out_ref[block, :, width:] = gram


def second_even_kernel(*refs, parts):
    weights, gram_ref, partial_ref = refs[:3]
    stores, out_ref = halved(refs[3 : 3 + 4 * parts], parts), refs[-1]
    width = stores[0][0][0].shape[0]
    for index in range(out_ref.shape[0]):
        half, place = place_of(1 + index, False)
        out_ref[index, :, 0:width] = sweep(
            weights, range(parts), stores[half], place, partial_ref[1 + index]
        )
        out_ref[index, :, width:] = gram_ref[...]


def second_own_kernel(*refs, parts):
    weights, gram_ref, partial_ref = refs[:3]
    stores, out_ref = pairs(refs[4 : 4 + 2 * parts]), refs[-1]
    width = stores[0][0].shape[0]
    out_ref[:, 0:width] = sweep(weights, range(parts), stores, 0, partial_ref[0])
    out_ref[:, width:] = gram_ref[...]


def exact(left, right, dims):
    return lax.dot_general(
        left, right, dims, precision=lax.Precision.HIGHEST, preferred_element_type=jnp.float32
    )


def grown_kernel(*refs):
    inverse_ref, piece_refs, (grown_ref, degree_ref) = refs[0], refs[1:-2], refs[-2:]
    vectors = grown_ref.shape[0]
    width = degree_ref.shape[1]
    total = piece_refs[0][...]
    for ref in piece_refs[1:]:
        total = total + ref[...]
    degree = total[vectors : vectors + 1, :]
    grown = total[0:vectors, :] / degree
    degree_ref[...] = degree
    grown_ref[:, 0:width] = grown * inverse_ref[...]
    gram = exact(grown, grown, ROWS_BY_ROWS)
    grown_ref[:, width:] = jnp.concatenate([gram, jnp.zeros((vectors, 128 - vectors), jnp.float32)], axis=1)


def inverse_factor(gram, panel=16):
    size = gram.shape[0]
    shape = (size, 2 * size)
    line = lax.broadcasted_iota(jnp.int32, (size, size), 0)
    lane = lax.broadcasted_iota(jnp.int32, (size, size), 1)
    table = jnp.concatenate([gram, jnp.where(line == lane, 1.0, 0.0)], axis=1)
    tall = lax.broadcasted_iota(jnp.int32, shape, 0)
    pivots = jnp.zeros(shape, jnp.float32)
    for first in range(0, size, panel):
        columns = [jnp.broadcast_to(table[:, step : step + 1], shape) for step in range(first, first + panel)]
        for place, step in enumerate(range(first, first + panel)):
            pivot = columns[place][step : step + 1, :]
            pivots = jnp.where(tall == step, pivot, pivots)
            factor = jnp.where(tall > step, columns[place] * (1.0 / pivot), 0.0)
            for later in range(place + 1, panel):
                columns[later] = columns[later] - factor * columns[later][step : step + 1, :]
            table = table - factor * table[step : step + 1, :]
    return table[:, size:] * lax.rsqrt(pivots[:, size:])


def grown_two_kernel(*refs, count):
    degree_ref, piece_refs, (grown_ref, gram_ref) = refs[0], refs[1:-2], refs[-2:]
    vectors, width = grown_ref.shape
    total = piece_refs[0][...]
    for ref in piece_refs[1:]:
        total = total + ref[...]
    factor = inverse_factor(total[:, width : width + vectors] * (1.0 / count))
    grown = exact(factor, total[:, 0:width] / degree_ref[...], ROWS_BY_COLUMNS)
    grown_ref[...] = grown
    gram_ref[...] = exact(grown, grown, ROWS_BY_ROWS)


def finish_kernel(*refs, count):
    grown_ref, gram_refs, out_ref = refs[0], refs[1:-1], refs[-1]
    gram = gram_refs[0][...]
    for ref in gram_refs[1:]:
        gram = gram + ref[...]
    out_ref[...] = exact(inverse_factor(gram * (1.0 / count)), grown_ref[...], ROWS_BY_COLUMNS)


def swap(values, mask):
    size = lax.axis_size(("row", "col"))
    return lax.ppermute(values, ("row", "col"), [(index, index ^ mask) for index in range(size)])


def resident_shards(frames, start):
    row_size, column_size = lax.axis_size("row"), lax.axis_size("col")
    count = frames.shape[1] * row_size * column_size
    features, width = frames.shape
    vectors = start.shape[0]

    core, across, along, skip = column_size, column_size * row_size // 2, 1, column_size // 2
    beside = 2 * core
    near = (along, across, along | across)
    far = (beside, skip, skip | beside)
    parts, half = 4, 4

    skip_piece = swap(frames, skip)
    beside_piece = swap(frames, beside)
    row_pieces = [frames] + [swap(frames, mask) for mask in near]
    both_piece = swap(skip_piece, beside)
    near_columns = [beside_piece, swap(frames, core), swap(beside_piece, core)]
    far_columns = [skip_piece, both_piece, swap(skip_piece, core), swap(both_piece, core)]

    operands = 4 * features
    columns = half * width
    stored = (bf16(width, columns),) * (2 * parts)
    totals = pltpu.VMEM((width, 128), jnp.float32)
    *near_store, sums, left = call(
        functools.partial(build_near_kernel, row_parts=parts, column_parts=half),
        (*stored, f32(8, width), bf16(parts * width, operands)),
        (*row_pieces, *near_columns),
        scratch=(pltpu.VMEM((operands, columns), jnp.bfloat16), totals),
        flops=1,
        name="build_near",
    )
    *far_store, packed = call(
        functools.partial(build_far_kernel, row_parts=parts, column_parts=half),
        (*stored, f32(vectors + 8, width)),
        (left, sums, start, *far_columns),
        scratch=(pltpu.VMEM((operands, columns), jnp.bfloat16), totals),
        flops=1,
        name="build_far",
    )
    all_packed = [packed] + [swap(packed, mask) for mask in near]

    def spread(odds, evens):
        odds = swap(odds, core)
        both = evens + odds[1:]
        return odds[0], both, [swap(both[place], mask) for place, mask in enumerate(far)]

    def total_gram(gram):
        gram = gram + swap(gram, core)
        gram = functools.reduce(jnp.add, [swap(gram, mask) for mask in near], gram)
        return [gram] + [swap(gram, mask) for mask in far]

    rows = vectors + DEGREE_ROWS
    block = 2 * 3 * rows * parts * width * width
    odds, inverse, weights = call(
        functools.partial(first_kernel, parts=parts),
        (f32(half, vectors + 8, width), f32(1, width), bf16(2 * rows, parts * width)),
        (*all_packed, *near_store, *far_store),
        flops=half * block,
        name="first_odd",
    )
    evens = call(
        functools.partial(far_kernel, parts=parts),
        f32(half - 1, vectors + 8, width),
        (weights, *near_store, *far_store),
        flops=(half - 1) * block,
        name="first_even",
    )
    own_odd, both, others = spread(odds, evens)
    own_even = call(
        functools.partial(own_kernel, parts=parts),
        f32(vectors + 8, width),
        (weights, both, *near_store),
        flops=block,
        name="first_own",
    )
    weighted, degree = call(
        grown_kernel,
        (f32(vectors, width + 128), f32(1, width)),
        (inverse, own_even, own_odd, *others),
        name="grown",
    )
    pieces = [weighted] + [swap(weighted, mask) for mask in near]
    odd_partial, even_partial = call(
        second_start_kernel,
        (f32(half, vectors, width),) * 2,
        (weighted, *near_store[0:2], *far_store[0:2]),
        scratch=(pltpu.VMEM((2 * vectors, width), jnp.bfloat16),),
        flops=2 * half * block // parts,
        name="second_start",
    )
    rest = parts - 1
    odds, gram, weights = call(
        functools.partial(second_odd_kernel, parts=rest),
        (f32(half, vectors, width + 128), f32(vectors, 128), bf16(2 * vectors, rest * width)),
        (*pieces, odd_partial, *near_store[2:], *far_store[2:]),
        flops=half * block,
        name="second_odd",
    )
    evens = call(
        functools.partial(second_even_kernel, parts=rest),
        f32(half - 1, vectors, width + 128),
        (weights, gram, even_partial, *near_store[2:], *far_store[2:]),
        flops=(half - 1) * block,
        name="second_even",
    )
    own_odd, both, others = spread(odds, evens)
    own_even = call(
        functools.partial(second_own_kernel, parts=rest),
        f32(vectors, width + 128),
        (weights, gram, even_partial, both, *near_store[2:]),
        flops=block,
        name="second_own",
    )
    grown_two, gram_two = call(
        functools.partial(grown_two_kernel, count=count),
        (f32(vectors, width), f32(vectors, vectors)),
        (degree, own_even, own_odd, *others),
        name="grown_two",
    )
    return call(
        functools.partial(finish_kernel, count=count),
        f32(vectors, width),
        (grown_two, *total_gram(gram_two)),
        name="finish",
    )


def build_block(block_points, block_squares, column_points, column_squares):
    products = lax.dot_general(
        block_points, column_points, (((0,), (0,)), ((), ())), precision=lax.Precision.HIGHEST
    )
    distance = block_squares[:, None] + column_squares[None, :] - 2.0 * products
    return jnp.exp(-distance / (0.5 * block_points.shape[0]))


def stored_shards(frames, start):
    block_points = lax.all_gather(frames, "col", axis=1, tiled=True)
    column_points = lax.all_gather(frames, "row", axis=1, tiled=True)
    block_squares = jnp.sum(block_points * block_points, axis=0)
    column_squares = jnp.sum(column_points * column_points, axis=0)
    frame_count = frames.shape[1] * lax.axis_size("row") * lax.axis_size("col")
    block_rows = block_points.shape[1]
    height = min(512, block_rows)
    stored = [
        build_block(
            block_points[:, first : first + height],
            block_squares[first : first + height],
            column_points,
            column_squares,
        )
        for first in range(0, block_rows, height)
    ]

    def settle(partial_value):
        return lax.psum_scatter(partial_value, "col", scatter_dimension=1, tiled=True)

    def kernel_product(weights):
        spread_weights = lax.all_gather(weights, "row", axis=1, tiled=True)
        return settle(
            jnp.concatenate([exact(spread_weights, part, ROWS_BY_ROWS) for part in stored], axis=1)
        )

    def orthonormal(vectors):
        gram = lax.psum(exact(vectors, vectors, ROWS_BY_ROWS), ("row", "col")) / frame_count
        return jax.scipy.linalg.solve_triangular(jnp.linalg.cholesky(gram), vectors, lower=True)

    sums = jnp.concatenate([jnp.sum(part, axis=1)[None, :] for part in stored], axis=1)
    inverse = 1.0 / settle(sums)
    degree = kernel_product(inverse)
    basis_one = orthonormal(kernel_product(start * inverse) / degree)
    return orthonormal(kernel_product(basis_one * inverse) / degree)


def shards(frames, start):
    row_size, column_size = lax.axis_size("row"), lax.axis_size("col")
    entries = row_size * column_size * frames.shape[1] ** 2
    if (row_size, column_size) == (8, 4) and 4 * entries <= RESIDENT_BYTES:
        return resident_shards(frames, start)
    return stored_shards(frames, start)


def solution(mesh):
    return jax.shard_map(
        shards,
        mesh=mesh,
        in_specs=(P(None, ("row", "col")), P(None, ("row", "col"))),
        out_specs=P(None, ("row", "col")),
        check_vma=False,
    )
```

time: 94.6 us -> 92.9 us (0.982)
  waiting for transfers between devices: 35.2 us -> 29.2 us
  starting transfers between devices: 34 us -> 37.1 us
    ppermute x31, waiting for transfers between devices: 35.2 us -> 29.2 us  [swap(): lax.ppermute(values, ('row', 'col'), [(index, index ^ mask) for index in...]
    ppermute x31, starting transfers between devices: 34 us -> 37.1 us  [swap(): lax.ppermute(values, ('row', 'col'), [(index, index ^ mask) for index in...]
    pallas_call x9 -> x12, Pallas kernels: 24.1 us -> 24.4 us  [call(): pl.pallas_call(body, out_shape=out_shape, in_specs=[VMEM] * len(operands)...]
  transfers between devices with their start and end apart: 31 -> 31, of which waited for: 19 -> 17; matrix products, arithmetic and copies ran while one was open for 0% -> 0% of each run, Pallas kernels for 12% -> 13%
where the time goes in v3:
time: 92.9 us; the launch traced here: 92.8 us
  starting transfers between devices  37.1 us (40%)
  waiting for transfers between devices  29.2 us (31%)
  Pallas kernels  24.4 us (26%)
  local copies, waits for them, and re-layouts  1.79 us (2%)
    ppermute x31, starting transfers between devices, swap(): lax.ppermute(values, ('row', 'col'), [(index, index ^ mask) for index in...  37.1 us
    ppermute x31, waiting for transfers between devices, swap(): lax.ppermute(values, ('row', 'col'), [(index, index ^ mask) for index in...  29.2 us
    pallas_call x12, Pallas kernels, call(): pl.pallas_call(body, out_shape=out_shape, in_specs=[VMEM] * len(operands)...  24.4 us
  transfers between devices with their start and end apart: 31, of which 17 were waited for; matrix products, arithmetic and copies ran while one was open for 0% of the time, Pallas kernels for 13%

profile of v3, /device:TPU:0, one launch (start us, length us, event | category | flops | bytes accessed | tf_op | source)
XLA Modules:
  0.0 92.8 jit_solution(9468605942135853101)
XLA Ops:
  0.0 4.0 %collective-permute-start.6 = (f32[64,512]{1,0:T(8,128)}, f32[64,512]{1,0:T(8,128)S(1)}, u32[]{:S(2)}, u32[]{:S(2)}) collective-permute-start(f32[64,512]{1,0:T(8,128)} %refs_0_.1), channel_id=1, source_target_pairs={{0,2},{1,3},{2,0},{3,1},{4,6},{5,7},{6,4},{7,5},{8,10},{9,11},{10,... | collective-permute-start | bytes 393224 | tf_op jit(solution)/shard_map/ppermute | solution.py:319
  4.0 1.5 %collective-permute-start.3 = (f32[64,512]{1,0:T(8,128)}, f32[64,512]{1,0:T(8,128)S(1)}, u32[]{:S(2)}, u32[]{:S(2)}) collective-permute-start(f32[64,512]{1,0:T(8,128)} %refs_0_.1), channel_id=1, source_target_pairs={{0,8},{1,9},{2,10},{3,11},{4,12},{5,13},{6,14},{7,15},{8,0},{9,1},... | collective-permute-start | bytes 393224 | tf_op jit(solution)/shard_map/ppermute | solution.py:319
  5.5 2.5 %collective-permute-start.2 = (f32[64,512]{1,0:T(8,128)}, f32[64,512]{1,0:T(8,128)S(1)}, u32[]{:S(2)}, u32[]{:S(2)}) collective-permute-start(f32[64,512]{1,0:T(8,128)} %refs_0_.1), channel_id=1, source_target_pairs={{0,17},{1,16},{2,19},{3,18},{4,21},{5,20},{6,23},{7,22},{8,25},{9,... | collective-permute-start | bytes 393224 | tf_op jit(solution)/shard_map/ppermute | solution.py:319
  8.1 2.6 %collective-permute-done.6.refs_3_ = f32[64,512]{1,0:T(8,128)S(1)} collective-permute-done((f32[64,512]{1,0:T(8,128)}, f32[64,512]{1,0:T(8,128)S(1)}, u32[]{:S(2)}, u32[]{:S(2)}) %collective-permute-start.6) | collective-permute-done | bytes 131104 | tf_op jit(solution)/shard_map/ppermute | solution.py:319
  10.6 1.5 %collective-permute-start.7 = (f32[64,512]{1,0:T(8,128)S(1)}, f32[64,512]{1,0:T(8,128)S(1)}, u32[]{:S(2)}, u32[]{:S(2)}) collective-permute-start(f32[64,512]{1,0:T(8,128)S(1)} %collective-permute-done.6.refs_3_), channel_id=1, source_target_pairs={{0,8},{1,9},{2,10},{3,11},{4,12},{5,13},{6,14},{7,15},{8,0},{9,1},... | collective-permute-start | bytes 393224 | tf_op jit(solution)/shard_map/ppermute | solution.py:319
  12.2 1.5 %collective-permute-start.1 = (f32[64,512]{1,0:T(8,128)}, f32[64,512]{1,0:T(8,128)S(1)}, u32[]{:S(2)}, u32[]{:S(2)}) collective-permute-start(f32[64,512]{1,0:T(8,128)} %refs_0_.1), channel_id=1, source_target_pairs={{0,16},{1,17},{2,18},{3,19},{4,20},{5,21},{6,22},{7,23},{8,24},{9,... | collective-permute-start | bytes 393224 | tf_op jit(solution)/shard_map/ppermute | solution.py:319
  13.7 0.7 collective-permute-start
  15.0 0.7 collective-permute-done.7.refs_4_
  15.6 1.8 %collective-permute-done.1.refs_2_ = f32[64,512]{1,0:T(8,128)S(1)} collective-permute-done((f32[64,512]{1,0:T(8,128)}, f32[64,512]{1,0:T(8,128)S(1)}, u32[]{:S(2)}, u32[]{:S(2)}) %collective-permute-start.1) | collective-permute-done | bytes 131104 | tf_op jit(solution)/shard_map/ppermute | solution.py:319
  17.4 1.5 %collective-permute-done.refs_1_ = f32[64,512]{1,0:T(8,128)S(1)} collective-permute-done((f32[64,512]{1,0:T(8,128)}, f32[64,512]{1,0:T(8,128)S(1)}, u32[]{:S(2)}, u32[]{:S(2)}) %collective-permute-start) | collective-permute-done | bytes 131104 | tf_op jit(solution)/shard_map/ppermute | solution.py:319
  18.9 0.9 copy-done
  19.8 5.2 %build_near.1 = (bf16[512,2048]{1,0:T(8,128)(2,1)S(1)}, bf16[512,2048]{1,0:T(8,128)(2,1)S(1)}, bf16[512,2048]{1,0:T(8,128)(2,1)S(1)}, bf16[512,2048]{1,0:T(8,128...) custom-call(f32[64,512]{1,0:T(8,128)S(1)} %copy-done, ...), custom_call_target="tpu_custom_call" | custom-call | flops 1 | tf_op jit(solution)/shard_map/build_near/pallas_call | solution.py:18
  25.1 0.8 copy-done.1
  25.9 3.8 %build_far.1 = (bf16[512,2048]{1,0:T(8,128)(2,1)S(1)}, bf16[512,2048]{1,0:T(8,128)(2,1)S(1)}, bf16[512,2048]{1,0:T(8,128)(2,1)S(1)}, bf16[512,2048]{1,0:T(8,128)...) custom-call(bf16[2048,256]{1,0:T(8,128)(2,1)S(1)} %get-tuple-element, ...), custom_call_target="tpu_custom_call" | custom-call | flops 1 | tf_op jit(solution)/shard_map/build_far/pallas_call | solution.py:18
  29.7 0.7 collective-permute-start.12
  30.5 1.5 %collective-permute-start.11 = (f32[40,512]{1,0:T(8,128)S(1)}, f32[40,512]{1,0:T(8,128)S(1)}, u32[]{:S(2)}, u32[]{:S(2)}) collective-permute-start(f32[40,512]{1,0:T(8,128)S(1)} %get-tuple-element.38.refs_0_), channel_id=1, source_target_pairs={{0,16},{1,17},{2,18},{3,19},{4,20},{5,21},{6,22},{7,23},{8,24},{9,... | collective-permute-start | bytes 245768 | tf_op jit(solution)/shard_map/ppermute | solution.py:319
  32.0 1.3 %collective-permute-start.10 = (f32[40,512]{1,0:T(8,128)S(1)}, f32[40,512]{1,0:T(8,128)S(1)}, u32[]{:S(2)}, u32[]{:S(2)}) collective-permute-start(f32[40,512]{1,0:T(8,128)S(1)} %get-tuple-element.38.refs_0_), channel_id=1, source_target_pairs={{0,1},{1,0},{2,3},{3,2},{4,5},{5,4},{6,7},{7,6},{8,9},{9,8},{10,11... | collective-permute-start | bytes 245768 | tf_op jit(solution)/shard_map/ppermute | solution.py:319
  33.3 2.0 %collective-permute-done.12.refs_3_ = f32[40,512]{1,0:T(8,128)S(1)} collective-permute-done((f32[40,512]{1,0:T(8,128)S(1)}, f32[40,512]{1,0:T(8,128)S(1)}, u32[]{:S(2)}, u32[]{:S(2)}) %collective-permute-start.12) | collective-permute-done | bytes 81952 | tf_op jit(solution)/shard_map/ppermute | solution.py:319
  35.8 0.6 collective-permute-done.10.refs_1_
  36.4 2.9 %first_odd.1 = (f32[4,40,512]{2,1,0:T(8,128)S(1)}, f32[1,512]{1,0:T(1,128)S(1)}, bf16[96,2048]{1,0:T(8,128)(2,1)S(1)}) custom-call(f32[40,512]{1,0:T(8,128)S(1)} %get-tuple-element.38.refs_0_, f32[40,512]{1,0:T(8,128)S(1)} %collective-permute-done.10.refs_1_, f32[40,512]{1,0:T(8,128)S(1)} %collective-permute-done.11.refs_2_, ...), custom_call_target="tpu_custom_call" | custom-call | flops 1207959552 | tf_op jit(solution)/shard_map/first_odd/pallas_call | solution.py:18
  39.4 2.4 %first_even.1 = f32[3,40,512]{2,1,0:T(8,128)S(1)} custom-call(bf16[96,2048]{1,0:T(8,128)(2,1)S(1)} %get-tuple-element.56.refs_0_, bf16[512,2048]{1,0:T(8,128)(2,1)S(1)} %get-tuple-element.39.refs_4_.refs_1_.refs_2_.high_ref, bf16[512,2048]{1,0:T(8,128)(2,1)S(1)} %get-tuple-element.40.refs_5_.refs_2_.refs_3_.low_ref, ...), custom_call_target="tpu_custom_call" | custom-call | flops 905969664 | tf_op jit(solution)/shard_map/first_even/pallas_call | solution.py:18
  41.9 3.4 %collective-permute-start.16 = (f32[40,512]{1,0:T(8,128)S(1)}, f32[40,512]{1,0:T(8,128)S(1)}, u32[]{:S(2)}, u32[]{:S(2)}) collective-permute-start(f32[40,512]{1,0:T(8,128)S(1)} %get-tuple-element.70), channel_id=1, source_target_pairs={{0,10},{1,11},{2,8},{3,9},{4,14},{5,15},{6,12},{7,13},{8,2},{9,3},... | collective-permute-start | bytes 245768 | tf_op jit(solution)/shard_map/ppermute | solution.py:319
  45.4 1.4 %collective-permute-start.14 = (f32[40,512]{1,0:T(8,128)S(1)}, f32[40,512]{1,0:T(8,128)S(1)}, u32[]{:S(2)}, u32[]{:S(2)}) collective-permute-start(f32[40,512]{1,0:T(8,128)S(1)} %get-tuple-element.72), channel_id=1, source_target_pairs={{0,8},{1,9},{2,10},{3,11},{4,12},{5,13},{6,14},{7,15},{8,0},{9,1},... | collective-permute-start | bytes 245768 | tf_op jit(solution)/shard_map/ppermute | solution.py:319
  46.8 0.8 first_own.1.refs_1_
  47.6 4.9 %collective-permute-done.16.refs_5_ = f32[40,512]{1,0:T(8,128)S(1)} collective-permute-done((f32[40,512]{1,0:T(8,128)S(1)}, f32[40,512]{1,0:T(8,128)S(1)}, u32[]{:S(2)}, u32[]{:S(2)}) %collective-permute-start.16) | collective-permute-done | bytes 81952 | tf_op jit(solution)/shard_map/ppermute | solution.py:319
  52.5 1.2 %collective-permute-done.15.refs_4_ = f32[40,512]{1,0:T(8,128)S(1)} collective-permute-done((f32[40,512]{1,0:T(8,128)S(1)}, f32[40,512]{1,0:T(8,128)S(1)}, u32[]{:S(2)}, u32[]{:S(2)}) %collective-permute-start.15) | collective-permute-done | bytes 81952 | tf_op jit(solution)/shard_map/ppermute | solution.py:319
  54.0 0.8 collective-permute-start.18
  54.8 2.7 %collective-permute-start.17 = (f32[32,640]{1,0:T(8,128)S(1)}, f32[32,640]{1,0:T(8,128)S(1)}, u32[]{:S(2)}, u32[]{:S(2)}) collective-permute-start(f32[32,640]{1,0:T(8,128)S(1)} %get-tuple-element.59.piece_ref.refs_0_), channel_id=1, source_target_pairs={{0,1},{1,0},{2,3},{3,2},{4,5},{5,4},{6,7},{7,6},{8,9},{9,8},{10,11... | collective-permute-start | bytes 245768 | tf_op jit(solution)/shard_map/ppermute | solution.py:319
  57.5 1.5 %second_start.1 = (f32[4,32,512]{2,1,0:T(8,128)S(1)}, f32[4,32,512]{2,1,0:T(8,128)S(1)}) custom-call(f32[32,640]{1,0:T(8,128)S(1)} %get-tuple-element.59.piece_ref.refs_0_, bf16[512,2048]{1,0:T(8,128)(2,1)S(1)} %get-tuple-element.39.refs_4_.refs_1_.refs_2_.high_ref, bf16[512,2048]{1,0:T(8,128)(2,1)S(1)} %get-tuple-element.40.refs_5_.refs_2_.refs_3_.low_ref, ...), custom_call_target="tpu_custom_call" | custom-call | flops 603979776 | tf_op jit(solution)/shard_map/second_start/pallas_call | solution.py:18
  59.0 1.1 %collective-permute-done.19.refs_3_ = f32[32,640]{1,0:T(8,128)S(1)} collective-permute-done((f32[32,640]{1,0:T(8,128)S(1)}, f32[32,640]{1,0:T(8,128)S(1)}, u32[]{:S(2)}, u32[]{:S(2)}) %collective-permute-start.19) | collective-permute-done | bytes 81952 | tf_op jit(solution)/shard_map/ppermute | solution.py:319
  60.1 2.3 %second_odd.1 = (f32[4,32,640]{2,1,0:T(8,128)S(1)}, f32[32,128]{1,0:T(8,128)S(1)}, bf16[64,1536]{1,0:T(8,128)(2,1)S(1)}) custom-call(f32[32,640]{1,0:T(8,128)S(1)} %get-tuple-element.59.piece_ref.refs_0_, f32[32,640]{1,0:T(8,128)S(1)} %collective-permute-done.17.refs_1_, f32[32,640]{1,0:T(8,128)S(1)} %collective-permute-done.18.refs_2_, ...), custom_call_target="tpu_custom_call" | custom-call | flops 1207959552 | tf_op jit(solution)/shard_map/second_odd/pallas_call | solution.py:18
  62.4 1.7 %second_even.1 = f32[3,32,640]{2,1,0:T(8,128)S(1)} custom-call(bf16[64,1536]{1,0:T(8,128)(2,1)S(1)} %get-tuple-element.61.refs_0_, f32[32,128]{1,0:T(8,128)S(1)} %get-tuple-element.62.refs_1_, f32[4,32,512]{2,1,0:T(8,128)S(1)} %get-tuple-element.63.refs_2_, bf16[512,2048]{1,0:T(8,128)(2,1)S(1)} %get-tuple-element.41.refs_6_.refs_3_.refs_4_.refs_5_, ...), custom_call_target="tpu_custom_call" | custom-call | flops 905969664 | tf_op jit(solution)/shard_map/second_even/pallas_call | solution.py:18
  64.3 3.5 %collective-permute-start.23 = (f32[32,640]{1,0:T(8,128)S(1)}, f32[32,640]{1,0:T(8,128)S(1)}, u32[]{:S(2)}, u32[]{:S(2)}) collective-permute-start(f32[32,640]{1,0:T(8,128)S(1)} %get-tuple-element.67), channel_id=1, source_target_pairs={{0,10},{1,11},{2,8},{3,9},{4,14},{5,15},{6,12},{7,13},{8,2},{9,3},... | collective-permute-start | bytes 245768 | tf_op jit(solution)/shard_map/ppermute | solution.py:319
  67.7 1.0 %collective-permute-start.21 = (f32[32,640]{1,0:T(8,128)S(1)}, f32[32,640]{1,0:T(8,128)S(1)}, u32[]{:S(2)}, u32[]{:S(2)}) collective-permute-start(f32[32,640]{1,0:T(8,128)S(1)} %get-tuple-element.69), channel_id=1, source_target_pairs={{0,8},{1,9},{2,10},{3,11},{4,12},{5,13},{6,14},{7,15},{8,0},{9,1},... | collective-permute-start | bytes 245768 | tf_op jit(solution)/shard_map/ppermute | solution.py:319
  68.7 0.6 second_own.1.refs_1_
  69.4 5.5 %collective-permute-done.23.refs_5_ = f32[32,640]{1,0:T(8,128)S(1)} collective-permute-done((f32[32,640]{1,0:T(8,128)S(1)}, f32[32,640]{1,0:T(8,128)S(1)}, u32[]{:S(2)}, u32[]{:S(2)}) %collective-permute-start.23) | collective-permute-done | bytes 81952 | tf_op jit(solution)/shard_map/ppermute | solution.py:319
  74.9 0.6 collective-permute-done.22.refs_4_
  75.5 1.2 %grown_two.1 = (f32[32,512]{1,0:T(8,128)S(1)}, f32[32,32]{1,0:T(8,128)S(1)}) custom-call(f32[1,512]{1,0:T(1,128)S(1)} %get-tuple-element.58.refs_0_, f32[32,640]{1,0:T(8,128)S(1)} %second_own.1.refs_1_, f32[32,640]{1,0:T(8,128)S(1)} %slice_bitcast_fusion.3.refs_2_, f32[32,640]{1,0:T(8,128)S(1)} %collective-permute-done.21.refs_3_, ...), custom_call_target="tpu_custom_call" | custom-call | tf_op jit(solution)/shard_map/grown_two/pallas_call | solution.py:18
  76.7 1.2 %collective-permute-done.24 = f32[32,32]{1,0:T(8,128)S(1)} collective-permute-done((f32[32,32]{1,0:T(8,128)S(1)}, f32[32,32]{1,0:T(8,128)S(1)}, u32[]{:S(2)}, u32[]{:S(2)}) %collective-permute-start.24) | collective-permute-done | bytes 4128 | tf_op jit(solution)/shard_map/ppermute | solution.py:319
  77.9 0.7 collective-permute-start.27
  78.6 0.9 collective-permute-start.26
  79.4 1.9 %collective-permute-start.25 = (f32[32,32]{1,0:T(8,128)S(1)}, f32[32,32]{1,0:T(8,128)S(1)}, u32[]{:S(2)}, u32[]{:S(2)}) collective-permute-start(f32[32,32]{1,0:T(8,128)S(1)} %add.20), channel_id=1, source_target_pairs={{0,1},{1,0},{2,3},{3,2},{4,5},{5,4},{6,7},{7,6},{8,9},{9,8},{10,11... | collective-permute-start | bytes 12296 | tf_op jit(solution)/shard_map/ppermute | solution.py:319
  81.4 1.2 %collective-permute-done.27 = f32[32,32]{1,0:T(8,128)S(1)} collective-permute-done((f32[32,32]{1,0:T(8,128)S(1)}, f32[32,32]{1,0:T(8,128)S(1)}, u32[]{:S(2)}, u32[]{:S(2)}) %collective-permute-start.27) | collective-permute-done | bytes 4128 | tf_op jit(solution)/shard_map/ppermute | solution.py:319
  83.2 3.3 %collective-permute-start.30 = (f32[32,32]{1,0:T(8,128)S(1)}, f32[32,32]{1,0:T(8,128)S(1)}, u32[]{:S(2)}, u32[]{:S(2)}) collective-permute-start(f32[32,32]{1,0:T(8,128)S(1)} %add_add_fusion.refs_1_), channel_id=1, source_target_pairs={{0,10},{1,11},{2,8},{3,9},{4,14},{5,15},{6,12},{7,13},{8,2},{9,3},... | collective-permute-start | bytes 12296 | tf_op jit(solution)/shard_map/ppermute | solution.py:319
  86.8 1.3 %collective-permute-start.28 = (f32[32,32]{1,0:T(8,128)S(1)}, f32[32,32]{1,0:T(8,128)S(1)}, u32[]{:S(2)}, u32[]{:S(2)}) collective-permute-start(f32[32,32]{1,0:T(8,128)S(1)} %add_add_fusion.refs_1_), channel_id=1, source_target_pairs={{0,8},{1,9},{2,10},{3,11},{4,12},{5,13},{6,14},{7,15},{8,0},{9,1},... | collective-permute-start | bytes 12296 | tf_op jit(solution)/shard_map/ppermute | solution.py:319
  88.0 0.7 collective-permute-done.30.refs_4_
  88.7 2.4 %collective-permute-done.29.refs_3_ = f32[32,32]{1,0:T(8,128)S(1)} collective-permute-done((f32[32,32]{1,0:T(8,128)S(1)}, f32[32,32]{1,0:T(8,128)S(1)}, u32[]{:S(2)}, u32[]{:S(2)}) %collective-permute-start.29) | collective-permute-done | bytes 4128 | tf_op jit(solution)/shard_map/ppermute | solution.py:319
  91.2 1.6 %finish.1 = f32[32,512]{1,0:T(8,128)} custom-call(f32[32,512]{1,0:T(8,128)S(1)} %get-tuple-element.65.refs_0_, f32[32,32]{1,0:T(8,128)S(1)} %add_add_fusion.refs_1_, f32[32,32]{1,0:T(8,128)S(1)} %collective-permute-done.28.refs_2_, f32[32,32]{1,0:T(8,128)S(1)} %collective-permute-done.29.refs_3_, f32[32,32]{1,0:T(8,128)S(1)} %collective-permute-done.30.refs_4_), custom_call_target="tpu_custom_call" | custom-call | tf_op jit(solution)/shard_map/finish/pallas_call | solution.py:18
  (38 shorter events, 2.5 us)
Async XLA Ops:
  0.0 10.6 %collective-permute-start.6 = (f32[64,512]{1,0:T(8,128)}, f32[64,512]{1,0:T(8,128)S(1)}, u32[]{:S(2)}, u32[]{:S(2)}) collective-permute-start(f32[64,512]{1,0:T(8,128)} %refs_0_.1), channel_id=1, source_target_pairs={{0,2},{1,3},{2,0},{3,1},{4,6},{5,7},{6,4},{7,5},{8,10},{9,11},{10,... | collective-permute-start | bytes 393224 | tf_op jit(solution)/shard_map/ppermute | solution.py:319
  4.0 9.7 %collective-permute-start.4 = (f32[64,512]{1,0:T(8,128)}, f32[64,512]{1,0:T(8,128)S(1)}, u32[]{:S(2)}, u32[]{:S(2)}) collective-permute-start(f32[64,512]{1,0:T(8,128)} %refs_0_.1), channel_id=1, source_target_pairs={{0,4},{1,5},{2,6},{3,7},{4,0},{5,1},{6,2},{7,3},{8,12},{9,13},{10,... | collective-permute-start | bytes 393224 | tf_op jit(solution)/shard_map/ppermute | solution.py:319
  4.0 10.4 %collective-permute-start.3 = (f32[64,512]{1,0:T(8,128)}, f32[64,512]{1,0:T(8,128)S(1)}, u32[]{:S(2)}, u32[]{:S(2)}) collective-permute-start(f32[64,512]{1,0:T(8,128)} %refs_0_.1), channel_id=1, source_target_pairs={{0,8},{1,9},{2,10},{3,11},{4,12},{5,13},{6,14},{7,15},{8,0},{9,1},... | collective-permute-start | bytes 393224 | tf_op jit(solution)/shard_map/ppermute | solution.py:319
  5.5 8.9 %collective-permute-start.2 = (f32[64,512]{1,0:T(8,128)}, f32[64,512]{1,0:T(8,128)S(1)}, u32[]{:S(2)}, u32[]{:S(2)}) collective-permute-start(f32[64,512]{1,0:T(8,128)} %refs_0_.1), channel_id=1, source_target_pairs={{0,17},{1,16},{2,19},{3,18},{4,21},{5,20},{6,23},{7,22},{8,25},{9,... | collective-permute-start | bytes 393224 | tf_op jit(solution)/shard_map/ppermute | solution.py:319
  10.6 5.0 %collective-permute-start.7 = (f32[64,512]{1,0:T(8,128)S(1)}, f32[64,512]{1,0:T(8,128)S(1)}, u32[]{:S(2)}, u32[]{:S(2)}) collective-permute-start(f32[64,512]{1,0:T(8,128)S(1)} %collective-permute-done.6.refs_3_), channel_id=1, source_target_pairs={{0,8},{1,9},{2,10},{3,11},{4,12},{5,13},{6,14},{7,15},{8,0},{9,1},... | collective-permute-start | bytes 393224 | tf_op jit(solution)/shard_map/ppermute | solution.py:319
  12.2 5.2 %collective-permute-start.1 = (f32[64,512]{1,0:T(8,128)}, f32[64,512]{1,0:T(8,128)S(1)}, u32[]{:S(2)}, u32[]{:S(2)}) collective-permute-start(f32[64,512]{1,0:T(8,128)} %refs_0_.1), channel_id=1, source_target_pairs={{0,16},{1,17},{2,18},{3,19},{4,20},{5,21},{6,22},{7,23},{8,24},{9,... | collective-permute-start | bytes 393224 | tf_op jit(solution)/shard_map/ppermute | solution.py:319
  13.7 5.2 %collective-permute-start = (f32[64,512]{1,0:T(8,128)}, f32[64,512]{1,0:T(8,128)S(1)}, u32[]{:S(2)}, u32[]{:S(2)}) collective-permute-start(f32[64,512]{1,0:T(8,128)} %refs_0_.1), channel_id=1, source_target_pairs={{0,1},{1,0},{2,3},{3,2},{4,5},{5,4},{6,7},{7,6},{8,9},{9,8},{10,11... | collective-permute-start | bytes 393224 | tf_op jit(solution)/shard_map/ppermute | solution.py:319
  14.4 4.5 %collective-permute-start.5 = (f32[64,512]{1,0:T(8,128)S(1)}, f32[64,512]{1,0:T(8,128)S(1)}, u32[]{:S(2)}, u32[]{:S(2)}) collective-permute-start(f32[64,512]{1,0:T(8,128)S(1)} %collective-permute-done.3.refs_4_), channel_id=1, source_target_pairs={{0,4},{1,5},{2,6},{3,7},{4,0},{5,1},{6,2},{7,3},{8,12},{9,13},{10,... | collective-permute-start | bytes 393224 | tf_op jit(solution)/shard_map/ppermute | solution.py:319
  14.5 10.6 %collective-permute-start.8 = (f32[64,512]{1,0:T(8,128)S(1)}, f32[64,512]{1,0:T(8,128)S(1)}, u32[]{:S(2)}, u32[]{:S(2)}) collective-permute-start(f32[64,512]{1,0:T(8,128)S(1)} %collective-permute-done.6.refs_3_), channel_id=1, source_target_pairs={{0,4},{1,5},{2,6},{3,7},{4,0},{5,1},{6,2},{7,3},{8,12},{9,13},{10,... | collective-permute-start | bytes 393224 | tf_op jit(solution)/shard_map/ppermute | solution.py:319
  15.6 9.5 %collective-permute-start.9 = (f32[64,512]{1,0:T(8,128)S(1)}, f32[64,512]{1,0:T(8,128)S(1)}, u32[]{:S(2)}, u32[]{:S(2)}) collective-permute-start(f32[64,512]{1,0:T(8,128)S(1)} %collective-permute-done.7.refs_4_), channel_id=1, source_target_pairs={{0,4},{1,5},{2,6},{3,7},{4,0},{5,1},{6,2},{7,3},{8,12},{9,13},{10,... | collective-permute-start | bytes 393224 | tf_op jit(solution)/shard_map/ppermute | solution.py:319
  18.9 0.9 copy-start
  25.1 0.8 copy-start.1
  29.7 5.5 %collective-permute-start.12 = (f32[40,512]{1,0:T(8,128)S(1)}, f32[40,512]{1,0:T(8,128)S(1)}, u32[]{:S(2)}, u32[]{:S(2)}) collective-permute-start(f32[40,512]{1,0:T(8,128)S(1)} %get-tuple-element.38.refs_0_), channel_id=1, source_target_pairs={{0,17},{1,16},{2,19},{3,18},{4,21},{5,20},{6,23},{7,22},{8,25},{9,... | collective-permute-start | bytes 245768 | tf_op jit(solution)/shard_map/ppermute | solution.py:319
  30.5 5.3 %collective-permute-start.11 = (f32[40,512]{1,0:T(8,128)S(1)}, f32[40,512]{1,0:T(8,128)S(1)}, u32[]{:S(2)}, u32[]{:S(2)}) collective-permute-start(f32[40,512]{1,0:T(8,128)S(1)} %get-tuple-element.38.refs_0_), channel_id=1, source_target_pairs={{0,16},{1,17},{2,18},{3,19},{4,20},{5,21},{6,22},{7,23},{8,24},{9,... | collective-permute-start | bytes 245768 | tf_op jit(solution)/shard_map/ppermute | solution.py:319
  32.0 4.4 %collective-permute-start.10 = (f32[40,512]{1,0:T(8,128)S(1)}, f32[40,512]{1,0:T(8,128)S(1)}, u32[]{:S(2)}, u32[]{:S(2)}) collective-permute-start(f32[40,512]{1,0:T(8,128)S(1)} %get-tuple-element.38.refs_0_), channel_id=1, source_target_pairs={{0,1},{1,0},{2,3},{3,2},{4,5},{5,4},{6,7},{7,6},{8,9},{9,8},{10,11... | collective-permute-start | bytes 245768 | tf_op jit(solution)/shard_map/ppermute | solution.py:319
  39.4 2.5 %collective-permute-start.13 = (f32[4,40,512]{2,1,0:T(8,128)S(1)}, f32[4,40,512]{2,1,0:T(8,128)S(1)}, u32[]{:S(2)}, u32[]{:S(2)}) collective-permute-start(f32[4,40,512]{2,1,0:T(8,128)S(1)} %get-tuple-element.57), channel_id=1, source_target_pairs={{0,4},{1,5},{2,6},{3,7},{4,0},{5,1},{6,2},{7,3},{8,12},{9,13},{10,... | collective-permute-start | bytes 983048 | tf_op jit(solution)/shard_map/ppermute | solution.py:319
  41.9 10.6 %collective-permute-start.16 = (f32[40,512]{1,0:T(8,128)S(1)}, f32[40,512]{1,0:T(8,128)S(1)}, u32[]{:S(2)}, u32[]{:S(2)}) collective-permute-start(f32[40,512]{1,0:T(8,128)S(1)} %get-tuple-element.70), channel_id=1, source_target_pairs={{0,10},{1,11},{2,8},{3,9},{4,14},{5,15},{6,12},{7,13},{8,2},{9,3},... | collective-permute-start | bytes 245768 | tf_op jit(solution)/shard_map/ppermute | solution.py:319
  45.3 8.4 %collective-permute-start.15 = (f32[40,512]{1,0:T(8,128)S(1)}, f32[40,512]{1,0:T(8,128)S(1)}, u32[]{:S(2)}, u32[]{:S(2)}) collective-permute-start(f32[40,512]{1,0:T(8,128)S(1)} %get-tuple-element.71), channel_id=1, source_target_pairs={{0,2},{1,3},{2,0},{3,1},{4,6},{5,7},{6,4},{7,5},{8,10},{9,11},{10,... | collective-permute-start | bytes 245768 | tf_op jit(solution)/shard_map/ppermute | solution.py:319
  45.4 8.3 %collective-permute-start.14 = (f32[40,512]{1,0:T(8,128)S(1)}, f32[40,512]{1,0:T(8,128)S(1)}, u32[]{:S(2)}, u32[]{:S(2)}) collective-permute-start(f32[40,512]{1,0:T(8,128)S(1)} %get-tuple-element.72), channel_id=1, source_target_pairs={{0,8},{1,9},{2,10},{3,11},{4,12},{5,13},{6,14},{7,15},{8,0},{9,1},... | collective-permute-start | bytes 245768 | tf_op jit(solution)/shard_map/ppermute | solution.py:319
  53.9 6.2 %collective-permute-start.19 = (f32[32,640]{1,0:T(8,128)S(1)}, f32[32,640]{1,0:T(8,128)S(1)}, u32[]{:S(2)}, u32[]{:S(2)}) collective-permute-start(f32[32,640]{1,0:T(8,128)S(1)} %get-tuple-element.59.piece_ref.refs_0_), channel_id=1, source_target_pairs={{0,17},{1,16},{2,19},{3,18},{4,21},{5,20},{6,23},{7,22},{8,25},{9,... | collective-permute-start | bytes 245768 | tf_op jit(solution)/shard_map/ppermute | solution.py:319
  54.0 6.2 %collective-permute-start.18 = (f32[32,640]{1,0:T(8,128)S(1)}, f32[32,640]{1,0:T(8,128)S(1)}, u32[]{:S(2)}, u32[]{:S(2)}) collective-permute-start(f32[32,640]{1,0:T(8,128)S(1)} %get-tuple-element.59.piece_ref.refs_0_), channel_id=1, source_target_pairs={{0,16},{1,17},{2,18},{3,19},{4,20},{5,21},{6,22},{7,23},{8,24},{9,... | collective-permute-start | bytes 245768 | tf_op jit(solution)/shard_map/ppermute | solution.py:319
  54.8 5.3 %collective-permute-start.17 = (f32[32,640]{1,0:T(8,128)S(1)}, f32[32,640]{1,0:T(8,128)S(1)}, u32[]{:S(2)}, u32[]{:S(2)}) collective-permute-start(f32[32,640]{1,0:T(8,128)S(1)} %get-tuple-element.59.piece_ref.refs_0_), channel_id=1, source_target_pairs={{0,1},{1,0},{2,3},{3,2},{4,5},{5,4},{6,7},{7,6},{8,9},{9,8},{10,11... | collective-permute-start | bytes 245768 | tf_op jit(solution)/shard_map/ppermute | solution.py:319
  62.4 1.8 %collective-permute-start.20 = (f32[4,32,640]{2,1,0:T(8,128)S(1)}, f32[4,32,640]{2,1,0:T(8,128)S(1)}, u32[]{:S(2)}, u32[]{:S(2)}) collective-permute-start(f32[4,32,640]{2,1,0:T(8,128)S(1)} %get-tuple-element.64), channel_id=1, source_target_pairs={{0,4},{1,5},{2,6},{3,7},{4,0},{5,1},{6,2},{7,3},{8,12},{9,13},{10,... | collective-permute-start | bytes 983048 | tf_op jit(solution)/shard_map/ppermute | solution.py:319
  64.3 10.6 %collective-permute-start.23 = (f32[32,640]{1,0:T(8,128)S(1)}, f32[32,640]{1,0:T(8,128)S(1)}, u32[]{:S(2)}, u32[]{:S(2)}) collective-permute-start(f32[32,640]{1,0:T(8,128)S(1)} %get-tuple-element.67), channel_id=1, source_target_pairs={{0,10},{1,11},{2,8},{3,9},{4,14},{5,15},{6,12},{7,13},{8,2},{9,3},... | collective-permute-start | bytes 245768 | tf_op jit(solution)/shard_map/ppermute | solution.py:319
  67.7 7.8 %collective-permute-start.22 = (f32[32,640]{1,0:T(8,128)S(1)}, f32[32,640]{1,0:T(8,128)S(1)}, u32[]{:S(2)}, u32[]{:S(2)}) collective-permute-start(f32[32,640]{1,0:T(8,128)S(1)} %get-tuple-element.68), channel_id=1, source_target_pairs={{0,2},{1,3},{2,0},{3,1},{4,6},{5,7},{6,4},{7,5},{8,10},{9,11},{10,... | collective-permute-start | bytes 245768 | tf_op jit(solution)/shard_map/ppermute | solution.py:319
  67.7 7.8 %collective-permute-start.21 = (f32[32,640]{1,0:T(8,128)S(1)}, f32[32,640]{1,0:T(8,128)S(1)}, u32[]{:S(2)}, u32[]{:S(2)}) collective-permute-start(f32[32,640]{1,0:T(8,128)S(1)} %get-tuple-element.69), channel_id=1, source_target_pairs={{0,8},{1,9},{2,10},{3,11},{4,12},{5,13},{6,14},{7,15},{8,0},{9,1},... | collective-permute-start | bytes 245768 | tf_op jit(solution)/shard_map/ppermute | solution.py:319
  76.7 1.2 %collective-permute-start.24 = (f32[32,32]{1,0:T(8,128)S(1)}, f32[32,32]{1,0:T(8,128)S(1)}, u32[]{:S(2)}, u32[]{:S(2)}) collective-permute-start(f32[32,32]{1,0:T(8,128)S(1)} %get-tuple-element.66), channel_id=1, source_target_pairs={{0,4},{1,5},{2,6},{3,7},{4,0},{5,1},{6,2},{7,3},{8,12},{9,13},{10,... | collective-permute-start | bytes 12296 | tf_op jit(solution)/shard_map/ppermute | solution.py:319
  77.9 4.7 %collective-permute-start.27 = (f32[32,32]{1,0:T(8,128)S(1)}, f32[32,32]{1,0:T(8,128)S(1)}, u32[]{:S(2)}, u32[]{:S(2)}) collective-permute-start(f32[32,32]{1,0:T(8,128)S(1)} %add.20), channel_id=1, source_target_pairs={{0,17},{1,16},{2,19},{3,18},{4,21},{5,20},{6,23},{7,22},{8,25},{9,... | collective-permute-start | bytes 12296 | tf_op jit(solution)/shard_map/ppermute | solution.py:319
  78.6 4.0 %collective-permute-start.26 = (f32[32,32]{1,0:T(8,128)S(1)}, f32[32,32]{1,0:T(8,128)S(1)}, u32[]{:S(2)}, u32[]{:S(2)}) collective-permute-start(f32[32,32]{1,0:T(8,128)S(1)} %add.20), channel_id=1, source_target_pairs={{0,16},{1,17},{2,18},{3,19},{4,20},{5,21},{6,22},{7,23},{8,24},{9,... | collective-permute-start | bytes 12296 | tf_op jit(solution)/shard_map/ppermute | solution.py:319
  79.4 3.7 %collective-permute-start.25 = (f32[32,32]{1,0:T(8,128)S(1)}, f32[32,32]{1,0:T(8,128)S(1)}, u32[]{:S(2)}, u32[]{:S(2)}) collective-permute-start(f32[32,32]{1,0:T(8,128)S(1)} %add.20), channel_id=1, source_target_pairs={{0,1},{1,0},{2,3},{3,2},{4,5},{5,4},{6,7},{7,6},{8,9},{9,8},{10,11... | collective-permute-start | bytes 12296 | tf_op jit(solution)/shard_map/ppermute | solution.py:319
  83.2 5.5 %collective-permute-start.30 = (f32[32,32]{1,0:T(8,128)S(1)}, f32[32,32]{1,0:T(8,128)S(1)}, u32[]{:S(2)}, u32[]{:S(2)}) collective-permute-start(f32[32,32]{1,0:T(8,128)S(1)} %add_add_fusion.refs_1_), channel_id=1, source_target_pairs={{0,10},{1,11},{2,8},{3,9},{4,14},{5,15},{6,12},{7,13},{8,2},{9,3},... | collective-permute-start | bytes 12296 | tf_op jit(solution)/shard_map/ppermute | solution.py:319
  86.5 4.6 %collective-permute-start.29 = (f32[32,32]{1,0:T(8,128)S(1)}, f32[32,32]{1,0:T(8,128)S(1)}, u32[]{:S(2)}, u32[]{:S(2)}) collective-permute-start(f32[32,32]{1,0:T(8,128)S(1)} %add_add_fusion.refs_1_), channel_id=1, source_target_pairs={{0,2},{1,3},{2,0},{3,1},{4,6},{5,7},{6,4},{7,5},{8,10},{9,11},{10,... | collective-permute-start | bytes 12296 | tf_op jit(solution)/shard_map/ppermute | solution.py:319
  86.8 4.4 %collective-permute-start.28 = (f32[32,32]{1,0:T(8,128)S(1)}, f32[32,32]{1,0:T(8,128)S(1)}, u32[]{:S(2)}, u32[]{:S(2)}) collective-permute-start(f32[32,32]{1,0:T(8,128)S(1)} %add_add_fusion.refs_1_), channel_id=1, source_target_pairs={{0,8},{1,9},{2,10},{3,11},{4,12},{5,13},{6,14},{7,15},{8,0},{9,1},... | collective-permute-start | bytes 12296 | tf_op jit(solution)/shard_map/ppermute | solution.py:319

commit v4 on v3

--- a/solution.py
+++ b/solution.py
@@ -44,6 +44,24 @@
     high = values.astype(jnp.bfloat16).astype(jnp.float32)
     middle = (values - high).astype(jnp.bfloat16).astype(jnp.float32)
     return high, middle, values - high - middle
+
+
+def pack(values):
+    return jnp.concatenate([values[:, first : first + 128] for first in range(0, values.shape[1], 128)], axis=0)
+
+
+def unpack(packed, lines, width):
+    count = width // 128
+    return jnp.concatenate([packed[block * lines : (block + 1) * lines] for block in range(count)], axis=1)
+
+
+def pack_square(square):
+    lines = square.shape[0] * square.shape[0] // 128
+    return jnp.concatenate([square[first : first + lines] for first in range(0, square.shape[0], lines)], axis=1)
+
+
+def unpack_square(packed, size):
+    return jnp.concatenate([packed[:, first : first + size] for first in range(0, packed.shape[1], size)], axis=0)
 
 
 def row_operand(points, left, span):
@@ -104,27 +122,36 @@
     scale = point_scale(features)
     for part, ref in enumerate(column_refs):
         column_operand(ref[...] * scale, right, slice(part * width, (part + 1) * width))
+    sums_ref[...] = jnp.zeros_like(sums_ref)
     for part, (high_ref, low_ref) in enumerate(pairs(outs[: 2 * row_parts])):
         lines = slice(part * width, (part + 1) * width)
         row_operand(row_refs[part][...].T * scale, left_ref, lines)
         sums_ref[part : part + 1, :] = build_rows(left_ref.at[lines, :], right, high_ref, low_ref, totals)
-    sums_ref[row_parts:, :] = jnp.zeros((sums_ref.shape[0] - row_parts, width), jnp.float32)
 
 
 def build_far_kernel(*refs, row_parts, column_parts):
-    left_ref, sums_ref, start_ref, column_refs = refs[0], refs[1], refs[2], refs[3 : 3 + column_parts]
-    outs = refs[3 + column_parts :]
-    packed_ref, right, totals = outs[2 * row_parts :]
+    left_ref, near_right, near_sums_ref, start_ref, last_ref = refs[:5]
+    column_refs, outs = refs[5 : 5 + column_parts], refs[5 + column_parts :]
+    packed_ref, right, left, totals = outs[2 * row_parts + 4 :]
     vectors, width = start_ref.shape
-    scale = point_scale(column_refs[0].shape[0])
-    packed_ref[0:vectors, :] = start_ref[...]
-    packed_ref[vectors:, :] = sums_ref[...]
+    lanes = width // 128
+    scale = point_scale(last_ref.shape[0])
+    packed_ref[0 : vectors * lanes, :] = pack(start_ref[...])
     for part, ref in enumerate(column_refs):
         column_operand(ref[...] * scale, right, slice(part * width, (part + 1) * width))
-    for part, (high_ref, low_ref) in enumerate(pairs(outs[: 2 * row_parts])):
+    stores = pairs(outs[: 2 * row_parts + 4])
+
+    def put(part, sums):
+        line = (vectors + part) * lanes
+        packed_ref[line : line + lanes, :] = pack(sums)
+
+    for part in range(row_parts):
         lines = slice(part * width, (part + 1) * width)
-        line = vectors + part
-        packed_ref[line : line + 1, :] += build_rows(left_ref.at[lines, :], right, high_ref, low_ref, totals)
+        sums = build_rows(left_ref.at[lines, :], right, *stores[part], totals)
+        put(part, near_sums_ref[part : part + 1, :] + sums)
+    row_operand(last_ref[...].T * scale, left, slice(0, width))
+    sums = build_rows(left, near_right, *stores[row_parts], totals)
+    put(row_parts, sums + build_rows(left, right, *stores[row_parts + 1], totals))
 
 
 def sweep(weights, parts, stores, block, initial=None, tile=256):
@@ -160,25 +187,38 @@
     return pairs(refs[: 2 * parts]), pairs(refs[2 * parts : 4 * parts])
 
 
+def put_product(out_ref, product, vectors):
+    width = product.shape[1]
+    lanes = width // 128
+    last = vectors * lanes
+    out_ref[0:last, :] = pack(product[0:vectors])
+    out_ref[last : last + 8, :] = jnp.zeros((8, 128), jnp.float32)
+    out_ref[last : last + lanes, :] = pack(product[vectors : vectors + 1])
+
+
 def first_kernel(*refs, parts):
     packed_refs, stores = refs[:parts], halved(refs[parts : 5 * parts], parts)
     out_ref, inverse_ref, weights = refs[5 * parts :]
     rows = weights.shape[0] // 2
     vectors = rows - DEGREE_ROWS
-    width = packed_refs[0].shape[1]
-    kept = out_ref.shape[1]
+    width = inverse_ref.shape[1]
+    lanes = width // 128
+
+    def sums(peer, part):
+        line = (vectors + part) * lanes
+        return unpack(packed_refs[peer][line : line + lanes, :], 1, width)
+
     for part in range(parts):
         span = slice(part * width, (part + 1) * width)
-        density = packed_refs[0][vectors + part : vectors + part + 1, :]
+        density = sums(0, part)
         for peer in range(1, parts):
-            line = vectors + (part ^ peer)
-            density = density + packed_refs[peer][line : line + 1, :]
+            density = density + sums(peer, part ^ peer)
         inverse = 1.0 / density
         if part == 0:
             inverse_ref[...] = inverse
         line = lax.broadcasted_iota(jnp.int32, (DEGREE_ROWS, width), 0)
         for first, piece in (
-            (0, packed_refs[part][0:vectors, :] * inverse),
+            (0, unpack(packed_refs[part][0 : vectors * lanes, :], vectors, width) * inverse),
             (vectors, jnp.where(line == 0, inverse, 0.0)),
         ):
             high, low = halves(piece)
@@ -187,70 +227,78 @@
             weights[rows + first : rows + last, span] = low
     for block in range(out_ref.shape[0]):
         half, place = place_of(block, True)
-        out_ref[block] = sweep(weights, range(parts), stores[half], place)[0:kept]
-
-
-def far_kernel(*refs, parts):
+        put_product(out_ref.at[block], sweep(weights, range(parts), stores[half], place), vectors)
+
+
+def far_kernel(*refs, parts, vectors):
     weights, stores, out_ref = refs[0], halved(refs[1 : 1 + 4 * parts], parts), refs[-1]
     for index in range(out_ref.shape[0]):
         half, place = place_of(1 + index, False)
-        out_ref[index] = sweep(weights, range(parts), stores[half], place)[0 : out_ref.shape[1]]
-
-
-def own_kernel(*refs, parts):
+        put_product(out_ref.at[index], sweep(weights, range(parts), stores[half], place), vectors)
+
+
+def own_kernel(*refs, parts, vectors):
     weights, stores, out_ref = refs[0], pairs(refs[2 : 2 + 2 * parts]), refs[-1]
-    out_ref[...] = sweep(weights, range(parts), stores, 0)[0 : out_ref.shape[0]]
-
-
-def second_start_kernel(piece_ref, high_ref, low_ref, far_high_ref, far_low_ref, odd_ref, even_ref, weights):
-    vectors, width = piece_ref.shape[0], high_ref.shape[0]
-    high, low = halves(piece_ref[:, 0:width])
-    weights[0:vectors, :] = high
-    weights[vectors:, :] = low
-    stores = (high_ref, low_ref), (far_high_ref, far_low_ref)
-    for odd, out_ref in ((True, odd_ref), (False, even_ref)):
+    put_product(out_ref, sweep(weights, range(parts), stores, 0), vectors)
+
+
+def put_weights(weights, packed, place):
+    vectors = weights.shape[0] // 2
+    width = weights.shape[1] if place is None else packed.shape[0] // vectors * 128
+    values = unpack(packed[0 : vectors * (width // 128), :], vectors, width)
+    span = slice(0, width) if place is None else slice(place * width, (place + 1) * width)
+    high, low = halves(values)
+    weights[0:vectors, span] = high
+    weights[vectors:, span] = low
+
+
+def second_part_kernel(piece_ref, *refs):
+    stores, (odd_ref, even_ref, weights) = pairs(refs[0:4]), refs[-3:]
+    earlier = refs[4:-3] or (None, None)
+    put_weights(weights, piece_ref[...], None)
+    for odd, earlier_ref, out_ref in ((True, earlier[0], odd_ref), (False, earlier[1], even_ref)):
         for block in range(out_ref.shape[0]):
             half, place = place_of(block, odd)
-            out_ref[block] = sweep(weights, (0,), [stores[half]], place)
+            initial = None if earlier_ref is None else earlier_ref[block]
+            out_ref[block] = sweep(weights, (0,), [stores[half]], place, initial)
+
+
+def put_second(out_ref, product, gram):
+    last = out_ref.shape[0] - gram.shape[0]
+    out_ref[0:last, :] = pack(product)
+    out_ref[last:, :] = gram
 
 
 def second_odd_kernel(*refs, parts):
-    piece_refs, partial_ref = refs[: 1 + parts], refs[1 + parts]
-    stores = halved(refs[2 + parts : 2 + 5 * parts], parts)
-    out_ref, gram_ref, weights = refs[2 + 5 * parts :]
-    vectors, width = piece_refs[0].shape[0], stores[0][0][0].shape[0]
-    gram = piece_refs[0][:, width:]
-    for part, ref in enumerate(piece_refs[1:]):
-        gram = gram + ref[:, width:]
-        span = slice(part * width, (part + 1) * width)
-        high, low = halves(ref[:, 0:width])
-        weights[0:vectors, span] = high
-        weights[vectors:, span] = low
+    piece_refs, refs = refs[:4], refs[4:]
+    partial_ref, stores = refs[0], halved(refs[1 : 1 + 4 * parts], parts)
+    out_ref, gram_ref, weights = refs[1 + 4 * parts :]
+    last = piece_refs[0].shape[0] - gram_ref.shape[0]
+    gram = piece_refs[0][last:, :]
+    for ref in piece_refs[1:]:
+        gram = gram + ref[last:, :]
     gram_ref[...] = gram
+    for part, ref in enumerate(piece_refs[-parts:]):
+        put_weights(weights, ref[...], part)
     for block in range(out_ref.shape[0]):
         half, place = place_of(block, True)
-        out_ref[block, :, 0:width] = sweep(weights, range(parts), stores[half], place, partial_ref[block])
-        out_ref[block, :, width:] = gram
+        product = sweep(weights, range(parts), stores[half], place, partial_ref[block])
+        put_second(out_ref.at[block], product, gram)
 
 
 def second_even_kernel(*refs, parts):
     weights, gram_ref, partial_ref = refs[:3]
     stores, out_ref = halved(refs[3 : 3 + 4 * parts], parts), refs[-1]
-    width = stores[0][0][0].shape[0]
     for index in range(out_ref.shape[0]):
         half, place = place_of(1 + index, False)
-        out_ref[index, :, 0:width] = sweep(
-            weights, range(parts), stores[half], place, partial_ref[1 + index]
-        )
-        out_ref[index, :, width:] = gram_ref[...]
+        product = sweep(weights, range(parts), stores[half], place, partial_ref[1 + index])
+        put_second(out_ref.at[index], product, gram_ref[...])
 
 
 def second_own_kernel(*refs, parts):
     weights, gram_ref, partial_ref = refs[:3]
     stores, out_ref = pairs(refs[4 : 4 + 2 * parts]), refs[-1]
-    width = stores[0][0].shape[0]
-    out_ref[:, 0:width] = sweep(weights, range(parts), stores, 0, partial_ref[0])
-    out_ref[:, width:] = gram_ref[...]
+    put_second(out_ref, sweep(weights, range(parts), stores, 0, partial_ref[0]), gram_ref[...])
 
 
 def exact(left, right, dims):
@@ -259,19 +307,25 @@
     )
 
 
+def add_up(refs):
+    total = refs[0][...]
+    for ref in refs[1:]:
+        total = total + ref[...]
+    return total
+
+
 def grown_kernel(*refs):
     inverse_ref, piece_refs, (grown_ref, degree_ref) = refs[0], refs[1:-2], refs[-2:]
-    vectors = grown_ref.shape[0]
     width = degree_ref.shape[1]
-    total = piece_refs[0][...]
-    for ref in piece_refs[1:]:
-        total = total + ref[...]
-    degree = total[vectors : vectors + 1, :]
-    grown = total[0:vectors, :] / degree
+    lanes = width // 128
+    vectors = (grown_ref.shape[0] - 8) // lanes
+    total = add_up(piece_refs)
+    last = vectors * lanes
+    degree = unpack(total[last : last + lanes], 1, width)
+    grown = unpack(total[0:last], vectors, width) / degree
     degree_ref[...] = degree
-    grown_ref[:, 0:width] = grown * inverse_ref[...]
-    gram = exact(grown, grown, ROWS_BY_ROWS)
-    grown_ref[:, width:] = jnp.concatenate([gram, jnp.zeros((vectors, 128 - vectors), jnp.float32)], axis=1)
+    grown_ref[0:last, :] = pack(grown * inverse_ref[...])
+    grown_ref[last:, :] = pack_square(exact(grown, grown, ROWS_BY_ROWS))
 
 
 def inverse_factor(gram, panel=16):
@@ -297,26 +351,48 @@
 def grown_two_kernel(*refs, count):
     degree_ref, piece_refs, (grown_ref, gram_ref) = refs[0], refs[1:-2], refs[-2:]
     vectors, width = grown_ref.shape
-    total = piece_refs[0][...]
-    for ref in piece_refs[1:]:
-        total = total + ref[...]
-    factor = inverse_factor(total[:, width : width + vectors] * (1.0 / count))
-    grown = exact(factor, total[:, 0:width] / degree_ref[...], ROWS_BY_COLUMNS)
+    total = add_up(piece_refs)
+    last = vectors * (width // 128)
+    factor = inverse_factor(unpack_square(total[last:], vectors) * (1.0 / count))
+    product = unpack(total[0:last], vectors, width)
+    grown = exact(factor, product / degree_ref[...], ROWS_BY_COLUMNS)
     grown_ref[...] = grown
-    gram_ref[...] = exact(grown, grown, ROWS_BY_ROWS)
+    gram_ref[...] = pack_square(exact(grown, grown, ROWS_BY_ROWS))
 
 
 def finish_kernel(*refs, count):
     grown_ref, gram_refs, out_ref = refs[0], refs[1:-1], refs[-1]
-    gram = gram_refs[0][...]
-    for ref in gram_refs[1:]:
-        gram = gram + ref[...]
+    gram = unpack_square(add_up(gram_refs), grown_ref.shape[0])
     out_ref[...] = exact(inverse_factor(gram * (1.0 / count)), grown_ref[...], ROWS_BY_COLUMNS)
 
 
 def swap(values, mask):
     size = lax.axis_size(("row", "col"))
     return lax.ppermute(values, ("row", "col"), [(index, index ^ mask) for index in range(size)])
+
+
+def fetch_kernel(frames_ref, start_ref, own_ref, own_start_ref, sems):
+    copies = [
+        pltpu.make_async_copy(source, target, sems.at[index])
+        for index, (source, target) in enumerate(((frames_ref, own_ref), (start_ref, own_start_ref)))
+    ]
+    for copy in copies:
+        copy.start()
+    for copy in copies:
+        copy.wait()
+
+
+def fetch(frames, start):
+    return pl.pallas_call(
+        fetch_kernel,
+        out_shape=(f32(*frames.shape), f32(*start.shape)),
+        in_specs=[pl.BlockSpec(memory_space=pltpu.HBM)] * 2,
+        out_specs=(VMEM, VMEM),
+        scratch_shapes=[pltpu.SemaphoreType.DMA((2,))],
+        compiler_params=pltpu.CompilerParams(vmem_limit_bytes=1 << 20),
+        cost_estimate=pl.CostEstimate(flops=1 << 34, bytes_accessed=0, transcendentals=0),
+        name="fetch",
+    )(pltpu.with_memory_space_constraint(frames, pltpu.HBM), pltpu.with_memory_space_constraint(start, pltpu.HBM))
 
 
 def resident_shards(frames, start):
@@ -325,39 +401,52 @@
     features, width = frames.shape
     vectors = start.shape[0]
 
-    core, across, along, skip = column_size, column_size * row_size // 2, 1, column_size // 2
-    beside = 2 * core
-    near = (along, across, along | across)
-    far = (beside, skip, skip | beside)
+    core, across, skip = column_size, column_size * row_size // 2, column_size // 2
+    beside, along = 2 * core, 1
+    near = (across, skip, across | skip)
+    far = (beside, along, beside | along)
     parts, half = 4, 4
 
     skip_piece = swap(frames, skip)
-    beside_piece = swap(frames, beside)
-    row_pieces = [frames] + [swap(frames, mask) for mask in near]
-    both_piece = swap(skip_piece, beside)
-    near_columns = [beside_piece, swap(frames, core), swap(beside_piece, core)]
-    far_columns = [skip_piece, both_piece, swap(skip_piece, core), swap(both_piece, core)]
+    own, own_start = fetch(frames, start)
+    beside_piece = swap(own, beside)
+    along_piece = swap(own, along)
+    across_piece = swap(own, across)
+    corner_piece = swap(along_piece, beside)
+    row_pieces = [across_piece, skip_piece]
+    last_piece = swap(skip_piece, across)
+    near_columns = [beside_piece, swap(own, core), swap(beside_piece, core)]
+    far_columns = [along_piece, corner_piece, swap(along_piece, core), swap(corner_piece, core)]
 
     operands = 4 * features
     columns = half * width
-    stored = (bf16(width, columns),) * (2 * parts)
+    lanes = width // 128
+    packed_lines = vectors * lanes + 8
+    rest = parts - 1
+    stored = (bf16(width, columns),) * 2
     totals = pltpu.VMEM((width, 128), jnp.float32)
-    *near_store, sums, left = call(
-        functools.partial(build_near_kernel, row_parts=parts, column_parts=half),
-        (*stored, f32(8, width), bf16(parts * width, operands)),
-        (*row_pieces, *near_columns),
-        scratch=(pltpu.VMEM((operands, columns), jnp.bfloat16), totals),
+    *near_store, sums, left, right = call(
+        functools.partial(build_near_kernel, row_parts=rest, column_parts=half),
+        (*(stored * rest), f32(8, width), bf16(rest * width, operands), bf16(operands, columns)),
+        (own, *row_pieces, *near_columns),
+        scratch=(totals,),
         flops=1,
         name="build_near",
     )
-    *far_store, packed = call(
-        functools.partial(build_far_kernel, row_parts=parts, column_parts=half),
-        (*stored, f32(vectors + 8, width)),
-        (left, sums, start, *far_columns),
-        scratch=(pltpu.VMEM((operands, columns), jnp.bfloat16), totals),
+    *far_store, last_high, last_low, far_high, far_low, packed = call(
+        functools.partial(build_far_kernel, row_parts=rest, column_parts=half),
+        (*(stored * (rest + 2)), f32((vectors + parts) * lanes, 128)),
+        (left, right, sums, own_start, last_piece, *far_columns),
+        scratch=(
+            pltpu.VMEM((operands, columns), jnp.bfloat16),
+            pltpu.VMEM((width, operands), jnp.bfloat16),
+            totals,
+        ),
         flops=1,
         name="build_far",
     )
+    near_store = (*near_store, last_high, last_low)
+    far_store = (*far_store, far_high, far_low)
     all_packed = [packed] + [swap(packed, mask) for mask in near]
 
     def spread(odds, evens):
@@ -367,74 +456,78 @@
 
     def total_gram(gram):
         gram = gram + swap(gram, core)
-        gram = functools.reduce(jnp.add, [swap(gram, mask) for mask in near], gram)
-        return [gram] + [swap(gram, mask) for mask in far]
+        gram = functools.reduce(jnp.add, [swap(gram, mask) for mask in far], gram)
+        return [gram] + [swap(gram, mask) for mask in near]
 
     rows = vectors + DEGREE_ROWS
     block = 2 * 3 * rows * parts * width * width
     odds, inverse, weights = call(
         functools.partial(first_kernel, parts=parts),
-        (f32(half, vectors + 8, width), f32(1, width), bf16(2 * rows, parts * width)),
+        (f32(half, packed_lines, 128), f32(1, width), bf16(2 * rows, parts * width)),
         (*all_packed, *near_store, *far_store),
         flops=half * block,
         name="first_odd",
     )
     evens = call(
-        functools.partial(far_kernel, parts=parts),
-        f32(half - 1, vectors + 8, width),
+        functools.partial(far_kernel, parts=parts, vectors=vectors),
+        f32(half - 1, packed_lines, 128),
         (weights, *near_store, *far_store),
         flops=(half - 1) * block,
         name="first_even",
     )
     own_odd, both, others = spread(odds, evens)
     own_even = call(
-        functools.partial(own_kernel, parts=parts),
-        f32(vectors + 8, width),
+        functools.partial(own_kernel, parts=parts, vectors=vectors),
+        f32(packed_lines, 128),
         (weights, both, *near_store),
         flops=block,
         name="first_own",
     )
     weighted, degree = call(
         grown_kernel,
-        (f32(vectors, width + 128), f32(1, width)),
+        (f32(packed_lines, 128), f32(1, width)),
         (inverse, own_even, own_odd, *others),
         name="grown",
     )
     pieces = [weighted] + [swap(weighted, mask) for mask in near]
-    odd_partial, even_partial = call(
-        second_start_kernel,
-        (f32(half, vectors, width),) * 2,
-        (weighted, *near_store[0:2], *far_store[0:2]),
-        scratch=(pltpu.VMEM((2 * vectors, width), jnp.bfloat16),),
-        flops=2 * half * block // parts,
-        name="second_start",
-    )
-    rest = parts - 1
+    partial = ()
+    for part in range(2):
+        partial = call(
+            second_part_kernel,
+            (f32(half, vectors, width),) * 2,
+            (pieces[part], *near_store[2 * part : 2 * part + 2], *far_store[2 * part : 2 * part + 2], *partial),
+            scratch=(pltpu.VMEM((2 * vectors, width), jnp.bfloat16),),
+            flops=2 * half * block // parts,
+            name="second_part",
+        )
+    odd_partial, even_partial = partial
+    rest = parts - 2
+    near_store, far_store = near_store[4:], far_store[4:]
     odds, gram, weights = call(
         functools.partial(second_odd_kernel, parts=rest),
-        (f32(half, vectors, width + 128), f32(vectors, 128), bf16(2 * vectors, rest * width)),
-        (*pieces, odd_partial, *near_store[2:], *far_store[2:]),
+        (f32(half, packed_lines, 128), f32(8, 128), bf16(2 * vectors, rest * width)),
+        (*pieces, odd_partial, *near_store, *far_store),
         flops=half * block,
         name="second_odd",
     )
     evens = call(
         functools.partial(second_even_kernel, parts=rest),
-        f32(half - 1, vectors, width + 128),
-        (weights, gram, even_partial, *near_store[2:], *far_store[2:]),
+        f32(half - 1, packed_lines, 128),
+        (weights, gram, even_partial, *near_store, *far_store),
         flops=(half - 1) * block,
         name="second_even",
     )
     own_odd, both, others = spread(odds, evens)
     own_even = call(
         functools.partial(second_own_kernel, parts=rest),
-        f32(vectors, width + 128),
-        (weights, gram, even_partial, both, *near_store[2:]),
+        f32(packed_lines, 128),
+        (weights, gram, even_partial, both, *near_store),
         flops=block,
         name="second_own",
     )
     grown_two, gram_two = call(
         functools.partial(grown_two_kernel, count=count),
-        (f32(vectors, width), f32(vectors, vectors)),
+        (f32(vectors, width), f32(8, 128)),
         (degree, own_even, own_odd, *others),
         name="grown_two",
     )
@@ -495,7 +588,8 @@
 def shards(frames, start):
     row_size, column_size = lax.axis_size("row"), lax.axis_size("col")
     entries = row_size * column_size * frames.shape[1] ** 2
-    if (row_size, column_size) == (8, 4) and 4 * entries <= RESIDENT_BYTES:
+    shapes = (row_size, column_size, start.shape[0], frames.shape[1] % 128)
+    if shapes == (8, 4, 32, 0) and 4 * entries <= RESIDENT_BYTES:
         return resident_shards(frames, start)
     return stored_shards(frames, start)
 

time: 92.9 us -> 86.3 us (0.929)
  waiting for transfers between devices: 29.2 us -> 23.2 us
  Pallas kernels: 24.4 us -> 26.2 us
  local copies, waits for them, and re-layouts: 1.79 us -> 0.05 us
    ppermute x31, waiting for transfers between devices: 29.2 us -> 23.2 us  [swap(): lax.ppermute(values, ('row', 'col'), [(index, index ^ mask) for index in...]
    unnamed x4 -> x2, local copies, waits for them, and re-layouts: 1.74 us -> 0.01 us
    pallas_call x0 -> x1, Pallas kernels: none -> 0.99 us  [fetch(): pl.pallas_call(fetch_kernel, out_shape=(f32(*frames.shape), f32(*start.sh...]
    pallas_call x12 -> x13, Pallas kernels: 24.4 us -> 25.2 us  [call(): pl.pallas_call(body, out_shape=out_shape, in_specs=[VMEM] * len(operands)...]
  transfers between devices with their start and end apart: 31 -> 31, of which waited for: 17 -> 18; matrix products, arithmetic and copies ran while one was open for 0% -> 0% of each run, Pallas kernels for 13% -> 14%
where the time goes in v4:
time: 86.3 us; the launch traced here: 86.1 us
  starting transfers between devices  36.5 us (42%)
  Pallas kernels  26.2 us (30%)
  waiting for transfers between devices  23.2 us (27%)
    ppermute x31, starting transfers between devices, swap(): lax.ppermute(values, ('row', 'col'), [(index, index ^ mask) for index in...  36.5 us
    pallas_call x13, Pallas kernels, call(): pl.pallas_call(body, out_shape=out_shape, in_specs=[VMEM] * len(operands)...  25.2 us
    ppermute x31, waiting for transfers between devices, swap(): lax.ppermute(values, ('row', 'col'), [(index, index ^ mask) for index in...  23.2 us
  transfers between devices with their start and end apart: 31, of which 18 were waited for; matrix products, arithmetic and copies ran while one was open for 0% of the time, Pallas kernels for 14%

profile of v4, /device:TPU:0, one launch (start us, length us, event | category | flops | bytes accessed | tf_op | source)
XLA Modules:
  0.0 86.1 jit_solution(7902671865479642033)
XLA Ops:
  0.0 1.0 %fetch.1 = (f32[64,512]{1,0:T(8,128)S(1)}, f32[32,512]{1,0:T(8,128)S(1)}) custom-call(f32[64,512]{1,0:T(8,128)} %frames_ref.1, f32[32,512]{1,0:T(8,128)} %start_ref.1), custom_call_target="tpu_custom_call" | custom-call | flops 17179869184 | tf_op jit(solution)/shard_map/fetch/pallas_call | solution.py:386
  1.0 3.1 %collective-permute-start.6 = (f32[64,512]{1,0:T(8,128)S(1)}, f32[64,512]{1,0:T(8,128)S(1)}, u32[]{:S(2)}, u32[]{:S(2)}) collective-permute-start(f32[64,512]{1,0:T(8,128)S(1)} %get-tuple-element.41.refs_0_), channel_id=1, source_target_pairs={{0,1},{1,0},{2,3},{3,2},{4,5},{5,4},{6,7},{7,6},{8,9},{9,8},{10,11... | collective-permute-start | bytes 393224 | tf_op jit(solution)/shard_map/ppermute | solution.py:371
  4.1 2.6 %collective-permute-start.1 = (f32[64,512]{1,0:T(8,128)S(1)}, f32[64,512]{1,0:T(8,128)S(1)}, u32[]{:S(2)}, u32[]{:S(2)}) collective-permute-start(f32[64,512]{1,0:T(8,128)S(1)} %copy-done), channel_id=1, source_target_pairs={{0,2},{1,3},{2,0},{3,1},{4,6},{5,7},{6,4},{7,5},{8,10},{9,11},{10,... | collective-permute-start | bytes 393224 | tf_op jit(solution)/shard_map/ppermute | solution.py:371
  6.7 1.5 %collective-permute-start.2 = (f32[64,512]{1,0:T(8,128)S(1)}, f32[64,512]{1,0:T(8,128)S(1)}, u32[]{:S(2)}, u32[]{:S(2)}) collective-permute-start(f32[64,512]{1,0:T(8,128)S(1)} %get-tuple-element.41.refs_0_), channel_id=1, source_target_pairs={{0,8},{1,9},{2,10},{3,11},{4,12},{5,13},{6,14},{7,15},{8,0},{9,1},... | collective-permute-start | bytes 393224 | tf_op jit(solution)/shard_map/ppermute | solution.py:371
  8.2 1.3 %collective-permute-done.6.refs_5_ = f32[64,512]{1,0:T(8,128)S(1)} collective-permute-done((f32[64,512]{1,0:T(8,128)S(1)}, f32[64,512]{1,0:T(8,128)S(1)}, u32[]{:S(2)}, u32[]{:S(2)}) %collective-permute-start.6) | collective-permute-done | bytes 131104 | tf_op jit(solution)/shard_map/ppermute | solution.py:371
  9.4 1.8 %collective-permute-start.7 = (f32[64,512]{1,0:T(8,128)S(1)}, f32[64,512]{1,0:T(8,128)S(1)}, u32[]{:S(2)}, u32[]{:S(2)}) collective-permute-start(f32[64,512]{1,0:T(8,128)S(1)} %collective-permute-done.6.refs_5_), channel_id=1, source_target_pairs={{0,8},{1,9},{2,10},{3,11},{4,12},{5,13},{6,14},{7,15},{8,0},{9,1},... | collective-permute-start | bytes 393224 | tf_op jit(solution)/shard_map/ppermute | solution.py:371
  11.3 1.5 %collective-permute-start = (f32[64,512]{1,0:T(8,128)S(1)}, f32[64,512]{1,0:T(8,128)S(1)}, u32[]{:S(2)}, u32[]{:S(2)}) collective-permute-start(f32[64,512]{1,0:T(8,128)S(1)} %get-tuple-element.41.refs_0_), channel_id=1, source_target_pairs={{0,16},{1,17},{2,18},{3,19},{4,20},{5,21},{6,22},{7,23},{8,24},{9,... | collective-permute-start | bytes 393224 | tf_op jit(solution)/shard_map/ppermute | solution.py:371
  13.3 1.5 %collective-permute-start.5 = (f32[64,512]{1,0:T(8,128)S(1)}, f32[64,512]{1,0:T(8,128)S(1)}, u32[]{:S(2)}, u32[]{:S(2)}) collective-permute-start(f32[64,512]{1,0:T(8,128)S(1)} %collective-permute-done.1.refs_2_), channel_id=1, source_target_pairs={{0,16},{1,17},{2,18},{3,19},{4,20},{5,21},{6,22},{7,23},{8,24},{9,... | collective-permute-start | bytes 393224 | tf_op jit(solution)/shard_map/ppermute | solution.py:371
  14.9 1.6 %collective-permute-done.refs_1_ = f32[64,512]{1,0:T(8,128)S(1)} collective-permute-done((f32[64,512]{1,0:T(8,128)S(1)}, f32[64,512]{1,0:T(8,128)S(1)}, u32[]{:S(2)}, u32[]{:S(2)}) %collective-permute-start) | collective-permute-done | bytes 131104 | tf_op jit(solution)/shard_map/ppermute | solution.py:371
  16.4 4.3 %build_near.1 = (bf16[512,2048]{1,0:T(8,128)(2,1)S(1)}, bf16[512,2048]{1,0:T(8,128)(2,1)S(1)}, bf16[512,2048]{1,0:T(8,128)(2,1)S(1)}, bf16[512,2048]{1,0:T(8,128...) custom-call(f32[64,512]{1,0:T(8,128)S(1)} %get-tuple-element.41.refs, ...), custom_call_target="tpu_custom_call" | custom-call | flops 1 | tf_op jit(solution)/shard_map/build_near/pallas_call | solution.py:18
  20.8 5.3 %build_far.1 = (bf16[512,2048]{1,0:T(8,128)(2,1)S(1)}, bf16[512,2048]{1,0:T(8,128)(2,1)S(1)}, bf16[512,2048]{1,0:T(8,128)(2,1)S(1)}, bf16[512,2048]{1,0:T(8,128)...) custom-call(bf16[1536,256]{1,0:T(8,128)(2,1)S(1)} %get-tuple-element, ...), custom_call_target="tpu_custom_call" | custom-call | flops 1 | tf_op jit(solution)/shard_map/build_far/pallas_call | solution.py:18
  26.1 3.8 %collective-permute-start.12 = (f32[144,128]{1,0:T(8,128)S(1)}, f32[144,128]{1,0:T(8,128)S(1)}, u32[]{:S(2)}, u32[]{:S(2)}) collective-permute-start(f32[144,128]{1,0:T(8,128)S(1)} %get-tuple-element.46.refs_0_), channel_id=1, source_target_pairs={{0,18},{1,19},{2,16},{3,17},{4,22},{5,23},{6,20},{7,21},{8,26},{9,... | collective-permute-start | bytes 221192 | tf_op jit(solution)/shard_map/ppermute | solution.py:371
  30.0 0.5 collective-permute-start.10
  30.5 3.8 %collective-permute-done.12.refs_3_ = f32[144,128]{1,0:T(8,128)S(1)} collective-permute-done((f32[144,128]{1,0:T(8,128)S(1)}, f32[144,128]{1,0:T(8,128)S(1)}, u32[]{:S(2)}, u32[]{:S(2)}) %collective-permute-start.12) | collective-permute-done | bytes 73760 | tf_op jit(solution)/shard_map/ppermute | solution.py:371
  34.3 0.8 collective-permute-done.11.refs_2_
  35.1 3.1 %first_odd.1 = (f32[4,136,128]{2,1,0:T(8,128)S(1)}, f32[1,512]{1,0:T(1,128)S(1)}, bf16[96,2048]{1,0:T(8,128)(2,1)S(1)}) custom-call(f32[144,128]{1,0:T(8,128)S(1)} %get-tuple-element.46.refs_0_, f32[144,128]{1,0:T(8,128)S(1)} %collective-permute-done.10.refs_1_, f32[144,128]{1,0:T(8,128)S(1)} %collective-permute-done.11.refs_2_, ...), custom_call_target="tpu_custom_call" | custom-call | flops 1207959552 | tf_op jit(solution)/shard_map/first_odd/pallas_call | solution.py:18
  38.4 2.2 %first_even.1 = f32[3,136,128]{2,1,0:T(8,128)S(1)} custom-call(bf16[96,2048]{1,0:T(8,128)(2,1)S(1)} %get-tuple-element.64.refs_0_, bf16[512,2048]{1,0:T(8,128)(2,1)S(1)} %get-tuple-element.47.refs_4_.refs_1_.refs_2_.refs_0_, bf16[512,2048]{1,0:T(8,128)(2,1)S(1)} %get-tuple-element.48.refs_5_.refs_2_.refs_3_.refs_1_, ...), custom_call_target="tpu_custom_call" | custom-call | flops 905969664 | tf_op jit(solution)/shard_map/first_even/pallas_call | solution.py:18
  40.7 1.4 %collective-permute-start.16 = (f32[136,128]{1,0:T(8,128)S(1)}, f32[136,128]{1,0:T(8,128)S(1)}, u32[]{:S(2)}, u32[]{:S(2)}) collective-permute-start(f32[136,128]{1,0:T(8,128)S(1)} %get-tuple-element.80), channel_id=1, source_target_pairs={{0,9},{1,8},{2,11},{3,10},{4,13},{5,12},{6,15},{7,14},{8,1},{9,0},... | collective-permute-start | bytes 208904 | tf_op jit(solution)/shard_map/ppermute | solution.py:371
  42.1 1.8 %collective-permute-start.15 = (f32[136,128]{1,0:T(8,128)S(1)}, f32[136,128]{1,0:T(8,128)S(1)}, u32[]{:S(2)}, u32[]{:S(2)}) collective-permute-start(f32[136,128]{1,0:T(8,128)S(1)} %get-tuple-element.81), channel_id=1, source_target_pairs={{0,1},{1,0},{2,3},{3,2},{4,5},{5,4},{6,7},{7,6},{8,9},{9,8},{10,11... | collective-permute-start | bytes 208904 | tf_op jit(solution)/shard_map/ppermute | solution.py:371
  44.2 0.8 first_own.1.refs_1_
  45.1 1.2 %collective-permute-done.16.refs_5_ = f32[136,128]{1,0:T(8,128)S(1)} collective-permute-done((f32[136,128]{1,0:T(8,128)S(1)}, f32[136,128]{1,0:T(8,128)S(1)}, u32[]{:S(2)}, u32[]{:S(2)}) %collective-permute-start.16) | collective-permute-done | bytes 69664 | tf_op jit(solution)/shard_map/ppermute | solution.py:371
  46.3 1.6 %collective-permute-done.15.refs_4_ = f32[136,128]{1,0:T(8,128)S(1)} collective-permute-done((f32[136,128]{1,0:T(8,128)S(1)}, f32[136,128]{1,0:T(8,128)S(1)}, u32[]{:S(2)}, u32[]{:S(2)}) %collective-permute-start.15) | collective-permute-done | bytes 69664 | tf_op jit(solution)/shard_map/ppermute | solution.py:371
  48.5 1.0 %collective-permute-start.17 = (f32[136,128]{1,0:T(8,128)S(1)}, f32[136,128]{1,0:T(8,128)S(1)}, u32[]{:S(2)}, u32[]{:S(2)}) collective-permute-start(f32[136,128]{1,0:T(8,128)S(1)} %get-tuple-element.67.piece_ref.refs_0_), channel_id=1, source_target_pairs={{0,16},{1,17},{2,18},{3,19},{4,20},{5,21},{6,22},{7,23},{8,24},{9,... | collective-permute-start | bytes 208904 | tf_op jit(solution)/shard_map/ppermute | solution.py:371
  49.5 2.1 %collective-permute-start.19 = (f32[136,128]{1,0:T(8,128)S(1)}, f32[136,128]{1,0:T(8,128)S(1)}, u32[]{:S(2)}, u32[]{:S(2)}) collective-permute-start(f32[136,128]{1,0:T(8,128)S(1)} %get-tuple-element.67.piece_ref.refs_0_), channel_id=1, source_target_pairs={{0,18},{1,19},{2,16},{3,17},{4,22},{5,23},{6,20},{7,21},{8,26},{9,... | collective-permute-start | bytes 208904 | tf_op jit(solution)/shard_map/ppermute | solution.py:371
  51.6 1.3 %collective-permute-start.18 = (f32[136,128]{1,0:T(8,128)S(1)}, f32[136,128]{1,0:T(8,128)S(1)}, u32[]{:S(2)}, u32[]{:S(2)}) collective-permute-start(f32[136,128]{1,0:T(8,128)S(1)} %get-tuple-element.67.piece_ref.refs_0_), channel_id=1, source_target_pairs={{0,2},{1,3},{2,0},{3,1},{4,6},{5,7},{6,4},{7,5},{8,10},{9,11},{10,... | collective-permute-start | bytes 208904 | tf_op jit(solution)/shard_map/ppermute | solution.py:371
  52.9 1.5 %second_part.2 = (f32[4,32,512]{2,1,0:T(8,128)S(1)}, f32[4,32,512]{2,1,0:T(8,128)S(1)}) custom-call(f32[136,128]{1,0:T(8,128)S(1)} %get-tuple-element.67.piece_ref.refs_0_, bf16[512,2048]{1,0:T(8,128)(2,1)S(1)} %get-tuple-element.47.refs_4_.refs_1_.refs_2_.refs_0_, bf16[512,2048]{1,0:T(8,128)(2,1)S(1)} %get-tuple-element.48.refs_5_.refs_2_.refs_3_.refs_1_, ...), custom_call_target="tpu_custom_call" | custom-call | flops 603979776 | tf_op jit(solution)/shard_map/second_part/pallas_call | solution.py:18
  54.4 1.6 %second_part.3 = (f32[4,32,512]{2,1,0:T(8,128)S(1)}, f32[4,32,512]{2,1,0:T(8,128)S(1)}) custom-call(f32[136,128]{1,0:T(8,128)S(1)} %collective-permute-done.17.piece_ref.refs_1_, bf16[512,2048]{1,0:T(8,128)(2,1)S(1)} %get-tuple-element.49.refs_6_.refs_3_.refs_4_.refs_0_, bf16[512,2048]{1,0:T(8,128)(2,1)S(1)} %get-tuple-element.50.refs_7_.refs_4_.refs_5_.refs_1_, ...), custom_call_target="tpu_custom_call" | custom-call | flops 603979776 | tf_op jit(solution)/shard_map/second_part/pallas_call | solution.py:18
  56.0 2.3 %collective-permute-done.19.refs_3_ = f32[136,128]{1,0:T(8,128)S(1)} collective-permute-done((f32[136,128]{1,0:T(8,128)S(1)}, f32[136,128]{1,0:T(8,128)S(1)}, u32[]{:S(2)}, u32[]{:S(2)}) %collective-permute-start.19) | collective-permute-done | bytes 69664 | tf_op jit(solution)/shard_map/ppermute | solution.py:371
  58.3 0.8 collective-permute-done.18.refs_2_
  59.1 1.6 %second_odd.1 = (f32[4,136,128]{2,1,0:T(8,128)S(1)}, f32[8,128]{1,0:T(8,128)S(1)}, bf16[64,1024]{1,0:T(8,128)(2,1)S(1)}) custom-call(f32[136,128]{1,0:T(8,128)S(1)} %get-tuple-element.67.piece_ref.refs_0_, f32[136,128]{1,0:T(8,128)S(1)} %collective-permute-done.17.piece_ref.refs_1_, f32[136,128]{1,0:T(8,128)S(1)} %collective-permute-done.18.refs_2_, ...), custom_call_target="tpu_custom_call" | custom-call | flops 1207959552 | tf_op jit(solution)/shard_map/second_odd/pallas_call | solution.py:18
  60.7 1.2 %second_even.1 = f32[3,136,128]{2,1,0:T(8,128)S(1)} custom-call(bf16[64,1024]{1,0:T(8,128)(2,1)S(1)} %get-tuple-element.71.refs_0_, f32[8,128]{1,0:T(8,128)S(1)} %get-tuple-element.72.refs_1_, f32[4,32,512]{2,1,0:T(8,128)S(1)} %get-tuple-element.73.refs_2_, bf16[512,2048]{1,0:T(8,128)(2,1)S(1)} %get-tuple-element.51.refs_8_.refs_5_.refs_6_.refs_3_.refs_4_, ...), custom_call_target="tpu_custom_call" | custom-call | flops 905969664 | tf_op jit(solution)/shard_map/second_even/pallas_call | solution.py:18
  62.3 0.5 collective-permute-start.23
  62.8 2.0 %collective-permute-start.22 = (f32[136,128]{1,0:T(8,128)S(1)}, f32[136,128]{1,0:T(8,128)S(1)}, u32[]{:S(2)}, u32[]{:S(2)}) collective-permute-start(f32[136,128]{1,0:T(8,128)S(1)} %get-tuple-element.78), channel_id=1, source_target_pairs={{0,1},{1,0},{2,3},{3,2},{4,5},{5,4},{6,7},{7,6},{8,9},{9,8},{10,11... | collective-permute-start | bytes 208904 | tf_op jit(solution)/shard_map/ppermute | solution.py:371
  64.8 1.0 %collective-permute-start.21 = (f32[136,128]{1,0:T(8,128)S(1)}, f32[136,128]{1,0:T(8,128)S(1)}, u32[]{:S(2)}, u32[]{:S(2)}) collective-permute-start(f32[136,128]{1,0:T(8,128)S(1)} %get-tuple-element.79), channel_id=1, source_target_pairs={{0,8},{1,9},{2,10},{3,11},{4,12},{5,13},{6,14},{7,15},{8,0},{9,1},... | collective-permute-start | bytes 208904 | tf_op jit(solution)/shard_map/ppermute | solution.py:371
  66.3 2.0 %collective-permute-done.23.refs_5_ = f32[136,128]{1,0:T(8,128)S(1)} collective-permute-done((f32[136,128]{1,0:T(8,128)S(1)}, f32[136,128]{1,0:T(8,128)S(1)}, u32[]{:S(2)}, u32[]{:S(2)}) %collective-permute-start.23) | collective-permute-done | bytes 69664 | tf_op jit(solution)/shard_map/ppermute | solution.py:371
  68.5 0.6 collective-permute-done.21.refs_3_
  69.1 1.2 %grown_two.1 = (f32[32,512]{1,0:T(8,128)S(1)}, f32[8,128]{1,0:T(8,128)S(1)}) custom-call(f32[1,512]{1,0:T(1,128)S(1)} %get-tuple-element.66.refs_0_, f32[136,128]{1,0:T(8,128)S(1)} %second_own.1.refs_1_, f32[136,128]{1,0:T(8,128)S(1)} %slice_bitcast_fusion.3.refs_2_, f32[136,128]{1,0:T(8,128)S(1)} %collective-permute-done.21.refs_3_, ...), custom_call_target="tpu_custom_call" | custom-call | tf_op jit(solution)/shard_map/grown_two/pallas_call | solution.py:18
  70.4 1.2 %collective-permute-done.24 = f32[8,128]{1,0:T(8,128)S(1)} collective-permute-done((f32[8,128]{1,0:T(8,128)S(1)}, f32[8,128]{1,0:T(8,128)S(1)}, u32[]{:S(2)}, u32[]{:S(2)}) %collective-permute-start.24) | collective-permute-done | bytes 4128 | tf_op jit(solution)/shard_map/ppermute | solution.py:371
  72.0 2.0 %collective-permute-start.26 = (f32[8,128]{1,0:T(8,128)S(1)}, f32[8,128]{1,0:T(8,128)S(1)}, u32[]{:S(2)}, u32[]{:S(2)}) collective-permute-start(f32[8,128]{1,0:T(8,128)S(1)} %add.20), channel_id=1, source_target_pairs={{0,1},{1,0},{2,3},{3,2},{4,5},{5,4},{6,7},{7,6},{8,9},{9,8},{10,11... | collective-permute-start | bytes 12296 | tf_op jit(solution)/shard_map/ppermute | solution.py:371
  74.0 1.0 %collective-permute-start.25 = (f32[8,128]{1,0:T(8,128)S(1)}, f32[8,128]{1,0:T(8,128)S(1)}, u32[]{:S(2)}, u32[]{:S(2)}) collective-permute-start(f32[8,128]{1,0:T(8,128)S(1)} %add.20), channel_id=1, source_target_pairs={{0,8},{1,9},{2,10},{3,11},{4,12},{5,13},{6,14},{7,15},{8,0},{9,1},... | collective-permute-start | bytes 12296 | tf_op jit(solution)/shard_map/ppermute | solution.py:371
  75.0 1.0 %collective-permute-done.27 = f32[8,128]{1,0:T(8,128)S(1)} collective-permute-done((f32[8,128]{1,0:T(8,128)S(1)}, f32[8,128]{1,0:T(8,128)S(1)}, u32[]{:S(2)}, u32[]{:S(2)}) %collective-permute-start.27) | collective-permute-done | bytes 4128 | tf_op jit(solution)/shard_map/ppermute | solution.py:371
  76.0 1.6 %collective-permute-done.25 = f32[8,128]{1,0:T(8,128)S(1)} collective-permute-done((f32[8,128]{1,0:T(8,128)S(1)}, f32[8,128]{1,0:T(8,128)S(1)}, u32[]{:S(2)}, u32[]{:S(2)}) %collective-permute-start.25) | collective-permute-done | bytes 4128 | tf_op jit(solution)/shard_map/ppermute | solution.py:371
  77.6 0.8 collective-permute-start.30
  78.5 2.5 %collective-permute-start.29 = (f32[8,128]{1,0:T(8,128)S(1)}, f32[8,128]{1,0:T(8,128)S(1)}, u32[]{:S(2)}, u32[]{:S(2)}) collective-permute-start(f32[8,128]{1,0:T(8,128)S(1)} %add_add_fusion.refs_1_), channel_id=1, source_target_pairs={{0,2},{1,3},{2,0},{3,1},{4,6},{5,7},{6,4},{7,5},{8,10},{9,11},{10,... | collective-permute-start | bytes 12296 | tf_op jit(solution)/shard_map/ppermute | solution.py:371
  80.9 1.1 %collective-permute-start.28 = (f32[8,128]{1,0:T(8,128)S(1)}, f32[8,128]{1,0:T(8,128)S(1)}, u32[]{:S(2)}, u32[]{:S(2)}) collective-permute-start(f32[8,128]{1,0:T(8,128)S(1)} %add_add_fusion.refs_1_), channel_id=1, source_target_pairs={{0,16},{1,17},{2,18},{3,19},{4,20},{5,21},{6,22},{7,23},{8,24},{9,... | collective-permute-start | bytes 12296 | tf_op jit(solution)/shard_map/ppermute | solution.py:371
  82.0 1.0 %collective-permute-done.30.refs_4_ = f32[8,128]{1,0:T(8,128)S(1)} collective-permute-done((f32[8,128]{1,0:T(8,128)S(1)}, f32[8,128]{1,0:T(8,128)S(1)}, u32[]{:S(2)}, u32[]{:S(2)}) %collective-permute-start.30) | collective-permute-done | bytes 4128 | tf_op jit(solution)/shard_map/ppermute | solution.py:371
  83.0 1.5 %collective-permute-done.28.refs_2_ = f32[8,128]{1,0:T(8,128)S(1)} collective-permute-done((f32[8,128]{1,0:T(8,128)S(1)}, f32[8,128]{1,0:T(8,128)S(1)}, u32[]{:S(2)}, u32[]{:S(2)}) %collective-permute-start.28) | collective-permute-done | bytes 4128 | tf_op jit(solution)/shard_map/ppermute | solution.py:371
  84.5 1.6 %finish.1 = f32[32,512]{1,0:T(8,128)} custom-call(f32[32,512]{1,0:T(8,128)S(1)} %get-tuple-element.75.refs_0_, f32[8,128]{1,0:T(8,128)S(1)} %add_add_fusion.refs_1_, f32[8,128]{1,0:T(8,128)S(1)} %collective-permute-done.28.refs_2_, f32[8,128]{1,0:T(8,128)S(1)} %collective-permute-done.29.refs_3_, f32[8,128]{1,0:T(8,128)S(1)} %collective-permute-done.30.refs_4_), custom_call_target="tpu_custom_call" | custom-call | tf_op jit(solution)/shard_map/finish/pallas_call | solution.py:18
  (38 shorter events, 3.3 us)
Async XLA Ops:
  0.0 4.1 %copy-start = (f32[64,512]{1,0:T(8,128)S(1)}, f32[64,512]{1,0:T(8,128)}, u32[]{:S(2)}) copy-start(f32[64,512]{1,0:T(8,128)} %frames_ref.1) | copy-start | bytes 393220
  1.0 8.4 %collective-permute-start.6 = (f32[64,512]{1,0:T(8,128)S(1)}, f32[64,512]{1,0:T(8,128)S(1)}, u32[]{:S(2)}, u32[]{:S(2)}) collective-permute-start(f32[64,512]{1,0:T(8,128)S(1)} %get-tuple-element.41.refs_0_), channel_id=1, source_target_pairs={{0,1},{1,0},{2,3},{3,2},{4,5},{5,4},{6,7},{7,6},{8,9},{9,8},{10,11... | collective-permute-start | bytes 393224 | tf_op jit(solution)/shard_map/ppermute | solution.py:371
  4.1 8.7 %collective-permute-start.1 = (f32[64,512]{1,0:T(8,128)S(1)}, f32[64,512]{1,0:T(8,128)S(1)}, u32[]{:S(2)}, u32[]{:S(2)}) collective-permute-start(f32[64,512]{1,0:T(8,128)S(1)} %copy-done), channel_id=1, source_target_pairs={{0,2},{1,3},{2,0},{3,1},{4,6},{5,7},{6,4},{7,5},{8,10},{9,11},{10,... | collective-permute-start | bytes 393224 | tf_op jit(solution)/shard_map/ppermute | solution.py:371
  6.7 6.1 %collective-permute-start.2 = (f32[64,512]{1,0:T(8,128)S(1)}, f32[64,512]{1,0:T(8,128)S(1)}, u32[]{:S(2)}, u32[]{:S(2)}) collective-permute-start(f32[64,512]{1,0:T(8,128)S(1)} %get-tuple-element.41.refs_0_), channel_id=1, source_target_pairs={{0,8},{1,9},{2,10},{3,11},{4,12},{5,13},{6,14},{7,15},{8,0},{9,1},... | collective-permute-start | bytes 393224 | tf_op jit(solution)/shard_map/ppermute | solution.py:371
  8.2 5.1 %collective-permute-start.3 = (f32[64,512]{1,0:T(8,128)S(1)}, f32[64,512]{1,0:T(8,128)S(1)}, u32[]{:S(2)}, u32[]{:S(2)}) collective-permute-start(f32[64,512]{1,0:T(8,128)S(1)} %get-tuple-element.41.refs_0_), channel_id=1, source_target_pairs={{0,4},{1,5},{2,6},{3,7},{4,0},{5,1},{6,2},{7,3},{8,12},{9,13},{10,... | collective-permute-start | bytes 393224 | tf_op jit(solution)/shard_map/ppermute | solution.py:371
  9.4 5.4 %collective-permute-start.7 = (f32[64,512]{1,0:T(8,128)S(1)}, f32[64,512]{1,0:T(8,128)S(1)}, u32[]{:S(2)}, u32[]{:S(2)}) collective-permute-start(f32[64,512]{1,0:T(8,128)S(1)} %collective-permute-done.6.refs_5_), channel_id=1, source_target_pairs={{0,8},{1,9},{2,10},{3,11},{4,12},{5,13},{6,14},{7,15},{8,0},{9,1},... | collective-permute-start | bytes 393224 | tf_op jit(solution)/shard_map/ppermute | solution.py:371
  11.3 5.2 %collective-permute-start = (f32[64,512]{1,0:T(8,128)S(1)}, f32[64,512]{1,0:T(8,128)S(1)}, u32[]{:S(2)}, u32[]{:S(2)}) collective-permute-start(f32[64,512]{1,0:T(8,128)S(1)} %get-tuple-element.41.refs_0_), channel_id=1, source_target_pairs={{0,16},{1,17},{2,18},{3,19},{4,20},{5,21},{6,22},{7,23},{8,24},{9,... | collective-permute-start | bytes 393224 | tf_op jit(solution)/shard_map/ppermute | solution.py:371
  12.8 8.0 %collective-permute-start.8 = (f32[64,512]{1,0:T(8,128)S(1)}, f32[64,512]{1,0:T(8,128)S(1)}, u32[]{:S(2)}, u32[]{:S(2)}) collective-permute-start(f32[64,512]{1,0:T(8,128)S(1)} %collective-permute-done.6.refs_5_), channel_id=1, source_target_pairs={{0,4},{1,5},{2,6},{3,7},{4,0},{5,1},{6,2},{7,3},{8,12},{9,13},{10,... | collective-permute-start | bytes 393224 | tf_op jit(solution)/shard_map/ppermute | solution.py:371
  12.8 3.6 %collective-permute-start.4 = (f32[64,512]{1,0:T(8,128)S(1)}, f32[64,512]{1,0:T(8,128)S(1)}, u32[]{:S(2)}, u32[]{:S(2)}) collective-permute-start(f32[64,512]{1,0:T(8,128)S(1)} %collective-permute-done.2.refs_3_), channel_id=1, source_target_pairs={{0,4},{1,5},{2,6},{3,7},{4,0},{5,1},{6,2},{7,3},{8,12},{9,13},{10,... | collective-permute-start | bytes 393224 | tf_op jit(solution)/shard_map/ppermute | solution.py:371
  13.3 7.4 %collective-permute-start.5 = (f32[64,512]{1,0:T(8,128)S(1)}, f32[64,512]{1,0:T(8,128)S(1)}, u32[]{:S(2)}, u32[]{:S(2)}) collective-permute-start(f32[64,512]{1,0:T(8,128)S(1)} %collective-permute-done.1.refs_2_), channel_id=1, source_target_pairs={{0,16},{1,17},{2,18},{3,19},{4,20},{5,21},{6,22},{7,23},{8,24},{9,... | collective-permute-start | bytes 393224 | tf_op jit(solution)/shard_map/ppermute | solution.py:371
  14.8 5.9 %collective-permute-start.9 = (f32[64,512]{1,0:T(8,128)S(1)}, f32[64,512]{1,0:T(8,128)S(1)}, u32[]{:S(2)}, u32[]{:S(2)}) collective-permute-start(f32[64,512]{1,0:T(8,128)S(1)} %collective-permute-done.7.refs_6_), channel_id=1, source_target_pairs={{0,4},{1,5},{2,6},{3,7},{4,0},{5,1},{6,2},{7,3},{8,12},{9,13},{10,... | collective-permute-start | bytes 393224 | tf_op jit(solution)/shard_map/ppermute | solution.py:371
  26.1 8.2 %collective-permute-start.12 = (f32[144,128]{1,0:T(8,128)S(1)}, f32[144,128]{1,0:T(8,128)S(1)}, u32[]{:S(2)}, u32[]{:S(2)}) collective-permute-start(f32[144,128]{1,0:T(8,128)S(1)} %get-tuple-element.46.refs_0_), channel_id=1, source_target_pairs={{0,18},{1,19},{2,16},{3,17},{4,22},{5,23},{6,20},{7,21},{8,26},{9,... | collective-permute-start | bytes 221192 | tf_op jit(solution)/shard_map/ppermute | solution.py:371
  29.9 5.3 %collective-permute-start.11 = (f32[144,128]{1,0:T(8,128)S(1)}, f32[144,128]{1,0:T(8,128)S(1)}, u32[]{:S(2)}, u32[]{:S(2)}) collective-permute-start(f32[144,128]{1,0:T(8,128)S(1)} %get-tuple-element.46.refs_0_), channel_id=1, source_target_pairs={{0,2},{1,3},{2,0},{3,1},{4,6},{5,7},{6,4},{7,5},{8,10},{9,11},{10,... | collective-permute-start | bytes 221192 | tf_op jit(solution)/shard_map/ppermute | solution.py:371
  30.0 5.1 %collective-permute-start.10 = (f32[144,128]{1,0:T(8,128)S(1)}, f32[144,128]{1,0:T(8,128)S(1)}, u32[]{:S(2)}, u32[]{:S(2)}) collective-permute-start(f32[144,128]{1,0:T(8,128)S(1)} %get-tuple-element.46.refs_0_), channel_id=1, source_target_pairs={{0,16},{1,17},{2,18},{3,19},{4,20},{5,21},{6,22},{7,23},{8,24},{9,... | collective-permute-start | bytes 221192 | tf_op jit(solution)/shard_map/ppermute | solution.py:371
  38.3 2.3 %collective-permute-start.13 = (f32[4,136,128]{2,1,0:T(8,128)S(1)}, f32[4,136,128]{2,1,0:T(8,128)S(1)}, u32[]{:S(2)}, u32[]{:S(2)}) collective-permute-start(f32[4,136,128]{2,1,0:T(8,128)S(1)} %get-tuple-element.65), channel_id=1, source_target_pairs={{0,4},{1,5},{2,6},{3,7},{4,0},{5,1},{6,2},{7,3},{8,12},{9,13},{10,... | collective-permute-start | bytes 835592 | tf_op jit(solution)/shard_map/ppermute | solution.py:371
  40.7 5.6 %collective-permute-start.16 = (f32[136,128]{1,0:T(8,128)S(1)}, f32[136,128]{1,0:T(8,128)S(1)}, u32[]{:S(2)}, u32[]{:S(2)}) collective-permute-start(f32[136,128]{1,0:T(8,128)S(1)} %get-tuple-element.80), channel_id=1, source_target_pairs={{0,9},{1,8},{2,11},{3,10},{4,13},{5,12},{6,15},{7,14},{8,1},{9,0},... | collective-permute-start | bytes 208904 | tf_op jit(solution)/shard_map/ppermute | solution.py:371
  42.1 5.9 %collective-permute-start.15 = (f32[136,128]{1,0:T(8,128)S(1)}, f32[136,128]{1,0:T(8,128)S(1)}, u32[]{:S(2)}, u32[]{:S(2)}) collective-permute-start(f32[136,128]{1,0:T(8,128)S(1)} %get-tuple-element.81), channel_id=1, source_target_pairs={{0,1},{1,0},{2,3},{3,2},{4,5},{5,4},{6,7},{7,6},{8,9},{9,8},{10,11... | collective-permute-start | bytes 208904 | tf_op jit(solution)/shard_map/ppermute | solution.py:371
  43.9 4.3 %collective-permute-start.14 = (f32[136,128]{1,0:T(8,128)S(1)}, f32[136,128]{1,0:T(8,128)S(1)}, u32[]{:S(2)}, u32[]{:S(2)}) collective-permute-start(f32[136,128]{1,0:T(8,128)S(1)} %get-tuple-element.82), channel_id=1, source_target_pairs={{0,8},{1,9},{2,10},{3,11},{4,12},{5,13},{6,14},{7,15},{8,0},{9,1},... | collective-permute-start | bytes 208904 | tf_op jit(solution)/shard_map/ppermute | solution.py:371
  48.5 5.9 %collective-permute-start.17 = (f32[136,128]{1,0:T(8,128)S(1)}, f32[136,128]{1,0:T(8,128)S(1)}, u32[]{:S(2)}, u32[]{:S(2)}) collective-permute-start(f32[136,128]{1,0:T(8,128)S(1)} %get-tuple-element.67.piece_ref.refs_0_), channel_id=1, source_target_pairs={{0,16},{1,17},{2,18},{3,19},{4,20},{5,21},{6,22},{7,23},{8,24},{9,... | collective-permute-start | bytes 208904 | tf_op jit(solution)/shard_map/ppermute | solution.py:371
  49.5 8.8 %collective-permute-start.19 = (f32[136,128]{1,0:T(8,128)S(1)}, f32[136,128]{1,0:T(8,128)S(1)}, u32[]{:S(2)}, u32[]{:S(2)}) collective-permute-start(f32[136,128]{1,0:T(8,128)S(1)} %get-tuple-element.67.piece_ref.refs_0_), channel_id=1, source_target_pairs={{0,18},{1,19},{2,16},{3,17},{4,22},{5,23},{6,20},{7,21},{8,26},{9,... | collective-permute-start | bytes 208904 | tf_op jit(solution)/shard_map/ppermute | solution.py:371
  51.6 7.5 %collective-permute-start.18 = (f32[136,128]{1,0:T(8,128)S(1)}, f32[136,128]{1,0:T(8,128)S(1)}, u32[]{:S(2)}, u32[]{:S(2)}) collective-permute-start(f32[136,128]{1,0:T(8,128)S(1)} %get-tuple-element.67.piece_ref.refs_0_), channel_id=1, source_target_pairs={{0,2},{1,3},{2,0},{3,1},{4,6},{5,7},{6,4},{7,5},{8,10},{9,11},{10,... | collective-permute-start | bytes 208904 | tf_op jit(solution)/shard_map/ppermute | solution.py:371
  60.6 1.6 %collective-permute-start.20 = (f32[4,136,128]{2,1,0:T(8,128)S(1)}, f32[4,136,128]{2,1,0:T(8,128)S(1)}, u32[]{:S(2)}, u32[]{:S(2)}) collective-permute-start(f32[4,136,128]{2,1,0:T(8,128)S(1)} %get-tuple-element.74), channel_id=1, source_target_pairs={{0,4},{1,5},{2,6},{3,7},{4,0},{5,1},{6,2},{7,3},{8,12},{9,13},{10,... | collective-permute-start | bytes 835592 | tf_op jit(solution)/shard_map/ppermute | solution.py:371
  62.3 6.1 %collective-permute-start.23 = (f32[136,128]{1,0:T(8,128)S(1)}, f32[136,128]{1,0:T(8,128)S(1)}, u32[]{:S(2)}, u32[]{:S(2)}) collective-permute-start(f32[136,128]{1,0:T(8,128)S(1)} %get-tuple-element.77), channel_id=1, source_target_pairs={{0,9},{1,8},{2,11},{3,10},{4,13},{5,12},{6,15},{7,14},{8,1},{9,0},... | collective-permute-start | bytes 208904 | tf_op jit(solution)/shard_map/ppermute | solution.py:371
  62.8 5.7 %collective-permute-start.22 = (f32[136,128]{1,0:T(8,128)S(1)}, f32[136,128]{1,0:T(8,128)S(1)}, u32[]{:S(2)}, u32[]{:S(2)}) collective-permute-start(f32[136,128]{1,0:T(8,128)S(1)} %get-tuple-element.78), channel_id=1, source_target_pairs={{0,1},{1,0},{2,3},{3,2},{4,5},{5,4},{6,7},{7,6},{8,9},{9,8},{10,11... | collective-permute-start | bytes 208904 | tf_op jit(solution)/shard_map/ppermute | solution.py:371
  64.8 4.3 %collective-permute-start.21 = (f32[136,128]{1,0:T(8,128)S(1)}, f32[136,128]{1,0:T(8,128)S(1)}, u32[]{:S(2)}, u32[]{:S(2)}) collective-permute-start(f32[136,128]{1,0:T(8,128)S(1)} %get-tuple-element.79), channel_id=1, source_target_pairs={{0,8},{1,9},{2,10},{3,11},{4,12},{5,13},{6,14},{7,15},{8,0},{9,1},... | collective-permute-start | bytes 208904 | tf_op jit(solution)/shard_map/ppermute | solution.py:371
  70.3 1.2 %collective-permute-start.24 = (f32[8,128]{1,0:T(8,128)S(1)}, f32[8,128]{1,0:T(8,128)S(1)}, u32[]{:S(2)}, u32[]{:S(2)}) collective-permute-start(f32[8,128]{1,0:T(8,128)S(1)} %get-tuple-element.76), channel_id=1, source_target_pairs={{0,4},{1,5},{2,6},{3,7},{4,0},{5,1},{6,2},{7,3},{8,12},{9,13},{10,... | collective-permute-start | bytes 12296 | tf_op jit(solution)/shard_map/ppermute | solution.py:371
  71.5 4.5 %collective-permute-start.27 = (f32[8,128]{1,0:T(8,128)S(1)}, f32[8,128]{1,0:T(8,128)S(1)}, u32[]{:S(2)}, u32[]{:S(2)}) collective-permute-start(f32[8,128]{1,0:T(8,128)S(1)} %add.20), channel_id=1, source_target_pairs={{0,9},{1,8},{2,11},{3,10},{4,13},{5,12},{6,15},{7,14},{8,1},{9,0},... | collective-permute-start | bytes 12296 | tf_op jit(solution)/shard_map/ppermute | solution.py:371
  72.0 4.1 %collective-permute-start.26 = (f32[8,128]{1,0:T(8,128)S(1)}, f32[8,128]{1,0:T(8,128)S(1)}, u32[]{:S(2)}, u32[]{:S(2)}) collective-permute-start(f32[8,128]{1,0:T(8,128)S(1)} %add.20), channel_id=1, source_target_pairs={{0,1},{1,0},{2,3},{3,2},{4,5},{5,4},{6,7},{7,6},{8,9},{9,8},{10,11... | collective-permute-start | bytes 12296 | tf_op jit(solution)/shard_map/ppermute | solution.py:371
  74.0 3.6 %collective-permute-start.25 = (f32[8,128]{1,0:T(8,128)S(1)}, f32[8,128]{1,0:T(8,128)S(1)}, u32[]{:S(2)}, u32[]{:S(2)}) collective-permute-start(f32[8,128]{1,0:T(8,128)S(1)} %add.20), channel_id=1, source_target_pairs={{0,8},{1,9},{2,10},{3,11},{4,12},{5,13},{6,14},{7,15},{8,0},{9,1},... | collective-permute-start | bytes 12296 | tf_op jit(solution)/shard_map/ppermute | solution.py:371
  77.6 5.4 %collective-permute-start.30 = (f32[8,128]{1,0:T(8,128)S(1)}, f32[8,128]{1,0:T(8,128)S(1)}, u32[]{:S(2)}, u32[]{:S(2)}) collective-permute-start(f32[8,128]{1,0:T(8,128)S(1)} %add_add_fusion.refs_1_), channel_id=1, source_target_pairs={{0,18},{1,19},{2,16},{3,17},{4,22},{5,23},{6,20},{7,21},{8,26},{9,... | collective-permute-start | bytes 12296 | tf_op jit(solution)/shard_map/ppermute | solution.py:371
  78.5 4.6 %collective-permute-start.29 = (f32[8,128]{1,0:T(8,128)S(1)}, f32[8,128]{1,0:T(8,128)S(1)}, u32[]{:S(2)}, u32[]{:S(2)}) collective-permute-start(f32[8,128]{1,0:T(8,128)S(1)} %add_add_fusion.refs_1_), channel_id=1, source_target_pairs={{0,2},{1,3},{2,0},{3,1},{4,6},{5,7},{6,4},{7,5},{8,10},{9,11},{10,... | collective-permute-start | bytes 12296 | tf_op jit(solution)/shard_map/ppermute | solution.py:371
  80.9 3.6 %collective-permute-start.28 = (f32[8,128]{1,0:T(8,128)S(1)}, f32[8,128]{1,0:T(8,128)S(1)}, u32[]{:S(2)}, u32[]{:S(2)}) collective-permute-start(f32[8,128]{1,0:T(8,128)S(1)} %add_add_fusion.refs_1_), channel_id=1, source_target_pairs={{0,16},{1,17},{2,18},{3,19},{4,20},{5,21},{6,22},{7,23},{8,24},{9,... | collective-permute-start | bytes 12296 | tf_op jit(solution)/shard_map/ppermute | solution.py:371

commit v5 on v4

--- a/solution.py
+++ b/solution.py
@@ -411,7 +411,7 @@
     own, own_start = fetch(frames, start)
     beside_piece = swap(own, beside)
     along_piece = swap(own, along)
-    across_piece = swap(own, across)
+    across_piece = swap(swap(own, across | core), core)
     corner_piece = swap(along_piece, beside)
     row_pieces = [across_piece, skip_piece]
     last_piece = swap(skip_piece, across)
@@ -456,8 +456,8 @@
 
     def total_gram(gram):
         gram = gram + swap(gram, core)
-        gram = functools.reduce(jnp.add, [swap(gram, mask) for mask in far], gram)
-        return [gram] + [swap(gram, mask) for mask in near]
+        gram = functools.reduce(jnp.add, [swap(gram, mask | core) for mask in far], gram)
+        return [gram] + [swap(gram, mask | core) for mask in near]
 
     rows = vectors + DEGREE_ROWS
     block = 2 * 3 * rows * parts * width * width

time: 86.3 us -> 84.5 us (0.979)
  starting transfers between devices: 36.5 us -> 35.3 us
    ppermute x31 -> x32, starting transfers between devices: 36.5 us -> 35.3 us  [swap(): lax.ppermute(values, ('row', 'col'), [(index, index ^ mask) for index in...]
    ppermute x31 -> x32, waiting for transfers between devices: 23.2 us -> 22.6 us  [swap(): lax.ppermute(values, ('row', 'col'), [(index, index ^ mask) for index in...]
  transfers between devices with their start and end apart: 31 -> 32, of which waited for: 18 -> 20; matrix products, arithmetic and copies ran while one was open for 0% -> 0% of each run, Pallas kernels for 14% -> 14%
where the time goes in v5:
time: 84.5 us; the launch traced here: 84.3 us
  starting transfers between devices  35.3 us (42%)
  Pallas kernels  26.2 us (31%)
  waiting for transfers between devices  22.6 us (27%)
    ppermute x32, starting transfers between devices, swap(): lax.ppermute(values, ('row', 'col'), [(index, index ^ mask) for index in...  35.3 us
    pallas_call x13, Pallas kernels, call(): pl.pallas_call(body, out_shape=out_shape, in_specs=[VMEM] * len(operands)...  25.2 us
    ppermute x32, waiting for transfers between devices, swap(): lax.ppermute(values, ('row', 'col'), [(index, index ^ mask) for index in...  22.6 us
  transfers between devices with their start and end apart: 32, of which 20 were waited for; matrix products, arithmetic and copies ran while one was open for 0% of the time, Pallas kernels for 14%

profile of v5, /device:TPU:0, one launch (start us, length us, event | category | flops | bytes accessed | tf_op | source)
XLA Modules:
  0.0 84.3 jit_solution(9048664423305668041)
XLA Ops:
  0.0 1.0 %fetch.1 = (f32[64,512]{1,0:T(8,128)S(1)}, f32[32,512]{1,0:T(8,128)S(1)}) custom-call(f32[64,512]{1,0:T(8,128)} %frames_ref.1, f32[32,512]{1,0:T(8,128)} %start_ref.1), custom_call_target="tpu_custom_call" | custom-call | flops 17179869184 | tf_op jit(solution)/shard_map/fetch/pallas_call | solution.py:386
  1.0 3.1 %collective-permute-start.7 = (f32[64,512]{1,0:T(8,128)S(1)}, f32[64,512]{1,0:T(8,128)S(1)}, u32[]{:S(2)}, u32[]{:S(2)}) collective-permute-start(f32[64,512]{1,0:T(8,128)S(1)} %get-tuple-element.41.refs_0_), channel_id=1, source_target_pairs={{0,1},{1,0},{2,3},{3,2},{4,5},{5,4},{6,7},{7,6},{8,9},{9,8},{10,11... | collective-permute-start | bytes 393224 | tf_op jit(solution)/shard_map/ppermute | solution.py:371
  4.1 2.6 %collective-permute-start.2 = (f32[64,512]{1,0:T(8,128)S(1)}, f32[64,512]{1,0:T(8,128)S(1)}, u32[]{:S(2)}, u32[]{:S(2)}) collective-permute-start(f32[64,512]{1,0:T(8,128)S(1)} %copy-done), channel_id=1, source_target_pairs={{0,2},{1,3},{2,0},{3,1},{4,6},{5,7},{6,4},{7,5},{8,10},{9,11},{10,... | collective-permute-start | bytes 393224 | tf_op jit(solution)/shard_map/ppermute | solution.py:371
  6.7 1.5 %collective-permute-start.3 = (f32[64,512]{1,0:T(8,128)S(1)}, f32[64,512]{1,0:T(8,128)S(1)}, u32[]{:S(2)}, u32[]{:S(2)}) collective-permute-start(f32[64,512]{1,0:T(8,128)S(1)} %get-tuple-element.41.refs_0_), channel_id=1, source_target_pairs={{0,8},{1,9},{2,10},{3,11},{4,12},{5,13},{6,14},{7,15},{8,0},{9,1},... | collective-permute-start | bytes 393224 | tf_op jit(solution)/shard_map/ppermute | solution.py:371
  8.3 1.5 %collective-permute-start.4 = (f32[64,512]{1,0:T(8,128)S(1)}, f32[64,512]{1,0:T(8,128)S(1)}, u32[]{:S(2)}, u32[]{:S(2)}) collective-permute-start(f32[64,512]{1,0:T(8,128)S(1)} %get-tuple-element.41.refs_0_), channel_id=1, source_target_pairs={{0,4},{1,5},{2,6},{3,7},{4,0},{5,1},{6,2},{7,3},{8,12},{9,13},{10,... | collective-permute-start | bytes 393224 | tf_op jit(solution)/shard_map/ppermute | solution.py:371
  9.8 1.4 %collective-permute-start.8 = (f32[64,512]{1,0:T(8,128)S(1)}, f32[64,512]{1,0:T(8,128)S(1)}, u32[]{:S(2)}, u32[]{:S(2)}) collective-permute-start(f32[64,512]{1,0:T(8,128)S(1)} %collective-permute-done.7.refs_5_), channel_id=1, source_target_pairs={{0,8},{1,9},{2,10},{3,11},{4,12},{5,13},{6,14},{7,15},{8,0},{9,1},... | collective-permute-start | bytes 393224 | tf_op jit(solution)/shard_map/ppermute | solution.py:371
  11.3 1.6 %collective-permute-done.2.refs_2_ = f32[64,512]{1,0:T(8,128)S(1)} collective-permute-done((f32[64,512]{1,0:T(8,128)S(1)}, f32[64,512]{1,0:T(8,128)S(1)}, u32[]{:S(2)}, u32[]{:S(2)}) %collective-permute-start.2) | collective-permute-done | bytes 131104 | tf_op jit(solution)/shard_map/ppermute | solution.py:371
  14.1 0.8 collective-permute-start.6
  15.3 4.3 %build_near.1 = (bf16[512,2048]{1,0:T(8,128)(2,1)S(1)}, bf16[512,2048]{1,0:T(8,128)(2,1)S(1)}, bf16[512,2048]{1,0:T(8,128)(2,1)S(1)}, bf16[512,2048]{1,0:T(8,128...) custom-call(f32[64,512]{1,0:T(8,128)S(1)} %get-tuple-element.41.refs, ...), custom_call_target="tpu_custom_call" | custom-call | flops 1 | tf_op jit(solution)/shard_map/build_near/pallas_call | solution.py:18
  19.8 5.3 %build_far.1 = (bf16[512,2048]{1,0:T(8,128)(2,1)S(1)}, bf16[512,2048]{1,0:T(8,128)(2,1)S(1)}, bf16[512,2048]{1,0:T(8,128)(2,1)S(1)}, bf16[512,2048]{1,0:T(8,128)...) custom-call(bf16[1536,256]{1,0:T(8,128)(2,1)S(1)} %get-tuple-element, ...), custom_call_target="tpu_custom_call" | custom-call | flops 1 | tf_op jit(solution)/shard_map/build_far/pallas_call | solution.py:18
  25.1 2.0 %collective-permute-start.13 = (f32[144,128]{1,0:T(8,128)S(1)}, f32[144,128]{1,0:T(8,128)S(1)}, u32[]{:S(2)}, u32[]{:S(2)}) collective-permute-start(f32[144,128]{1,0:T(8,128)S(1)} %get-tuple-element.46.refs_0_), channel_id=1, source_target_pairs={{0,18},{1,19},{2,16},{3,17},{4,22},{5,23},{6,20},{7,21},{8,26},{9,... | collective-permute-start | bytes 221192 | tf_op jit(solution)/shard_map/ppermute | solution.py:371
  27.1 1.3 %collective-permute-start.12 = (f32[144,128]{1,0:T(8,128)S(1)}, f32[144,128]{1,0:T(8,128)S(1)}, u32[]{:S(2)}, u32[]{:S(2)}) collective-permute-start(f32[144,128]{1,0:T(8,128)S(1)} %get-tuple-element.46.refs_0_), channel_id=1, source_target_pairs={{0,2},{1,3},{2,0},{3,1},{4,6},{5,7},{6,4},{7,5},{8,10},{9,11},{10,... | collective-permute-start | bytes 221192 | tf_op jit(solution)/shard_map/ppermute | solution.py:371
  28.5 1.1 %collective-permute-start.11 = (f32[144,128]{1,0:T(8,128)S(1)}, f32[144,128]{1,0:T(8,128)S(1)}, u32[]{:S(2)}, u32[]{:S(2)}) collective-permute-start(f32[144,128]{1,0:T(8,128)S(1)} %get-tuple-element.46.refs_0_), channel_id=1, source_target_pairs={{0,16},{1,17},{2,18},{3,19},{4,20},{5,21},{6,22},{7,23},{8,24},{9,... | collective-permute-start | bytes 221192 | tf_op jit(solution)/shard_map/ppermute | solution.py:371
  29.5 5.2 %collective-permute-done.13.refs_3_ = f32[144,128]{1,0:T(8,128)S(1)} collective-permute-done((f32[144,128]{1,0:T(8,128)S(1)}, f32[144,128]{1,0:T(8,128)S(1)}, u32[]{:S(2)}, u32[]{:S(2)}) %collective-permute-start.13) | collective-permute-done | bytes 73760 | tf_op jit(solution)/shard_map/ppermute | solution.py:371
  34.7 0.7 collective-permute-done.12.refs_2_
  35.5 3.1 %first_odd.1 = (f32[4,136,128]{2,1,0:T(8,128)S(1)}, f32[1,512]{1,0:T(1,128)S(1)}, bf16[96,2048]{1,0:T(8,128)(2,1)S(1)}) custom-call(f32[144,128]{1,0:T(8,128)S(1)} %get-tuple-element.46.refs_0_, f32[144,128]{1,0:T(8,128)S(1)} %collective-permute-done.11.refs_1_, f32[144,128]{1,0:T(8,128)S(1)} %collective-permute-done.12.refs_2_, ...), custom_call_target="tpu_custom_call" | custom-call | flops 1207959552 | tf_op jit(solution)/shard_map/first_odd/pallas_call | solution.py:18
  38.7 2.2 %first_even.1 = f32[3,136,128]{2,1,0:T(8,128)S(1)} custom-call(bf16[96,2048]{1,0:T(8,128)(2,1)S(1)} %get-tuple-element.64.refs_0_, bf16[512,2048]{1,0:T(8,128)(2,1)S(1)} %get-tuple-element.47.refs_4_.refs_1_.refs_2_.refs_0_, bf16[512,2048]{1,0:T(8,128)(2,1)S(1)} %get-tuple-element.48.refs_5_.refs_2_.refs_3_.refs_1_, ...), custom_call_target="tpu_custom_call" | custom-call | flops 905969664 | tf_op jit(solution)/shard_map/first_even/pallas_call | solution.py:18
  41.1 1.1 %collective-permute-start.17 = (f32[136,128]{1,0:T(8,128)S(1)}, f32[136,128]{1,0:T(8,128)S(1)}, u32[]{:S(2)}, u32[]{:S(2)}) collective-permute-start(f32[136,128]{1,0:T(8,128)S(1)} %get-tuple-element.80), channel_id=1, source_target_pairs={{0,9},{1,8},{2,11},{3,10},{4,13},{5,12},{6,15},{7,14},{8,1},{9,0},... | collective-permute-start | bytes 208904 | tf_op jit(solution)/shard_map/ppermute | solution.py:371
  42.1 1.8 %collective-permute-start.16 = (f32[136,128]{1,0:T(8,128)S(1)}, f32[136,128]{1,0:T(8,128)S(1)}, u32[]{:S(2)}, u32[]{:S(2)}) collective-permute-start(f32[136,128]{1,0:T(8,128)S(1)} %get-tuple-element.81), channel_id=1, source_target_pairs={{0,1},{1,0},{2,3},{3,2},{4,5},{5,4},{6,7},{7,6},{8,9},{9,8},{10,11... | collective-permute-start | bytes 208904 | tf_op jit(solution)/shard_map/ppermute | solution.py:371
  43.9 0.7 collective-permute-start.15
  44.6 0.8 first_own.1.refs_1_
  45.5 1.6 %collective-permute-done.17.refs_5_ = f32[136,128]{1,0:T(8,128)S(1)} collective-permute-done((f32[136,128]{1,0:T(8,128)S(1)}, f32[136,128]{1,0:T(8,128)S(1)}, u32[]{:S(2)}, u32[]{:S(2)}) %collective-permute-start.17) | collective-permute-done | bytes 69664 | tf_op jit(solution)/shard_map/ppermute | solution.py:371
  47.0 0.9 %collective-permute-done.16.refs_4_ = f32[136,128]{1,0:T(8,128)S(1)} collective-permute-done((f32[136,128]{1,0:T(8,128)S(1)}, f32[136,128]{1,0:T(8,128)S(1)}, u32[]{:S(2)}, u32[]{:S(2)}) %collective-permute-start.16) | collective-permute-done | bytes 69664 | tf_op jit(solution)/shard_map/ppermute | solution.py:371
  48.5 1.1 %collective-permute-start.18 = (f32[136,128]{1,0:T(8,128)S(1)}, f32[136,128]{1,0:T(8,128)S(1)}, u32[]{:S(2)}, u32[]{:S(2)}) collective-permute-start(f32[136,128]{1,0:T(8,128)S(1)} %get-tuple-element.67.piece_ref.refs_0_), channel_id=1, source_target_pairs={{0,16},{1,17},{2,18},{3,19},{4,20},{5,21},{6,22},{7,23},{8,24},{9,... | collective-permute-start | bytes 208904 | tf_op jit(solution)/shard_map/ppermute | solution.py:371
  49.6 1.9 %collective-permute-start.20 = (f32[136,128]{1,0:T(8,128)S(1)}, f32[136,128]{1,0:T(8,128)S(1)}, u32[]{:S(2)}, u32[]{:S(2)}) collective-permute-start(f32[136,128]{1,0:T(8,128)S(1)} %get-tuple-element.67.piece_ref.refs_0_), channel_id=1, source_target_pairs={{0,18},{1,19},{2,16},{3,17},{4,22},{5,23},{6,20},{7,21},{8,26},{9,... | collective-permute-start | bytes 208904 | tf_op jit(solution)/shard_map/ppermute | solution.py:371
  51.6 1.3 %collective-permute-start.19 = (f32[136,128]{1,0:T(8,128)S(1)}, f32[136,128]{1,0:T(8,128)S(1)}, u32[]{:S(2)}, u32[]{:S(2)}) collective-permute-start(f32[136,128]{1,0:T(8,128)S(1)} %get-tuple-element.67.piece_ref.refs_0_), channel_id=1, source_target_pairs={{0,2},{1,3},{2,0},{3,1},{4,6},{5,7},{6,4},{7,5},{8,10},{9,11},{10,... | collective-permute-start | bytes 208904 | tf_op jit(solution)/shard_map/ppermute | solution.py:371
  52.9 1.5 %second_part.2 = (f32[4,32,512]{2,1,0:T(8,128)S(1)}, f32[4,32,512]{2,1,0:T(8,128)S(1)}) custom-call(f32[136,128]{1,0:T(8,128)S(1)} %get-tuple-element.67.piece_ref.refs_0_, bf16[512,2048]{1,0:T(8,128)(2,1)S(1)} %get-tuple-element.47.refs_4_.refs_1_.refs_2_.refs_0_, bf16[512,2048]{1,0:T(8,128)(2,1)S(1)} %get-tuple-element.48.refs_5_.refs_2_.refs_3_.refs_1_, ...), custom_call_target="tpu_custom_call" | custom-call | flops 603979776 | tf_op jit(solution)/shard_map/second_part/pallas_call | solution.py:18
  54.4 1.6 %second_part.3 = (f32[4,32,512]{2,1,0:T(8,128)S(1)}, f32[4,32,512]{2,1,0:T(8,128)S(1)}) custom-call(f32[136,128]{1,0:T(8,128)S(1)} %collective-permute-done.18.piece_ref.refs_1_, bf16[512,2048]{1,0:T(8,128)(2,1)S(1)} %get-tuple-element.49.refs_6_.refs_3_.refs_4_.refs_0_, bf16[512,2048]{1,0:T(8,128)(2,1)S(1)} %get-tuple-element.50.refs_7_.refs_4_.refs_5_.refs_1_, ...), custom_call_target="tpu_custom_call" | custom-call | flops 603979776 | tf_op jit(solution)/shard_map/second_part/pallas_call | solution.py:18
  56.0 1.4 %collective-permute-done.20.refs_3_ = f32[136,128]{1,0:T(8,128)S(1)} collective-permute-done((f32[136,128]{1,0:T(8,128)S(1)}, f32[136,128]{1,0:T(8,128)S(1)}, u32[]{:S(2)}, u32[]{:S(2)}) %collective-permute-start.20) | collective-permute-done | bytes 69664 | tf_op jit(solution)/shard_map/ppermute | solution.py:371
  57.4 1.6 %second_odd.1 = (f32[4,136,128]{2,1,0:T(8,128)S(1)}, f32[8,128]{1,0:T(8,128)S(1)}, bf16[64,1024]{1,0:T(8,128)(2,1)S(1)}) custom-call(f32[136,128]{1,0:T(8,128)S(1)} %get-tuple-element.67.piece_ref.refs_0_, f32[136,128]{1,0:T(8,128)S(1)} %collective-permute-done.18.piece_ref.refs_1_, f32[136,128]{1,0:T(8,128)S(1)} %collective-permute-done.19.refs_2_, ...), custom_call_target="tpu_custom_call" | custom-call | flops 1207959552 | tf_op jit(solution)/shard_map/second_odd/pallas_call | solution.py:18
  59.0 1.2 %second_even.1 = f32[3,136,128]{2,1,0:T(8,128)S(1)} custom-call(bf16[64,1024]{1,0:T(8,128)(2,1)S(1)} %get-tuple-element.71.refs_0_, f32[8,128]{1,0:T(8,128)S(1)} %get-tuple-element.72.refs_1_, f32[4,32,512]{2,1,0:T(8,128)S(1)} %get-tuple-element.73.refs_2_, bf16[512,2048]{1,0:T(8,128)(2,1)S(1)} %get-tuple-element.51.refs_8_.refs_5_.refs_6_.refs_3_.refs_4_, ...), custom_call_target="tpu_custom_call" | custom-call | flops 905969664 | tf_op jit(solution)/shard_map/second_even/pallas_call | solution.py:18
  60.6 2.1 %collective-permute-start.24 = (f32[136,128]{1,0:T(8,128)S(1)}, f32[136,128]{1,0:T(8,128)S(1)}, u32[]{:S(2)}, u32[]{:S(2)}) collective-permute-start(f32[136,128]{1,0:T(8,128)S(1)} %get-tuple-element.77), channel_id=1, source_target_pairs={{0,9},{1,8},{2,11},{3,10},{4,13},{5,12},{6,15},{7,14},{8,1},{9,0},... | collective-permute-start | bytes 208904 | tf_op jit(solution)/shard_map/ppermute | solution.py:371
  62.7 2.0 %collective-permute-start.23 = (f32[136,128]{1,0:T(8,128)S(1)}, f32[136,128]{1,0:T(8,128)S(1)}, u32[]{:S(2)}, u32[]{:S(2)}) collective-permute-start(f32[136,128]{1,0:T(8,128)S(1)} %get-tuple-element.78), channel_id=1, source_target_pairs={{0,1},{1,0},{2,3},{3,2},{4,5},{5,4},{6,7},{7,6},{8,9},{9,8},{10,11... | collective-permute-start | bytes 208904 | tf_op jit(solution)/shard_map/ppermute | solution.py:371
  65.2 1.1 %collective-permute-done.24.refs_5_ = f32[136,128]{1,0:T(8,128)S(1)} collective-permute-done((f32[136,128]{1,0:T(8,128)S(1)}, f32[136,128]{1,0:T(8,128)S(1)}, u32[]{:S(2)}, u32[]{:S(2)}) %collective-permute-start.24) | collective-permute-done | bytes 69664 | tf_op jit(solution)/shard_map/ppermute | solution.py:371
  66.3 2.1 %collective-permute-done.23.refs_4_ = f32[136,128]{1,0:T(8,128)S(1)} collective-permute-done((f32[136,128]{1,0:T(8,128)S(1)}, f32[136,128]{1,0:T(8,128)S(1)}, u32[]{:S(2)}, u32[]{:S(2)}) %collective-permute-start.23) | collective-permute-done | bytes 69664 | tf_op jit(solution)/shard_map/ppermute | solution.py:371
  68.4 0.6 collective-permute-done.22.refs_3_
  69.0 1.2 %grown_two.1 = (f32[32,512]{1,0:T(8,128)S(1)}, f32[8,128]{1,0:T(8,128)S(1)}) custom-call(f32[1,512]{1,0:T(1,128)S(1)} %get-tuple-element.66.refs_0_, f32[136,128]{1,0:T(8,128)S(1)} %second_own.1.refs_1_, f32[136,128]{1,0:T(8,128)S(1)} %slice_bitcast_fusion.3.refs_2_, f32[136,128]{1,0:T(8,128)S(1)} %collective-permute-done.22.refs_3_, ...), custom_call_target="tpu_custom_call" | custom-call | tf_op jit(solution)/shard_map/grown_two/pallas_call | solution.py:18
  70.3 1.2 %collective-permute-done.25 = f32[8,128]{1,0:T(8,128)S(1)} collective-permute-done((f32[8,128]{1,0:T(8,128)S(1)}, f32[8,128]{1,0:T(8,128)S(1)}, u32[]{:S(2)}, u32[]{:S(2)}) %collective-permute-start.25) | collective-permute-done | bytes 4128 | tf_op jit(solution)/shard_map/ppermute | solution.py:371
  71.6 1.9 %collective-permute-start.27 = (f32[8,128]{1,0:T(8,128)S(1)}, f32[8,128]{1,0:T(8,128)S(1)}, u32[]{:S(2)}, u32[]{:S(2)}) collective-permute-start(f32[8,128]{1,0:T(8,128)S(1)} %add.20), channel_id=1, source_target_pairs={{0,5},{1,4},{2,7},{3,6},{4,1},{5,0},{6,3},{7,2},{8,13},{9,12},{10,... | collective-permute-start | bytes 12296 | tf_op jit(solution)/shard_map/ppermute | solution.py:371
  73.5 0.9 %collective-permute-start.26 = (f32[8,128]{1,0:T(8,128)S(1)}, f32[8,128]{1,0:T(8,128)S(1)}, u32[]{:S(2)}, u32[]{:S(2)}) collective-permute-start(f32[8,128]{1,0:T(8,128)S(1)} %add.20), channel_id=1, source_target_pairs={{0,12},{1,13},{2,14},{3,15},{4,8},{5,9},{6,10},{7,11},{8,4},{9,5},... | collective-permute-start | bytes 12296 | tf_op jit(solution)/shard_map/ppermute | solution.py:371
  74.4 0.9 %collective-permute-done.28 = f32[8,128]{1,0:T(8,128)S(1)} collective-permute-done((f32[8,128]{1,0:T(8,128)S(1)}, f32[8,128]{1,0:T(8,128)S(1)}, u32[]{:S(2)}, u32[]{:S(2)}) %collective-permute-start.28) | collective-permute-done | bytes 4128 | tf_op jit(solution)/shard_map/ppermute | solution.py:371
  75.4 1.1 %collective-permute-done.26 = f32[8,128]{1,0:T(8,128)S(1)} collective-permute-done((f32[8,128]{1,0:T(8,128)S(1)}, f32[8,128]{1,0:T(8,128)S(1)}, u32[]{:S(2)}, u32[]{:S(2)}) %collective-permute-start.26) | collective-permute-done | bytes 4128 | tf_op jit(solution)/shard_map/ppermute | solution.py:371
  76.5 1.1 %collective-permute-start.31 = (f32[8,128]{1,0:T(8,128)S(1)}, f32[8,128]{1,0:T(8,128)S(1)}, u32[]{:S(2)}, u32[]{:S(2)}) collective-permute-start(f32[8,128]{1,0:T(8,128)S(1)} %add_add_fusion.refs_1_), channel_id=1, source_target_pairs={{0,22},{1,23},{2,20},{3,21},{4,18},{5,19},{6,16},{7,17},{8,30},{9,... | collective-permute-start | bytes 12296 | tf_op jit(solution)/shard_map/ppermute | solution.py:371
  77.6 2.1 %collective-permute-start.30 = (f32[8,128]{1,0:T(8,128)S(1)}, f32[8,128]{1,0:T(8,128)S(1)}, u32[]{:S(2)}, u32[]{:S(2)}) collective-permute-start(f32[8,128]{1,0:T(8,128)S(1)} %add_add_fusion.refs_1_), channel_id=1, source_target_pairs={{0,6},{1,7},{2,4},{3,5},{4,2},{5,3},{6,0},{7,1},{8,14},{9,15},{10,... | collective-permute-start | bytes 12296 | tf_op jit(solution)/shard_map/ppermute | solution.py:371
  79.7 0.7 collective-permute-start.29
  80.4 0.9 %collective-permute-done.31.refs_4_ = f32[8,128]{1,0:T(8,128)S(1)} collective-permute-done((f32[8,128]{1,0:T(8,128)S(1)}, f32[8,128]{1,0:T(8,128)S(1)}, u32[]{:S(2)}, u32[]{:S(2)}) %collective-permute-start.31) | collective-permute-done | bytes 4128 | tf_op jit(solution)/shard_map/ppermute | solution.py:371
  81.5 1.2 %collective-permute-done.29.refs_2_ = f32[8,128]{1,0:T(8,128)S(1)} collective-permute-done((f32[8,128]{1,0:T(8,128)S(1)}, f32[8,128]{1,0:T(8,128)S(1)}, u32[]{:S(2)}, u32[]{:S(2)}) %collective-permute-start.29) | collective-permute-done | bytes 4128 | tf_op jit(solution)/shard_map/ppermute | solution.py:371
  82.7 1.6 %finish.1 = f32[32,512]{1,0:T(8,128)} custom-call(f32[32,512]{1,0:T(8,128)S(1)} %get-tuple-element.75.refs_0_, f32[8,128]{1,0:T(8,128)S(1)} %add_add_fusion.refs_1_, f32[8,128]{1,0:T(8,128)S(1)} %collective-permute-done.29.refs_2_, f32[8,128]{1,0:T(8,128)S(1)} %collective-permute-done.30.refs_3_, f32[8,128]{1,0:T(8,128)S(1)} %collective-permute-done.31.refs_4_), custom_call_target="tpu_custom_call" | custom-call | tf_op jit(solution)/shard_map/finish/pallas_call | solution.py:18
  (40 shorter events, 4.0 us)
Async XLA Ops:
  0.0 4.1 %copy-start = (f32[64,512]{1,0:T(8,128)S(1)}, f32[64,512]{1,0:T(8,128)}, u32[]{:S(2)}) copy-start(f32[64,512]{1,0:T(8,128)} %frames_ref.1) | copy-start | bytes 393220
  1.0 8.8 %collective-permute-start.7 = (f32[64,512]{1,0:T(8,128)S(1)}, f32[64,512]{1,0:T(8,128)S(1)}, u32[]{:S(2)}, u32[]{:S(2)}) collective-permute-start(f32[64,512]{1,0:T(8,128)S(1)} %get-tuple-element.41.refs_0_), channel_id=1, source_target_pairs={{0,1},{1,0},{2,3},{3,2},{4,5},{5,4},{6,7},{7,6},{8,9},{9,8},{10,11... | collective-permute-start | bytes 393224 | tf_op jit(solution)/shard_map/ppermute | solution.py:371
  4.1 8.7 %collective-permute-start.2 = (f32[64,512]{1,0:T(8,128)S(1)}, f32[64,512]{1,0:T(8,128)S(1)}, u32[]{:S(2)}, u32[]{:S(2)}) collective-permute-start(f32[64,512]{1,0:T(8,128)S(1)} %copy-done), channel_id=1, source_target_pairs={{0,2},{1,3},{2,0},{3,1},{4,6},{5,7},{6,4},{7,5},{8,10},{9,11},{10,... | collective-permute-start | bytes 393224 | tf_op jit(solution)/shard_map/ppermute | solution.py:371
  6.7 6.1 %collective-permute-start.3 = (f32[64,512]{1,0:T(8,128)S(1)}, f32[64,512]{1,0:T(8,128)S(1)}, u32[]{:S(2)}, u32[]{:S(2)}) collective-permute-start(f32[64,512]{1,0:T(8,128)S(1)} %get-tuple-element.41.refs_0_), channel_id=1, source_target_pairs={{0,8},{1,9},{2,10},{3,11},{4,12},{5,13},{6,14},{7,15},{8,0},{9,1},... | collective-permute-start | bytes 393224 | tf_op jit(solution)/shard_map/ppermute | solution.py:371
  8.2 5.7 %collective-permute-start = (f32[64,512]{1,0:T(8,128)S(1)}, f32[64,512]{1,0:T(8,128)S(1)}, u32[]{:S(2)}, u32[]{:S(2)}) collective-permute-start(f32[64,512]{1,0:T(8,128)S(1)} %get-tuple-element.41.refs_0_), channel_id=1, source_target_pairs={{0,20},{1,21},{2,22},{3,23},{4,16},{5,17},{6,18},{7,19},{8,28},{9,... | collective-permute-start | bytes 393224 | tf_op jit(solution)/shard_map/ppermute | solution.py:371
  8.3 5.8 %collective-permute-start.4 = (f32[64,512]{1,0:T(8,128)S(1)}, f32[64,512]{1,0:T(8,128)S(1)}, u32[]{:S(2)}, u32[]{:S(2)}) collective-permute-start(f32[64,512]{1,0:T(8,128)S(1)} %get-tuple-element.41.refs_0_), channel_id=1, source_target_pairs={{0,4},{1,5},{2,6},{3,7},{4,0},{5,1},{6,2},{7,3},{8,12},{9,13},{10,... | collective-permute-start | bytes 393224 | tf_op jit(solution)/shard_map/ppermute | solution.py:371
  9.8 5.4 %collective-permute-start.8 = (f32[64,512]{1,0:T(8,128)S(1)}, f32[64,512]{1,0:T(8,128)S(1)}, u32[]{:S(2)}, u32[]{:S(2)}) collective-permute-start(f32[64,512]{1,0:T(8,128)S(1)} %collective-permute-done.7.refs_5_), channel_id=1, source_target_pairs={{0,8},{1,9},{2,10},{3,11},{4,12},{5,13},{6,14},{7,15},{8,0},{9,1},... | collective-permute-start | bytes 393224 | tf_op jit(solution)/shard_map/ppermute | solution.py:371
  12.8 7.0 %collective-permute-start.9 = (f32[64,512]{1,0:T(8,128)S(1)}, f32[64,512]{1,0:T(8,128)S(1)}, u32[]{:S(2)}, u32[]{:S(2)}) collective-permute-start(f32[64,512]{1,0:T(8,128)S(1)} %collective-permute-done.7.refs_5_), channel_id=1, source_target_pairs={{0,4},{1,5},{2,6},{3,7},{4,0},{5,1},{6,2},{7,3},{8,12},{9,13},{10,... | collective-permute-start | bytes 393224 | tf_op jit(solution)/shard_map/ppermute | solution.py:371
  12.8 2.4 %collective-permute-start.5 = (f32[64,512]{1,0:T(8,128)S(1)}, f32[64,512]{1,0:T(8,128)S(1)}, u32[]{:S(2)}, u32[]{:S(2)}) collective-permute-start(f32[64,512]{1,0:T(8,128)S(1)} %collective-permute-done.3.refs_3_), channel_id=1, source_target_pairs={{0,4},{1,5},{2,6},{3,7},{4,0},{5,1},{6,2},{7,3},{8,12},{9,13},{10,... | collective-permute-start | bytes 393224 | tf_op jit(solution)/shard_map/ppermute | solution.py:371
  13.9 1.3 %collective-permute-start.1 = (f32[64,512]{1,0:T(8,128)S(1)}, f32[64,512]{1,0:T(8,128)S(1)}, u32[]{:S(2)}, u32[]{:S(2)}) collective-permute-start(f32[64,512]{1,0:T(8,128)S(1)} %collective-permute-done), channel_id=1, source_target_pairs={{0,4},{1,5},{2,6},{3,7},{4,0},{5,1},{6,2},{7,3},{8,12},{9,13},{10,... | collective-permute-start | bytes 393224 | tf_op jit(solution)/shard_map/ppermute | solution.py:371
  14.1 5.7 %collective-permute-start.6 = (f32[64,512]{1,0:T(8,128)S(1)}, f32[64,512]{1,0:T(8,128)S(1)}, u32[]{:S(2)}, u32[]{:S(2)}) collective-permute-start(f32[64,512]{1,0:T(8,128)S(1)} %collective-permute-done.2.refs_2_), channel_id=1, source_target_pairs={{0,16},{1,17},{2,18},{3,19},{4,20},{5,21},{6,22},{7,23},{8,24},{9,... | collective-permute-start | bytes 393224 | tf_op jit(solution)/shard_map/ppermute | solution.py:371
  15.2 4.6 %collective-permute-start.10 = (f32[64,512]{1,0:T(8,128)S(1)}, f32[64,512]{1,0:T(8,128)S(1)}, u32[]{:S(2)}, u32[]{:S(2)}) collective-permute-start(f32[64,512]{1,0:T(8,128)S(1)} %collective-permute-done.8.refs_6_), channel_id=1, source_target_pairs={{0,4},{1,5},{2,6},{3,7},{4,0},{5,1},{6,2},{7,3},{8,12},{9,13},{10,... | collective-permute-start | bytes 393224 | tf_op jit(solution)/shard_map/ppermute | solution.py:371
  25.1 9.7 %collective-permute-start.13 = (f32[144,128]{1,0:T(8,128)S(1)}, f32[144,128]{1,0:T(8,128)S(1)}, u32[]{:S(2)}, u32[]{:S(2)}) collective-permute-start(f32[144,128]{1,0:T(8,128)S(1)} %get-tuple-element.46.refs_0_), channel_id=1, source_target_pairs={{0,18},{1,19},{2,16},{3,17},{4,22},{5,23},{6,20},{7,21},{8,26},{9,... | collective-permute-start | bytes 221192 | tf_op jit(solution)/shard_map/ppermute | solution.py:371
  27.1 8.3 %collective-permute-start.12 = (f32[144,128]{1,0:T(8,128)S(1)}, f32[144,128]{1,0:T(8,128)S(1)}, u32[]{:S(2)}, u32[]{:S(2)}) collective-permute-start(f32[144,128]{1,0:T(8,128)S(1)} %get-tuple-element.46.refs_0_), channel_id=1, source_target_pairs={{0,2},{1,3},{2,0},{3,1},{4,6},{5,7},{6,4},{7,5},{8,10},{9,11},{10,... | collective-permute-start | bytes 221192 | tf_op jit(solution)/shard_map/ppermute | solution.py:371
  28.5 7.0 %collective-permute-start.11 = (f32[144,128]{1,0:T(8,128)S(1)}, f32[144,128]{1,0:T(8,128)S(1)}, u32[]{:S(2)}, u32[]{:S(2)}) collective-permute-start(f32[144,128]{1,0:T(8,128)S(1)} %get-tuple-element.46.refs_0_), channel_id=1, source_target_pairs={{0,16},{1,17},{2,18},{3,19},{4,20},{5,21},{6,22},{7,23},{8,24},{9,... | collective-permute-start | bytes 221192 | tf_op jit(solution)/shard_map/ppermute | solution.py:371
  38.6 2.4 %collective-permute-start.14 = (f32[4,136,128]{2,1,0:T(8,128)S(1)}, f32[4,136,128]{2,1,0:T(8,128)S(1)}, u32[]{:S(2)}, u32[]{:S(2)}) collective-permute-start(f32[4,136,128]{2,1,0:T(8,128)S(1)} %get-tuple-element.65), channel_id=1, source_target_pairs={{0,4},{1,5},{2,6},{3,7},{4,0},{5,1},{6,2},{7,3},{8,12},{9,13},{10,... | collective-permute-start | bytes 835592 | tf_op jit(solution)/shard_map/ppermute | solution.py:371
  41.1 5.9 %collective-permute-start.17 = (f32[136,128]{1,0:T(8,128)S(1)}, f32[136,128]{1,0:T(8,128)S(1)}, u32[]{:S(2)}, u32[]{:S(2)}) collective-permute-start(f32[136,128]{1,0:T(8,128)S(1)} %get-tuple-element.80), channel_id=1, source_target_pairs={{0,9},{1,8},{2,11},{3,10},{4,13},{5,12},{6,15},{7,14},{8,1},{9,0},... | collective-permute-start | bytes 208904 | tf_op jit(solution)/shard_map/ppermute | solution.py:371
  42.1 5.8 %collective-permute-start.16 = (f32[136,128]{1,0:T(8,128)S(1)}, f32[136,128]{1,0:T(8,128)S(1)}, u32[]{:S(2)}, u32[]{:S(2)}) collective-permute-start(f32[136,128]{1,0:T(8,128)S(1)} %get-tuple-element.81), channel_id=1, source_target_pairs={{0,1},{1,0},{2,3},{3,2},{4,5},{5,4},{6,7},{7,6},{8,9},{9,8},{10,11... | collective-permute-start | bytes 208904 | tf_op jit(solution)/shard_map/ppermute | solution.py:371
  43.9 4.3 %collective-permute-start.15 = (f32[136,128]{1,0:T(8,128)S(1)}, f32[136,128]{1,0:T(8,128)S(1)}, u32[]{:S(2)}, u32[]{:S(2)}) collective-permute-start(f32[136,128]{1,0:T(8,128)S(1)} %get-tuple-element.82), channel_id=1, source_target_pairs={{0,8},{1,9},{2,10},{3,11},{4,12},{5,13},{6,14},{7,15},{8,0},{9,1},... | collective-permute-start | bytes 208904 | tf_op jit(solution)/shard_map/ppermute | solution.py:371
  48.5 5.9 %collective-permute-start.18 = (f32[136,128]{1,0:T(8,128)S(1)}, f32[136,128]{1,0:T(8,128)S(1)}, u32[]{:S(2)}, u32[]{:S(2)}) collective-permute-start(f32[136,128]{1,0:T(8,128)S(1)} %get-tuple-element.67.piece_ref.refs_0_), channel_id=1, source_target_pairs={{0,16},{1,17},{2,18},{3,19},{4,20},{5,21},{6,22},{7,23},{8,24},{9,... | collective-permute-start | bytes 208904 | tf_op jit(solution)/shard_map/ppermute | solution.py:371
  49.6 7.8 %collective-permute-start.20 = (f32[136,128]{1,0:T(8,128)S(1)}, f32[136,128]{1,0:T(8,128)S(1)}, u32[]{:S(2)}, u32[]{:S(2)}) collective-permute-start(f32[136,128]{1,0:T(8,128)S(1)} %get-tuple-element.67.piece_ref.refs_0_), channel_id=1, source_target_pairs={{0,18},{1,19},{2,16},{3,17},{4,22},{5,23},{6,20},{7,21},{8,26},{9,... | collective-permute-start | bytes 208904 | tf_op jit(solution)/shard_map/ppermute | solution.py:371
  51.6 5.8 %collective-permute-start.19 = (f32[136,128]{1,0:T(8,128)S(1)}, f32[136,128]{1,0:T(8,128)S(1)}, u32[]{:S(2)}, u32[]{:S(2)}) collective-permute-start(f32[136,128]{1,0:T(8,128)S(1)} %get-tuple-element.67.piece_ref.refs_0_), channel_id=1, source_target_pairs={{0,2},{1,3},{2,0},{3,1},{4,6},{5,7},{6,4},{7,5},{8,10},{9,11},{10,... | collective-permute-start | bytes 208904 | tf_op jit(solution)/shard_map/ppermute | solution.py:371
  59.0 1.6 %collective-permute-start.21 = (f32[4,136,128]{2,1,0:T(8,128)S(1)}, f32[4,136,128]{2,1,0:T(8,128)S(1)}, u32[]{:S(2)}, u32[]{:S(2)}) collective-permute-start(f32[4,136,128]{2,1,0:T(8,128)S(1)} %get-tuple-element.74), channel_id=1, source_target_pairs={{0,4},{1,5},{2,6},{3,7},{4,0},{5,1},{6,2},{7,3},{8,12},{9,13},{10,... | collective-permute-start | bytes 835592 | tf_op jit(solution)/shard_map/ppermute | solution.py:371
  60.6 5.7 %collective-permute-start.24 = (f32[136,128]{1,0:T(8,128)S(1)}, f32[136,128]{1,0:T(8,128)S(1)}, u32[]{:S(2)}, u32[]{:S(2)}) collective-permute-start(f32[136,128]{1,0:T(8,128)S(1)} %get-tuple-element.77), channel_id=1, source_target_pairs={{0,9},{1,8},{2,11},{3,10},{4,13},{5,12},{6,15},{7,14},{8,1},{9,0},... | collective-permute-start | bytes 208904 | tf_op jit(solution)/shard_map/ppermute | solution.py:371
  62.7 5.7 %collective-permute-start.23 = (f32[136,128]{1,0:T(8,128)S(1)}, f32[136,128]{1,0:T(8,128)S(1)}, u32[]{:S(2)}, u32[]{:S(2)}) collective-permute-start(f32[136,128]{1,0:T(8,128)S(1)} %get-tuple-element.78), channel_id=1, source_target_pairs={{0,1},{1,0},{2,3},{3,2},{4,5},{5,4},{6,7},{7,6},{8,9},{9,8},{10,11... | collective-permute-start | bytes 208904 | tf_op jit(solution)/shard_map/ppermute | solution.py:371
  64.7 4.3 %collective-permute-start.22 = (f32[136,128]{1,0:T(8,128)S(1)}, f32[136,128]{1,0:T(8,128)S(1)}, u32[]{:S(2)}, u32[]{:S(2)}) collective-permute-start(f32[136,128]{1,0:T(8,128)S(1)} %get-tuple-element.79), channel_id=1, source_target_pairs={{0,8},{1,9},{2,10},{3,11},{4,12},{5,13},{6,14},{7,15},{8,0},{9,1},... | collective-permute-start | bytes 208904 | tf_op jit(solution)/shard_map/ppermute | solution.py:371
  70.2 1.2 %collective-permute-start.25 = (f32[8,128]{1,0:T(8,128)S(1)}, f32[8,128]{1,0:T(8,128)S(1)}, u32[]{:S(2)}, u32[]{:S(2)}) collective-permute-start(f32[8,128]{1,0:T(8,128)S(1)} %get-tuple-element.76), channel_id=1, source_target_pairs={{0,4},{1,5},{2,6},{3,7},{4,0},{5,1},{6,2},{7,3},{8,12},{9,13},{10,... | collective-permute-start | bytes 12296 | tf_op jit(solution)/shard_map/ppermute | solution.py:371
  71.4 3.9 %collective-permute-start.28 = (f32[8,128]{1,0:T(8,128)S(1)}, f32[8,128]{1,0:T(8,128)S(1)}, u32[]{:S(2)}, u32[]{:S(2)}) collective-permute-start(f32[8,128]{1,0:T(8,128)S(1)} %add.20), channel_id=1, source_target_pairs={{0,13},{1,12},{2,15},{3,14},{4,9},{5,8},{6,11},{7,10},{8,5},{9,4},... | collective-permute-start | bytes 12296 | tf_op jit(solution)/shard_map/ppermute | solution.py:371
  71.6 3.7 %collective-permute-start.27 = (f32[8,128]{1,0:T(8,128)S(1)}, f32[8,128]{1,0:T(8,128)S(1)}, u32[]{:S(2)}, u32[]{:S(2)}) collective-permute-start(f32[8,128]{1,0:T(8,128)S(1)} %add.20), channel_id=1, source_target_pairs={{0,5},{1,4},{2,7},{3,6},{4,1},{5,0},{6,3},{7,2},{8,13},{9,12},{10,... | collective-permute-start | bytes 12296 | tf_op jit(solution)/shard_map/ppermute | solution.py:371
  73.5 3.0 %collective-permute-start.26 = (f32[8,128]{1,0:T(8,128)S(1)}, f32[8,128]{1,0:T(8,128)S(1)}, u32[]{:S(2)}, u32[]{:S(2)}) collective-permute-start(f32[8,128]{1,0:T(8,128)S(1)} %add.20), channel_id=1, source_target_pairs={{0,12},{1,13},{2,14},{3,15},{4,8},{5,9},{6,10},{7,11},{8,4},{9,5},... | collective-permute-start | bytes 12296 | tf_op jit(solution)/shard_map/ppermute | solution.py:371
  76.5 4.8 %collective-permute-start.31 = (f32[8,128]{1,0:T(8,128)S(1)}, f32[8,128]{1,0:T(8,128)S(1)}, u32[]{:S(2)}, u32[]{:S(2)}) collective-permute-start(f32[8,128]{1,0:T(8,128)S(1)} %add_add_fusion.refs_1_), channel_id=1, source_target_pairs={{0,22},{1,23},{2,20},{3,21},{4,18},{5,19},{6,16},{7,17},{8,30},{9,... | collective-permute-start | bytes 12296 | tf_op jit(solution)/shard_map/ppermute | solution.py:371
  77.6 3.9 %collective-permute-start.30 = (f32[8,128]{1,0:T(8,128)S(1)}, f32[8,128]{1,0:T(8,128)S(1)}, u32[]{:S(2)}, u32[]{:S(2)}) collective-permute-start(f32[8,128]{1,0:T(8,128)S(1)} %add_add_fusion.refs_1_), channel_id=1, source_target_pairs={{0,6},{1,7},{2,4},{3,5},{4,2},{5,3},{6,0},{7,1},{8,14},{9,15},{10,... | collective-permute-start | bytes 12296 | tf_op jit(solution)/shard_map/ppermute | solution.py:371
  79.7 3.0 %collective-permute-start.29 = (f32[8,128]{1,0:T(8,128)S(1)}, f32[8,128]{1,0:T(8,128)S(1)}, u32[]{:S(2)}, u32[]{:S(2)}) collective-permute-start(f32[8,128]{1,0:T(8,128)S(1)} %add_add_fusion.refs_1_), channel_id=1, source_target_pairs={{0,20},{1,21},{2,22},{3,23},{4,16},{5,17},{6,18},{7,19},{8,28},{9,... | collective-permute-start | bytes 12296 | tf_op jit(solution)/shard_map/ppermute | solution.py:371

commit v6 on v5

--- a/solution.py
+++ b/solution.py
@@ -456,8 +456,8 @@
 
     def total_gram(gram):
         gram = gram + swap(gram, core)
-        gram = functools.reduce(jnp.add, [swap(gram, mask | core) for mask in far], gram)
-        return [gram] + [swap(gram, mask | core) for mask in near]
+        gram = functools.reduce(jnp.add, [swap(gram, mask | core) for mask in near], gram)
+        return [gram] + [swap(gram, mask | core) for mask in far]
 
     rows = vectors + DEGREE_ROWS
     block = 2 * 3 * rows * parts * width * width

time: 84.5 us -> 84.5 us (level)
  transfers between devices with their start and end apart: 32 -> 32, of which waited for: 20 -> 19; matrix products, arithmetic and copies ran while one was open for 0% -> 0% of each run, Pallas kernels for 14% -> 14%
where the time goes in v6:
time: 84.5 us; the launch traced here: 84.3 us
  starting transfers between devices  35.3 us (42%)
  Pallas kernels  26.2 us (31%)
  waiting for transfers between devices  22.6 us (27%)
    ppermute x32, starting transfers between devices, swap(): lax.ppermute(values, ('row', 'col'), [(index, index ^ mask) for index in...  35.3 us
    pallas_call x13, Pallas kernels, call(): pl.pallas_call(body, out_shape=out_shape, in_specs=[VMEM] * len(operands)...  25.2 us
    ppermute x32, waiting for transfers between devices, swap(): lax.ppermute(values, ('row', 'col'), [(index, index ^ mask) for index in...  22.6 us
  transfers between devices with their start and end apart: 32, of which 19 were waited for; matrix products, arithmetic and copies ran while one was open for 0% of the time, Pallas kernels for 14%

profile of v6, /device:TPU:0, one launch (start us, length us, event | category | flops | bytes accessed | tf_op | source)
XLA Modules:
  0.0 84.3 jit_solution(6957182795768580172)
XLA Ops:
  0.0 1.0 %fetch.1 = (f32[64,512]{1,0:T(8,128)S(1)}, f32[32,512]{1,0:T(8,128)S(1)}) custom-call(f32[64,512]{1,0:T(8,128)} %frames_ref.1, f32[32,512]{1,0:T(8,128)} %start_ref.1), custom_call_target="tpu_custom_call" | custom-call | flops 17179869184 | tf_op jit(solution)/shard_map/fetch/pallas_call | solution.py:386
  1.0 3.1 %collective-permute-start.7 = (f32[64,512]{1,0:T(8,128)S(1)}, f32[64,512]{1,0:T(8,128)S(1)}, u32[]{:S(2)}, u32[]{:S(2)}) collective-permute-start(f32[64,512]{1,0:T(8,128)S(1)} %get-tuple-element.41.refs_0_), channel_id=1, source_target_pairs={{0,1},{1,0},{2,3},{3,2},{4,5},{5,4},{6,7},{7,6},{8,9},{9,8},{10,11... | collective-permute-start | bytes 393224 | tf_op jit(solution)/shard_map/ppermute | solution.py:371
  4.1 2.6 %collective-permute-start.2 = (f32[64,512]{1,0:T(8,128)S(1)}, f32[64,512]{1,0:T(8,128)S(1)}, u32[]{:S(2)}, u32[]{:S(2)}) collective-permute-start(f32[64,512]{1,0:T(8,128)S(1)} %copy-done), channel_id=1, source_target_pairs={{0,2},{1,3},{2,0},{3,1},{4,6},{5,7},{6,4},{7,5},{8,10},{9,11},{10,... | collective-permute-start | bytes 393224 | tf_op jit(solution)/shard_map/ppermute | solution.py:371
  6.7 1.5 %collective-permute-start.3 = (f32[64,512]{1,0:T(8,128)S(1)}, f32[64,512]{1,0:T(8,128)S(1)}, u32[]{:S(2)}, u32[]{:S(2)}) collective-permute-start(f32[64,512]{1,0:T(8,128)S(1)} %get-tuple-element.41.refs_0_), channel_id=1, source_target_pairs={{0,8},{1,9},{2,10},{3,11},{4,12},{5,13},{6,14},{7,15},{8,0},{9,1},... | collective-permute-start | bytes 393224 | tf_op jit(solution)/shard_map/ppermute | solution.py:371
  8.3 1.5 %collective-permute-start.4 = (f32[64,512]{1,0:T(8,128)S(1)}, f32[64,512]{1,0:T(8,128)S(1)}, u32[]{:S(2)}, u32[]{:S(2)}) collective-permute-start(f32[64,512]{1,0:T(8,128)S(1)} %get-tuple-element.41.refs_0_), channel_id=1, source_target_pairs={{0,4},{1,5},{2,6},{3,7},{4,0},{5,1},{6,2},{7,3},{8,12},{9,13},{10,... | collective-permute-start | bytes 393224 | tf_op jit(solution)/shard_map/ppermute | solution.py:371
  9.8 1.4 %collective-permute-start.8 = (f32[64,512]{1,0:T(8,128)S(1)}, f32[64,512]{1,0:T(8,128)S(1)}, u32[]{:S(2)}, u32[]{:S(2)}) collective-permute-start(f32[64,512]{1,0:T(8,128)S(1)} %collective-permute-done.7.refs_5_), channel_id=1, source_target_pairs={{0,8},{1,9},{2,10},{3,11},{4,12},{5,13},{6,14},{7,15},{8,0},{9,1},... | collective-permute-start | bytes 393224 | tf_op jit(solution)/shard_map/ppermute | solution.py:371
  11.3 1.6 %collective-permute-done.2.refs_2_ = f32[64,512]{1,0:T(8,128)S(1)} collective-permute-done((f32[64,512]{1,0:T(8,128)S(1)}, f32[64,512]{1,0:T(8,128)S(1)}, u32[]{:S(2)}, u32[]{:S(2)}) %collective-permute-start.2) | collective-permute-done | bytes 131104 | tf_op jit(solution)/shard_map/ppermute | solution.py:371
  14.1 0.8 collective-permute-start.6
  15.3 4.3 %build_near.1 = (bf16[512,2048]{1,0:T(8,128)(2,1)S(1)}, bf16[512,2048]{1,0:T(8,128)(2,1)S(1)}, bf16[512,2048]{1,0:T(8,128)(2,1)S(1)}, bf16[512,2048]{1,0:T(8,128...) custom-call(f32[64,512]{1,0:T(8,128)S(1)} %get-tuple-element.41.refs, ...), custom_call_target="tpu_custom_call" | custom-call | flops 1 | tf_op jit(solution)/shard_map/build_near/pallas_call | solution.py:18
  19.8 5.3 %build_far.1 = (bf16[512,2048]{1,0:T(8,128)(2,1)S(1)}, bf16[512,2048]{1,0:T(8,128)(2,1)S(1)}, bf16[512,2048]{1,0:T(8,128)(2,1)S(1)}, bf16[512,2048]{1,0:T(8,128)...) custom-call(bf16[1536,256]{1,0:T(8,128)(2,1)S(1)} %get-tuple-element, ...), custom_call_target="tpu_custom_call" | custom-call | flops 1 | tf_op jit(solution)/shard_map/build_far/pallas_call | solution.py:18
  25.1 2.0 %collective-permute-start.13 = (f32[144,128]{1,0:T(8,128)S(1)}, f32[144,128]{1,0:T(8,128)S(1)}, u32[]{:S(2)}, u32[]{:S(2)}) collective-permute-start(f32[144,128]{1,0:T(8,128)S(1)} %get-tuple-element.46.refs_0_), channel_id=1, source_target_pairs={{0,18},{1,19},{2,16},{3,17},{4,22},{5,23},{6,20},{7,21},{8,26},{9,... | collective-permute-start | bytes 221192 | tf_op jit(solution)/shard_map/ppermute | solution.py:371
  27.1 1.3 %collective-permute-start.12 = (f32[144,128]{1,0:T(8,128)S(1)}, f32[144,128]{1,0:T(8,128)S(1)}, u32[]{:S(2)}, u32[]{:S(2)}) collective-permute-start(f32[144,128]{1,0:T(8,128)S(1)} %get-tuple-element.46.refs_0_), channel_id=1, source_target_pairs={{0,2},{1,3},{2,0},{3,1},{4,6},{5,7},{6,4},{7,5},{8,10},{9,11},{10,... | collective-permute-start | bytes 221192 | tf_op jit(solution)/shard_map/ppermute | solution.py:371
  28.5 1.1 %collective-permute-start.11 = (f32[144,128]{1,0:T(8,128)S(1)}, f32[144,128]{1,0:T(8,128)S(1)}, u32[]{:S(2)}, u32[]{:S(2)}) collective-permute-start(f32[144,128]{1,0:T(8,128)S(1)} %get-tuple-element.46.refs_0_), channel_id=1, source_target_pairs={{0,16},{1,17},{2,18},{3,19},{4,20},{5,21},{6,22},{7,23},{8,24},{9,... | collective-permute-start | bytes 221192 | tf_op jit(solution)/shard_map/ppermute | solution.py:371
  29.5 5.2 %collective-permute-done.13.refs_3_ = f32[144,128]{1,0:T(8,128)S(1)} collective-permute-done((f32[144,128]{1,0:T(8,128)S(1)}, f32[144,128]{1,0:T(8,128)S(1)}, u32[]{:S(2)}, u32[]{:S(2)}) %collective-permute-start.13) | collective-permute-done | bytes 73760 | tf_op jit(solution)/shard_map/ppermute | solution.py:371
  34.7 0.7 collective-permute-done.12.refs_2_
  35.5 3.1 %first_odd.1 = (f32[4,136,128]{2,1,0:T(8,128)S(1)}, f32[1,512]{1,0:T(1,128)S(1)}, bf16[96,2048]{1,0:T(8,128)(2,1)S(1)}) custom-call(f32[144,128]{1,0:T(8,128)S(1)} %get-tuple-element.46.refs_0_, f32[144,128]{1,0:T(8,128)S(1)} %collective-permute-done.11.refs_1_, f32[144,128]{1,0:T(8,128)S(1)} %collective-permute-done.12.refs_2_, ...), custom_call_target="tpu_custom_call" | custom-call | flops 1207959552 | tf_op jit(solution)/shard_map/first_odd/pallas_call | solution.py:18
  38.7 2.2 %first_even.1 = f32[3,136,128]{2,1,0:T(8,128)S(1)} custom-call(bf16[96,2048]{1,0:T(8,128)(2,1)S(1)} %get-tuple-element.64.refs_0_, bf16[512,2048]{1,0:T(8,128)(2,1)S(1)} %get-tuple-element.47.refs_4_.refs_1_.refs_2_.refs_0_, bf16[512,2048]{1,0:T(8,128)(2,1)S(1)} %get-tuple-element.48.refs_5_.refs_2_.refs_3_.refs_1_, ...), custom_call_target="tpu_custom_call" | custom-call | flops 905969664 | tf_op jit(solution)/shard_map/first_even/pallas_call | solution.py:18
  41.1 1.1 %collective-permute-start.17 = (f32[136,128]{1,0:T(8,128)S(1)}, f32[136,128]{1,0:T(8,128)S(1)}, u32[]{:S(2)}, u32[]{:S(2)}) collective-permute-start(f32[136,128]{1,0:T(8,128)S(1)} %get-tuple-element.80), channel_id=1, source_target_pairs={{0,9},{1,8},{2,11},{3,10},{4,13},{5,12},{6,15},{7,14},{8,1},{9,0},... | collective-permute-start | bytes 208904 | tf_op jit(solution)/shard_map/ppermute | solution.py:371
  42.1 1.8 %collective-permute-start.16 = (f32[136,128]{1,0:T(8,128)S(1)}, f32[136,128]{1,0:T(8,128)S(1)}, u32[]{:S(2)}, u32[]{:S(2)}) collective-permute-start(f32[136,128]{1,0:T(8,128)S(1)} %get-tuple-element.81), channel_id=1, source_target_pairs={{0,1},{1,0},{2,3},{3,2},{4,5},{5,4},{6,7},{7,6},{8,9},{9,8},{10,11... | collective-permute-start | bytes 208904 | tf_op jit(solution)/shard_map/ppermute | solution.py:371
  43.9 0.7 collective-permute-start.15
  44.6 0.8 first_own.1.refs_1_
  45.5 1.6 %collective-permute-done.17.refs_5_ = f32[136,128]{1,0:T(8,128)S(1)} collective-permute-done((f32[136,128]{1,0:T(8,128)S(1)}, f32[136,128]{1,0:T(8,128)S(1)}, u32[]{:S(2)}, u32[]{:S(2)}) %collective-permute-start.17) | collective-permute-done | bytes 69664 | tf_op jit(solution)/shard_map/ppermute | solution.py:371
  47.0 0.9 %collective-permute-done.16.refs_4_ = f32[136,128]{1,0:T(8,128)S(1)} collective-permute-done((f32[136,128]{1,0:T(8,128)S(1)}, f32[136,128]{1,0:T(8,128)S(1)}, u32[]{:S(2)}, u32[]{:S(2)}) %collective-permute-start.16) | collective-permute-done | bytes 69664 | tf_op jit(solution)/shard_map/ppermute | solution.py:371
  48.5 1.1 %collective-permute-start.18 = (f32[136,128]{1,0:T(8,128)S(1)}, f32[136,128]{1,0:T(8,128)S(1)}, u32[]{:S(2)}, u32[]{:S(2)}) collective-permute-start(f32[136,128]{1,0:T(8,128)S(1)} %get-tuple-element.67.piece_ref.refs_0_), channel_id=1, source_target_pairs={{0,16},{1,17},{2,18},{3,19},{4,20},{5,21},{6,22},{7,23},{8,24},{9,... | collective-permute-start | bytes 208904 | tf_op jit(solution)/shard_map/ppermute | solution.py:371
  49.6 1.9 %collective-permute-start.20 = (f32[136,128]{1,0:T(8,128)S(1)}, f32[136,128]{1,0:T(8,128)S(1)}, u32[]{:S(2)}, u32[]{:S(2)}) collective-permute-start(f32[136,128]{1,0:T(8,128)S(1)} %get-tuple-element.67.piece_ref.refs_0_), channel_id=1, source_target_pairs={{0,18},{1,19},{2,16},{3,17},{4,22},{5,23},{6,20},{7,21},{8,26},{9,... | collective-permute-start | bytes 208904 | tf_op jit(solution)/shard_map/ppermute | solution.py:371
  51.6 1.3 %collective-permute-start.19 = (f32[136,128]{1,0:T(8,128)S(1)}, f32[136,128]{1,0:T(8,128)S(1)}, u32[]{:S(2)}, u32[]{:S(2)}) collective-permute-start(f32[136,128]{1,0:T(8,128)S(1)} %get-tuple-element.67.piece_ref.refs_0_), channel_id=1, source_target_pairs={{0,2},{1,3},{2,0},{3,1},{4,6},{5,7},{6,4},{7,5},{8,10},{9,11},{10,... | collective-permute-start | bytes 208904 | tf_op jit(solution)/shard_map/ppermute | solution.py:371
  52.9 1.5 %second_part.2 = (f32[4,32,512]{2,1,0:T(8,128)S(1)}, f32[4,32,512]{2,1,0:T(8,128)S(1)}) custom-call(f32[136,128]{1,0:T(8,128)S(1)} %get-tuple-element.67.piece_ref.refs_0_, bf16[512,2048]{1,0:T(8,128)(2,1)S(1)} %get-tuple-element.47.refs_4_.refs_1_.refs_2_.refs_0_, bf16[512,2048]{1,0:T(8,128)(2,1)S(1)} %get-tuple-element.48.refs_5_.refs_2_.refs_3_.refs_1_, ...), custom_call_target="tpu_custom_call" | custom-call | flops 603979776 | tf_op jit(solution)/shard_map/second_part/pallas_call | solution.py:18
  54.4 1.6 %second_part.3 = (f32[4,32,512]{2,1,0:T(8,128)S(1)}, f32[4,32,512]{2,1,0:T(8,128)S(1)}) custom-call(f32[136,128]{1,0:T(8,128)S(1)} %collective-permute-done.18.piece_ref.refs_1_, bf16[512,2048]{1,0:T(8,128)(2,1)S(1)} %get-tuple-element.49.refs_6_.refs_3_.refs_4_.refs_0_, bf16[512,2048]{1,0:T(8,128)(2,1)S(1)} %get-tuple-element.50.refs_7_.refs_4_.refs_5_.refs_1_, ...), custom_call_target="tpu_custom_call" | custom-call | flops 603979776 | tf_op jit(solution)/shard_map/second_part/pallas_call | solution.py:18
  56.0 1.4 %collective-permute-done.20.refs_3_ = f32[136,128]{1,0:T(8,128)S(1)} collective-permute-done((f32[136,128]{1,0:T(8,128)S(1)}, f32[136,128]{1,0:T(8,128)S(1)}, u32[]{:S(2)}, u32[]{:S(2)}) %collective-permute-start.20) | collective-permute-done | bytes 69664 | tf_op jit(solution)/shard_map/ppermute | solution.py:371
  57.4 1.6 %second_odd.1 = (f32[4,136,128]{2,1,0:T(8,128)S(1)}, f32[8,128]{1,0:T(8,128)S(1)}, bf16[64,1024]{1,0:T(8,128)(2,1)S(1)}) custom-call(f32[136,128]{1,0:T(8,128)S(1)} %get-tuple-element.67.piece_ref.refs_0_, f32[136,128]{1,0:T(8,128)S(1)} %collective-permute-done.18.piece_ref.refs_1_, f32[136,128]{1,0:T(8,128)S(1)} %collective-permute-done.19.refs_2_, ...), custom_call_target="tpu_custom_call" | custom-call | flops 1207959552 | tf_op jit(solution)/shard_map/second_odd/pallas_call | solution.py:18
  59.0 1.2 %second_even.1 = f32[3,136,128]{2,1,0:T(8,128)S(1)} custom-call(bf16[64,1024]{1,0:T(8,128)(2,1)S(1)} %get-tuple-element.71.refs_0_, f32[8,128]{1,0:T(8,128)S(1)} %get-tuple-element.72.refs_1_, f32[4,32,512]{2,1,0:T(8,128)S(1)} %get-tuple-element.73.refs_2_, bf16[512,2048]{1,0:T(8,128)(2,1)S(1)} %get-tuple-element.51.refs_8_.refs_5_.refs_6_.refs_3_.refs_4_, ...), custom_call_target="tpu_custom_call" | custom-call | flops 905969664 | tf_op jit(solution)/shard_map/second_even/pallas_call | solution.py:18
  60.6 2.1 %collective-permute-start.24 = (f32[136,128]{1,0:T(8,128)S(1)}, f32[136,128]{1,0:T(8,128)S(1)}, u32[]{:S(2)}, u32[]{:S(2)}) collective-permute-start(f32[136,128]{1,0:T(8,128)S(1)} %get-tuple-element.77), channel_id=1, source_target_pairs={{0,9},{1,8},{2,11},{3,10},{4,13},{5,12},{6,15},{7,14},{8,1},{9,0},... | collective-permute-start | bytes 208904 | tf_op jit(solution)/shard_map/ppermute | solution.py:371
  62.7 2.0 %collective-permute-start.23 = (f32[136,128]{1,0:T(8,128)S(1)}, f32[136,128]{1,0:T(8,128)S(1)}, u32[]{:S(2)}, u32[]{:S(2)}) collective-permute-start(f32[136,128]{1,0:T(8,128)S(1)} %get-tuple-element.78), channel_id=1, source_target_pairs={{0,1},{1,0},{2,3},{3,2},{4,5},{5,4},{6,7},{7,6},{8,9},{9,8},{10,11... | collective-permute-start | bytes 208904 | tf_op jit(solution)/shard_map/ppermute | solution.py:371
  65.2 1.1 %collective-permute-done.24.refs_5_ = f32[136,128]{1,0:T(8,128)S(1)} collective-permute-done((f32[136,128]{1,0:T(8,128)S(1)}, f32[136,128]{1,0:T(8,128)S(1)}, u32[]{:S(2)}, u32[]{:S(2)}) %collective-permute-start.24) | collective-permute-done | bytes 69664 | tf_op jit(solution)/shard_map/ppermute | solution.py:371
  66.3 2.1 %collective-permute-done.23.refs_4_ = f32[136,128]{1,0:T(8,128)S(1)} collective-permute-done((f32[136,128]{1,0:T(8,128)S(1)}, f32[136,128]{1,0:T(8,128)S(1)}, u32[]{:S(2)}, u32[]{:S(2)}) %collective-permute-start.23) | collective-permute-done | bytes 69664 | tf_op jit(solution)/shard_map/ppermute | solution.py:371
  69.0 1.2 %grown_two.1 = (f32[32,512]{1,0:T(8,128)S(1)}, f32[8,128]{1,0:T(8,128)S(1)}) custom-call(f32[1,512]{1,0:T(1,128)S(1)} %get-tuple-element.66.refs_0_, f32[136,128]{1,0:T(8,128)S(1)} %second_own.1.refs_1_, f32[136,128]{1,0:T(8,128)S(1)} %slice_bitcast_fusion.3.refs_2_, f32[136,128]{1,0:T(8,128)S(1)} %collective-permute-done.22.refs_3_, ...), custom_call_target="tpu_custom_call" | custom-call | tf_op jit(solution)/shard_map/grown_two/pallas_call | solution.py:18
  70.3 1.2 %collective-permute-done.25 = f32[8,128]{1,0:T(8,128)S(1)} collective-permute-done((f32[8,128]{1,0:T(8,128)S(1)}, f32[8,128]{1,0:T(8,128)S(1)}, u32[]{:S(2)}, u32[]{:S(2)}) %collective-permute-start.25) | collective-permute-done | bytes 4128 | tf_op jit(solution)/shard_map/ppermute | solution.py:371
  71.4 0.8 collective-permute-start.28
  72.2 2.4 %collective-permute-start.27 = (f32[8,128]{1,0:T(8,128)S(1)}, f32[8,128]{1,0:T(8,128)S(1)}, u32[]{:S(2)}, u32[]{:S(2)}) collective-permute-start(f32[8,128]{1,0:T(8,128)S(1)} %add.20), channel_id=1, source_target_pairs={{0,6},{1,7},{2,4},{3,5},{4,2},{5,3},{6,0},{7,1},{8,14},{9,15},{10,... | collective-permute-start | bytes 12296 | tf_op jit(solution)/shard_map/ppermute | solution.py:371
  74.6 0.7 collective-permute-start.26
  75.3 0.9 %collective-permute-done.28 = f32[8,128]{1,0:T(8,128)S(1)} collective-permute-done((f32[8,128]{1,0:T(8,128)S(1)}, f32[8,128]{1,0:T(8,128)S(1)}, u32[]{:S(2)}, u32[]{:S(2)}) %collective-permute-start.28) | collective-permute-done | bytes 4128 | tf_op jit(solution)/shard_map/ppermute | solution.py:371
  76.3 1.4 %collective-permute-done.26 = f32[8,128]{1,0:T(8,128)S(1)} collective-permute-done((f32[8,128]{1,0:T(8,128)S(1)}, f32[8,128]{1,0:T(8,128)S(1)}, u32[]{:S(2)}, u32[]{:S(2)}) %collective-permute-start.26) | collective-permute-done | bytes 4128 | tf_op jit(solution)/shard_map/ppermute | solution.py:371
  77.6 0.8 collective-permute-start.31
  78.5 1.2 %collective-permute-start.30 = (f32[8,128]{1,0:T(8,128)S(1)}, f32[8,128]{1,0:T(8,128)S(1)}, u32[]{:S(2)}, u32[]{:S(2)}) collective-permute-start(f32[8,128]{1,0:T(8,128)S(1)} %add_add_fusion.refs_1_), channel_id=1, source_target_pairs={{0,5},{1,4},{2,7},{3,6},{4,1},{5,0},{6,3},{7,2},{8,13},{9,12},{10,... | collective-permute-start | bytes 12296 | tf_op jit(solution)/shard_map/ppermute | solution.py:371
  79.7 0.9 %collective-permute-start.29 = (f32[8,128]{1,0:T(8,128)S(1)}, f32[8,128]{1,0:T(8,128)S(1)}, u32[]{:S(2)}, u32[]{:S(2)}) collective-permute-start(f32[8,128]{1,0:T(8,128)S(1)} %add_add_fusion.refs_1_), channel_id=1, source_target_pairs={{0,12},{1,13},{2,14},{3,15},{4,8},{5,9},{6,10},{7,11},{8,4},{9,5},... | collective-permute-start | bytes 12296 | tf_op jit(solution)/shard_map/ppermute | solution.py:371
  80.6 0.9 %collective-permute-done.31.refs_4_ = f32[8,128]{1,0:T(8,128)S(1)} collective-permute-done((f32[8,128]{1,0:T(8,128)S(1)}, f32[8,128]{1,0:T(8,128)S(1)}, u32[]{:S(2)}, u32[]{:S(2)}) %collective-permute-start.31) | collective-permute-done | bytes 4128 | tf_op jit(solution)/shard_map/ppermute | solution.py:371
  81.6 1.1 %collective-permute-done.29.refs_2_ = f32[8,128]{1,0:T(8,128)S(1)} collective-permute-done((f32[8,128]{1,0:T(8,128)S(1)}, f32[8,128]{1,0:T(8,128)S(1)}, u32[]{:S(2)}, u32[]{:S(2)}) %collective-permute-start.29) | collective-permute-done | bytes 4128 | tf_op jit(solution)/shard_map/ppermute | solution.py:371
  82.7 1.6 %finish.1 = f32[32,512]{1,0:T(8,128)} custom-call(f32[32,512]{1,0:T(8,128)S(1)} %get-tuple-element.75.refs_0_, f32[8,128]{1,0:T(8,128)S(1)} %add_add_fusion.refs_1_, f32[8,128]{1,0:T(8,128)S(1)} %collective-permute-done.29.refs_2_, f32[8,128]{1,0:T(8,128)S(1)} %collective-permute-done.30.refs_3_, f32[8,128]{1,0:T(8,128)S(1)} %collective-permute-done.31.refs_4_), custom_call_target="tpu_custom_call" | custom-call | tf_op jit(solution)/shard_map/finish/pallas_call | solution.py:18
  (40 shorter events, 4.3 us)
Async XLA Ops:
  0.0 4.1 %copy-start = (f32[64,512]{1,0:T(8,128)S(1)}, f32[64,512]{1,0:T(8,128)}, u32[]{:S(2)}) copy-start(f32[64,512]{1,0:T(8,128)} %frames_ref.1) | copy-start | bytes 393220
  1.0 8.8 %collective-permute-start.7 = (f32[64,512]{1,0:T(8,128)S(1)}, f32[64,512]{1,0:T(8,128)S(1)}, u32[]{:S(2)}, u32[]{:S(2)}) collective-permute-start(f32[64,512]{1,0:T(8,128)S(1)} %get-tuple-element.41.refs_0_), channel_id=1, source_target_pairs={{0,1},{1,0},{2,3},{3,2},{4,5},{5,4},{6,7},{7,6},{8,9},{9,8},{10,11... | collective-permute-start | bytes 393224 | tf_op jit(solution)/shard_map/ppermute | solution.py:371
  4.1 8.7 %collective-permute-start.2 = (f32[64,512]{1,0:T(8,128)S(1)}, f32[64,512]{1,0:T(8,128)S(1)}, u32[]{:S(2)}, u32[]{:S(2)}) collective-permute-start(f32[64,512]{1,0:T(8,128)S(1)} %copy-done), channel_id=1, source_target_pairs={{0,2},{1,3},{2,0},{3,1},{4,6},{5,7},{6,4},{7,5},{8,10},{9,11},{10,... | collective-permute-start | bytes 393224 | tf_op jit(solution)/shard_map/ppermute | solution.py:371
  6.7 6.1 %collective-permute-start.3 = (f32[64,512]{1,0:T(8,128)S(1)}, f32[64,512]{1,0:T(8,128)S(1)}, u32[]{:S(2)}, u32[]{:S(2)}) collective-permute-start(f32[64,512]{1,0:T(8,128)S(1)} %get-tuple-element.41.refs_0_), channel_id=1, source_target_pairs={{0,8},{1,9},{2,10},{3,11},{4,12},{5,13},{6,14},{7,15},{8,0},{9,1},... | collective-permute-start | bytes 393224 | tf_op jit(solution)/shard_map/ppermute | solution.py:371
  8.2 5.7 %collective-permute-start = (f32[64,512]{1,0:T(8,128)S(1)}, f32[64,512]{1,0:T(8,128)S(1)}, u32[]{:S(2)}, u32[]{:S(2)}) collective-permute-start(f32[64,512]{1,0:T(8,128)S(1)} %get-tuple-element.41.refs_0_), channel_id=1, source_target_pairs={{0,20},{1,21},{2,22},{3,23},{4,16},{5,17},{6,18},{7,19},{8,28},{9,... | collective-permute-start | bytes 393224 | tf_op jit(solution)/shard_map/ppermute | solution.py:371
  8.3 5.8 %collective-permute-start.4 = (f32[64,512]{1,0:T(8,128)S(1)}, f32[64,512]{1,0:T(8,128)S(1)}, u32[]{:S(2)}, u32[]{:S(2)}) collective-permute-start(f32[64,512]{1,0:T(8,128)S(1)} %get-tuple-element.41.refs_0_), channel_id=1, source_target_pairs={{0,4},{1,5},{2,6},{3,7},{4,0},{5,1},{6,2},{7,3},{8,12},{9,13},{10,... | collective-permute-start | bytes 393224 | tf_op jit(solution)/shard_map/ppermute | solution.py:371
  9.8 5.4 %collective-permute-start.8 = (f32[64,512]{1,0:T(8,128)S(1)}, f32[64,512]{1,0:T(8,128)S(1)}, u32[]{:S(2)}, u32[]{:S(2)}) collective-permute-start(f32[64,512]{1,0:T(8,128)S(1)} %collective-permute-done.7.refs_5_), channel_id=1, source_target_pairs={{0,8},{1,9},{2,10},{3,11},{4,12},{5,13},{6,14},{7,15},{8,0},{9,1},... | collective-permute-start | bytes 393224 | tf_op jit(solution)/shard_map/ppermute | solution.py:371
  12.8 7.0 %collective-permute-start.9 = (f32[64,512]{1,0:T(8,128)S(1)}, f32[64,512]{1,0:T(8,128)S(1)}, u32[]{:S(2)}, u32[]{:S(2)}) collective-permute-start(f32[64,512]{1,0:T(8,128)S(1)} %collective-permute-done.7.refs_5_), channel_id=1, source_target_pairs={{0,4},{1,5},{2,6},{3,7},{4,0},{5,1},{6,2},{7,3},{8,12},{9,13},{10,... | collective-permute-start | bytes 393224 | tf_op jit(solution)/shard_map/ppermute | solution.py:371
  12.8 2.4 %collective-permute-start.5 = (f32[64,512]{1,0:T(8,128)S(1)}, f32[64,512]{1,0:T(8,128)S(1)}, u32[]{:S(2)}, u32[]{:S(2)}) collective-permute-start(f32[64,512]{1,0:T(8,128)S(1)} %collective-permute-done.3.refs_3_), channel_id=1, source_target_pairs={{0,4},{1,5},{2,6},{3,7},{4,0},{5,1},{6,2},{7,3},{8,12},{9,13},{10,... | collective-permute-start | bytes 393224 | tf_op jit(solution)/shard_map/ppermute | solution.py:371
  13.9 1.3 %collective-permute-start.1 = (f32[64,512]{1,0:T(8,128)S(1)}, f32[64,512]{1,0:T(8,128)S(1)}, u32[]{:S(2)}, u32[]{:S(2)}) collective-permute-start(f32[64,512]{1,0:T(8,128)S(1)} %collective-permute-done), channel_id=1, source_target_pairs={{0,4},{1,5},{2,6},{3,7},{4,0},{5,1},{6,2},{7,3},{8,12},{9,13},{10,... | collective-permute-start | bytes 393224 | tf_op jit(solution)/shard_map/ppermute | solution.py:371
  14.1 5.7 %collective-permute-start.6 = (f32[64,512]{1,0:T(8,128)S(1)}, f32[64,512]{1,0:T(8,128)S(1)}, u32[]{:S(2)}, u32[]{:S(2)}) collective-permute-start(f32[64,512]{1,0:T(8,128)S(1)} %collective-permute-done.2.refs_2_), channel_id=1, source_target_pairs={{0,16},{1,17},{2,18},{3,19},{4,20},{5,21},{6,22},{7,23},{8,24},{9,... | collective-permute-start | bytes 393224 | tf_op jit(solution)/shard_map/ppermute | solution.py:371
  15.2 4.6 %collective-permute-start.10 = (f32[64,512]{1,0:T(8,128)S(1)}, f32[64,512]{1,0:T(8,128)S(1)}, u32[]{:S(2)}, u32[]{:S(2)}) collective-permute-start(f32[64,512]{1,0:T(8,128)S(1)} %collective-permute-done.8.refs_6_), channel_id=1, source_target_pairs={{0,4},{1,5},{2,6},{3,7},{4,0},{5,1},{6,2},{7,3},{8,12},{9,13},{10,... | collective-permute-start | bytes 393224 | tf_op jit(solution)/shard_map/ppermute | solution.py:371
  25.1 9.7 %collective-permute-start.13 = (f32[144,128]{1,0:T(8,128)S(1)}, f32[144,128]{1,0:T(8,128)S(1)}, u32[]{:S(2)}, u32[]{:S(2)}) collective-permute-start(f32[144,128]{1,0:T(8,128)S(1)} %get-tuple-element.46.refs_0_), channel_id=1, source_target_pairs={{0,18},{1,19},{2,16},{3,17},{4,22},{5,23},{6,20},{7,21},{8,26},{9,... | collective-permute-start | bytes 221192 | tf_op jit(solution)/shard_map/ppermute | solution.py:371
  27.1 8.3 %collective-permute-start.12 = (f32[144,128]{1,0:T(8,128)S(1)}, f32[144,128]{1,0:T(8,128)S(1)}, u32[]{:S(2)}, u32[]{:S(2)}) collective-permute-start(f32[144,128]{1,0:T(8,128)S(1)} %get-tuple-element.46.refs_0_), channel_id=1, source_target_pairs={{0,2},{1,3},{2,0},{3,1},{4,6},{5,7},{6,4},{7,5},{8,10},{9,11},{10,... | collective-permute-start | bytes 221192 | tf_op jit(solution)/shard_map/ppermute | solution.py:371
  28.5 7.0 %collective-permute-start.11 = (f32[144,128]{1,0:T(8,128)S(1)}, f32[144,128]{1,0:T(8,128)S(1)}, u32[]{:S(2)}, u32[]{:S(2)}) collective-permute-start(f32[144,128]{1,0:T(8,128)S(1)} %get-tuple-element.46.refs_0_), channel_id=1, source_target_pairs={{0,16},{1,17},{2,18},{3,19},{4,20},{5,21},{6,22},{7,23},{8,24},{9,... | collective-permute-start | bytes 221192 | tf_op jit(solution)/shard_map/ppermute | solution.py:371
  38.6 2.4 %collective-permute-start.14 = (f32[4,136,128]{2,1,0:T(8,128)S(1)}, f32[4,136,128]{2,1,0:T(8,128)S(1)}, u32[]{:S(2)}, u32[]{:S(2)}) collective-permute-start(f32[4,136,128]{2,1,0:T(8,128)S(1)} %get-tuple-element.65), channel_id=1, source_target_pairs={{0,4},{1,5},{2,6},{3,7},{4,0},{5,1},{6,2},{7,3},{8,12},{9,13},{10,... | collective-permute-start | bytes 835592 | tf_op jit(solution)/shard_map/ppermute | solution.py:371
  41.1 5.9 %collective-permute-start.17 = (f32[136,128]{1,0:T(8,128)S(1)}, f32[136,128]{1,0:T(8,128)S(1)}, u32[]{:S(2)}, u32[]{:S(2)}) collective-permute-start(f32[136,128]{1,0:T(8,128)S(1)} %get-tuple-element.80), channel_id=1, source_target_pairs={{0,9},{1,8},{2,11},{3,10},{4,13},{5,12},{6,15},{7,14},{8,1},{9,0},... | collective-permute-start | bytes 208904 | tf_op jit(solution)/shard_map/ppermute | solution.py:371
  42.1 5.8 %collective-permute-start.16 = (f32[136,128]{1,0:T(8,128)S(1)}, f32[136,128]{1,0:T(8,128)S(1)}, u32[]{:S(2)}, u32[]{:S(2)}) collective-permute-start(f32[136,128]{1,0:T(8,128)S(1)} %get-tuple-element.81), channel_id=1, source_target_pairs={{0,1},{1,0},{2,3},{3,2},{4,5},{5,4},{6,7},{7,6},{8,9},{9,8},{10,11... | collective-permute-start | bytes 208904 | tf_op jit(solution)/shard_map/ppermute | solution.py:371
  43.9 4.3 %collective-permute-start.15 = (f32[136,128]{1,0:T(8,128)S(1)}, f32[136,128]{1,0:T(8,128)S(1)}, u32[]{:S(2)}, u32[]{:S(2)}) collective-permute-start(f32[136,128]{1,0:T(8,128)S(1)} %get-tuple-element.82), channel_id=1, source_target_pairs={{0,8},{1,9},{2,10},{3,11},{4,12},{5,13},{6,14},{7,15},{8,0},{9,1},... | collective-permute-start | bytes 208904 | tf_op jit(solution)/shard_map/ppermute | solution.py:371
  48.5 5.9 %collective-permute-start.18 = (f32[136,128]{1,0:T(8,128)S(1)}, f32[136,128]{1,0:T(8,128)S(1)}, u32[]{:S(2)}, u32[]{:S(2)}) collective-permute-start(f32[136,128]{1,0:T(8,128)S(1)} %get-tuple-element.67.piece_ref.refs_0_), channel_id=1, source_target_pairs={{0,16},{1,17},{2,18},{3,19},{4,20},{5,21},{6,22},{7,23},{8,24},{9,... | collective-permute-start | bytes 208904 | tf_op jit(solution)/shard_map/ppermute | solution.py:371
  49.6 7.8 %collective-permute-start.20 = (f32[136,128]{1,0:T(8,128)S(1)}, f32[136,128]{1,0:T(8,128)S(1)}, u32[]{:S(2)}, u32[]{:S(2)}) collective-permute-start(f32[136,128]{1,0:T(8,128)S(1)} %get-tuple-element.67.piece_ref.refs_0_), channel_id=1, source_target_pairs={{0,18},{1,19},{2,16},{3,17},{4,22},{5,23},{6,20},{7,21},{8,26},{9,... | collective-permute-start | bytes 208904 | tf_op jit(solution)/shard_map/ppermute | solution.py:371
  51.6 5.8 %collective-permute-start.19 = (f32[136,128]{1,0:T(8,128)S(1)}, f32[136,128]{1,0:T(8,128)S(1)}, u32[]{:S(2)}, u32[]{:S(2)}) collective-permute-start(f32[136,128]{1,0:T(8,128)S(1)} %get-tuple-element.67.piece_ref.refs_0_), channel_id=1, source_target_pairs={{0,2},{1,3},{2,0},{3,1},{4,6},{5,7},{6,4},{7,5},{8,10},{9,11},{10,... | collective-permute-start | bytes 208904 | tf_op jit(solution)/shard_map/ppermute | solution.py:371
  59.0 1.6 %collective-permute-start.21 = (f32[4,136,128]{2,1,0:T(8,128)S(1)}, f32[4,136,128]{2,1,0:T(8,128)S(1)}, u32[]{:S(2)}, u32[]{:S(2)}) collective-permute-start(f32[4,136,128]{2,1,0:T(8,128)S(1)} %get-tuple-element.74), channel_id=1, source_target_pairs={{0,4},{1,5},{2,6},{3,7},{4,0},{5,1},{6,2},{7,3},{8,12},{9,13},{10,... | collective-permute-start | bytes 835592 | tf_op jit(solution)/shard_map/ppermute | solution.py:371
  60.6 5.7 %collective-permute-start.24 = (f32[136,128]{1,0:T(8,128)S(1)}, f32[136,128]{1,0:T(8,128)S(1)}, u32[]{:S(2)}, u32[]{:S(2)}) collective-permute-start(f32[136,128]{1,0:T(8,128)S(1)} %get-tuple-element.77), channel_id=1, source_target_pairs={{0,9},{1,8},{2,11},{3,10},{4,13},{5,12},{6,15},{7,14},{8,1},{9,0},... | collective-permute-start | bytes 208904 | tf_op jit(solution)/shard_map/ppermute | solution.py:371
  62.7 5.7 %collective-permute-start.23 = (f32[136,128]{1,0:T(8,128)S(1)}, f32[136,128]{1,0:T(8,128)S(1)}, u32[]{:S(2)}, u32[]{:S(2)}) collective-permute-start(f32[136,128]{1,0:T(8,128)S(1)} %get-tuple-element.78), channel_id=1, source_target_pairs={{0,1},{1,0},{2,3},{3,2},{4,5},{5,4},{6,7},{7,6},{8,9},{9,8},{10,11... | collective-permute-start | bytes 208904 | tf_op jit(solution)/shard_map/ppermute | solution.py:371
  64.7 4.3 %collective-permute-start.22 = (f32[136,128]{1,0:T(8,128)S(1)}, f32[136,128]{1,0:T(8,128)S(1)}, u32[]{:S(2)}, u32[]{:S(2)}) collective-permute-start(f32[136,128]{1,0:T(8,128)S(1)} %get-tuple-element.79), channel_id=1, source_target_pairs={{0,8},{1,9},{2,10},{3,11},{4,12},{5,13},{6,14},{7,15},{8,0},{9,1},... | collective-permute-start | bytes 208904 | tf_op jit(solution)/shard_map/ppermute | solution.py:371
  70.2 1.2 %collective-permute-start.25 = (f32[8,128]{1,0:T(8,128)S(1)}, f32[8,128]{1,0:T(8,128)S(1)}, u32[]{:S(2)}, u32[]{:S(2)}) collective-permute-start(f32[8,128]{1,0:T(8,128)S(1)} %get-tuple-element.76), channel_id=1, source_target_pairs={{0,4},{1,5},{2,6},{3,7},{4,0},{5,1},{6,2},{7,3},{8,12},{9,13},{10,... | collective-permute-start | bytes 12296 | tf_op jit(solution)/shard_map/ppermute | solution.py:371
  71.4 4.8 %collective-permute-start.28 = (f32[8,128]{1,0:T(8,128)S(1)}, f32[8,128]{1,0:T(8,128)S(1)}, u32[]{:S(2)}, u32[]{:S(2)}) collective-permute-start(f32[8,128]{1,0:T(8,128)S(1)} %add.20), channel_id=1, source_target_pairs={{0,22},{1,23},{2,20},{3,21},{4,18},{5,19},{6,16},{7,17},{8,30},{9,... | collective-permute-start | bytes 12296 | tf_op jit(solution)/shard_map/ppermute | solution.py:371
  72.2 4.1 %collective-permute-start.27 = (f32[8,128]{1,0:T(8,128)S(1)}, f32[8,128]{1,0:T(8,128)S(1)}, u32[]{:S(2)}, u32[]{:S(2)}) collective-permute-start(f32[8,128]{1,0:T(8,128)S(1)} %add.20), channel_id=1, source_target_pairs={{0,6},{1,7},{2,4},{3,5},{4,2},{5,3},{6,0},{7,1},{8,14},{9,15},{10,... | collective-permute-start | bytes 12296 | tf_op jit(solution)/shard_map/ppermute | solution.py:371
  74.6 3.0 %collective-permute-start.26 = (f32[8,128]{1,0:T(8,128)S(1)}, f32[8,128]{1,0:T(8,128)S(1)}, u32[]{:S(2)}, u32[]{:S(2)}) collective-permute-start(f32[8,128]{1,0:T(8,128)S(1)} %add.20), channel_id=1, source_target_pairs={{0,20},{1,21},{2,22},{3,23},{4,16},{5,17},{6,18},{7,19},{8,28},{9,... | collective-permute-start | bytes 12296 | tf_op jit(solution)/shard_map/ppermute | solution.py:371
  77.6 3.9 %collective-permute-start.31 = (f32[8,128]{1,0:T(8,128)S(1)}, f32[8,128]{1,0:T(8,128)S(1)}, u32[]{:S(2)}, u32[]{:S(2)}) collective-permute-start(f32[8,128]{1,0:T(8,128)S(1)} %add_add_fusion.refs_1_), channel_id=1, source_target_pairs={{0,13},{1,12},{2,15},{3,14},{4,9},{5,8},{6,11},{7,10},{8,5},{9,4},... | collective-permute-start | bytes 12296 | tf_op jit(solution)/shard_map/ppermute | solution.py:371
  78.5 3.1 %collective-permute-start.30 = (f32[8,128]{1,0:T(8,128)S(1)}, f32[8,128]{1,0:T(8,128)S(1)}, u32[]{:S(2)}, u32[]{:S(2)}) collective-permute-start(f32[8,128]{1,0:T(8,128)S(1)} %add_add_fusion.refs_1_), channel_id=1, source_target_pairs={{0,5},{1,4},{2,7},{3,6},{4,1},{5,0},{6,3},{7,2},{8,13},{9,12},{10,... | collective-permute-start | bytes 12296 | tf_op jit(solution)/shard_map/ppermute | solution.py:371
  79.7 3.0 %collective-permute-start.29 = (f32[8,128]{1,0:T(8,128)S(1)}, f32[8,128]{1,0:T(8,128)S(1)}, u32[]{:S(2)}, u32[]{:S(2)}) collective-permute-start(f32[8,128]{1,0:T(8,128)S(1)} %add_add_fusion.refs_1_), channel_id=1, source_target_pairs={{0,12},{1,13},{2,14},{3,15},{4,8},{5,9},{6,10},{7,11},{8,4},{9,5},... | collective-permute-start | bytes 12296 | tf_op jit(solution)/shard_map/ppermute | solution.py:371

commit v7 on v5

--- a/solution.py
+++ b/solution.py
@@ -154,7 +154,7 @@
     put(row_parts, sums + build_rows(left, right, *stores[row_parts + 1], totals))
 
 
-def sweep(weights, parts, stores, block, initial=None, tile=256):
+def sweep(weights, parts, stores, block, initial=None, tile=512):
     rows = weights.shape[0] // 2
     width = stores[0][0].shape[0]
     pieces = []

time: 84.5 us -> 84.5 us (level)
  no operation moved by 1% of the time
where the time goes in v7:
time: 84.5 us; the launch traced here: 84.3 us
  starting transfers between devices  35.3 us (42%)
  Pallas kernels  26.2 us (31%)
  waiting for transfers between devices  22.6 us (27%)
    ppermute x32, starting transfers between devices, swap(): lax.ppermute(values, ('row', 'col'), [(index, index ^ mask) for index in...  35.3 us
    pallas_call x13, Pallas kernels, call(): pl.pallas_call(body, out_shape=out_shape, in_specs=[VMEM] * len(operands)...  25.2 us
    ppermute x32, waiting for transfers between devices, swap(): lax.ppermute(values, ('row', 'col'), [(index, index ^ mask) for index in...  22.6 us
  transfers between devices with their start and end apart: 32, of which 20 were waited for; matrix products, arithmetic and copies ran while one was open for 0% of the time, Pallas kernels for 14%

profile of v7, /device:TPU:0, one launch (start us, length us, event | category | flops | bytes accessed | tf_op | source)
XLA Modules:
  0.0 84.3 jit_solution(16905249648122892468)
XLA Ops:
  0.0 1.0 %fetch.1 = (f32[64,512]{1,0:T(8,128)S(1)}, f32[32,512]{1,0:T(8,128)S(1)}) custom-call(f32[64,512]{1,0:T(8,128)} %frames_ref.1, f32[32,512]{1,0:T(8,128)} %start_ref.1), custom_call_target="tpu_custom_call" | custom-call | flops 17179869184 | tf_op jit(solution)/shard_map/fetch/pallas_call | solution.py:386
  1.0 3.1 %collective-permute-start.7 = (f32[64,512]{1,0:T(8,128)S(1)}, f32[64,512]{1,0:T(8,128)S(1)}, u32[]{:S(2)}, u32[]{:S(2)}) collective-permute-start(f32[64,512]{1,0:T(8,128)S(1)} %get-tuple-element.41.refs_0_), channel_id=1, source_target_pairs={{0,1},{1,0},{2,3},{3,2},{4,5},{5,4},{6,7},{7,6},{8,9},{9,8},{10,11... | collective-permute-start | bytes 393224 | tf_op jit(solution)/shard_map/ppermute | solution.py:371
  4.1 2.6 %collective-permute-start.2 = (f32[64,512]{1,0:T(8,128)S(1)}, f32[64,512]{1,0:T(8,128)S(1)}, u32[]{:S(2)}, u32[]{:S(2)}) collective-permute-start(f32[64,512]{1,0:T(8,128)S(1)} %copy-done), channel_id=1, source_target_pairs={{0,2},{1,3},{2,0},{3,1},{4,6},{5,7},{6,4},{7,5},{8,10},{9,11},{10,... | collective-permute-start | bytes 393224 | tf_op jit(solution)/shard_map/ppermute | solution.py:371
  6.7 1.5 %collective-permute-start.3 = (f32[64,512]{1,0:T(8,128)S(1)}, f32[64,512]{1,0:T(8,128)S(1)}, u32[]{:S(2)}, u32[]{:S(2)}) collective-permute-start(f32[64,512]{1,0:T(8,128)S(1)} %get-tuple-element.41.refs_0_), channel_id=1, source_target_pairs={{0,8},{1,9},{2,10},{3,11},{4,12},{5,13},{6,14},{7,15},{8,0},{9,1},... | collective-permute-start | bytes 393224 | tf_op jit(solution)/shard_map/ppermute | solution.py:371
  8.3 1.5 %collective-permute-start.4 = (f32[64,512]{1,0:T(8,128)S(1)}, f32[64,512]{1,0:T(8,128)S(1)}, u32[]{:S(2)}, u32[]{:S(2)}) collective-permute-start(f32[64,512]{1,0:T(8,128)S(1)} %get-tuple-element.41.refs_0_), channel_id=1, source_target_pairs={{0,4},{1,5},{2,6},{3,7},{4,0},{5,1},{6,2},{7,3},{8,12},{9,13},{10,... | collective-permute-start | bytes 393224 | tf_op jit(solution)/shard_map/ppermute | solution.py:371
  9.8 1.4 %collective-permute-start.8 = (f32[64,512]{1,0:T(8,128)S(1)}, f32[64,512]{1,0:T(8,128)S(1)}, u32[]{:S(2)}, u32[]{:S(2)}) collective-permute-start(f32[64,512]{1,0:T(8,128)S(1)} %collective-permute-done.7.refs_5_), channel_id=1, source_target_pairs={{0,8},{1,9},{2,10},{3,11},{4,12},{5,13},{6,14},{7,15},{8,0},{9,1},... | collective-permute-start | bytes 393224 | tf_op jit(solution)/shard_map/ppermute | solution.py:371
  11.3 1.6 %collective-permute-done.2.refs_2_ = f32[64,512]{1,0:T(8,128)S(1)} collective-permute-done((f32[64,512]{1,0:T(8,128)S(1)}, f32[64,512]{1,0:T(8,128)S(1)}, u32[]{:S(2)}, u32[]{:S(2)}) %collective-permute-start.2) | collective-permute-done | bytes 131104 | tf_op jit(solution)/shard_map/ppermute | solution.py:371
  14.1 0.8 collective-permute-start.6
  15.3 4.3 %build_near.1 = (bf16[512,2048]{1,0:T(8,128)(2,1)S(1)}, bf16[512,2048]{1,0:T(8,128)(2,1)S(1)}, bf16[512,2048]{1,0:T(8,128)(2,1)S(1)}, bf16[512,2048]{1,0:T(8,128...) custom-call(f32[64,512]{1,0:T(8,128)S(1)} %get-tuple-element.41.refs, ...), custom_call_target="tpu_custom_call" | custom-call | flops 1 | tf_op jit(solution)/shard_map/build_near/pallas_call | solution.py:18
  19.8 5.3 %build_far.1 = (bf16[512,2048]{1,0:T(8,128)(2,1)S(1)}, bf16[512,2048]{1,0:T(8,128)(2,1)S(1)}, bf16[512,2048]{1,0:T(8,128)(2,1)S(1)}, bf16[512,2048]{1,0:T(8,128)...) custom-call(bf16[1536,256]{1,0:T(8,128)(2,1)S(1)} %get-tuple-element, ...), custom_call_target="tpu_custom_call" | custom-call | flops 1 | tf_op jit(solution)/shard_map/build_far/pallas_call | solution.py:18
  25.1 2.0 %collective-permute-start.13 = (f32[144,128]{1,0:T(8,128)S(1)}, f32[144,128]{1,0:T(8,128)S(1)}, u32[]{:S(2)}, u32[]{:S(2)}) collective-permute-start(f32[144,128]{1,0:T(8,128)S(1)} %get-tuple-element.46.refs_0_), channel_id=1, source_target_pairs={{0,18},{1,19},{2,16},{3,17},{4,22},{5,23},{6,20},{7,21},{8,26},{9,... | collective-permute-start | bytes 221192 | tf_op jit(solution)/shard_map/ppermute | solution.py:371
  27.1 1.3 %collective-permute-start.12 = (f32[144,128]{1,0:T(8,128)S(1)}, f32[144,128]{1,0:T(8,128)S(1)}, u32[]{:S(2)}, u32[]{:S(2)}) collective-permute-start(f32[144,128]{1,0:T(8,128)S(1)} %get-tuple-element.46.refs_0_), channel_id=1, source_target_pairs={{0,2},{1,3},{2,0},{3,1},{4,6},{5,7},{6,4},{7,5},{8,10},{9,11},{10,... | collective-permute-start | bytes 221192 | tf_op jit(solution)/shard_map/ppermute | solution.py:371
  28.5 1.1 %collective-permute-start.11 = (f32[144,128]{1,0:T(8,128)S(1)}, f32[144,128]{1,0:T(8,128)S(1)}, u32[]{:S(2)}, u32[]{:S(2)}) collective-permute-start(f32[144,128]{1,0:T(8,128)S(1)} %get-tuple-element.46.refs_0_), channel_id=1, source_target_pairs={{0,16},{1,17},{2,18},{3,19},{4,20},{5,21},{6,22},{7,23},{8,24},{9,... | collective-permute-start | bytes 221192 | tf_op jit(solution)/shard_map/ppermute | solution.py:371
  29.5 5.2 %collective-permute-done.13.refs_3_ = f32[144,128]{1,0:T(8,128)S(1)} collective-permute-done((f32[144,128]{1,0:T(8,128)S(1)}, f32[144,128]{1,0:T(8,128)S(1)}, u32[]{:S(2)}, u32[]{:S(2)}) %collective-permute-start.13) | collective-permute-done | bytes 73760 | tf_op jit(solution)/shard_map/ppermute | solution.py:371
  34.7 0.7 collective-permute-done.12.refs_2_
  35.5 3.1 %first_odd.1 = (f32[4,136,128]{2,1,0:T(8,128)S(1)}, f32[1,512]{1,0:T(1,128)S(1)}, bf16[96,2048]{1,0:T(8,128)(2,1)S(1)}) custom-call(f32[144,128]{1,0:T(8,128)S(1)} %get-tuple-element.46.refs_0_, f32[144,128]{1,0:T(8,128)S(1)} %collective-permute-done.11.refs_1_, f32[144,128]{1,0:T(8,128)S(1)} %collective-permute-done.12.refs_2_, ...), custom_call_target="tpu_custom_call" | custom-call | flops 1207959552 | tf_op jit(solution)/shard_map/first_odd/pallas_call | solution.py:18
  38.7 2.2 %first_even.1 = f32[3,136,128]{2,1,0:T(8,128)S(1)} custom-call(bf16[96,2048]{1,0:T(8,128)(2,1)S(1)} %get-tuple-element.64.refs_0_, bf16[512,2048]{1,0:T(8,128)(2,1)S(1)} %get-tuple-element.47.refs_4_.refs_1_.refs_2_.refs_0_, bf16[512,2048]{1,0:T(8,128)(2,1)S(1)} %get-tuple-element.48.refs_5_.refs_2_.refs_3_.refs_1_, ...), custom_call_target="tpu_custom_call" | custom-call | flops 905969664 | tf_op jit(solution)/shard_map/first_even/pallas_call | solution.py:18
  41.1 1.1 %collective-permute-start.17 = (f32[136,128]{1,0:T(8,128)S(1)}, f32[136,128]{1,0:T(8,128)S(1)}, u32[]{:S(2)}, u32[]{:S(2)}) collective-permute-start(f32[136,128]{1,0:T(8,128)S(1)} %get-tuple-element.80), channel_id=1, source_target_pairs={{0,9},{1,8},{2,11},{3,10},{4,13},{5,12},{6,15},{7,14},{8,1},{9,0},... | collective-permute-start | bytes 208904 | tf_op jit(solution)/shard_map/ppermute | solution.py:371
  42.1 1.8 %collective-permute-start.16 = (f32[136,128]{1,0:T(8,128)S(1)}, f32[136,128]{1,0:T(8,128)S(1)}, u32[]{:S(2)}, u32[]{:S(2)}) collective-permute-start(f32[136,128]{1,0:T(8,128)S(1)} %get-tuple-element.81), channel_id=1, source_target_pairs={{0,1},{1,0},{2,3},{3,2},{4,5},{5,4},{6,7},{7,6},{8,9},{9,8},{10,11... | collective-permute-start | bytes 208904 | tf_op jit(solution)/shard_map/ppermute | solution.py:371
  43.9 0.7 collective-permute-start.15
  44.6 0.8 first_own.1.refs_1_
  45.5 1.6 %collective-permute-done.17.refs_5_ = f32[136,128]{1,0:T(8,128)S(1)} collective-permute-done((f32[136,128]{1,0:T(8,128)S(1)}, f32[136,128]{1,0:T(8,128)S(1)}, u32[]{:S(2)}, u32[]{:S(2)}) %collective-permute-start.17) | collective-permute-done | bytes 69664 | tf_op jit(solution)/shard_map/ppermute | solution.py:371
  47.0 0.9 %collective-permute-done.16.refs_4_ = f32[136,128]{1,0:T(8,128)S(1)} collective-permute-done((f32[136,128]{1,0:T(8,128)S(1)}, f32[136,128]{1,0:T(8,128)S(1)}, u32[]{:S(2)}, u32[]{:S(2)}) %collective-permute-start.16) | collective-permute-done | bytes 69664 | tf_op jit(solution)/shard_map/ppermute | solution.py:371
  48.5 1.1 %collective-permute-start.18 = (f32[136,128]{1,0:T(8,128)S(1)}, f32[136,128]{1,0:T(8,128)S(1)}, u32[]{:S(2)}, u32[]{:S(2)}) collective-permute-start(f32[136,128]{1,0:T(8,128)S(1)} %get-tuple-element.67.piece_ref.refs_0_), channel_id=1, source_target_pairs={{0,16},{1,17},{2,18},{3,19},{4,20},{5,21},{6,22},{7,23},{8,24},{9,... | collective-permute-start | bytes 208904 | tf_op jit(solution)/shard_map/ppermute | solution.py:371
  49.6 1.9 %collective-permute-start.20 = (f32[136,128]{1,0:T(8,128)S(1)}, f32[136,128]{1,0:T(8,128)S(1)}, u32[]{:S(2)}, u32[]{:S(2)}) collective-permute-start(f32[136,128]{1,0:T(8,128)S(1)} %get-tuple-element.67.piece_ref.refs_0_), channel_id=1, source_target_pairs={{0,18},{1,19},{2,16},{3,17},{4,22},{5,23},{6,20},{7,21},{8,26},{9,... | collective-permute-start | bytes 208904 | tf_op jit(solution)/shard_map/ppermute | solution.py:371
  51.6 1.3 %collective-permute-start.19 = (f32[136,128]{1,0:T(8,128)S(1)}, f32[136,128]{1,0:T(8,128)S(1)}, u32[]{:S(2)}, u32[]{:S(2)}) collective-permute-start(f32[136,128]{1,0:T(8,128)S(1)} %get-tuple-element.67.piece_ref.refs_0_), channel_id=1, source_target_pairs={{0,2},{1,3},{2,0},{3,1},{4,6},{5,7},{6,4},{7,5},{8,10},{9,11},{10,... | collective-permute-start | bytes 208904 | tf_op jit(solution)/shard_map/ppermute | solution.py:371
  52.9 1.5 %second_part.2 = (f32[4,32,512]{2,1,0:T(8,128)S(1)}, f32[4,32,512]{2,1,0:T(8,128)S(1)}) custom-call(f32[136,128]{1,0:T(8,128)S(1)} %get-tuple-element.67.piece_ref.refs_0_, bf16[512,2048]{1,0:T(8,128)(2,1)S(1)} %get-tuple-element.47.refs_4_.refs_1_.refs_2_.refs_0_, bf16[512,2048]{1,0:T(8,128)(2,1)S(1)} %get-tuple-element.48.refs_5_.refs_2_.refs_3_.refs_1_, ...), custom_call_target="tpu_custom_call" | custom-call | flops 603979776 | tf_op jit(solution)/shard_map/second_part/pallas_call | solution.py:18
  54.4 1.6 %second_part.3 = (f32[4,32,512]{2,1,0:T(8,128)S(1)}, f32[4,32,512]{2,1,0:T(8,128)S(1)}) custom-call(f32[136,128]{1,0:T(8,128)S(1)} %collective-permute-done.18.piece_ref.refs_1_, bf16[512,2048]{1,0:T(8,128)(2,1)S(1)} %get-tuple-element.49.refs_6_.refs_3_.refs_4_.refs_0_, bf16[512,2048]{1,0:T(8,128)(2,1)S(1)} %get-tuple-element.50.refs_7_.refs_4_.refs_5_.refs_1_, ...), custom_call_target="tpu_custom_call" | custom-call | flops 603979776 | tf_op jit(solution)/shard_map/second_part/pallas_call | solution.py:18
  56.0 1.4 %collective-permute-done.20.refs_3_ = f32[136,128]{1,0:T(8,128)S(1)} collective-permute-done((f32[136,128]{1,0:T(8,128)S(1)}, f32[136,128]{1,0:T(8,128)S(1)}, u32[]{:S(2)}, u32[]{:S(2)}) %collective-permute-start.20) | collective-permute-done | bytes 69664 | tf_op jit(solution)/shard_map/ppermute | solution.py:371
  57.4 1.6 %second_odd.1 = (f32[4,136,128]{2,1,0:T(8,128)S(1)}, f32[8,128]{1,0:T(8,128)S(1)}, bf16[64,1024]{1,0:T(8,128)(2,1)S(1)}) custom-call(f32[136,128]{1,0:T(8,128)S(1)} %get-tuple-element.67.piece_ref.refs_0_, f32[136,128]{1,0:T(8,128)S(1)} %collective-permute-done.18.piece_ref.refs_1_, f32[136,128]{1,0:T(8,128)S(1)} %collective-permute-done.19.refs_2_, ...), custom_call_target="tpu_custom_call" | custom-call | flops 1207959552 | tf_op jit(solution)/shard_map/second_odd/pallas_call | solution.py:18
  59.0 1.2 %second_even.1 = f32[3,136,128]{2,1,0:T(8,128)S(1)} custom-call(bf16[64,1024]{1,0:T(8,128)(2,1)S(1)} %get-tuple-element.71.refs_0_, f32[8,128]{1,0:T(8,128)S(1)} %get-tuple-element.72.refs_1_, f32[4,32,512]{2,1,0:T(8,128)S(1)} %get-tuple-element.73.refs_2_, bf16[512,2048]{1,0:T(8,128)(2,1)S(1)} %get-tuple-element.51.refs_8_.refs_5_.refs_6_.refs_3_.refs_4_, ...), custom_call_target="tpu_custom_call" | custom-call | flops 905969664 | tf_op jit(solution)/shard_map/second_even/pallas_call | solution.py:18
  60.6 2.1 %collective-permute-start.24 = (f32[136,128]{1,0:T(8,128)S(1)}, f32[136,128]{1,0:T(8,128)S(1)}, u32[]{:S(2)}, u32[]{:S(2)}) collective-permute-start(f32[136,128]{1,0:T(8,128)S(1)} %get-tuple-element.77), channel_id=1, source_target_pairs={{0,9},{1,8},{2,11},{3,10},{4,13},{5,12},{6,15},{7,14},{8,1},{9,0},... | collective-permute-start | bytes 208904 | tf_op jit(solution)/shard_map/ppermute | solution.py:371
  62.7 2.0 %collective-permute-start.23 = (f32[136,128]{1,0:T(8,128)S(1)}, f32[136,128]{1,0:T(8,128)S(1)}, u32[]{:S(2)}, u32[]{:S(2)}) collective-permute-start(f32[136,128]{1,0:T(8,128)S(1)} %get-tuple-element.78), channel_id=1, source_target_pairs={{0,1},{1,0},{2,3},{3,2},{4,5},{5,4},{6,7},{7,6},{8,9},{9,8},{10,11... | collective-permute-start | bytes 208904 | tf_op jit(solution)/shard_map/ppermute | solution.py:371
  65.2 1.1 %collective-permute-done.24.refs_5_ = f32[136,128]{1,0:T(8,128)S(1)} collective-permute-done((f32[136,128]{1,0:T(8,128)S(1)}, f32[136,128]{1,0:T(8,128)S(1)}, u32[]{:S(2)}, u32[]{:S(2)}) %collective-permute-start.24) | collective-permute-done | bytes 69664 | tf_op jit(solution)/shard_map/ppermute | solution.py:371
  66.3 2.1 %collective-permute-done.23.refs_4_ = f32[136,128]{1,0:T(8,128)S(1)} collective-permute-done((f32[136,128]{1,0:T(8,128)S(1)}, f32[136,128]{1,0:T(8,128)S(1)}, u32[]{:S(2)}, u32[]{:S(2)}) %collective-permute-start.23) | collective-permute-done | bytes 69664 | tf_op jit(solution)/shard_map/ppermute | solution.py:371
  68.4 0.6 collective-permute-done.22.refs_3_
  69.0 1.2 %grown_two.1 = (f32[32,512]{1,0:T(8,128)S(1)}, f32[8,128]{1,0:T(8,128)S(1)}) custom-call(f32[1,512]{1,0:T(1,128)S(1)} %get-tuple-element.66.refs_0_, f32[136,128]{1,0:T(8,128)S(1)} %second_own.1.refs_1_, f32[136,128]{1,0:T(8,128)S(1)} %slice_bitcast_fusion.3.refs_2_, f32[136,128]{1,0:T(8,128)S(1)} %collective-permute-done.22.refs_3_, ...), custom_call_target="tpu_custom_call" | custom-call | tf_op jit(solution)/shard_map/grown_two/pallas_call | solution.py:18
  70.3 1.2 %collective-permute-done.25 = f32[8,128]{1,0:T(8,128)S(1)} collective-permute-done((f32[8,128]{1,0:T(8,128)S(1)}, f32[8,128]{1,0:T(8,128)S(1)}, u32[]{:S(2)}, u32[]{:S(2)}) %collective-permute-start.25) | collective-permute-done | bytes 4128 | tf_op jit(solution)/shard_map/ppermute | solution.py:371
  71.6 1.9 %collective-permute-start.27 = (f32[8,128]{1,0:T(8,128)S(1)}, f32[8,128]{1,0:T(8,128)S(1)}, u32[]{:S(2)}, u32[]{:S(2)}) collective-permute-start(f32[8,128]{1,0:T(8,128)S(1)} %add.20), channel_id=1, source_target_pairs={{0,5},{1,4},{2,7},{3,6},{4,1},{5,0},{6,3},{7,2},{8,13},{9,12},{10,... | collective-permute-start | bytes 12296 | tf_op jit(solution)/shard_map/ppermute | solution.py:371
  73.5 0.9 %collective-permute-start.26 = (f32[8,128]{1,0:T(8,128)S(1)}, f32[8,128]{1,0:T(8,128)S(1)}, u32[]{:S(2)}, u32[]{:S(2)}) collective-permute-start(f32[8,128]{1,0:T(8,128)S(1)} %add.20), channel_id=1, source_target_pairs={{0,12},{1,13},{2,14},{3,15},{4,8},{5,9},{6,10},{7,11},{8,4},{9,5},... | collective-permute-start | bytes 12296 | tf_op jit(solution)/shard_map/ppermute | solution.py:371
  74.4 0.9 %collective-permute-done.28 = f32[8,128]{1,0:T(8,128)S(1)} collective-permute-done((f32[8,128]{1,0:T(8,128)S(1)}, f32[8,128]{1,0:T(8,128)S(1)}, u32[]{:S(2)}, u32[]{:S(2)}) %collective-permute-start.28) | collective-permute-done | bytes 4128 | tf_op jit(solution)/shard_map/ppermute | solution.py:371
  75.4 1.1 %collective-permute-done.26 = f32[8,128]{1,0:T(8,128)S(1)} collective-permute-done((f32[8,128]{1,0:T(8,128)S(1)}, f32[8,128]{1,0:T(8,128)S(1)}, u32[]{:S(2)}, u32[]{:S(2)}) %collective-permute-start.26) | collective-permute-done | bytes 4128 | tf_op jit(solution)/shard_map/ppermute | solution.py:371
  76.5 1.1 %collective-permute-start.31 = (f32[8,128]{1,0:T(8,128)S(1)}, f32[8,128]{1,0:T(8,128)S(1)}, u32[]{:S(2)}, u32[]{:S(2)}) collective-permute-start(f32[8,128]{1,0:T(8,128)S(1)} %add_add_fusion.refs_1_), channel_id=1, source_target_pairs={{0,22},{1,23},{2,20},{3,21},{4,18},{5,19},{6,16},{7,17},{8,30},{9,... | collective-permute-start | bytes 12296 | tf_op jit(solution)/shard_map/ppermute | solution.py:371
  77.6 2.1 %collective-permute-start.30 = (f32[8,128]{1,0:T(8,128)S(1)}, f32[8,128]{1,0:T(8,128)S(1)}, u32[]{:S(2)}, u32[]{:S(2)}) collective-permute-start(f32[8,128]{1,0:T(8,128)S(1)} %add_add_fusion.refs_1_), channel_id=1, source_target_pairs={{0,6},{1,7},{2,4},{3,5},{4,2},{5,3},{6,0},{7,1},{8,14},{9,15},{10,... | collective-permute-start | bytes 12296 | tf_op jit(solution)/shard_map/ppermute | solution.py:371
  79.7 0.7 collective-permute-start.29
  80.4 0.9 %collective-permute-done.31.refs_4_ = f32[8,128]{1,0:T(8,128)S(1)} collective-permute-done((f32[8,128]{1,0:T(8,128)S(1)}, f32[8,128]{1,0:T(8,128)S(1)}, u32[]{:S(2)}, u32[]{:S(2)}) %collective-permute-start.31) | collective-permute-done | bytes 4128 | tf_op jit(solution)/shard_map/ppermute | solution.py:371
  81.5 1.2 %collective-permute-done.29.refs_2_ = f32[8,128]{1,0:T(8,128)S(1)} collective-permute-done((f32[8,128]{1,0:T(8,128)S(1)}, f32[8,128]{1,0:T(8,128)S(1)}, u32[]{:S(2)}, u32[]{:S(2)}) %collective-permute-start.29) | collective-permute-done | bytes 4128 | tf_op jit(solution)/shard_map/ppermute | solution.py:371
  82.7 1.6 %finish.1 = f32[32,512]{1,0:T(8,128)} custom-call(f32[32,512]{1,0:T(8,128)S(1)} %get-tuple-element.75.refs_0_, f32[8,128]{1,0:T(8,128)S(1)} %add_add_fusion.refs_1_, f32[8,128]{1,0:T(8,128)S(1)} %collective-permute-done.29.refs_2_, f32[8,128]{1,0:T(8,128)S(1)} %collective-permute-done.30.refs_3_, f32[8,128]{1,0:T(8,128)S(1)} %collective-permute-done.31.refs_4_), custom_call_target="tpu_custom_call" | custom-call | tf_op jit(solution)/shard_map/finish/pallas_call | solution.py:18
  (40 shorter events, 4.0 us)
Async XLA Ops:
  0.0 4.1 %copy-start = (f32[64,512]{1,0:T(8,128)S(1)}, f32[64,512]{1,0:T(8,128)}, u32[]{:S(2)}) copy-start(f32[64,512]{1,0:T(8,128)} %frames_ref.1) | copy-start | bytes 393220
  1.0 8.8 %collective-permute-start.7 = (f32[64,512]{1,0:T(8,128)S(1)}, f32[64,512]{1,0:T(8,128)S(1)}, u32[]{:S(2)}, u32[]{:S(2)}) collective-permute-start(f32[64,512]{1,0:T(8,128)S(1)} %get-tuple-element.41.refs_0_), channel_id=1, source_target_pairs={{0,1},{1,0},{2,3},{3,2},{4,5},{5,4},{6,7},{7,6},{8,9},{9,8},{10,11... | collective-permute-start | bytes 393224 | tf_op jit(solution)/shard_map/ppermute | solution.py:371
  4.1 8.7 %collective-permute-start.2 = (f32[64,512]{1,0:T(8,128)S(1)}, f32[64,512]{1,0:T(8,128)S(1)}, u32[]{:S(2)}, u32[]{:S(2)}) collective-permute-start(f32[64,512]{1,0:T(8,128)S(1)} %copy-done), channel_id=1, source_target_pairs={{0,2},{1,3},{2,0},{3,1},{4,6},{5,7},{6,4},{7,5},{8,10},{9,11},{10,... | collective-permute-start | bytes 393224 | tf_op jit(solution)/shard_map/ppermute | solution.py:371
  6.7 6.1 %collective-permute-start.3 = (f32[64,512]{1,0:T(8,128)S(1)}, f32[64,512]{1,0:T(8,128)S(1)}, u32[]{:S(2)}, u32[]{:S(2)}) collective-permute-start(f32[64,512]{1,0:T(8,128)S(1)} %get-tuple-element.41.refs_0_), channel_id=1, source_target_pairs={{0,8},{1,9},{2,10},{3,11},{4,12},{5,13},{6,14},{7,15},{8,0},{9,1},... | collective-permute-start | bytes 393224 | tf_op jit(solution)/shard_map/ppermute | solution.py:371
  8.2 5.7 %collective-permute-start = (f32[64,512]{1,0:T(8,128)S(1)}, f32[64,512]{1,0:T(8,128)S(1)}, u32[]{:S(2)}, u32[]{:S(2)}) collective-permute-start(f32[64,512]{1,0:T(8,128)S(1)} %get-tuple-element.41.refs_0_), channel_id=1, source_target_pairs={{0,20},{1,21},{2,22},{3,23},{4,16},{5,17},{6,18},{7,19},{8,28},{9,... | collective-permute-start | bytes 393224 | tf_op jit(solution)/shard_map/ppermute | solution.py:371
  8.3 5.8 %collective-permute-start.4 = (f32[64,512]{1,0:T(8,128)S(1)}, f32[64,512]{1,0:T(8,128)S(1)}, u32[]{:S(2)}, u32[]{:S(2)}) collective-permute-start(f32[64,512]{1,0:T(8,128)S(1)} %get-tuple-element.41.refs_0_), channel_id=1, source_target_pairs={{0,4},{1,5},{2,6},{3,7},{4,0},{5,1},{6,2},{7,3},{8,12},{9,13},{10,... | collective-permute-start | bytes 393224 | tf_op jit(solution)/shard_map/ppermute | solution.py:371
  9.8 5.4 %collective-permute-start.8 = (f32[64,512]{1,0:T(8,128)S(1)}, f32[64,512]{1,0:T(8,128)S(1)}, u32[]{:S(2)}, u32[]{:S(2)}) collective-permute-start(f32[64,512]{1,0:T(8,128)S(1)} %collective-permute-done.7.refs_5_), channel_id=1, source_target_pairs={{0,8},{1,9},{2,10},{3,11},{4,12},{5,13},{6,14},{7,15},{8,0},{9,1},... | collective-permute-start | bytes 393224 | tf_op jit(solution)/shard_map/ppermute | solution.py:371
  12.8 7.0 %collective-permute-start.9 = (f32[64,512]{1,0:T(8,128)S(1)}, f32[64,512]{1,0:T(8,128)S(1)}, u32[]{:S(2)}, u32[]{:S(2)}) collective-permute-start(f32[64,512]{1,0:T(8,128)S(1)} %collective-permute-done.7.refs_5_), channel_id=1, source_target_pairs={{0,4},{1,5},{2,6},{3,7},{4,0},{5,1},{6,2},{7,3},{8,12},{9,13},{10,... | collective-permute-start | bytes 393224 | tf_op jit(solution)/shard_map/ppermute | solution.py:371
  12.8 2.4 %collective-permute-start.5 = (f32[64,512]{1,0:T(8,128)S(1)}, f32[64,512]{1,0:T(8,128)S(1)}, u32[]{:S(2)}, u32[]{:S(2)}) collective-permute-start(f32[64,512]{1,0:T(8,128)S(1)} %collective-permute-done.3.refs_3_), channel_id=1, source_target_pairs={{0,4},{1,5},{2,6},{3,7},{4,0},{5,1},{6,2},{7,3},{8,12},{9,13},{10,... | collective-permute-start | bytes 393224 | tf_op jit(solution)/shard_map/ppermute | solution.py:371
  13.9 1.3 %collective-permute-start.1 = (f32[64,512]{1,0:T(8,128)S(1)}, f32[64,512]{1,0:T(8,128)S(1)}, u32[]{:S(2)}, u32[]{:S(2)}) collective-permute-start(f32[64,512]{1,0:T(8,128)S(1)} %collective-permute-done), channel_id=1, source_target_pairs={{0,4},{1,5},{2,6},{3,7},{4,0},{5,1},{6,2},{7,3},{8,12},{9,13},{10,... | collective-permute-start | bytes 393224 | tf_op jit(solution)/shard_map/ppermute | solution.py:371
  14.1 5.7 %collective-permute-start.6 = (f32[64,512]{1,0:T(8,128)S(1)}, f32[64,512]{1,0:T(8,128)S(1)}, u32[]{:S(2)}, u32[]{:S(2)}) collective-permute-start(f32[64,512]{1,0:T(8,128)S(1)} %collective-permute-done.2.refs_2_), channel_id=1, source_target_pairs={{0,16},{1,17},{2,18},{3,19},{4,20},{5,21},{6,22},{7,23},{8,24},{9,... | collective-permute-start | bytes 393224 | tf_op jit(solution)/shard_map/ppermute | solution.py:371
  15.2 4.6 %collective-permute-start.10 = (f32[64,512]{1,0:T(8,128)S(1)}, f32[64,512]{1,0:T(8,128)S(1)}, u32[]{:S(2)}, u32[]{:S(2)}) collective-permute-start(f32[64,512]{1,0:T(8,128)S(1)} %collective-permute-done.8.refs_6_), channel_id=1, source_target_pairs={{0,4},{1,5},{2,6},{3,7},{4,0},{5,1},{6,2},{7,3},{8,12},{9,13},{10,... | collective-permute-start | bytes 393224 | tf_op jit(solution)/shard_map/ppermute | solution.py:371
  25.1 9.7 %collective-permute-start.13 = (f32[144,128]{1,0:T(8,128)S(1)}, f32[144,128]{1,0:T(8,128)S(1)}, u32[]{:S(2)}, u32[]{:S(2)}) collective-permute-start(f32[144,128]{1,0:T(8,128)S(1)} %get-tuple-element.46.refs_0_), channel_id=1, source_target_pairs={{0,18},{1,19},{2,16},{3,17},{4,22},{5,23},{6,20},{7,21},{8,26},{9,... | collective-permute-start | bytes 221192 | tf_op jit(solution)/shard_map/ppermute | solution.py:371
  27.1 8.3 %collective-permute-start.12 = (f32[144,128]{1,0:T(8,128)S(1)}, f32[144,128]{1,0:T(8,128)S(1)}, u32[]{:S(2)}, u32[]{:S(2)}) collective-permute-start(f32[144,128]{1,0:T(8,128)S(1)} %get-tuple-element.46.refs_0_), channel_id=1, source_target_pairs={{0,2},{1,3},{2,0},{3,1},{4,6},{5,7},{6,4},{7,5},{8,10},{9,11},{10,... | collective-permute-start | bytes 221192 | tf_op jit(solution)/shard_map/ppermute | solution.py:371
  28.5 7.0 %collective-permute-start.11 = (f32[144,128]{1,0:T(8,128)S(1)}, f32[144,128]{1,0:T(8,128)S(1)}, u32[]{:S(2)}, u32[]{:S(2)}) collective-permute-start(f32[144,128]{1,0:T(8,128)S(1)} %get-tuple-element.46.refs_0_), channel_id=1, source_target_pairs={{0,16},{1,17},{2,18},{3,19},{4,20},{5,21},{6,22},{7,23},{8,24},{9,... | collective-permute-start | bytes 221192 | tf_op jit(solution)/shard_map/ppermute | solution.py:371
  38.6 2.4 %collective-permute-start.14 = (f32[4,136,128]{2,1,0:T(8,128)S(1)}, f32[4,136,128]{2,1,0:T(8,128)S(1)}, u32[]{:S(2)}, u32[]{:S(2)}) collective-permute-start(f32[4,136,128]{2,1,0:T(8,128)S(1)} %get-tuple-element.65), channel_id=1, source_target_pairs={{0,4},{1,5},{2,6},{3,7},{4,0},{5,1},{6,2},{7,3},{8,12},{9,13},{10,... | collective-permute-start | bytes 835592 | tf_op jit(solution)/shard_map/ppermute | solution.py:371
  41.1 5.9 %collective-permute-start.17 = (f32[136,128]{1,0:T(8,128)S(1)}, f32[136,128]{1,0:T(8,128)S(1)}, u32[]{:S(2)}, u32[]{:S(2)}) collective-permute-start(f32[136,128]{1,0:T(8,128)S(1)} %get-tuple-element.80), channel_id=1, source_target_pairs={{0,9},{1,8},{2,11},{3,10},{4,13},{5,12},{6,15},{7,14},{8,1},{9,0},... | collective-permute-start | bytes 208904 | tf_op jit(solution)/shard_map/ppermute | solution.py:371
  42.1 5.8 %collective-permute-start.16 = (f32[136,128]{1,0:T(8,128)S(1)}, f32[136,128]{1,0:T(8,128)S(1)}, u32[]{:S(2)}, u32[]{:S(2)}) collective-permute-start(f32[136,128]{1,0:T(8,128)S(1)} %get-tuple-element.81), channel_id=1, source_target_pairs={{0,1},{1,0},{2,3},{3,2},{4,5},{5,4},{6,7},{7,6},{8,9},{9,8},{10,11... | collective-permute-start | bytes 208904 | tf_op jit(solution)/shard_map/ppermute | solution.py:371
  43.9 4.3 %collective-permute-start.15 = (f32[136,128]{1,0:T(8,128)S(1)}, f32[136,128]{1,0:T(8,128)S(1)}, u32[]{:S(2)}, u32[]{:S(2)}) collective-permute-start(f32[136,128]{1,0:T(8,128)S(1)} %get-tuple-element.82), channel_id=1, source_target_pairs={{0,8},{1,9},{2,10},{3,11},{4,12},{5,13},{6,14},{7,15},{8,0},{9,1},... | collective-permute-start | bytes 208904 | tf_op jit(solution)/shard_map/ppermute | solution.py:371
  48.5 5.9 %collective-permute-start.18 = (f32[136,128]{1,0:T(8,128)S(1)}, f32[136,128]{1,0:T(8,128)S(1)}, u32[]{:S(2)}, u32[]{:S(2)}) collective-permute-start(f32[136,128]{1,0:T(8,128)S(1)} %get-tuple-element.67.piece_ref.refs_0_), channel_id=1, source_target_pairs={{0,16},{1,17},{2,18},{3,19},{4,20},{5,21},{6,22},{7,23},{8,24},{9,... | collective-permute-start | bytes 208904 | tf_op jit(solution)/shard_map/ppermute | solution.py:371
  49.6 7.8 %collective-permute-start.20 = (f32[136,128]{1,0:T(8,128)S(1)}, f32[136,128]{1,0:T(8,128)S(1)}, u32[]{:S(2)}, u32[]{:S(2)}) collective-permute-start(f32[136,128]{1,0:T(8,128)S(1)} %get-tuple-element.67.piece_ref.refs_0_), channel_id=1, source_target_pairs={{0,18},{1,19},{2,16},{3,17},{4,22},{5,23},{6,20},{7,21},{8,26},{9,... | collective-permute-start | bytes 208904 | tf_op jit(solution)/shard_map/ppermute | solution.py:371
  51.6 5.8 %collective-permute-start.19 = (f32[136,128]{1,0:T(8,128)S(1)}, f32[136,128]{1,0:T(8,128)S(1)}, u32[]{:S(2)}, u32[]{:S(2)}) collective-permute-start(f32[136,128]{1,0:T(8,128)S(1)} %get-tuple-element.67.piece_ref.refs_0_), channel_id=1, source_target_pairs={{0,2},{1,3},{2,0},{3,1},{4,6},{5,7},{6,4},{7,5},{8,10},{9,11},{10,... | collective-permute-start | bytes 208904 | tf_op jit(solution)/shard_map/ppermute | solution.py:371
  59.0 1.6 %collective-permute-start.21 = (f32[4,136,128]{2,1,0:T(8,128)S(1)}, f32[4,136,128]{2,1,0:T(8,128)S(1)}, u32[]{:S(2)}, u32[]{:S(2)}) collective-permute-start(f32[4,136,128]{2,1,0:T(8,128)S(1)} %get-tuple-element.74), channel_id=1, source_target_pairs={{0,4},{1,5},{2,6},{3,7},{4,0},{5,1},{6,2},{7,3},{8,12},{9,13},{10,... | collective-permute-start | bytes 835592 | tf_op jit(solution)/shard_map/ppermute | solution.py:371
  60.6 5.7 %collective-permute-start.24 = (f32[136,128]{1,0:T(8,128)S(1)}, f32[136,128]{1,0:T(8,128)S(1)}, u32[]{:S(2)}, u32[]{:S(2)}) collective-permute-start(f32[136,128]{1,0:T(8,128)S(1)} %get-tuple-element.77), channel_id=1, source_target_pairs={{0,9},{1,8},{2,11},{3,10},{4,13},{5,12},{6,15},{7,14},{8,1},{9,0},... | collective-permute-start | bytes 208904 | tf_op jit(solution)/shard_map/ppermute | solution.py:371
  62.7 5.7 %collective-permute-start.23 = (f32[136,128]{1,0:T(8,128)S(1)}, f32[136,128]{1,0:T(8,128)S(1)}, u32[]{:S(2)}, u32[]{:S(2)}) collective-permute-start(f32[136,128]{1,0:T(8,128)S(1)} %get-tuple-element.78), channel_id=1, source_target_pairs={{0,1},{1,0},{2,3},{3,2},{4,5},{5,4},{6,7},{7,6},{8,9},{9,8},{10,11... | collective-permute-start | bytes 208904 | tf_op jit(solution)/shard_map/ppermute | solution.py:371
  64.7 4.3 %collective-permute-start.22 = (f32[136,128]{1,0:T(8,128)S(1)}, f32[136,128]{1,0:T(8,128)S(1)}, u32[]{:S(2)}, u32[]{:S(2)}) collective-permute-start(f32[136,128]{1,0:T(8,128)S(1)} %get-tuple-element.79), channel_id=1, source_target_pairs={{0,8},{1,9},{2,10},{3,11},{4,12},{5,13},{6,14},{7,15},{8,0},{9,1},... | collective-permute-start | bytes 208904 | tf_op jit(solution)/shard_map/ppermute | solution.py:371
  70.2 1.2 %collective-permute-start.25 = (f32[8,128]{1,0:T(8,128)S(1)}, f32[8,128]{1,0:T(8,128)S(1)}, u32[]{:S(2)}, u32[]{:S(2)}) collective-permute-start(f32[8,128]{1,0:T(8,128)S(1)} %get-tuple-element.76), channel_id=1, source_target_pairs={{0,4},{1,5},{2,6},{3,7},{4,0},{5,1},{6,2},{7,3},{8,12},{9,13},{10,... | collective-permute-start | bytes 12296 | tf_op jit(solution)/shard_map/ppermute | solution.py:371
  71.4 3.9 %collective-permute-start.28 = (f32[8,128]{1,0:T(8,128)S(1)}, f32[8,128]{1,0:T(8,128)S(1)}, u32[]{:S(2)}, u32[]{:S(2)}) collective-permute-start(f32[8,128]{1,0:T(8,128)S(1)} %add.20), channel_id=1, source_target_pairs={{0,13},{1,12},{2,15},{3,14},{4,9},{5,8},{6,11},{7,10},{8,5},{9,4},... | collective-permute-start | bytes 12296 | tf_op jit(solution)/shard_map/ppermute | solution.py:371
  71.6 3.7 %collective-permute-start.27 = (f32[8,128]{1,0:T(8,128)S(1)}, f32[8,128]{1,0:T(8,128)S(1)}, u32[]{:S(2)}, u32[]{:S(2)}) collective-permute-start(f32[8,128]{1,0:T(8,128)S(1)} %add.20), channel_id=1, source_target_pairs={{0,5},{1,4},{2,7},{3,6},{4,1},{5,0},{6,3},{7,2},{8,13},{9,12},{10,... | collective-permute-start | bytes 12296 | tf_op jit(solution)/shard_map/ppermute | solution.py:371
  73.5 3.0 %collective-permute-start.26 = (f32[8,128]{1,0:T(8,128)S(1)}, f32[8,128]{1,0:T(8,128)S(1)}, u32[]{:S(2)}, u32[]{:S(2)}) collective-permute-start(f32[8,128]{1,0:T(8,128)S(1)} %add.20), channel_id=1, source_target_pairs={{0,12},{1,13},{2,14},{3,15},{4,8},{5,9},{6,10},{7,11},{8,4},{9,5},... | collective-permute-start | bytes 12296 | tf_op jit(solution)/shard_map/ppermute | solution.py:371
  76.5 4.8 %collective-permute-start.31 = (f32[8,128]{1,0:T(8,128)S(1)}, f32[8,128]{1,0:T(8,128)S(1)}, u32[]{:S(2)}, u32[]{:S(2)}) collective-permute-start(f32[8,128]{1,0:T(8,128)S(1)} %add_add_fusion.refs_1_), channel_id=1, source_target_pairs={{0,22},{1,23},{2,20},{3,21},{4,18},{5,19},{6,16},{7,17},{8,30},{9,... | collective-permute-start | bytes 12296 | tf_op jit(solution)/shard_map/ppermute | solution.py:371
  77.6 3.9 %collective-permute-start.30 = (f32[8,128]{1,0:T(8,128)S(1)}, f32[8,128]{1,0:T(8,128)S(1)}, u32[]{:S(2)}, u32[]{:S(2)}) collective-permute-start(f32[8,128]{1,0:T(8,128)S(1)} %add_add_fusion.refs_1_), channel_id=1, source_target_pairs={{0,6},{1,7},{2,4},{3,5},{4,2},{5,3},{6,0},{7,1},{8,14},{9,15},{10,... | collective-permute-start | bytes 12296 | tf_op jit(solution)/shard_map/ppermute | solution.py:371
  79.7 3.0 %collective-permute-start.29 = (f32[8,128]{1,0:T(8,128)S(1)}, f32[8,128]{1,0:T(8,128)S(1)}, u32[]{:S(2)}, u32[]{:S(2)}) collective-permute-start(f32[8,128]{1,0:T(8,128)S(1)} %add_add_fusion.refs_1_), channel_id=1, source_target_pairs={{0,20},{1,21},{2,22},{3,23},{4,16},{5,17},{6,18},{7,19},{8,28},{9,... | collective-permute-start | bytes 12296 | tf_op jit(solution)/shard_map/ppermute | solution.py:371
